TPU v7x, 32 devices: a whole 2x2x4 slice. The times are simulated.
32 devices in a mesh: outer: 4 (over z), inner: 8 (over y, x, core).
Axes of the slice: x: 2, y: 2, z: 4, core: 2. Of those that a mesh axis runs over, the one named last changes fastest.
Arguments:
- queries: bfloat16 [32768, 1024], P(('outer', 'inner')), may hold values from -6 to 6
- keys: bfloat16 [32768, 1024], P(('outer', 'inner')), may hold values from -0.5 to 0.5
- values: bfloat16 [32768, 1024], P(('outer', 'inner')), may hold values from -6 to 6
- level_weights: float32 [16, 8, 32768], P(None, None, ('outer', 'inner')), as said below
- out_weight: bfloat16 [1024, 1024], replicated, may hold values from -0.046875 to 0.046875
Outputs:
- mixed: bfloat16 [32768, 1024], P(('outer', 'inner'))
Inputs may be any that keep to these rules, and one draw needn't show every extreme that they name: `level_weights`: every entry is positive.
All inputs are finite; a program needn't handle non-finite values.
Results may differ from a plain program's by a relative error of at most 0.0057.
Values sent between devices are 32-bit elements; how exact they have to be, the bound alone decides.
No kernel may reach another device: no remote copies, remote signals or barrier semaphores. Data moves between devices by JAX's collectives and lax.ppermute only.
A program may use at most 128 MiB of HBM per device.

v0:
```python
import functools

import jax
import jax.numpy as jnp
from jax import lax
from jax.experimental import pallas as pl
from jax.experimental.pallas import tpu as pltpu
from jax.sharding import PartitionSpec as P

HEADS = 8
HEAD = 128
LOCAL_BITS = 10
TILE = 128
CHUNK = 256
F32 = jnp.float32
BF16 = jnp.bfloat16
MIB = 1 << 20


def bits_of(count):
    return count.bit_length() - 1


def swap(block, axis, stride):
    count = lax.axis_size(axis)
    return lax.ppermute(block, axis, [(place, place ^ stride) for place in range(count)])


def raise_to(block, axis, stride):
    count = lax.axis_size(axis)
    route = [(place, place | stride) for place in range(count) if not place & stride]
    return lax.ppermute(block, axis, route)


def cost(flops, moved):
    return pl.CostEstimate(flops=flops, bytes_accessed=moved, transcendentals=0)


def params(limit):
    return pltpu.CompilerParams(vmem_limit_bytes=limit * MIB)


def product(left, right):
    return jnp.dot(left, right, preferred_element_type=F32)


def product_nt(left, right):
    return lax.dot_general(left, right, (((1,), (1,)), ((), ())), preferred_element_type=F32)


def identity(size):
    row = lax.broadcasted_iota(jnp.int32, (size, size), 0)
    column = lax.broadcasted_iota(jnp.int32, (size, size), 1)
    return (row == column).astype(F32).astype(BF16)


def turned(block):
    return product_nt(identity(block.shape[1]), block).astype(BF16)


def state_kernel(half, keys, values, state):
    flipped = turned(values[...])
    for low in range(0, keys.shape[1], HEAD):
        part = slice(low, low + HEAD)
        state[part, :] = product(flipped[part, :], keys[:, part])


def block_state(half, keys, values):
    tokens, width = keys.shape
    step = 2 * HEAD
    steps = width // 2 // step
    column = pl.BlockSpec((tokens, step), lambda pair, half: (0, half[0] * steps + pair))
    return pl.pallas_call(
        state_kernel,
        grid_spec=pltpu.PrefetchScalarGridSpec(
            num_scalar_prefetch=1,
            grid=(steps,),
            in_specs=[column, column],
            out_specs=pl.BlockSpec((step, HEAD), lambda pair, half: (pair, 0)),
        ),
        out_shape=jax.ShapeDtypeStruct((width // 2, HEAD), F32),
        cost_estimate=cost(tokens * width * HEAD, 3 * MIB),
        compiler_params=params(58),
    )(half, keys, values)


def tile_mixing(rows):
    target = lax.broadcasted_iota(jnp.int32, (8, TILE), 1)
    source = lax.broadcasted_iota(jnp.int32, (8, TILE), 0)
    rows = [jnp.broadcast_to(row, (8, TILE)) for row in rows]
    within = jnp.bitwise_and(target, 7)
    differ = jnp.bitwise_xor(within, source)
    base = rows[3]
    for level in (2, 1, 0):
        base = jnp.where(differ < 1 << level, rows[level], base)
    parts = [jnp.where(source <= within, base, 0.0)]
    for bit in range(3, bits_of(TILE)):
        upper = jnp.bitwise_and(jnp.right_shift(target, bit), 1) == 1
        parts = [jnp.where(upper, rows[bit + 1], part) for part in parts] + [
            jnp.where(upper, part, 0.0) for part in parts
        ]
    return jnp.concatenate(parts, axis=0)


def local_kernel(first_head, queries, keys, values, weights, local, rows):
    head = pl.program_id(0) + first_head
    tokens = queries.shape[0]
    flipped = turned(values[...])
    rows[...] = weights[:, pl.ds(head, 1), :].reshape(rows.shape)

    def row(level, low, size):
        return rows[level : level + 1, low : low + size]

    nodes = [None] * bits_of(tokens // CHUNK)
    top = bits_of(CHUNK)
    for chunk in range(tokens // CHUNK):
        low = chunk * CHUNK
        span = slice(low, low + CHUNK)
        query, key = queries[span, :], keys[span, :]
        scores = product_nt(key, query)
        lower, upper = (
            tile_mixing([row(level, start, TILE) for level in range(top)]) for start in (low, low + TILE)
        )
        across = row(top, low + TILE, TILE)
        weighted = jnp.concatenate(
            [
                jnp.concatenate([scores[:TILE, :TILE] * lower, scores[:TILE, TILE:] * across], axis=1),
                jnp.concatenate([jnp.zeros_like(lower), scores[TILE:, TILE:] * upper], axis=1),
            ],
            axis=0,
        ).astype(BF16)
        total = product(flipped[:, span], weighted)
        for bit in range(len(nodes)):
            if chunk >> bit & 1:
                total = total + row(top + 1 + bit, low, CHUNK) * product_nt(nodes[bit].astype(BF16), query)
        local[:, span] = total
        if chunk + 1 < tokens // CHUNK:
            carry = product(flipped[:, span], key)
            bit = 0
            while chunk >> bit & 1:
                carry = nodes[bit] + carry
                bit += 1
            nodes[bit] = carry


def local_part(half, queries, keys, values, level_weights):
    tokens, width = queries.shape
    heads = width // HEAD // 2
    column = pl.BlockSpec((tokens, HEAD), lambda head: (0, half * heads + head))
    return pl.pallas_call(
        functools.partial(local_kernel, half * heads),
        grid=(heads,),
        in_specs=[column, column, column, pl.BlockSpec(level_weights.shape, lambda head: (0, 0, 0))],
        out_specs=pl.BlockSpec((HEAD, tokens), lambda head: (head, 0)),
        out_shape=jax.ShapeDtypeStruct((width // 2, tokens), F32),
        scratch_shapes=[pltpu.VMEM((level_weights.shape[0], tokens), F32)],
        cost_estimate=cost(3 * tokens * width * HEAD, 6 * MIB),
        compiler_params=params(40),
    )(queries, keys, values, level_weights)


def has_bit(place, bit):
    return jnp.bitwise_and(jnp.right_shift(place, bit), 1) == 1


def fill(states, base, half, place, digit_place, first_digit, mine, other):
    chips, count, piece = mine.shape[:3]
    core = jnp.bitwise_and(place, 1)
    chip = jnp.right_shift(place, 1)
    for owner in range(chips):
        slot = jnp.bitwise_xor(chip, owner)
        low = base + owner * piece
        for bit in range(count):
            state = jnp.where(core == half, mine[slot, bit], other[slot, bit])
            state = jnp.where(has_bit(digit_place, first_digit + bit), state, 0.0)
            states[first_digit + bit, low : low + piece, :] = state.astype(BF16)


def near_kernel(half, heads, place, queries, weights, local, first_mine, first_other, mine, other, near, states, rows):
    step = pl.program_id(0)
    bits = states.shape[0]

    @pl.when(step == 0)
    def _():
        inner_place = place[0]
        first = jnp.where(jnp.bitwise_and(inner_place, 1) == half, first_mine[...], first_other[...])
        states[0] = jnp.where(has_bit(inner_place, 0), first, 0.0).astype(BF16)
        fill(states, 0, half, inner_place, inner_place, 1, mine, other)

    low = pl.multiple_of(step * HEAD, HEAD)
    rows[...] = weights[:, pl.ds(step + half * heads, 1), :].reshape(rows.shape)
    total = local[...]
    for bit in range(bits):
        level = LOCAL_BITS + 1 + bit
        row = rows[level : level + 1, :]
        total = total + row * product_nt(states[bit, pl.ds(low, HEAD), :], queries[...])
    near[...] = total


def near_part(half, bits, place, queries, level_weights, local, first_mine, first_other, mine, other):
    tokens, width = queries.shape
    heads = width // HEAD // 2
    column = pl.BlockSpec((tokens, HEAD), lambda head: (0, half * heads + head))
    band = pl.BlockSpec((HEAD, tokens), lambda head: (head, 0))
    fixed = [pl.BlockSpec(part.shape, lambda head, rank=part.ndim: (0,) * rank)
             for part in (first_mine, first_other, mine, other)]
    return pl.pallas_call(
        functools.partial(near_kernel, half, heads),
        grid=(heads,),
        in_specs=[
            pl.BlockSpec(memory_space=pltpu.SMEM),
            column,
            pl.BlockSpec(level_weights.shape, lambda head: (0, 0, 0)),
            band,
            *fixed,
        ],
        out_specs=band,
        out_shape=jax.ShapeDtypeStruct((width // 2, tokens), F32),
        scratch_shapes=[
            pltpu.VMEM((bits, width // 2, HEAD), BF16),
            pltpu.VMEM((level_weights.shape[0], tokens), F32),
        ],
        cost_estimate=cost(bits * tokens * width * HEAD, 8 * MIB),
        compiler_params=params(40),
    )(place, queries, level_weights, local, first_mine, first_other, mine, other)


def far_kernel(bits, first_level, place, queries, weights, lower, upper, *rest):
    arrived, (out_weight, mixed, states, flipped, attended) = rest[: 2 * bits], rest[2 * bits :]
    rows, width = attended.shape

    @pl.when(pl.program_id(0) == 0)
    def _():
        for half in range(2):
            for bit in range(bits):
                fill(states, half * (width // 2), half, place[0], place[1], bit, arrived[2 * bit], arrived[2 * bit + 1])

    for half, near in enumerate((lower, upper)):
        for low in range(0, width // 2, HEAD):
            part = slice(half * (width // 2) + low, half * (width // 2) + low + HEAD)
            head = part.start // HEAD
            total = near[low : low + HEAD, :]
            for bit in range(bits):
                row = weights[first_level + bit, head : head + 1, :]
                total = total + row * product_nt(states[bit, part, :], queries[:, part])
            flipped[part, :] = total.astype(BF16)
    unit = identity(rows)
    for low in range(0, width, CHUNK):
        attended[:, low : low + CHUNK] = product_nt(unit, flipped[low : low + CHUNK, :]).astype(BF16)
    mixed[...] = product(attended[...], out_weight[...]).astype(BF16)


def far_part(first_level, place, queries, level_weights, lower, upper, arrived, out_weight):
    tokens, width = queries.shape
    bits = len(arrived) // 2
    rows = min(CHUNK, tokens)
    band = pl.BlockSpec((rows, width), lambda step: (step, 0))
    near = pl.BlockSpec((width // 2, rows), lambda step: (0, step))
    fixed = pl.BlockSpec(arrived[0].shape, lambda step: (0, 0, 0, 0))
    return pl.pallas_call(
        functools.partial(far_kernel, bits, first_level),
        grid=(tokens // rows,),
        in_specs=[
            pl.BlockSpec(memory_space=pltpu.SMEM),
            band,
            pl.BlockSpec(level_weights.shape[:2] + (rows,), lambda step: (0, 0, step)),
            near,
            near,
            *[fixed] * (2 * bits),
            pl.BlockSpec(out_weight.shape, lambda step: (0, 0)),
        ],
        out_specs=band,
        out_shape=jax.ShapeDtypeStruct((tokens, width), BF16),
        scratch_shapes=[
            pltpu.VMEM((bits, width, HEAD), BF16),
            pltpu.VMEM((width, rows), BF16),
            pltpu.VMEM((rows, width), BF16),
        ],
        cost_estimate=cost(2 * tokens * width * (width + bits * HEAD), 12 * MIB),
        compiler_params=params(24),
    )(place, queries, level_weights, lower, upper, *arrived, out_weight)


def spread(block, chips):
    return [swap(block, "inner", 2 * step) for step in range(1, chips)]


def body(queries, keys, values, level_weights, out_weight):
    inner, outer = lax.axis_size("inner"), lax.axis_size("outer")
    inner_bits, outer_bits = bits_of(inner), bits_of(outer)
    inner_place, outer_place = lax.axis_index("inner"), lax.axis_index("outer")
    place = jnp.stack([inner_place, outer_place]).astype(jnp.int32)
    core, chip = jnp.bitwise_and(inner_place, 1), jnp.right_shift(inner_place, 1)
    chips = inner // 2
    half = keys.shape[1] // 2
    piece = half // chips
    tie = lax.optimization_barrier

    give = block_state((1 - core).reshape(1).astype(jnp.int32), keys, values)
    first_mine = swap(give, "inner", 1)
    keep = block_state(core.reshape(1).astype(jnp.int32), keys, values)

    def piece_of(owner):
        low = owner * piece
        return lax.dynamic_slice_in_dim(keep, low, piece, 0) + lax.dynamic_slice_in_dim(first_mine, low, piece, 0)

    parts = [piece_of(jnp.bitwise_xor(chip, step)) for step in range(chips)]
    inputs = (queries, keys, values, level_weights)
    parts, inputs, keep = tie((parts, inputs, keep))
    first_other = raise_to(keep, "inner", 1)
    sums = [parts[0]] + [swap(parts[step], "inner", 2 * step) for step in range(1, chips)]
    local = [local_part(0, *inputs)]
    sums, first_other, local[0] = tie((sums, first_other, local[0]))
    tree = [sums]
    while len(tree[-1]) > 1:
        tree.append([tree[-1][at] + tree[-1][at + 1] for at in range(0, len(tree[-1]), 2)])

    sent = [
        jnp.stack([tree[bit][(step >> bit) ^ 1] for bit in range(inner_bits - 1)]) for step in range(chips)
    ]
    running = tree[-1][0]
    running, sent, inputs = tie((running, sent, inputs))
    arrived = swap(running, "outer", 1)
    got = [sent[0]] + [swap(sent[step], "inner", 2 * step) for step in range(1, chips)]
    local.append(local_part(1, *inputs))
    arrived, got, local[1] = tie((arrived, got, local[1]))

    def near(part, near_mine, near_other):
        return near_part(
            part, inner_bits, place, queries, level_weights, local[part], first_mine, first_other, near_mine, near_other
        )

    far = [arrived]
    nears = []
    pieces = []
    for bit in range(1, outer_bits):
        running = running + arrived
        arrived = swap(running, "outer", 1 << bit)
        pieces.append([far[-1]] + spread(far[-1], chips))
        if bit == 1:
            near_mine = jnp.stack(got)
            near_other = swap(near_mine, "inner", 1)
            nears.append(near(0, near_mine, near_other))
            arrived, pieces, nears = tie((arrived, pieces, nears))
        far.append(arrived)
    if outer_bits == 1:
        near_mine = jnp.stack(got)
        near_other = swap(near_mine, "inner", 1)
    (far[-1], near_mine, pieces) = tie((far[-1], near_mine, pieces))
    last = spread(far[-1], chips)
    arrivals = []

    def collect(blocks):
        mine = jnp.stack(blocks)[:, None]
        return [mine, swap(mine, "inner", 1)]

    for blocks in pieces:
        arrivals += collect(blocks)
    for part in range(len(nears), 2):
        nears.append(near(part, near_mine, near_other))
    last, nears = tie((last, nears))
    arrivals += collect([far[-1]] + last)
    first_level = LOCAL_BITS + 1 + inner_bits
    return far_part(first_level, place, queries, level_weights, *nears, arrivals, out_weight)


def solution(mesh):
    spec = P(("outer", "inner"), None)
    in_specs = (spec, spec, spec, P(None, None, ("outer", "inner")), P())
    return jax.shard_map(body, mesh=mesh, in_specs=in_specs, out_specs=spec, check_vma=False)
```

profile of v0, /device:TPU:0, one launch (start us, length us, event | category | flops | bytes accessed | tf_op | source)
XLA Modules:
  0.0 61.2 jit_solution(12635087806503617550)
XLA Ops:
  0.0 2.9 %shard_map.56 = f32[512,128]{1,0:T(8,128)} custom-call(s32[1]{0:T(128)} %bitcast.3.half, bf16[1024,1024]{1,0:T(8,128)(2,1)} %keys.5, bf16[1024,1024]{1,0:T(8,128)(2,1)} %values.5), custom_call_target="tpu_custom_call" | custom-call | flops 134217728 | bytes 3145728 | tf_op jit(solution)/shard_map/pallas_call | solution.py:73
  2.9 0.5 collective-permute-start
  3.4 0.0 copy-start
  3.4 3.1 %shard_map.55 = f32[512,128]{1,0:T(8,128)} custom-call(s32[1]{0:T(128)} %bitcast.2.half, bf16[1024,1024]{1,0:T(8,128)(2,1)} %keys.5, bf16[1024,1024]{1,0:T(8,128)(2,1)} %values.5), custom_call_target="tpu_custom_call" | custom-call | flops 134217728 | bytes 3145728 | tf_op jit(solution)/shard_map/pallas_call | solution.py:73
  6.5 0.0 collective-permute-done.first_mine
  6.5 1.0 %dynamic-slice_add_fusion = (f32[128,128]{1,0:T(8,128)S(1)}, f32[128,128]{1,0:T(8,128)S(1)}, f32[128,128]{1,0:T(8,128)S(1)}, f32[128,128]{1,0:T(8,128)S(1)}) fusion(f32[512,128]{1,0:T(8,128)S(1)} %collective-permute-done.first_mine, s32[]{:T(128)S(6)} %select_n.19, f32[512,128]{1,0:T(8,128)} %shard_map.55, s32[]{:T(128)S(6)} %select_n.18, s32[]{:T(128)S(6)} %select_n.17, ...), kind=kLoop, calls=%fused_computation.9 | loop fusion | flops 65536 | bytes 786448 | tf_op jit(solution)/shard_map/add | solution.py:305
  7.4 2.0 %collective-permute-start.4 = (f32[512,128]{1,0:T(8,128)}, f32[512,128]{1,0:T(8,128)S(1)}, u32[]{:S(2)}, u32[]{:S(2)}) collective-permute-start(f32[512,128]{1,0:T(8,128)} %shard_map.55), channel_id=1, source_target_pairs={{0,1},{2,3},{4,5},{6,7},{8,9},{10,11},{12,13},{14,15},{16,17},{18,... | collective-permute-start | bytes 786440 | tf_op jit(solution)/shard_map/ppermute | solution.py:32
  9.4 3.0 %collective-permute-start.1 = (f32[128,128]{1,0:T(8,128)S(1)}, f32[128,128]{1,0:T(8,128)S(1)}, u32[]{:S(2)}, u32[]{:S(2)}) collective-permute-start(f32[128,128]{1,0:T(8,128)S(1)} %get-tuple-element.53), channel_id=1, source_target_pairs={{0,2},{1,3},{2,0},{3,1},{4,6},{5,7},{6,4},{7,5},{8,10},{9,11},{10,... | collective-permute-start | bytes 196616 | tf_op jit(solution)/shard_map/ppermute | solution.py:26
  12.4 1.5 %collective-permute-start.2 = (f32[128,128]{1,0:T(8,128)S(1)}, f32[128,128]{1,0:T(8,128)S(1)}, u32[]{:S(2)}, u32[]{:S(2)}) collective-permute-start(f32[128,128]{1,0:T(8,128)S(1)} %get-tuple-element.54), channel_id=1, source_target_pairs={{0,4},{1,5},{2,6},{3,7},{4,0},{5,1},{6,2},{7,3},{8,12},{9,13},{10,... | collective-permute-start | bytes 196616 | tf_op jit(solution)/shard_map/ppermute | solution.py:26
  13.9 0.0 collective-permute-start.3
  14.0 0.0 copy-done
  14.0 0.0 copy-done.1
  14.0 0.0 copy-done.3
  14.0 1.6 %copy-done.2 = bf16[1024,1024]{1,0:T(8,128)(2,1)S(1)} copy-done((bf16[1024,1024]{1,0:T(8,128)(2,1)S(1)}, bf16[1024,1024]{1,0:T(8,128)(2,1)}, u32[]{:S(2)}) %copy-start.2) | copy-done | bytes 2097176
  15.6 5.4 %shard_map.57.local = f32[512,1024]{1,0:T(8,128)S(1)} custom-call(bf16[1024,1024]{1,0:T(8,128)(2,1)S(1)} %copy-done, bf16[1024,1024]{1,0:T(8,128)(2,1)S(1)} %copy-done.1, bf16[1024,1024]{1,0:T(8,128)(2,1)S(1)} %copy-done.2, f32[16,8,1024]{2,1,0:T(8,128)S(1)} %copy-done.3), custom_call_target="tpu_custom_call" | custom-call | flops 402653184 | bytes 6291456 | tf_op jit(solution)/shard_map/pallas_call | solution.py:150
  21.0 0.0 copy-start.4
  21.0 0.0 collective-permute-done.1
  21.0 0.0 collective-permute-done.2
  21.1 0.0 collective-permute-done.3
  21.1 0.0 collective-permute-done.4.first_other
  21.1 0.0 copy-start.9
  21.2 2.0 %collective-permute-start.6 = (f32[2,128,128]{2,1,0:T(8,128)S(1)}, f32[2,128,128]{2,1,0:T(8,128)S(1)}, u32[]{:S(2)}, u32[]{:S(2)}) collective-permute-start(f32[2,128,128]{2,1,0:T(8,128)S(1)} %get-tuple-element.67), channel_id=1, source_target_pairs={{0,2},{1,3},{2,0},{3,1},{4,6},{5,7},{6,4},{7,5},{8,10},{9,11},{10,... | collective-permute-start | bytes 393224 | tf_op jit(solution)/shard_map/ppermute | solution.py:26
  23.1 1.5 %collective-permute-start.7 = (f32[2,128,128]{2,1,0:T(8,128)S(1)}, f32[2,128,128]{2,1,0:T(8,128)S(1)}, u32[]{:S(2)}, u32[]{:S(2)}) collective-permute-start(f32[2,128,128]{2,1,0:T(8,128)S(1)} %get-tuple-element.68), channel_id=1, source_target_pairs={{0,4},{1,5},{2,6},{3,7},{4,0},{5,1},{6,2},{7,3},{8,12},{9,13},{10,... | collective-permute-start | bytes 393224 | tf_op jit(solution)/shard_map/ppermute | solution.py:26
  24.7 0.1 collective-permute-start.8
  24.7 2.0 %collective-permute-start.5 = (f32[128,128]{1,0:T(8,128)S(1)}, f32[128,128]{1,0:T(8,128)S(1)}, u32[]{:S(2)}, u32[]{:S(2)}) collective-permute-start(f32[128,128]{1,0:T(8,128)S(1)} %get-tuple-element.65), channel_id=1, source_target_pairs={{0,8},{8,0},{16,24},{24,16},{1,9},{9,1},{17,25},{25,17},{2,10},{10... | collective-permute-start | bytes 196616 | tf_op jit(solution)/shard_map/ppermute | solution.py:26
  26.7 5.4 %shard_map.58.local = f32[512,1024]{1,0:T(8,128)S(1)} custom-call(bf16[1024,1024]{1,0:T(8,128)(2,1)S(1)} %copy-done, bf16[1024,1024]{1,0:T(8,128)(2,1)S(1)} %copy-done.1, bf16[1024,1024]{1,0:T(8,128)(2,1)S(1)} %copy-done.2, f32[16,8,1024]{2,1,0:T(8,128)S(1)} %copy-done.3), custom_call_target="tpu_custom_call" | custom-call | flops 402653184 | bytes 6291456 | tf_op jit(solution)/shard_map/pallas_call | solution.py:150
  32.2 0.0 copy-done.4
  32.2 0.0 copy-done.9
  32.2 0.0 copy-start.6
  32.2 1.3 %copy-done.6 = f32[512,1024]{1,0:T(8,128)} copy-done((f32[512,1024]{1,0:T(8,128)}, f32[512,1024]{1,0:T(8,128)S(1)}, u32[]{:S(2)}) %copy-start.6) | copy-done | bytes 2097176
  33.5 0.0 collective-permute-done.5
  33.5 0.0 collective-permute-done.6
  33.5 0.0 collective-permute-done.7
  33.5 0.0 collective-permute-done.8
  33.6 0.1 collective-permute-start.13
  33.7 2.5 %collective-permute-start.12 = (f32[128,128]{1,0:T(8,128)S(1)}, f32[128,128]{1,0:T(8,128)S(1)}, u32[]{:S(2)}, u32[]{:S(2)}) collective-permute-start(f32[128,128]{1,0:T(8,128)S(1)} %collective-permute-done.5), channel_id=1, source_target_pairs={{0,6},{1,7},{2,4},{3,5},{4,2},{5,3},{6,0},{7,1},{8,14},{9,15},{10,... | collective-permute-start | bytes 196616 | tf_op jit(solution)/shard_map/ppermute | solution.py:26
  36.2 0.5 collective-permute-start.11
  36.7 0.5 collective-permute-start.10
  37.3 2.6 %collective-permute-start.9 = (f32[128,128]{1,0:T(8,128)S(1)}, f32[128,128]{1,0:T(8,128)S(1)}, u32[]{:S(2)}, u32[]{:S(2)}) collective-permute-start(f32[128,128]{1,0:T(8,128)S(1)} %add.51), channel_id=1, source_target_pairs={{0,16},{8,24},{16,0},{24,8},{1,17},{9,25},{17,1},{25,9},{2,18},{10... | collective-permute-start | bytes 196616 | tf_op jit(solution)/shard_map/ppermute | solution.py:26
  39.8 0.1 pad_add_fusion.place
  39.9 0.0 collective-permute-done.13.other
  39.9 1.6 %copy-done.5 = f32[512,1024]{1,0:T(8,128)S(1)} copy-done((f32[512,1024]{1,0:T(8,128)S(1)}, f32[512,1024]{1,0:T(8,128)}, u32[]{:S(2)}) %copy-start.5) | copy-done | bytes 2097176
  41.5 0.9 %copy-done.10 = f32[512,128]{1,0:T(8,128)S(1)} copy-done((f32[512,128]{1,0:T(8,128)S(1)}, f32[512,128]{1,0:T(8,128)}, u32[]{:S(2)}) %copy-start.10) | copy-done | bytes 262168
  42.5 3.1 %shard_map.59.lower = f32[512,1024]{1,0:T(8,128)S(1)} custom-call(s32[2]{0:T(128)S(1)} %pad_add_fusion.place, bf16[1024,1024]{1,0:T(8,128)(2,1)S(1)} %copy-done, f32[16,8,1024]{2,1,0:T(8,128)S(1)} %copy-done.3, f32[512,1024]{1,0:T(8,128)S(1)} %copy-done.5, f32[512,128]{1,0:T(8,128)S(1)} %collective-permute-done.first_mine, f32[512,128]{1,0:T(8,128)S(1)} %copy-done.10, ...), custom_call_target="tpu_custom_call" | custom-call | flops 402653184 | bytes 8388608 | tf_op jit(solution)/shard_map/pallas_call | solution.py:207
  45.6 0.0 collective-permute-done.9
  45.6 0.0 collective-permute-done.12
  45.6 0.0 collective-permute-done.11
  45.6 0.0 collective-permute-done.10
  45.6 2.5 %collective-permute-start.16 = (f32[128,128]{1,0:T(8,128)S(1)}, f32[128,128]{1,0:T(8,128)S(1)}, u32[]{:S(2)}, u32[]{:S(2)}) collective-permute-start(f32[128,128]{1,0:T(8,128)S(1)} %collective-permute-done.9), channel_id=1, source_target_pairs={{0,6},{1,7},{2,4},{3,5},{4,2},{5,3},{6,0},{7,1},{8,14},{9,15},{10,... | collective-permute-start | bytes 196616 | tf_op jit(solution)/shard_map/ppermute | solution.py:26
  48.1 0.5 collective-permute-start.15
  48.7 0.5 collective-permute-start.14
  49.2 0.0 copy-start.8
  49.2 0.1 collective-permute-start.17
  49.3 0.0 copy-done.7
  49.3 0.0 copy-done.11
  49.3 3.1 %shard_map.60.upper = f32[512,1024]{1,0:T(8,128)S(1)} custom-call(s32[2]{0:T(128)S(1)} %pad_add_fusion.place, bf16[1024,1024]{1,0:T(8,128)(2,1)S(1)} %copy-done, f32[16,8,1024]{2,1,0:T(8,128)S(1)} %copy-done.3, f32[512,1024]{1,0:T(8,128)S(1)} %copy-done.7, f32[512,128]{1,0:T(8,128)S(1)} %collective-permute-done.first_mine, f32[512,128]{1,0:T(8,128)S(1)} %copy-done.11, ...), custom_call_target="tpu_custom_call" | custom-call | flops 402653184 | bytes 8388608 | tf_op jit(solution)/shard_map/pallas_call | solution.py:207
  52.4 0.0 collective-permute-done.16
  52.5 0.0 collective-permute-done.15
  52.5 0.5 collective-permute-done.14
  52.9 0.1 collective-permute-start.18
  53.0 0.0 collective-permute-done.17
  53.0 1.5 %collective-permute-done.18.rest_3_ = f32[4,1,128,128]{3,2,1,0:T(8,128)S(1)} collective-permute-done((f32[4,1,128,128]{3,2,1,0:T(8,128)S(1)}, f32[4,1,128,128]{3,2,1,0:T(8,128)S(1)}, u32[]{:S(2)}, u32[]{:S(2)}) %collective-permute-start.18) | collective-permute-done | bytes 262176 | tf_op jit(solution)/shard_map/ppermute | solution.py:26
  54.5 0.0 copy-done.8
  54.5 6.6 %shard_map.61 = bf16[1024,1024]{1,0:T(8,128)(2,1)} custom-call(s32[2]{0:T(128)S(1)} %pad_add_fusion.place, bf16[1024,1024]{1,0:T(8,128)(2,1)S(1)} %copy-done, f32[16,8,1024]{2,1,0:T(8,128)S(1)} %copy-done.3, f32[512,1024]{1,0:T(8,128)S(1)} %shard_map.59.lower, f32[512,1024]{1,0:T(8,128)S(1)} %shard_map.60.upper, ...), custom_call_target="tpu_custom_call" | custom-call | flops 2684354560 | bytes 12582912 | tf_op jit(solution)/shard_map/pallas_call | solution.py:260
  (13 shorter events, 0.2 us)
Async XLA Ops:
  2.9 3.5 %collective-permute-start = (f32[512,128]{1,0:T(8,128)}, f32[512,128]{1,0:T(8,128)S(1)}, u32[]{:S(2)}, u32[]{:S(2)}) collective-permute-start(f32[512,128]{1,0:T(8,128)} %shard_map.56), channel_id=1, source_target_pairs={{0,1},{1,0},{2,3},{3,2},{4,5},{5,4},{6,7},{7,6},{8,9},{9,8},{10,11... | collective-permute-start | bytes 786440 | tf_op jit(solution)/shard_map/ppermute | solution.py:26
  3.4 10.6 %copy-start = (bf16[1024,1024]{1,0:T(8,128)(2,1)S(1)}, bf16[1024,1024]{1,0:T(8,128)(2,1)}, u32[]{:S(2)}) copy-start(bf16[1024,1024]{1,0:T(8,128)(2,1)} %queries.7) | copy-start | bytes 6291460
  3.4 10.6 %copy-start.1 = (bf16[1024,1024]{1,0:T(8,128)(2,1)S(1)}, bf16[1024,1024]{1,0:T(8,128)(2,1)}, u32[]{:S(2)}) copy-start(bf16[1024,1024]{1,0:T(8,128)(2,1)} %keys.5) | copy-start | bytes 6291460
  3.4 10.6 %copy-start.3 = (f32[16,8,1024]{2,1,0:T(8,128)S(1)}, f32[16,8,1024]{2,1,0:T(8,128)}, u32[]{:S(2)}) copy-start(f32[16,8,1024]{2,1,0:T(8,128)} %weights.7) | copy-start | bytes 1572868
  7.4 13.6 %collective-permute-start.4 = (f32[512,128]{1,0:T(8,128)}, f32[512,128]{1,0:T(8,128)S(1)}, u32[]{:S(2)}, u32[]{:S(2)}) collective-permute-start(f32[512,128]{1,0:T(8,128)} %shard_map.55), channel_id=1, source_target_pairs={{0,1},{2,3},{4,5},{6,7},{8,9},{10,11},{12,13},{14,15},{16,17},{18,... | collective-permute-start | bytes 786440 | tf_op jit(solution)/shard_map/ppermute | solution.py:32
  9.4 11.6 %collective-permute-start.1 = (f32[128,128]{1,0:T(8,128)S(1)}, f32[128,128]{1,0:T(8,128)S(1)}, u32[]{:S(2)}, u32[]{:S(2)}) collective-permute-start(f32[128,128]{1,0:T(8,128)S(1)} %get-tuple-element.53), channel_id=1, source_target_pairs={{0,2},{1,3},{2,0},{3,1},{4,6},{5,7},{6,4},{7,5},{8,10},{9,11},{10,... | collective-permute-start | bytes 196616 | tf_op jit(solution)/shard_map/ppermute | solution.py:26
  12.4 8.6 %collective-permute-start.2 = (f32[128,128]{1,0:T(8,128)S(1)}, f32[128,128]{1,0:T(8,128)S(1)}, u32[]{:S(2)}, u32[]{:S(2)}) collective-permute-start(f32[128,128]{1,0:T(8,128)S(1)} %get-tuple-element.54), channel_id=1, source_target_pairs={{0,4},{1,5},{2,6},{3,7},{4,0},{5,1},{6,2},{7,3},{8,12},{9,13},{10,... | collective-permute-start | bytes 196616 | tf_op jit(solution)/shard_map/ppermute | solution.py:26
  13.9 7.1 %collective-permute-start.3 = (f32[128,128]{1,0:T(8,128)S(1)}, f32[128,128]{1,0:T(8,128)S(1)}, u32[]{:S(2)}, u32[]{:S(2)}) collective-permute-start(f32[128,128]{1,0:T(8,128)S(1)} %get-tuple-element.55), channel_id=1, source_target_pairs={{0,6},{1,7},{2,4},{3,5},{4,2},{5,3},{6,0},{7,1},{8,14},{9,15},{10,... | collective-permute-start | bytes 196616 | tf_op jit(solution)/shard_map/ppermute | solution.py:26
  14.0 1.6 %copy-start.2 = (bf16[1024,1024]{1,0:T(8,128)(2,1)S(1)}, bf16[1024,1024]{1,0:T(8,128)(2,1)}, u32[]{:S(2)}) copy-start(bf16[1024,1024]{1,0:T(8,128)(2,1)} %values.5) | copy-start | bytes 6291460
  21.0 11.1 %copy-start.4 = (f32[512,1024]{1,0:T(8,128)}, f32[512,1024]{1,0:T(8,128)S(1)}, u32[]{:S(2)}) copy-start(f32[512,1024]{1,0:T(8,128)S(1)} %shard_map.57.local) | copy-start | bytes 6291460
  21.1 11.1 %copy-start.9 = (f32[512,128]{1,0:T(8,128)}, f32[512,128]{1,0:T(8,128)S(1)}, u32[]{:S(2)}) copy-start(f32[512,128]{1,0:T(8,128)S(1)} %collective-permute-done.4.first_other) | copy-start | bytes 786436
  21.2 12.4 %collective-permute-start.6 = (f32[2,128,128]{2,1,0:T(8,128)S(1)}, f32[2,128,128]{2,1,0:T(8,128)S(1)}, u32[]{:S(2)}, u32[]{:S(2)}) collective-permute-start(f32[2,128,128]{2,1,0:T(8,128)S(1)} %get-tuple-element.67), channel_id=1, source_target_pairs={{0,2},{1,3},{2,0},{3,1},{4,6},{5,7},{6,4},{7,5},{8,10},{9,11},{10,... | collective-permute-start | bytes 393224 | tf_op jit(solution)/shard_map/ppermute | solution.py:26
  23.1 10.4 %collective-permute-start.7 = (f32[2,128,128]{2,1,0:T(8,128)S(1)}, f32[2,128,128]{2,1,0:T(8,128)S(1)}, u32[]{:S(2)}, u32[]{:S(2)}) collective-permute-start(f32[2,128,128]{2,1,0:T(8,128)S(1)} %get-tuple-element.68), channel_id=1, source_target_pairs={{0,4},{1,5},{2,6},{3,7},{4,0},{5,1},{6,2},{7,3},{8,12},{9,13},{10,... | collective-permute-start | bytes 393224 | tf_op jit(solution)/shard_map/ppermute | solution.py:26
  24.7 8.9 %collective-permute-start.8 = (f32[2,128,128]{2,1,0:T(8,128)S(1)}, f32[2,128,128]{2,1,0:T(8,128)S(1)}, u32[]{:S(2)}, u32[]{:S(2)}) collective-permute-start(f32[2,128,128]{2,1,0:T(8,128)S(1)} %get-tuple-element.69), channel_id=1, source_target_pairs={{0,6},{1,7},{2,4},{3,5},{4,2},{5,3},{6,0},{7,1},{8,14},{9,15},{10,... | collective-permute-start | bytes 393224 | tf_op jit(solution)/shard_map/ppermute | solution.py:26
  24.7 8.8 %collective-permute-start.5 = (f32[128,128]{1,0:T(8,128)S(1)}, f32[128,128]{1,0:T(8,128)S(1)}, u32[]{:S(2)}, u32[]{:S(2)}) collective-permute-start(f32[128,128]{1,0:T(8,128)S(1)} %get-tuple-element.65), channel_id=1, source_target_pairs={{0,8},{8,0},{16,24},{24,16},{1,9},{9,1},{17,25},{25,17},{2,10},{10... | collective-permute-start | bytes 196616 | tf_op jit(solution)/shard_map/ppermute | solution.py:26
  32.2 1.4 %copy-start.6 = (f32[512,1024]{1,0:T(8,128)}, f32[512,1024]{1,0:T(8,128)S(1)}, u32[]{:S(2)}) copy-start(f32[512,1024]{1,0:T(8,128)S(1)} %shard_map.58.local) | copy-start | bytes 6291460
  33.6 6.3 %collective-permute-start.13 = (f32[4,2,128,128]{3,2,1,0:T(8,128)S(1)}, f32[4,2,128,128]{3,2,1,0:T(8,128)}, u32[]{:S(2)}, u32[]{:S(2)}) collective-permute-start(f32[4,2,128,128]{3,2,1,0:T(8,128)S(1)} %pad_maximum_fusion.mine), channel_id=1, source_target_pairs={{0,1},{1,0},{2,3},{3,2},{4,5},{5,4},{6,7},{7,6},{8,9},{9,8},{10,11... | collective-permute-start | bytes 1572872 | tf_op jit(solution)/shard_map/ppermute | solution.py:26
  33.7 11.9 %collective-permute-start.12 = (f32[128,128]{1,0:T(8,128)S(1)}, f32[128,128]{1,0:T(8,128)S(1)}, u32[]{:S(2)}, u32[]{:S(2)}) collective-permute-start(f32[128,128]{1,0:T(8,128)S(1)} %collective-permute-done.5), channel_id=1, source_target_pairs={{0,6},{1,7},{2,4},{3,5},{4,2},{5,3},{6,0},{7,1},{8,14},{9,15},{10,... | collective-permute-start | bytes 196616 | tf_op jit(solution)/shard_map/ppermute | solution.py:26
  36.2 9.4 %collective-permute-start.11 = (f32[128,128]{1,0:T(8,128)S(1)}, f32[128,128]{1,0:T(8,128)S(1)}, u32[]{:S(2)}, u32[]{:S(2)}) collective-permute-start(f32[128,128]{1,0:T(8,128)S(1)} %collective-permute-done.5), channel_id=1, source_target_pairs={{0,4},{1,5},{2,6},{3,7},{4,0},{5,1},{6,2},{7,3},{8,12},{9,13},{10,... | collective-permute-start | bytes 196616 | tf_op jit(solution)/shard_map/ppermute | solution.py:26
  36.7 8.9 %collective-permute-start.10 = (f32[128,128]{1,0:T(8,128)S(1)}, f32[128,128]{1,0:T(8,128)S(1)}, u32[]{:S(2)}, u32[]{:S(2)}) collective-permute-start(f32[128,128]{1,0:T(8,128)S(1)} %collective-permute-done.5), channel_id=1, source_target_pairs={{0,2},{1,3},{2,0},{3,1},{4,6},{5,7},{6,4},{7,5},{8,10},{9,11},{10,... | collective-permute-start | bytes 196616 | tf_op jit(solution)/shard_map/ppermute | solution.py:26
  37.3 8.3 %collective-permute-start.9 = (f32[128,128]{1,0:T(8,128)S(1)}, f32[128,128]{1,0:T(8,128)S(1)}, u32[]{:S(2)}, u32[]{:S(2)}) collective-permute-start(f32[128,128]{1,0:T(8,128)S(1)} %add.51), channel_id=1, source_target_pairs={{0,16},{8,24},{16,0},{24,8},{1,17},{9,25},{17,1},{25,9},{2,18},{10... | collective-permute-start | bytes 196616 | tf_op jit(solution)/shard_map/ppermute | solution.py:26
  39.9 1.6 %copy-start.5 = (f32[512,1024]{1,0:T(8,128)S(1)}, f32[512,1024]{1,0:T(8,128)}, u32[]{:S(2)}) copy-start(f32[512,1024]{1,0:T(8,128)} %copy-done.4) | copy-start | bytes 6291460
  41.5 0.9 %copy-start.10 = (f32[512,128]{1,0:T(8,128)S(1)}, f32[512,128]{1,0:T(8,128)}, u32[]{:S(2)}) copy-start(f32[512,128]{1,0:T(8,128)} %copy-done.9) | copy-start | bytes 786436
  42.5 6.9 %copy-start.7 = (f32[512,1024]{1,0:T(8,128)S(1)}, f32[512,1024]{1,0:T(8,128)}, u32[]{:S(2)}) copy-start(f32[512,1024]{1,0:T(8,128)} %copy-done.6) | copy-start | bytes 6291460
  42.5 6.9 %copy-start.11 = (f32[512,128]{1,0:T(8,128)S(1)}, f32[512,128]{1,0:T(8,128)}, u32[]{:S(2)}) copy-start(f32[512,128]{1,0:T(8,128)} %copy-done.9) | copy-start | bytes 786436
  45.6 6.8 %collective-permute-start.16 = (f32[128,128]{1,0:T(8,128)S(1)}, f32[128,128]{1,0:T(8,128)S(1)}, u32[]{:S(2)}, u32[]{:S(2)}) collective-permute-start(f32[128,128]{1,0:T(8,128)S(1)} %collective-permute-done.9), channel_id=1, source_target_pairs={{0,6},{1,7},{2,4},{3,5},{4,2},{5,3},{6,0},{7,1},{8,14},{9,15},{10,... | collective-permute-start | bytes 196616 | tf_op jit(solution)/shard_map/ppermute | solution.py:26
  48.1 4.3 %collective-permute-start.15 = (f32[128,128]{1,0:T(8,128)S(1)}, f32[128,128]{1,0:T(8,128)S(1)}, u32[]{:S(2)}, u32[]{:S(2)}) collective-permute-start(f32[128,128]{1,0:T(8,128)S(1)} %collective-permute-done.9), channel_id=1, source_target_pairs={{0,4},{1,5},{2,6},{3,7},{4,0},{5,1},{6,2},{7,3},{8,12},{9,13},{10,... | collective-permute-start | bytes 196616 | tf_op jit(solution)/shard_map/ppermute | solution.py:26
  48.7 4.3 %collective-permute-start.14 = (f32[128,128]{1,0:T(8,128)S(1)}, f32[128,128]{1,0:T(8,128)S(1)}, u32[]{:S(2)}, u32[]{:S(2)}) collective-permute-start(f32[128,128]{1,0:T(8,128)S(1)} %collective-permute-done.9), channel_id=1, source_target_pairs={{0,2},{1,3},{2,0},{3,1},{4,6},{5,7},{6,4},{7,5},{8,10},{9,11},{10,... | collective-permute-start | bytes 196616 | tf_op jit(solution)/shard_map/ppermute | solution.py:26
  49.2 5.3 %copy-start.8 = (bf16[1024,1024]{1,0:T(8,128)(2,1)S(1)}, bf16[1024,1024]{1,0:T(8,128)(2,1)}, u32[]{:S(2)}) copy-start(bf16[1024,1024]{1,0:T(8,128)(2,1)} %rest_4_.1) | copy-start | bytes 6291460
  49.2 3.8 %collective-permute-start.17 = (f32[4,1,128,128]{3,2,0,1:T(8,128)S(1)}, f32[4,1,128,128]{3,2,0,1:T(8,128)S(1)}, u32[]{:S(2)}, u32[]{:S(2)}) collective-permute-start(f32[4,1,128,128]{3,2,0,1:T(8,128)S(1)} %get-tuple-element.103), channel_id=1, source_target_pairs={{0,1},{1,0},{2,3},{3,2},{4,5},{5,4},{6,7},{7,6},{8,9},{9,8},{10,11... | collective-permute-start | bytes 786440 | tf_op jit(solution)/shard_map/ppermute | solution.py:26
  52.9 1.6 %collective-permute-start.18 = (f32[4,1,128,128]{3,2,1,0:T(8,128)S(1)}, f32[4,1,128,128]{3,2,1,0:T(8,128)S(1)}, u32[]{:S(2)}, u32[]{:S(2)}) collective-permute-start(f32[4,1,128,128]{3,2,1,0:T(8,128)S(1)} %maximum_bitcast_fusion.rest_2_), channel_id=1, source_target_pairs={{0,1},{1,0},{2,3},{3,2},{4,5},{5,4},{6,7},{7,6},{8,9},{9,8},{10,11... | collective-permute-start | bytes 786440 | tf_op jit(solution)/shard_map/ppermute | solution.py:26
where the time goes:
time: 61.5 us; the launch traced here: 61.2 us
  Pallas kernels  29.7 us (48%)
  starting transfers between devices  22.4 us (36%)
  local copies, waits for them, and re-layouts  5.51 us (9%)
  waiting for transfers between devices  2.01 us (3%)
  other arithmetic  1.2 us (2%)
    ppermute x18, starting transfers between devices, swap(): lax.ppermute(block, axis, [(place, place ^ stride) for place in range(cou...  20.5 us
    pallas_call x2, Pallas kernels, local_part(): pl.pallas_call(functools.partial(local_kernel, half * heads), grid=(heads...  10.9 us
    pallas_call x1, Pallas kernels, far_part(): pl.pallas_call(functools.partial(far_kernel, bits, first_level), grid=(to...  6.61 us
    pallas_call x2, Pallas kernels, near_part(): pl.pallas_call(functools.partial(near_kernel, half, heads), grid=(heads,)...  6.21 us
    pallas_call x2, Pallas kernels, block_state(): pl.pallas_call(state_kernel, grid_spec=pltpu.PrefetchScalarGridSpec(num_s...  6 us
    unnamed x24, local copies, waits for them, and re-layouts  5.51 us
    ppermute x18, waiting for transfers between devices, swap(): lax.ppermute(block, axis, [(place, place ^ stride) for place in range(cou...  2.01 us
    ppermute x1, starting transfers between devices, raise_to(): return lax.ppermute(block, axis, route)  1.97 us
  transfers between devices with their start and end apart: 19, of which 2 were waited for; matrix products, arithmetic and copies ran while one was open for 0% of the time, Pallas kernels for 33%

commit v1 on v0

v1 whole, which is shorter than its diff:
```python
import functools

import jax
import jax.numpy as jnp
from jax import lax
from jax.experimental import pallas as pl
from jax.experimental.pallas import tpu as pltpu
from jax.sharding import PartitionSpec as P

HEADS = 8
HEAD = 128
LOCAL_BITS = 10
TILE = 128
CHUNK = 256
F32 = jnp.float32
BF16 = jnp.bfloat16
MIB = 1 << 20


def bits_of(count):
    return count.bit_length() - 1


def swap(block, axis, stride):
    count = lax.axis_size(axis)
    return lax.ppermute(block, axis, [(place, place ^ stride) for place in range(count)])


def raise_to(block, axis, stride):
    count = lax.axis_size(axis)
    route = [(place, place | stride) for place in range(count) if not place & stride]
    return lax.ppermute(block, axis, route)


def cost(flops, moved):
    return pl.CostEstimate(flops=flops, bytes_accessed=moved, transcendentals=0)


def params(limit):
    return pltpu.CompilerParams(vmem_limit_bytes=limit * MIB)


def product(left, right):
    return jnp.dot(left, right, preferred_element_type=F32)


def product_nt(left, right):
    return lax.dot_general(left, right, (((1,), (1,)), ((), ())), preferred_element_type=F32)


def identity(size):
    row = lax.broadcasted_iota(jnp.int32, (size, size), 0)
    column = lax.broadcasted_iota(jnp.int32, (size, size), 1)
    return (row == column).astype(F32).astype(BF16)


def turned(block):
    return product_nt(identity(block.shape[1]), block).astype(BF16)


def state_kernel(half, keys, values, state):
    both = product(turned(values[...]), keys[...])
    for low in range(0, keys.shape[1], HEAD):
        part = slice(low, low + HEAD)
        state[part, :] = both[part, part]


def block_state(half, keys, values):
    tokens, width = keys.shape
    step = 2 * HEAD
    steps = width // 2 // step
    column = pl.BlockSpec((tokens, step), lambda pair, half: (0, half[0] * steps + pair))
    return pl.pallas_call(
        state_kernel,
        grid_spec=pltpu.PrefetchScalarGridSpec(
            num_scalar_prefetch=1,
            grid=(steps,),
            in_specs=[column, column],
            out_specs=pl.BlockSpec((step, HEAD), lambda pair, half: (pair, 0)),
        ),
        out_shape=jax.ShapeDtypeStruct((width // 2, HEAD), F32),
        cost_estimate=cost(tokens * width * HEAD, 3 * MIB),
        compiler_params=params(58),
    )(half, keys, values)


def tile_mixing(rows):
    target = lax.broadcasted_iota(jnp.int32, (8, TILE), 1)
    source = lax.broadcasted_iota(jnp.int32, (8, TILE), 0)
    rows = [jnp.broadcast_to(row, (8, TILE)) for row in rows]
    within = jnp.bitwise_and(target, 7)
    differ = jnp.bitwise_xor(within, source)
    base = rows[3]
    for level in (2, 1, 0):
        base = jnp.where(differ < 1 << level, rows[level], base)
    parts = [jnp.where(source <= within, base, 0.0)]
    for bit in range(3, bits_of(TILE)):
        upper = jnp.bitwise_and(jnp.right_shift(target, bit), 1) == 1
        parts = [jnp.where(upper, rows[bit + 1], part) for part in parts] + [
            jnp.where(upper, part, 0.0) for part in parts
        ]
    return jnp.concatenate(parts, axis=0)


def local_kernel(first_head, queries, keys, values, weights, local, rows):
    tokens, width = queries.shape
    chunks = tokens // CHUNK
    levels = rows.shape[1]
    top = bits_of(CHUNK)
    spans = [slice(low, low + CHUNK) for low in range(0, tokens, CHUNK)]
    parts = [slice(low, low + HEAD) for low in range(0, width, HEAD)]
    first = first_head + pl.program_id(0) * len(parts)
    for at in range(len(parts)):
        rows[at] = weights[:, pl.ds(first + at, 1), :].reshape(levels, tokens)
    flipped = turned(values[...])

    def row(at, level, low, size):
        return rows[at, level : level + 1, low : low + size]

    nodes = []
    for part in parts:
        line = [product(flipped[part, span], keys[span, part]) for span in spans[:-1]]
        known = [line]
        while len(known[-1]) > 1:
            below = known[-1]
            known.append([below[at] + below[at + 1] for at in range(0, len(below) - 1, 2)])
        nodes.append([[state.astype(BF16) for state in level] for level in known])
    scores = {}
    for at, part in enumerate(parts):
        for chunk, span in enumerate(spans):
            used = [bit for bit in range(bits_of(chunks)) if chunk >> bit & 1]
            left = [keys[span, part]] + [nodes[at][bit][(chunk >> bit) - 1] for bit in used]
            left = jnp.concatenate(left, axis=0) if used else left[0]
            scores[at, chunk] = product_nt(left, queries[span, part])
    for at, part in enumerate(parts):
        for chunk, span in enumerate(spans):
            low = chunk * CHUNK
            score = scores[at, chunk]
            lower, upper = (
                tile_mixing([row(at, level, start, TILE) for level in range(top)]) for start in (low, low + TILE)
            )
            across = row(at, top, low + TILE, TILE)
            weighted = jnp.concatenate(
                [
                    jnp.concatenate([score[:TILE, :TILE] * lower, score[:TILE, TILE:] * across], axis=1),
                    jnp.concatenate([jnp.zeros_like(lower), score[TILE:CHUNK, TILE:] * upper], axis=1),
                ],
                axis=0,
            ).astype(BF16)
            total = product(flipped[part, span], weighted)
            below = CHUNK
            for bit in range(bits_of(chunks)):
                if chunk >> bit & 1:
                    total = total + row(at, top + 1 + bit, low, CHUNK) * score[below : below + HEAD, :]
                    below += HEAD
            local[part, span] = total


def local_part(half, queries, keys, values, level_weights):
    tokens, width = queries.shape
    step = 2 * HEAD
    steps = width // step // 2
    column = pl.BlockSpec((tokens, step), lambda pair: (0, half * steps + pair))
    return pl.pallas_call(
        functools.partial(local_kernel, half * steps * 2),
        grid=(steps,),
        in_specs=[column, column, column, pl.BlockSpec(level_weights.shape, lambda pair: (0, 0, 0))],
        out_specs=pl.BlockSpec((step, tokens), lambda pair: (pair, 0)),
        out_shape=jax.ShapeDtypeStruct((width // 2, tokens), F32),
        scratch_shapes=[pltpu.VMEM((2, level_weights.shape[0], tokens), F32)],
        cost_estimate=cost(3 * tokens * width * HEAD, 6 * MIB),
        compiler_params=params(40),
    )(queries, keys, values, level_weights)


def has_bit(place, bit):
    return jnp.bitwise_and(jnp.right_shift(place, bit), 1) == 1


def fill(states, base, half, place, digit_place, first_digit, mine, other, first=None):
    core = jnp.bitwise_and(place, 1)
    side = jnp.bitwise_and(jnp.right_shift(place, 1), 1)
    count, quarters, size = mine.shape[:3]
    for quarter in range(quarters):
        slot = jnp.bitwise_xor(side, quarter)
        for bit in range(count):
            if first is not None and bit == 0:
                here, there = first[quarter * size : (quarter + 1) * size, :], other[0, quarter]
            else:
                here, there = mine[bit, slot], other[bit, slot]
            state = jnp.where(core == half, here, there)
            state = jnp.where(has_bit(digit_place, first_digit + bit), state, 0.0).astype(BF16)
            for at in range(0, size, HEAD):
                head = (base + quarter * size + at) // HEAD
                low = (first_digit + bit) * HEAD
                states[head, low : low + HEAD, :] = state[at : at + HEAD]


def near_kernel(half, heads, place, queries, weights, local, first, mine, other, near, states, rows):
    step = pl.program_id(0)
    bits = states.shape[1] // HEAD

    @pl.when(step == 0)
    def _():
        fill(states, 0, half, place[0], place[0], 0, mine, other, first)

    for at in range(rows.shape[0]):
        part = slice(at * HEAD, (at + 1) * HEAD)
        head = step * rows.shape[0] + at
        rows[at] = weights[:, pl.ds(half * heads + head, 1), :].reshape(rows.shape[1:])
        products = product_nt(states[head], queries[:, part])
        total = local[part, :]
        for bit in range(bits):
            level = LOCAL_BITS + 1 + bit
            total = total + rows[at, level : level + 1, :] * products[bit * HEAD : (bit + 1) * HEAD]
        near[part, :] = total


def near_part(half, bits, place, queries, level_weights, local, first, mine, other):
    tokens, width = queries.shape
    heads = width // HEAD // 2
    step = 2 * HEAD
    steps = width // step // 2
    column = pl.BlockSpec((tokens, step), lambda pair: (0, half * steps + pair))
    band = pl.BlockSpec((step, tokens), lambda pair: (pair, 0))
    fixed = [pl.BlockSpec(part.shape, lambda pair, rank=part.ndim: (0,) * rank)
             for part in (first, mine, other)]
    return pl.pallas_call(
        functools.partial(near_kernel, half, heads),
        grid=(steps,),
        in_specs=[
            pl.BlockSpec(memory_space=pltpu.SMEM),
            column,
            pl.BlockSpec(level_weights.shape, lambda pair: (0, 0, 0)),
            band,
            *fixed,
        ],
        out_specs=band,
        out_shape=jax.ShapeDtypeStruct((width // 2, tokens), F32),
        scratch_shapes=[
            pltpu.VMEM((heads, bits * HEAD, HEAD), BF16),
            pltpu.VMEM((2, level_weights.shape[0], tokens), F32),
        ],
        cost_estimate=cost(bits * tokens * width * HEAD, 8 * MIB),
        compiler_params=params(40),
    )(place, queries, level_weights, local, first, mine, other)


def far_kernel(first_level, place, queries, weights, lower, upper, *rest):
    arrived, (out_weight, mixed, states, flipped, attended) = rest[:-5], rest[-5:]
    rows, width = attended.shape
    bits = states.shape[1] // HEAD

    @pl.when(pl.program_id(0) == 0)
    def _():
        for half in range(2):
            digit = 0
            for mine, other in zip(arrived[::2], arrived[1::2]):
                fill(states, half * (width // 2), half, place[0], place[1], digit, mine, other)
                digit += mine.shape[0]

    for half, near in enumerate((lower, upper)):
        for low in range(0, width // 2, HEAD):
            part = slice(half * (width // 2) + low, half * (width // 2) + low + HEAD)
            head = part.start // HEAD
            products = product_nt(states[head], queries[:, part])
            total = near[low : low + HEAD, :]
            for bit in range(bits):
                row = weights[first_level + bit, head : head + 1, :]
                total = total + row * products[bit * HEAD : (bit + 1) * HEAD]
            flipped[part, :] = total.astype(BF16)
    unit = identity(CHUNK)
    for top in range(0, rows, CHUNK):
        for low in range(0, width, CHUNK):
            block = flipped[low : low + CHUNK, top : top + CHUNK]
            attended[top : top + CHUNK, low : low + CHUNK] = product_nt(unit, block).astype(BF16)
    mixed[...] = product(attended[...], out_weight[...]).astype(BF16)


def far_part(first_level, place, queries, level_weights, lower, upper, arrived, out_weight):
    tokens, width = queries.shape
    bits = sum(part.shape[0] for part in arrived[::2])
    rows = min(2 * CHUNK, tokens)
    band = pl.BlockSpec((rows, width), lambda step: (step, 0))
    near = pl.BlockSpec((width // 2, rows), lambda step: (0, step))
    fixed = [pl.BlockSpec(part.shape, lambda step: (0, 0, 0, 0)) for part in arrived]
    return pl.pallas_call(
        functools.partial(far_kernel, first_level),
        grid=(tokens // rows,),
        in_specs=[
            pl.BlockSpec(memory_space=pltpu.SMEM),
            band,
            pl.BlockSpec(level_weights.shape[:2] + (rows,), lambda step: (0, 0, step)),
            near,
            near,
            *fixed,
            pl.BlockSpec(out_weight.shape, lambda step: (0, 0)),
        ],
        out_specs=band,
        out_shape=jax.ShapeDtypeStruct((tokens, width), BF16),
        scratch_shapes=[
            pltpu.VMEM((width // HEAD, bits * HEAD, HEAD), BF16),
            pltpu.VMEM((width, rows), BF16),
            pltpu.VMEM((rows, width), BF16),
        ],
        cost_estimate=cost(2 * tokens * width * (width + bits * HEAD), 12 * MIB),
        compiler_params=params(28),
    )(place, queries, level_weights, lower, upper, *arrived, out_weight)


def body(queries, keys, values, level_weights, out_weight):
    inner, outer = lax.axis_size("inner"), lax.axis_size("outer")
    inner_bits, outer_bits = bits_of(inner), bits_of(outer)
    inner_place, outer_place = lax.axis_index("inner"), lax.axis_index("outer")
    place = jnp.stack([inner_place, outer_place]).astype(jnp.int32)
    core = jnp.bitwise_and(inner_place, 1)
    side = jnp.bitwise_and(jnp.right_shift(inner_place, 1), 1)
    half = keys.shape[1] // 2
    quarter = half // 2
    tie = lax.optimization_barrier

    give = block_state((1 - core).reshape(1).astype(jnp.int32), keys, values)
    first = swap(give, "inner", 1)
    keep = block_state(core.reshape(1).astype(jnp.int32), keys, values)

    def quarter_of(at):
        return lax.dynamic_slice_in_dim(keep, at * quarter, quarter, 0) + lax.dynamic_slice_in_dim(
            first, at * quarter, quarter, 0
        )

    own, passed = quarter_of(side), quarter_of(1 - side)
    running = own
    buckets = []
    for bit in range(1, inner_bits):
        buckets.append(swap(passed if bit == 1 else running, "inner", 1 << bit))
        running = running + buckets[-1]

    inputs = (queries, keys, values, level_weights)
    sent = jnp.stack([own] + buckets[1:])
    running, sent, inputs = tie((running, sent, inputs))
    arrived = swap(running, "outer", 1)
    local = [local_part(0, *inputs)]
    arrived, sent, local[0] = tie((arrived, sent, local[0]))
    others = swap(sent, "inner", 2)

    far = [arrived]
    beside = []
    for bit in range(1, outer_bits):
        running = running + arrived
        running, inputs = tie((running, inputs))
        arrived = swap(running, "outer", 1 << bit)
        if bit == 1:
            local.append(local_part(1, *inputs))
            arrived, far, others, local[1] = tie((arrived, far, others, local[1]))
        beside.append(swap(far[-1], "inner", 2))
        far.append(arrived)
    if len(local) < 2:
        local.append(local_part(1, *inputs))
    mine = jnp.stack(
        [keep.reshape(2, quarter, HEAD)] + [jnp.stack([bucket, others[at]]) for at, bucket in enumerate(buckets)]
    )
    other = swap(mine, "inner", 1)
    far[-1], local = tie((far[-1], local))
    last = swap(far[-1], "inner", 2)
    nears = [
        near_part(part, inner_bits, place, queries, level_weights, local[part], first, mine, other) for part in range(2)
    ]
    last, beside, nears = tie((last, beside, nears))
    far_mine = jnp.stack([jnp.stack(pair) for pair in zip(far, beside + [last])])
    arrivals = [far_mine, swap(far_mine, "inner", 1)]
    first_level = LOCAL_BITS + 1 + inner_bits
    return far_part(first_level, place, queries, level_weights, *nears, arrivals, out_weight)


def solution(mesh):
    spec = P(("outer", "inner"), None)
    in_specs = (spec, spec, spec, P(None, None, ("outer", "inner")), P())
    return jax.shard_map(body, mesh=mesh, in_specs=in_specs, out_specs=spec, check_vma=False)
```

time: 61.5 us -> 55.1 us (0.90)
  starting transfers between devices: 22.4 us -> 13 us
  waiting for transfers between devices: 2.01 us -> 10.6 us
  Pallas kernels: 29.7 us -> 22.4 us
  other arithmetic: 1.2 us -> 2.38 us
  local copies, waits for them, and re-layouts: 5.51 us -> 6.17 us
    ppermute x18 -> x10, waiting for transfers between devices: 2.01 us -> 10.6 us  [swap(): lax.ppermute(block, axis, [(place, place ^ stride) for place in range(cou...]
    pallas_call x5, Pallas kernels: 23.7 us -> 16.2 us  [the longest x1 6.14 us: far_part(): pl.pallas_call(functools.partial(far_kernel, first_level), grid=(tokens /...]
    ppermute x18 -> x10, starting transfers between devices: 20.5 us -> 13 us  [swap(): lax.ppermute(block, axis, [(place, place ^ stride) for place in range(cou...]
    ppermute x1 -> x0, starting transfers between devices: 1.97 us -> none  [raise_to(): return lax.ppermute(block, axis, route)]
    another operation x3 -> x7, other arithmetic: 0.1 us -> 1.35 us  [the longest x2 1.17 us: body(): sent = jnp.stack([own] + buckets[1:])]
    unnamed x24 -> x28, local copies, waits for them, and re-layouts: 5.51 us -> 6.16 us
  transfers between devices with their start and end apart: 19 -> 10, of which waited for: 2 -> 5; matrix products, arithmetic and copies ran while one was open for 0% -> 0% of each run, Pallas kernels for 33% -> 24%
where the time goes in v1:
time: 55.1 us; the launch traced here: 54.8 us
  Pallas kernels  22.4 us (41%)
  starting transfers between devices  13 us (24%)
  waiting for transfers between devices  10.6 us (19%)
  local copies, waits for them, and re-layouts  6.17 us (11%)
  other arithmetic  2.38 us (4%)
    ppermute x10, starting transfers between devices, swap(): lax.ppermute(block, axis, [(place, place ^ stride) for place in range(cou...  13 us
    ppermute x10, waiting for transfers between devices, swap(): lax.ppermute(block, axis, [(place, place ^ stride) for place in range(cou...  10.6 us
    pallas_call x2, Pallas kernels, block_state(): pl.pallas_call(state_kernel, grid_spec=pltpu.PrefetchScalarGridSpec(num_s...  6.22 us
    unnamed x28, local copies, waits for them, and re-layouts  6.16 us
    pallas_call x1, Pallas kernels, far_part(): pl.pallas_call(functools.partial(far_kernel, first_level), grid=(tokens /...  6.14 us
    pallas_call x2, Pallas kernels, near_part(): pl.pallas_call(functools.partial(near_kernel, half, heads), grid=(steps,)...  5.03 us
    pallas_call x2, Pallas kernels, local_part(): pl.pallas_call(functools.partial(local_kernel, half * steps * 2), grid=(s...  5 us
    another operation x2, other arithmetic, body(): sent = jnp.stack([own] + buckets[1:])  1.17 us
  transfers between devices with their start and end apart: 10, of which 5 were waited for; matrix products, arithmetic and copies ran while one was open for 0% of the time, Pallas kernels for 24%

profile of v1, /device:TPU:0, one launch (start us, length us, event | category | flops | bytes accessed | tf_op | source)
XLA Modules:
  0.0 54.8 jit_solution(17627791910632930384)
XLA Ops:
  0.0 3.0 %shard_map.56 = f32[512,128]{1,0:T(8,128)} custom-call(s32[1]{0:T(128)} %bitcast.3.half, bf16[1024,1024]{1,0:T(8,128)(2,1)} %keys.5, bf16[1024,1024]{1,0:T(8,128)(2,1)} %values.5), custom_call_target="tpu_custom_call" | custom-call | flops 134217728 | bytes 3145728 | tf_op jit(solution)/shard_map/pallas_call | solution.py:73
  3.0 0.5 collective-permute-start
  3.5 0.0 copy-start.1
  3.5 0.0 copy-start.3
  3.5 3.2 %shard_map.55 = f32[512,128]{1,0:T(8,128)} custom-call(s32[1]{0:T(128)} %bitcast.2.half, bf16[1024,1024]{1,0:T(8,128)(2,1)} %keys.5, bf16[1024,1024]{1,0:T(8,128)(2,1)} %values.5), custom_call_target="tpu_custom_call" | custom-call | flops 134217728 | bytes 3145728 | tf_op jit(solution)/shard_map/pallas_call | solution.py:73
  6.7 0.0 copy-start
  6.7 0.0 collective-permute-done.first
  6.7 0.0 copy-start.8
  6.7 1.2 %fusion = (f32[1,256,128]{2,1,0:T(8,128)S(1)}, f32[256,128]{1,0:T(8,128)S(1)}) fusion(f32[512,128]{1,0:T(8,128)S(1)} %collective-permute-done.first, s32[]{:T(128)S(6)} %select_n.8, f32[512,128]{1,0:T(8,128)} %shard_map.55, s32[]{:T(128)S(6)} %select_n.9), kind=kLoop, calls=%fused_computation.9 | loop fusion | flops 65536 | bytes 786440 | tf_op jit(solution)/shard_map/stack | solution.py:339
  7.8 2.6 %collective-permute-start.1 = (f32[256,128]{1,0:T(8,128)S(1)}, f32[256,128]{1,0:T(8,128)S(1)}, u32[]{:S(2)}, u32[]{:S(2)}) collective-permute-start(f32[256,128]{1,0:T(8,128)S(1)} %get-tuple-element.56), channel_id=1, source_target_pairs={{0,2},{1,3},{2,0},{3,1},{4,6},{5,7},{6,4},{7,5},{8,10},{9,11},{10,... | collective-permute-start | bytes 393224 | tf_op jit(solution)/shard_map/ppermute | solution.py:26
  10.4 4.1 %collective-permute-done.1 = f32[256,128]{1,0:T(8,128)S(1)} collective-permute-done((f32[256,128]{1,0:T(8,128)S(1)}, f32[256,128]{1,0:T(8,128)S(1)}, u32[]{:S(2)}, u32[]{:S(2)}) %collective-permute-start.1) | collective-permute-done | bytes 131104 | tf_op jit(solution)/shard_map/ppermute | solution.py:26
  14.6 0.9 %fusion.1 = f32[256,128]{1,0:T(8,128)S(1)} fusion(f32[256,128]{1,0:T(8,128)S(1)} %collective-permute-done.1, f32[512,128]{1,0:T(8,128)S(1)} %collective-permute-done.first, s32[]{:T(128)S(6)} %select_n.8, f32[512,128]{1,0:T(8,128)} %shard_map.55), kind=kLoop, calls=%fused_computation.10 | loop fusion | flops 65536 | bytes 524292 | tf_op jit(solution)/shard_map/add | solution.py:336
  15.5 1.8 %collective-permute-start.2 = (f32[256,128]{1,0:T(8,128)S(1)}, f32[256,128]{1,0:T(8,128)S(1)}, u32[]{:S(2)}, u32[]{:S(2)}) collective-permute-start(f32[256,128]{1,0:T(8,128)S(1)} %fusion.1), channel_id=1, source_target_pairs={{0,4},{1,5},{2,6},{3,7},{4,0},{5,1},{6,2},{7,3},{8,12},{9,13},{10,... | collective-permute-start | bytes 393224 | tf_op jit(solution)/shard_map/ppermute | solution.py:26
  17.3 3.5 %collective-permute-done.2 = f32[256,128]{1,0:T(8,128)S(1)} collective-permute-done((f32[256,128]{1,0:T(8,128)S(1)}, f32[256,128]{1,0:T(8,128)S(1)}, u32[]{:S(2)}, u32[]{:S(2)}) %collective-permute-start.2) | collective-permute-done | bytes 131104 | tf_op jit(solution)/shard_map/ppermute | solution.py:26
  20.9 1.7 %collective-permute-start.3 = (f32[256,128]{1,0:T(8,128)S(1)}, f32[256,128]{1,0:T(8,128)S(1)}, u32[]{:S(2)}, u32[]{:S(2)}) collective-permute-start(f32[256,128]{1,0:T(8,128)S(1)} %add.28), channel_id=1, source_target_pairs={{0,8},{8,0},{16,24},{24,16},{1,9},{9,1},{17,25},{25,17},{2,10},{10... | collective-permute-start | bytes 393224 | tf_op jit(solution)/shard_map/ppermute | solution.py:26
  22.6 0.0 copy-done.1
  22.6 0.0 copy-done.3
  22.6 0.0 copy-done
  22.6 0.0 copy-start.2
  22.6 1.6 %copy-done.2 = bf16[1024,1024]{1,0:T(8,128)(2,1)S(1)} copy-done((bf16[1024,1024]{1,0:T(8,128)(2,1)S(1)}, bf16[1024,1024]{1,0:T(8,128)(2,1)}, u32[]{:S(2)}) %copy-start.2) | copy-done | bytes 2097176
  24.2 2.5 %shard_map.57.local = f32[512,1024]{1,0:T(8,128)S(1)} custom-call(bf16[1024,1024]{1,0:T(8,128)(2,1)S(1)} %copy-done, bf16[1024,1024]{1,0:T(8,128)(2,1)S(1)} %copy-done.1, bf16[1024,1024]{1,0:T(8,128)(2,1)S(1)} %copy-done.2, f32[16,8,1024]{2,1,0:T(8,128)S(1)} %copy-done.3), custom_call_target="tpu_custom_call" | custom-call | flops 402653184 | bytes 6291456 | tf_op jit(solution)/shard_map/pallas_call | solution.py:164
  26.7 0.0 copy-done.8
  26.7 0.0 copy-start.4
  26.7 0.0 collective-permute-done.3
  26.7 1.6 %collective-permute-start.5 = (f32[2,256,128]{2,1,0:T(8,128)S(1)}, f32[2,256,128]{2,1,0:T(8,128)S(1)}, u32[]{:S(2)}, u32[]{:S(2)}) collective-permute-start(f32[2,256,128]{2,1,0:T(8,128)S(1)} %pad_maximum_fusion.2), channel_id=1, source_target_pairs={{0,2},{1,3},{2,0},{3,1},{4,6},{5,7},{6,4},{7,5},{8,10},{9,11},{10,... | collective-permute-start | bytes 786440 | tf_op jit(solution)/shard_map/ppermute | solution.py:26
  28.3 0.0 copy-start.11
  28.3 2.7 %collective-permute-start.4 = (f32[256,128]{1,0:T(8,128)S(1)}, f32[256,128]{1,0:T(8,128)S(1)}, u32[]{:S(2)}, u32[]{:S(2)}) collective-permute-start(f32[256,128]{1,0:T(8,128)S(1)} %add.29), channel_id=1, source_target_pairs={{0,16},{8,24},{16,0},{24,8},{1,17},{9,25},{17,1},{25,9},{2,18},{10... | collective-permute-start | bytes 393224 | tf_op jit(solution)/shard_map/ppermute | solution.py:26
  31.0 2.5 %shard_map.58.local = f32[512,1024]{1,0:T(8,128)S(1)} custom-call(bf16[1024,1024]{1,0:T(8,128)(2,1)S(1)} %copy-done, bf16[1024,1024]{1,0:T(8,128)(2,1)S(1)} %copy-done.1, bf16[1024,1024]{1,0:T(8,128)(2,1)S(1)} %copy-done.2, f32[16,8,1024]{2,1,0:T(8,128)S(1)} %copy-done.3), custom_call_target="tpu_custom_call" | custom-call | flops 402653184 | bytes 6291456 | tf_op jit(solution)/shard_map/pallas_call | solution.py:164
  33.5 0.0 copy-done.4
  33.5 0.0 copy-start.6
  33.5 1.3 %copy-done.6 = f32[512,1024]{1,0:T(8,128)} copy-done((f32[512,1024]{1,0:T(8,128)}, f32[512,1024]{1,0:T(8,128)S(1)}, u32[]{:S(2)}) %copy-start.6) | copy-done | bytes 2097176
  34.8 0.8 %collective-permute-done.4 = f32[256,128]{1,0:T(8,128)S(1)} collective-permute-done((f32[256,128]{1,0:T(8,128)S(1)}, f32[256,128]{1,0:T(8,128)S(1)}, u32[]{:S(2)}, u32[]{:S(2)}) %collective-permute-start.4) | collective-permute-done | bytes 131104 | tf_op jit(solution)/shard_map/ppermute | solution.py:26
  35.7 0.0 copy-start.12
  35.7 0.0 collective-permute-done.5
  35.7 0.0 copy-done.11
  35.7 0.1 pad_maximum_fusion.mine
  35.8 0.5 copy-done.12
  36.3 0.0 collective-permute-start.8
  36.3 0.6 %collective-permute-start.6 = (f32[256,128]{1,0:T(8,128)}, f32[256,128]{1,0:T(8,128)S(1)}, u32[]{:S(2)}, u32[]{:S(2)}) collective-permute-start(f32[256,128]{1,0:T(8,128)} %copy-done.12), channel_id=1, source_target_pairs={{0,2},{1,3},{2,0},{3,1},{4,6},{5,7},{6,4},{7,5},{8,10},{9,11},{10,... | collective-permute-start | bytes 393224 | tf_op jit(solution)/shard_map/ppermute | solution.py:26
  36.9 1.4 %collective-permute-start.7 = (f32[256,128]{1,0:T(8,128)S(1)}, f32[256,128]{1,0:T(8,128)S(1)}, u32[]{:S(2)}, u32[]{:S(2)}) collective-permute-start(f32[256,128]{1,0:T(8,128)S(1)} %collective-permute-done.3), channel_id=1, source_target_pairs={{0,2},{1,3},{2,0},{3,1},{4,6},{5,7},{6,4},{7,5},{8,10},{9,11},{10,... | collective-permute-start | bytes 393224 | tf_op jit(solution)/shard_map/ppermute | solution.py:26
  38.3 0.1 pad_add_fusion.place
  38.4 0.0 copy-start.5
  38.4 0.3 collective-permute-done.8.other
  38.7 0.0 copy-start.7
  38.7 1.8 %copy-done.7 = f32[512,1024]{1,0:T(8,128)S(1)} copy-done((f32[512,1024]{1,0:T(8,128)S(1)}, f32[512,1024]{1,0:T(8,128)}, u32[]{:S(2)}) %copy-start.7) | copy-done | bytes 2097176
  40.5 0.0 copy-start.9
  40.5 0.9 %copy-done.9 = f32[512,128]{1,0:T(8,128)S(1)} copy-done((f32[512,128]{1,0:T(8,128)S(1)}, f32[512,128]{1,0:T(8,128)}, u32[]{:S(2)}) %copy-start.9) | copy-done | bytes 262168
  41.4 2.5 %shard_map.60.upper = f32[512,1024]{1,0:T(8,128)S(1)} custom-call(s32[2]{0:T(128)S(1)} %pad_add_fusion.place, bf16[1024,1024]{1,0:T(8,128)(2,1)S(1)} %copy-done, f32[16,8,1024]{2,1,0:T(8,128)S(1)} %copy-done.3, f32[512,1024]{1,0:T(8,128)S(1)} %copy-done.7, f32[512,128]{1,0:T(8,128)S(1)} %copy-done.9, f32[3,2,256,128]{3,2,1,0:T(8,128)S(1)} %pad_maximum_fusion.mine, ...), custom_call_target="tpu_custom_call" | custom-call | flops 402653184 | bytes 8388608 | tf_op jit(solution)/shard_map/pallas_call | solution.py:228
  43.9 0.0 copy-done.5
  44.0 0.0 copy-start.13
  44.0 2.5 %shard_map.59.lower = f32[512,1024]{1,0:T(8,128)S(1)} custom-call(s32[2]{0:T(128)S(1)} %pad_add_fusion.place, bf16[1024,1024]{1,0:T(8,128)(2,1)S(1)} %copy-done, f32[16,8,1024]{2,1,0:T(8,128)S(1)} %copy-done.3, f32[512,1024]{1,0:T(8,128)S(1)} %copy-done.5, f32[512,128]{1,0:T(8,128)S(1)} %copy-done.9, f32[3,2,256,128]{3,2,1,0:T(8,128)S(1)} %pad_maximum_fusion.mine, ...), custom_call_target="tpu_custom_call" | custom-call | flops 402653184 | bytes 8388608 | tf_op jit(solution)/shard_map/pallas_call | solution.py:228
  46.5 0.0 copy-start.10
  46.5 0.0 collective-permute-done.6
  46.5 0.0 collective-permute-done.7
  46.6 0.0 copy-done.13
  46.6 0.2 collective-permute-start.9
  46.8 1.8 %collective-permute-done.9.rest_1_ = f32[2,2,256,128]{3,2,1,0:T(8,128)S(1)} collective-permute-done((f32[2,2,256,128]{3,2,1,0:T(8,128)S(1)}, f32[2,2,256,128]{3,2,1,0:T(8,128)S(1)}, u32[]{:S(2)}, u32[]{:S(2)}) %collective-permute-start.9) | collective-permute-done | bytes 524320 | tf_op jit(solution)/shard_map/ppermute | solution.py:26
  48.6 0.0 copy-done.10
  48.6 6.1 %shard_map.61 = bf16[1024,1024]{1,0:T(8,128)(2,1)} custom-call(s32[2]{0:T(128)S(1)} %pad_add_fusion.place, bf16[1024,1024]{1,0:T(8,128)(2,1)S(1)} %copy-done, f32[16,8,1024]{2,1,0:T(8,128)S(1)} %copy-done.3, f32[512,1024]{1,0:T(8,128)S(1)} %shard_map.59.lower, f32[512,1024]{1,0:T(8,128)S(1)} %shard_map.60.upper, ...), custom_call_target="tpu_custom_call" | custom-call | flops 2684354560 | bytes 12582912 | tf_op jit(solution)/shard_map/pallas_call | solution.py:287
  (8 shorter events, 0.2 us)
Async XLA Ops:
  3.0 3.7 %collective-permute-start = (f32[512,128]{1,0:T(8,128)}, f32[512,128]{1,0:T(8,128)S(1)}, u32[]{:S(2)}, u32[]{:S(2)}) collective-permute-start(f32[512,128]{1,0:T(8,128)} %shard_map.56), channel_id=1, source_target_pairs={{0,1},{1,0},{2,3},{3,2},{4,5},{5,4},{6,7},{7,6},{8,9},{9,8},{10,11... | collective-permute-start | bytes 786440 | tf_op jit(solution)/shard_map/ppermute | solution.py:26
  3.5 19.1 %copy-start.1 = (bf16[1024,1024]{1,0:T(8,128)(2,1)S(1)}, bf16[1024,1024]{1,0:T(8,128)(2,1)}, u32[]{:S(2)}) copy-start(bf16[1024,1024]{1,0:T(8,128)(2,1)} %keys.5) | copy-start | bytes 6291460
  3.5 19.1 %copy-start.3 = (f32[16,8,1024]{2,1,0:T(8,128)S(1)}, f32[16,8,1024]{2,1,0:T(8,128)}, u32[]{:S(2)}) copy-start(f32[16,8,1024]{2,1,0:T(8,128)} %weights.7) | copy-start | bytes 1572868
  6.7 15.9 %copy-start = (bf16[1024,1024]{1,0:T(8,128)(2,1)S(1)}, bf16[1024,1024]{1,0:T(8,128)(2,1)}, u32[]{:S(2)}) copy-start(bf16[1024,1024]{1,0:T(8,128)(2,1)} %queries.7) | copy-start | bytes 6291460
  6.7 20.0 %copy-start.8 = (f32[512,128]{1,0:T(8,128)}, f32[512,128]{1,0:T(8,128)S(1)}, u32[]{:S(2)}) copy-start(f32[512,128]{1,0:T(8,128)S(1)} %collective-permute-done.first) | copy-start | bytes 786436
  7.8 6.7 %collective-permute-start.1 = (f32[256,128]{1,0:T(8,128)S(1)}, f32[256,128]{1,0:T(8,128)S(1)}, u32[]{:S(2)}, u32[]{:S(2)}) collective-permute-start(f32[256,128]{1,0:T(8,128)S(1)} %get-tuple-element.56), channel_id=1, source_target_pairs={{0,2},{1,3},{2,0},{3,1},{4,6},{5,7},{6,4},{7,5},{8,10},{9,11},{10,... | collective-permute-start | bytes 393224 | tf_op jit(solution)/shard_map/ppermute | solution.py:26
  15.5 5.4 %collective-permute-start.2 = (f32[256,128]{1,0:T(8,128)S(1)}, f32[256,128]{1,0:T(8,128)S(1)}, u32[]{:S(2)}, u32[]{:S(2)}) collective-permute-start(f32[256,128]{1,0:T(8,128)S(1)} %fusion.1), channel_id=1, source_target_pairs={{0,4},{1,5},{2,6},{3,7},{4,0},{5,1},{6,2},{7,3},{8,12},{9,13},{10,... | collective-permute-start | bytes 393224 | tf_op jit(solution)/shard_map/ppermute | solution.py:26
  20.9 5.8 %collective-permute-start.3 = (f32[256,128]{1,0:T(8,128)S(1)}, f32[256,128]{1,0:T(8,128)S(1)}, u32[]{:S(2)}, u32[]{:S(2)}) collective-permute-start(f32[256,128]{1,0:T(8,128)S(1)} %add.28), channel_id=1, source_target_pairs={{0,8},{8,0},{16,24},{24,16},{1,9},{9,1},{17,25},{25,17},{2,10},{10... | collective-permute-start | bytes 393224 | tf_op jit(solution)/shard_map/ppermute | solution.py:26
  22.6 1.6 %copy-start.2 = (bf16[1024,1024]{1,0:T(8,128)(2,1)S(1)}, bf16[1024,1024]{1,0:T(8,128)(2,1)}, u32[]{:S(2)}) copy-start(bf16[1024,1024]{1,0:T(8,128)(2,1)} %values.5) | copy-start | bytes 6291460
  26.7 6.8 %copy-start.4 = (f32[512,1024]{1,0:T(8,128)}, f32[512,1024]{1,0:T(8,128)S(1)}, u32[]{:S(2)}) copy-start(f32[512,1024]{1,0:T(8,128)S(1)} %shard_map.57.local) | copy-start | bytes 6291460
  26.7 8.9 %collective-permute-start.5 = (f32[2,256,128]{2,1,0:T(8,128)S(1)}, f32[2,256,128]{2,1,0:T(8,128)S(1)}, u32[]{:S(2)}, u32[]{:S(2)}) collective-permute-start(f32[2,256,128]{2,1,0:T(8,128)S(1)} %pad_maximum_fusion.2), channel_id=1, source_target_pairs={{0,2},{1,3},{2,0},{3,1},{4,6},{5,7},{6,4},{7,5},{8,10},{9,11},{10,... | collective-permute-start | bytes 786440 | tf_op jit(solution)/shard_map/ppermute | solution.py:26
  28.3 7.4 %copy-start.11 = (f32[512,128]{1,0:T(8,128)S(1)}, f32[512,128]{1,0:T(8,128)}, u32[]{:S(2)}) copy-start(f32[512,128]{1,0:T(8,128)} %shard_map.55) | copy-start | bytes 786436
  28.3 7.3 %collective-permute-start.4 = (f32[256,128]{1,0:T(8,128)S(1)}, f32[256,128]{1,0:T(8,128)S(1)}, u32[]{:S(2)}, u32[]{:S(2)}) collective-permute-start(f32[256,128]{1,0:T(8,128)S(1)} %add.29), channel_id=1, source_target_pairs={{0,16},{8,24},{16,0},{24,8},{1,17},{9,25},{17,1},{25,9},{2,18},{10... | collective-permute-start | bytes 393224 | tf_op jit(solution)/shard_map/ppermute | solution.py:26
  33.5 1.3 %copy-start.6 = (f32[512,1024]{1,0:T(8,128)}, f32[512,1024]{1,0:T(8,128)S(1)}, u32[]{:S(2)}) copy-start(f32[512,1024]{1,0:T(8,128)S(1)} %shard_map.58.local) | copy-start | bytes 6291460
  35.7 0.7 %copy-start.12 = (f32[256,128]{1,0:T(8,128)}, f32[256,128]{1,0:T(8,128)S(1)}, u32[]{:S(2)}) copy-start(f32[256,128]{1,0:T(8,128)S(1)} %collective-permute-done.4) | copy-start | bytes 393220
  36.3 2.4 %collective-permute-start.8 = (f32[3,2,256,128]{3,2,1,0:T(8,128)S(1)}, f32[3,2,256,128]{3,2,1,0:T(8,128)}, u32[]{:S(2)}, u32[]{:S(2)}) collective-permute-start(f32[3,2,256,128]{3,2,1,0:T(8,128)S(1)} %pad_maximum_fusion.mine), channel_id=1, source_target_pairs={{0,1},{1,0},{2,3},{3,2},{4,5},{5,4},{6,7},{7,6},{8,9},{9,8},{10,11... | collective-permute-start | bytes 2359304 | tf_op jit(solution)/shard_map/ppermute | solution.py:26
  36.3 10.2 %collective-permute-start.6 = (f32[256,128]{1,0:T(8,128)}, f32[256,128]{1,0:T(8,128)S(1)}, u32[]{:S(2)}, u32[]{:S(2)}) collective-permute-start(f32[256,128]{1,0:T(8,128)} %copy-done.12), channel_id=1, source_target_pairs={{0,2},{1,3},{2,0},{3,1},{4,6},{5,7},{6,4},{7,5},{8,10},{9,11},{10,... | collective-permute-start | bytes 393224 | tf_op jit(solution)/shard_map/ppermute | solution.py:26
  36.9 9.6 %collective-permute-start.7 = (f32[256,128]{1,0:T(8,128)S(1)}, f32[256,128]{1,0:T(8,128)S(1)}, u32[]{:S(2)}, u32[]{:S(2)}) collective-permute-start(f32[256,128]{1,0:T(8,128)S(1)} %collective-permute-done.3), channel_id=1, source_target_pairs={{0,2},{1,3},{2,0},{3,1},{4,6},{5,7},{6,4},{7,5},{8,10},{9,11},{10,... | collective-permute-start | bytes 393224 | tf_op jit(solution)/shard_map/ppermute | solution.py:26
  38.4 5.5 %copy-start.5 = (f32[512,1024]{1,0:T(8,128)S(1)}, f32[512,1024]{1,0:T(8,128)}, u32[]{:S(2)}) copy-start(f32[512,1024]{1,0:T(8,128)} %copy-done.4) | copy-start | bytes 6291460
  38.7 1.8 %copy-start.7 = (f32[512,1024]{1,0:T(8,128)S(1)}, f32[512,1024]{1,0:T(8,128)}, u32[]{:S(2)}) copy-start(f32[512,1024]{1,0:T(8,128)} %copy-done.6) | copy-start | bytes 6291460
  40.5 0.9 %copy-start.9 = (f32[512,128]{1,0:T(8,128)S(1)}, f32[512,128]{1,0:T(8,128)}, u32[]{:S(2)}) copy-start(f32[512,128]{1,0:T(8,128)} %copy-done.8) | copy-start | bytes 786436
  44.0 2.6 %copy-start.13 = (f32[256,128]{1,0:T(8,128)S(1)}, f32[256,128]{1,0:T(8,128)}, u32[]{:S(2)}) copy-start(f32[256,128]{1,0:T(8,128)} %copy-done.12) | copy-start | bytes 393220
  46.5 2.1 %copy-start.10 = (bf16[1024,1024]{1,0:T(8,128)(2,1)S(1)}, bf16[1024,1024]{1,0:T(8,128)(2,1)}, u32[]{:S(2)}) copy-start(bf16[1024,1024]{1,0:T(8,128)(2,1)} %rest_2_.1) | copy-start | bytes 6291460
  46.6 2.0 %collective-permute-start.9 = (f32[2,2,256,128]{3,2,1,0:T(8,128)S(1)}, f32[2,2,256,128]{3,2,1,0:T(8,128)S(1)}, u32[]{:S(2)}, u32[]{:S(2)}) collective-permute-start(f32[2,2,256,128]{3,2,1,0:T(8,128)S(1)} %pad_maximum_fusion.1.rest_0_), channel_id=1, source_target_pairs={{0,1},{1,0},{2,3},{3,2},{4,5},{5,4},{6,7},{7,6},{8,9},{9,8},{10,11... | collective-permute-start | bytes 1572872 | tf_op jit(solution)/shard_map/ppermute | solution.py:26

commit v2 on v1

--- a/solution.py
+++ b/solution.py
@@ -58,30 +58,30 @@
     return product_nt(identity(block.shape[1]), block).astype(BF16)
 
 
-def state_kernel(half, keys, values, state):
+def state_kernel(place, keys, values, state):
     both = product(turned(values[...]), keys[...])
     for low in range(0, keys.shape[1], HEAD):
         part = slice(low, low + HEAD)
         state[part, :] = both[part, part]
 
 
-def block_state(half, keys, values):
+def block_state(place, share, keys, values):
     tokens, width = keys.shape
     step = 2 * HEAD
-    steps = width // 2 // step
-    column = pl.BlockSpec((tokens, step), lambda pair, half: (0, half[0] * steps + pair))
+    steps = width // share // step
+    column = pl.BlockSpec((tokens, step), lambda pair, place: (0, place[0] * steps + pair))
     return pl.pallas_call(
         state_kernel,
         grid_spec=pltpu.PrefetchScalarGridSpec(
             num_scalar_prefetch=1,
             grid=(steps,),
             in_specs=[column, column],
-            out_specs=pl.BlockSpec((step, HEAD), lambda pair, half: (pair, 0)),
+            out_specs=pl.BlockSpec((step, HEAD), lambda pair, place: (pair, 0)),
         ),
-        out_shape=jax.ShapeDtypeStruct((width // 2, HEAD), F32),
-        cost_estimate=cost(tokens * width * HEAD, 3 * MIB),
-        compiler_params=params(58),
-    )(half, keys, values)
+        out_shape=pltpu.VMEM((width // share, HEAD), F32),
+        cost_estimate=cost(2 * tokens * width * HEAD // share, 5 * MIB // share),
+        compiler_params=params(16),
+    )(place.reshape(1).astype(jnp.int32), keys, values)
 
 
 def tile_mixing(rows):
@@ -168,8 +168,8 @@
         out_specs=pl.BlockSpec((step, tokens), lambda pair: (pair, 0)),
         out_shape=jax.ShapeDtypeStruct((width // 2, tokens), F32),
         scratch_shapes=[pltpu.VMEM((2, level_weights.shape[0], tokens), F32)],
-        cost_estimate=cost(3 * tokens * width * HEAD, 6 * MIB),
-        compiler_params=params(40),
+        cost_estimate=cost(tokens * width, MIB // 4),
+        compiler_params=params(16),
     )(queries, keys, values, level_weights)
 
 
@@ -185,7 +185,7 @@
         slot = jnp.bitwise_xor(side, quarter)
         for bit in range(count):
             if first is not None and bit == 0:
-                here, there = first[quarter * size : (quarter + 1) * size, :], other[0, quarter]
+                here, there = first[quarter * size : (quarter + 1) * size, :], other[0, slot]
             else:
                 here, there = mine[bit, slot], other[bit, slot]
             state = jnp.where(core == half, here, there)
@@ -241,8 +241,8 @@
             pltpu.VMEM((heads, bits * HEAD, HEAD), BF16),
             pltpu.VMEM((2, level_weights.shape[0], tokens), F32),
         ],
-        cost_estimate=cost(bits * tokens * width * HEAD, 8 * MIB),
-        compiler_params=params(40),
+        cost_estimate=cost(tokens * width, MIB // 4),
+        compiler_params=params(16),
     )(place, queries, level_weights, local, first, mine, other)
 
 
@@ -319,46 +319,47 @@
     quarter = half // 2
     tie = lax.optimization_barrier
 
-    give = block_state((1 - core).reshape(1).astype(jnp.int32), keys, values)
+    inputs = tuple(pltpu.with_memory_space_constraint(part, pltpu.HBM) for part in (keys, values))
+    give = block_state(1 - core, 2, *inputs)
+    give, inputs = tie((give, inputs))
     first = swap(give, "inner", 1)
-    keep = block_state(core.reshape(1).astype(jnp.int32), keys, values)
-
-    def quarter_of(at):
-        return lax.dynamic_slice_in_dim(keep, at * quarter, quarter, 0) + lax.dynamic_slice_in_dim(
-            first, at * quarter, quarter, 0
-        )
-
-    own, passed = quarter_of(side), quarter_of(1 - side)
-    running = own
-    buckets = []
-    for bit in range(1, inner_bits):
-        buckets.append(swap(passed if bit == 1 else running, "inner", 1 << bit))
-        running = running + buckets[-1]
-
+
+    def quarter_of(at, state):
+        return state + lax.dynamic_slice_in_dim(first, at * quarter, quarter, 0)
+
+    keep_theirs = block_state(2 * core + 1 - side, 4, *inputs)
+    passed = quarter_of(1 - side, keep_theirs)
+    passed, inputs = tie((passed, inputs))
+    buckets = [swap(passed, "inner", 2)]
+    keep_ours = block_state(2 * core + side, 4, *inputs)
     inputs = (queries, keys, values, level_weights)
-    sent = jnp.stack([own] + buckets[1:])
-    running, sent, inputs = tie((running, sent, inputs))
-    arrived = swap(running, "outer", 1)
+    own = quarter_of(side, keep_ours)
+    others = [swap(own, "inner", 2)]
+    running = own + buckets[0]
+    running, inputs = tie((running, inputs))
     local = [local_part(0, *inputs)]
-    arrived, sent, local[0] = tie((arrived, sent, local[0]))
-    others = swap(sent, "inner", 2)
-
-    far = [arrived]
+    for bit in range(2, inner_bits):
+        arrived = swap(running, "inner", 1 << bit)
+        if bit == 2:
+            arrived, local[0] = tie((arrived, local[0]))
+        buckets.append(arrived)
+        running = running + arrived
+    sent = swap(jnp.stack(buckets[1:]), "inner", 2)
+
+    far = [swap(running, "outer", 1)]
     beside = []
     for bit in range(1, outer_bits):
-        running = running + arrived
+        running = running + far[-1]
         running, inputs = tie((running, inputs))
-        arrived = swap(running, "outer", 1 << bit)
+        far.append(swap(running, "outer", 1 << bit))
+        beside.append(swap(far[-2], "inner", 2))
         if bit == 1:
             local.append(local_part(1, *inputs))
-            arrived, far, others, local[1] = tie((arrived, far, others, local[1]))
-        beside.append(swap(far[-1], "inner", 2))
-        far.append(arrived)
+            far[-1], beside, sent, others, local[1] = tie((far[-1], beside, sent, others, local[1]))
     if len(local) < 2:
         local.append(local_part(1, *inputs))
-    mine = jnp.stack(
-        [keep.reshape(2, quarter, HEAD)] + [jnp.stack([bucket, others[at]]) for at, bucket in enumerate(buckets)]
-    )
+    others += [sent[at] for at in range(inner_bits - 2)]
+    mine = jnp.stack([jnp.stack([keep_ours, keep_theirs])] + [jnp.stack(pair) for pair in zip(buckets, others)])
     other = swap(mine, "inner", 1)
     far[-1], local = tie((far[-1], local))
     last = swap(far[-1], "inner", 2)

time: 55.1 us -> 51.2 us (0.929)
  waiting for transfers between devices: 10.6 us -> 6.57 us
  starting transfers between devices: 13 us -> 14.1 us
  other arithmetic: 2.38 us -> 1.48 us
    ppermute x10 -> x11, waiting for transfers between devices: 10.6 us -> 6.57 us  [swap(): lax.ppermute(block, axis, [(place, place ^ stride) for place in range(cou...]
    ppermute x10 -> x11, starting transfers between devices: 13 us -> 14.1 us  [swap(): lax.ppermute(block, axis, [(place, place ^ stride) for place in range(cou...]
    another operation x4 -> x3, other arithmetic: 1.26 us -> 0.13 us  [body(): jnp.stack([jnp.stack([keep_ours, keep_theirs])] + [jnp.stack(pair) for pa...]
    another operation x3, other arithmetic: 0.09 us -> 1.19 us  [body(): jnp.stack([jnp.stack(pair) for pair in zip(far, beside + [last])])]
    add x2 -> x3, other arithmetic: 0.94 us -> 0.06 us  [the longest x1 0.02 us: body(): running = own + buckets[0]]
    pallas_call x2 -> x3, Pallas kernels: 6.22 us -> 6.08 us  [block_state(): pl.pallas_call(state_kernel, grid_spec=pltpu.PrefetchScalarGridSpec(num_s...]
    unnamed x28 -> x26, local copies, waits for them, and re-layouts: 6.16 us -> 6.08 us
  transfers between devices with their start and end apart: 10 -> 11, of which waited for: 5 -> 4; matrix products, arithmetic and copies ran while one was open for 0% -> 0% of each run, Pallas kernels for 24% -> 27%
where the time goes in v2:
time: 51.2 us; the launch traced here: 50.9 us
  Pallas kernels  22.3 us (44%)
  starting transfers between devices  14.1 us (28%)
  waiting for transfers between devices  6.57 us (13%)
  local copies, waits for them, and re-layouts  6.08 us (12%)
  other arithmetic  1.48 us (3%)
    ppermute x11, starting transfers between devices, swap(): lax.ppermute(block, axis, [(place, place ^ stride) for place in range(cou...  14.1 us
    ppermute x11, waiting for transfers between devices, swap(): lax.ppermute(block, axis, [(place, place ^ stride) for place in range(cou...  6.57 us
    pallas_call x1, Pallas kernels, far_part(): pl.pallas_call(functools.partial(far_kernel, first_level), grid=(tokens /...  6.23 us
    pallas_call x3, Pallas kernels, block_state(): pl.pallas_call(state_kernel, grid_spec=pltpu.PrefetchScalarGridSpec(num_s...  6.08 us
    unnamed x26, local copies, waits for them, and re-layouts  6.08 us
    pallas_call x2, Pallas kernels, local_part(): pl.pallas_call(functools.partial(local_kernel, half * steps * 2), grid=(s...  5.02 us
    pallas_call x2, Pallas kernels, near_part(): pl.pallas_call(functools.partial(near_kernel, half, heads), grid=(steps,)...  5.01 us
    another operation x3, other arithmetic, body(): jnp.stack([jnp.stack(pair) for pair in zip(far, beside + [last])])  1.19 us
  transfers between devices with their start and end apart: 11, of which 4 were waited for; matrix products, arithmetic and copies ran while one was open for 0% of the time, Pallas kernels for 27%

profile of v2, /device:TPU:0, one launch (start us, length us, event | category | flops | bytes accessed | tf_op | source)
XLA Modules:
  0.0 50.9 jit_solution(4593116465900067378)
XLA Ops:
  0.0 2.4 %shard_map.55 = f32[512,128]{1,0:T(8,128)S(1)} custom-call(s32[1]{0:T(128)} %bitcast.4.place, bf16[1024,1024]{1,0:T(8,128)(2,1)} %keys.5, bf16[1024,1024]{1,0:T(8,128)(2,1)} %values.5), custom_call_target="tpu_custom_call" | custom-call | flops 134217728 | bytes 2621440 | tf_op jit(solution)/shard_map/pallas_call | solution.py:73
  2.4 0.5 %collective-permute-start = (f32[512,128]{1,0:T(8,128)S(1)}, f32[512,128]{1,0:T(8,128)S(1)}, u32[]{:S(2)}, u32[]{:S(2)}) collective-permute-start(f32[512,128]{1,0:T(8,128)S(1)} %shard_map.55), channel_id=1, source_target_pairs={{0,1},{1,0},{2,3},{3,2},{4,5},{5,4},{6,7},{7,6},{8,9},{9,8},{10,11... | collective-permute-start | bytes 786440 | tf_op jit(solution)/shard_map/ppermute | solution.py:26
  2.9 1.8 %shard_map.56 = f32[256,128]{1,0:T(8,128)S(1)} custom-call(s32[1]{0:T(128)} %bitcast.3.place, bf16[1024,1024]{1,0:T(8,128)(2,1)} %keys.5, bf16[1024,1024]{1,0:T(8,128)(2,1)} %values.5), custom_call_target="tpu_custom_call" | custom-call | flops 67108864 | bytes 1310720 | tf_op jit(solution)/shard_map/pallas_call | solution.py:73
  4.7 0.0 collective-permute-done.first
  4.7 0.0 copy-start.8
  4.7 2.6 %collective-permute-start.1 = (f32[256,128]{1,0:T(8,128)S(1)}, f32[256,128]{1,0:T(8,128)S(1)}, u32[]{:S(2)}, u32[]{:S(2)}) collective-permute-start(f32[256,128]{1,0:T(8,128)S(1)} %dynamic-slice_add_fusion.1), channel_id=1, source_target_pairs={{0,2},{1,3},{2,0},{3,1},{4,6},{5,7},{6,4},{7,5},{8,10},{9,11},{10,... | collective-permute-start | bytes 393224 | tf_op jit(solution)/shard_map/ppermute | solution.py:26
  7.3 0.0 copy-start
  7.3 0.0 copy-start.1
  7.3 0.0 copy-start.3
  7.3 1.9 %shard_map.57 = f32[256,128]{1,0:T(8,128)S(1)} custom-call(s32[1]{0:T(128)} %bitcast.2.place, bf16[1024,1024]{1,0:T(8,128)(2,1)} %keys.5, bf16[1024,1024]{1,0:T(8,128)(2,1)} %values.5), custom_call_target="tpu_custom_call" | custom-call | flops 67108864 | bytes 1310720 | tf_op jit(solution)/shard_map/pallas_call | solution.py:73
  9.3 2.2 %collective-permute-done.1 = f32[256,128]{1,0:T(8,128)S(1)} collective-permute-done((f32[256,128]{1,0:T(8,128)S(1)}, f32[256,128]{1,0:T(8,128)S(1)}, u32[]{:S(2)}, u32[]{:S(2)}) %collective-permute-start.1) | collective-permute-done | bytes 131104 | tf_op jit(solution)/shard_map/ppermute | solution.py:26
  11.5 0.0 copy-done.8
  11.5 1.8 %collective-permute-start.2 = (f32[256,128]{1,0:T(8,128)S(1)}, f32[256,128]{1,0:T(8,128)S(1)}, u32[]{:S(2)}, u32[]{:S(2)}) collective-permute-start(f32[256,128]{1,0:T(8,128)S(1)} %get-tuple-element.41), channel_id=1, source_target_pairs={{0,4},{1,5},{2,6},{3,7},{4,0},{5,1},{6,2},{7,3},{8,12},{9,13},{10,... | collective-permute-start | bytes 393224 | tf_op jit(solution)/shard_map/ppermute | solution.py:26
  13.3 0.0 copy-done
  13.3 0.0 copy-done.1
  13.3 0.0 copy-done.3
  13.3 0.0 copy-start.2
  13.4 1.6 %copy-done.2 = bf16[1024,1024]{1,0:T(8,128)(2,1)S(1)} copy-done((bf16[1024,1024]{1,0:T(8,128)(2,1)S(1)}, bf16[1024,1024]{1,0:T(8,128)(2,1)}, u32[]{:S(2)}) %copy-start.2) | copy-done | bytes 2097176
  14.9 2.5 %shard_map.58.local = f32[512,1024]{1,0:T(8,128)S(1)} custom-call(bf16[1024,1024]{1,0:T(8,128)(2,1)S(1)} %copy-done, bf16[1024,1024]{1,0:T(8,128)(2,1)S(1)} %copy-done.1, bf16[1024,1024]{1,0:T(8,128)(2,1)S(1)} %copy-done.2, f32[16,8,1024]{2,1,0:T(8,128)S(1)} %copy-done.3), custom_call_target="tpu_custom_call" | custom-call | flops 1048576 | bytes 262144 | tf_op jit(solution)/shard_map/pallas_call | solution.py:164
  17.4 0.0 copy-start.4
  17.5 0.0 collective-permute-done.2
  17.5 1.6 %collective-permute-start.3 = (f32[256,128]{1,0:T(8,128)S(1)}, f32[256,128]{1,0:T(8,128)S(1)}, u32[]{:S(2)}, u32[]{:S(2)}) collective-permute-start(f32[256,128]{1,0:T(8,128)S(1)} %add.34), channel_id=1, source_target_pairs={{0,8},{8,0},{16,24},{24,16},{1,9},{9,1},{17,25},{25,17},{2,10},{10... | collective-permute-start | bytes 393224 | tf_op jit(solution)/shard_map/ppermute | solution.py:26
  19.1 1.5 %collective-permute-start.7 = (f32[256,128]{1,0:T(8,128)S(1)}, f32[256,128]{1,0:T(8,128)S(1)}, u32[]{:S(2)}, u32[]{:S(2)}) collective-permute-start(f32[256,128]{1,0:T(8,128)S(1)} %get-tuple-element.66), channel_id=1, source_target_pairs={{0,2},{1,3},{2,0},{3,1},{4,6},{5,7},{6,4},{7,5},{8,10},{9,11},{10,... | collective-permute-start | bytes 393224 | tf_op jit(solution)/shard_map/ppermute | solution.py:26
  20.6 0.5 %collective-permute-start.6 = (f32[1,256,128]{2,1,0:T(8,128)S(1)}, f32[1,256,128]{2,1,0:T(8,128)S(1)}, u32[]{:S(2)}, u32[]{:S(2)}) collective-permute-start(f32[1,256,128]{2,1,0:T(8,128)S(1)} %bitcast.27), channel_id=1, source_target_pairs={{0,2},{1,3},{2,0},{3,1},{4,6},{5,7},{6,4},{7,5},{8,10},{9,11},{10,... | collective-permute-start | bytes 393224 | tf_op jit(solution)/shard_map/ppermute | solution.py:26
  21.2 1.4 %collective-permute-done.3 = f32[256,128]{1,0:T(8,128)S(1)} collective-permute-done((f32[256,128]{1,0:T(8,128)S(1)}, f32[256,128]{1,0:T(8,128)S(1)}, u32[]{:S(2)}, u32[]{:S(2)}) %collective-permute-start.3) | collective-permute-done | bytes 131104 | tf_op jit(solution)/shard_map/ppermute | solution.py:26
  22.5 2.6 %collective-permute-start.4 = (f32[256,128]{1,0:T(8,128)S(1)}, f32[256,128]{1,0:T(8,128)}, u32[]{:S(2)}, u32[]{:S(2)}) collective-permute-start(f32[256,128]{1,0:T(8,128)S(1)} %add.35), channel_id=1, source_target_pairs={{0,16},{8,24},{16,0},{24,8},{1,17},{9,25},{17,1},{25,9},{2,18},{10... | collective-permute-start | bytes 393224 | tf_op jit(solution)/shard_map/ppermute | solution.py:26
  25.2 1.5 %collective-permute-start.5 = (f32[256,128]{1,0:T(8,128)S(1)}, f32[256,128]{1,0:T(8,128)S(1)}, u32[]{:S(2)}, u32[]{:S(2)}) collective-permute-start(f32[256,128]{1,0:T(8,128)S(1)} %collective-permute-done.3), channel_id=1, source_target_pairs={{0,2},{1,3},{2,0},{3,1},{4,6},{5,7},{6,4},{7,5},{8,10},{9,11},{10,... | collective-permute-start | bytes 393224 | tf_op jit(solution)/shard_map/ppermute | solution.py:26
  26.7 2.5 %shard_map.59.local = f32[512,1024]{1,0:T(8,128)S(1)} custom-call(bf16[1024,1024]{1,0:T(8,128)(2,1)S(1)} %copy-done, bf16[1024,1024]{1,0:T(8,128)(2,1)S(1)} %copy-done.1, bf16[1024,1024]{1,0:T(8,128)(2,1)S(1)} %copy-done.2, f32[16,8,1024]{2,1,0:T(8,128)S(1)} %copy-done.3), custom_call_target="tpu_custom_call" | custom-call | flops 1048576 | bytes 262144 | tf_op jit(solution)/shard_map/pallas_call | solution.py:164
  29.2 0.0 copy-done.4
  29.3 0.0 copy-start.6
  29.3 1.3 %copy-done.6 = f32[512,1024]{1,0:T(8,128)} copy-done((f32[512,1024]{1,0:T(8,128)}, f32[512,1024]{1,0:T(8,128)S(1)}, u32[]{:S(2)}) %copy-start.6) | copy-done | bytes 2097176
  30.6 0.0 collective-permute-done.7
  30.6 0.0 collective-permute-done.6
  30.6 0.0 collective-permute-done.4
  30.6 0.0 collective-permute-done.5
  30.6 0.0 copy-start.11
  30.7 0.6 %copy-done.11 = f32[256,128]{1,0:T(8,128)} copy-done((f32[256,128]{1,0:T(8,128)}, f32[256,128]{1,0:T(8,128)S(1)}, u32[]{:S(2)}) %copy-start.11) | copy-done | bytes 131096
  31.3 0.1 pad_maximum_fusion.mine
  31.3 0.1 collective-permute-start.9
  31.4 1.1 %collective-permute-start.8 = (f32[256,128]{1,0:T(8,128)}, f32[256,128]{1,0:T(8,128)}, u32[]{:S(2)}, u32[]{:S(2)}) collective-permute-start(f32[256,128]{1,0:T(8,128)} %collective-permute-done.4), channel_id=1, source_target_pairs={{0,2},{1,3},{2,0},{3,1},{4,6},{5,7},{6,4},{7,5},{8,10},{9,11},{10,... | collective-permute-start | bytes 393224 | tf_op jit(solution)/shard_map/ppermute | solution.py:26
  32.5 0.1 pad_add_fusion.place
  32.6 0.0 copy-start.5
  32.6 1.2 %collective-permute-done.9.other = f32[3,2,256,128]{3,2,1,0:T(8,128)} collective-permute-done((f32[3,2,256,128]{3,2,1,0:T(8,128)S(1)}, f32[3,2,256,128]{3,2,1,0:T(8,128)}, u32[]{:S(2)}, u32[]{:S(2)}) %collective-permute-start.9) | collective-permute-done | bytes 786464 | tf_op jit(solution)/shard_map/ppermute | solution.py:26
  33.8 0.0 copy-start.7
  33.8 1.6 %copy-done.7 = f32[512,1024]{1,0:T(8,128)S(1)} copy-done((f32[512,1024]{1,0:T(8,128)S(1)}, f32[512,1024]{1,0:T(8,128)}, u32[]{:S(2)}) %copy-start.7) | copy-done | bytes 2097176
  35.4 0.0 copy-start.9
  35.4 0.9 %copy-done.9 = f32[512,128]{1,0:T(8,128)S(1)} copy-done((f32[512,128]{1,0:T(8,128)S(1)}, f32[512,128]{1,0:T(8,128)}, u32[]{:S(2)}) %copy-start.9) | copy-done | bytes 262168
  36.4 2.5 %shard_map.61.upper = f32[512,1024]{1,0:T(8,128)S(1)} custom-call(s32[2]{0:T(128)S(1)} %pad_add_fusion.place, bf16[1024,1024]{1,0:T(8,128)(2,1)S(1)} %copy-done, f32[16,8,1024]{2,1,0:T(8,128)S(1)} %copy-done.3, f32[512,1024]{1,0:T(8,128)S(1)} %copy-done.7, f32[512,128]{1,0:T(8,128)S(1)} %copy-done.9, f32[3,2,256,128]{3,2,1,0:T(8,128)S(1)} %pad_maximum_fusion.mine, ...), custom_call_target="tpu_custom_call" | custom-call | flops 1048576 | bytes 262144 | tf_op jit(solution)/shard_map/pallas_call | solution.py:228
  38.9 0.0 copy-done.5
  38.9 0.0 copy-start.12
  38.9 2.5 %shard_map.60.lower = f32[512,1024]{1,0:T(8,128)S(1)} custom-call(s32[2]{0:T(128)S(1)} %pad_add_fusion.place, bf16[1024,1024]{1,0:T(8,128)(2,1)S(1)} %copy-done, f32[16,8,1024]{2,1,0:T(8,128)S(1)} %copy-done.3, f32[512,1024]{1,0:T(8,128)S(1)} %copy-done.5, f32[512,128]{1,0:T(8,128)S(1)} %copy-done.9, f32[3,2,256,128]{3,2,1,0:T(8,128)S(1)} %pad_maximum_fusion.mine, ...), custom_call_target="tpu_custom_call" | custom-call | flops 1048576 | bytes 262144 | tf_op jit(solution)/shard_map/pallas_call | solution.py:228
  41.4 0.0 copy-start.10
  41.4 0.0 collective-permute-done.8
  41.4 0.0 copy-done.12
  41.5 1.1 %maximum_bitcast_fusion.4 = f32[1,2,256,128]{3,2,1,0:T(8,128)S(1)} fusion(f32[1,256,128]{2,1,0:T(8,128)} %bitcast.17, f32[1,256,128]{2,1,0:T(8,128)} %bitcast.16), kind=kLoop, calls=%fused_computation.6 | loop fusion | flops 65536 | bytes 524288 | tf_op jit(solution)/shard_map/stack | solution.py:370
  42.6 0.2 collective-permute-start.10
  42.8 1.8 %collective-permute-done.10.rest_1_ = f32[2,2,256,128]{3,2,1,0:T(8,128)S(1)} collective-permute-done((f32[2,2,256,128]{3,2,1,0:T(8,128)S(1)}, f32[2,2,256,128]{3,2,1,0:T(8,128)S(1)}, u32[]{:S(2)}, u32[]{:S(2)}) %collective-permute-start.10) | collective-permute-done | bytes 524320 | tf_op jit(solution)/shard_map/ppermute | solution.py:26
  44.6 0.0 copy-done.10
  44.6 6.2 %shard_map.62 = bf16[1024,1024]{1,0:T(8,128)(2,1)} custom-call(s32[2]{0:T(128)S(1)} %pad_add_fusion.place, bf16[1024,1024]{1,0:T(8,128)(2,1)S(1)} %copy-done, f32[16,8,1024]{2,1,0:T(8,128)S(1)} %copy-done.3, f32[512,1024]{1,0:T(8,128)S(1)} %shard_map.60.lower, f32[512,1024]{1,0:T(8,128)S(1)} %shard_map.61.upper, ...), custom_call_target="tpu_custom_call" | custom-call | flops 2684354560 | bytes 12582912 | tf_op jit(solution)/shard_map/pallas_call | solution.py:287
  (8 shorter events, 0.2 us)
Async XLA Ops:
  2.4 2.3 %collective-permute-start = (f32[512,128]{1,0:T(8,128)S(1)}, f32[512,128]{1,0:T(8,128)S(1)}, u32[]{:S(2)}, u32[]{:S(2)}) collective-permute-start(f32[512,128]{1,0:T(8,128)S(1)} %shard_map.55), channel_id=1, source_target_pairs={{0,1},{1,0},{2,3},{3,2},{4,5},{5,4},{6,7},{7,6},{8,9},{9,8},{10,11... | collective-permute-start | bytes 786440 | tf_op jit(solution)/shard_map/ppermute | solution.py:26
  4.7 6.8 %copy-start.8 = (f32[512,128]{1,0:T(8,128)}, f32[512,128]{1,0:T(8,128)S(1)}, u32[]{:S(2)}) copy-start(f32[512,128]{1,0:T(8,128)S(1)} %collective-permute-done.first) | copy-start | bytes 786436
  4.7 6.7 %collective-permute-start.1 = (f32[256,128]{1,0:T(8,128)S(1)}, f32[256,128]{1,0:T(8,128)S(1)}, u32[]{:S(2)}, u32[]{:S(2)}) collective-permute-start(f32[256,128]{1,0:T(8,128)S(1)} %dynamic-slice_add_fusion.1), channel_id=1, source_target_pairs={{0,2},{1,3},{2,0},{3,1},{4,6},{5,7},{6,4},{7,5},{8,10},{9,11},{10,... | collective-permute-start | bytes 393224 | tf_op jit(solution)/shard_map/ppermute | solution.py:26
  7.3 6.0 %copy-start = (bf16[1024,1024]{1,0:T(8,128)(2,1)S(1)}, bf16[1024,1024]{1,0:T(8,128)(2,1)}, u32[]{:S(2)}) copy-start(bf16[1024,1024]{1,0:T(8,128)(2,1)} %queries.7) | copy-start | bytes 6291460
  7.3 6.0 %copy-start.1 = (bf16[1024,1024]{1,0:T(8,128)(2,1)S(1)}, bf16[1024,1024]{1,0:T(8,128)(2,1)}, u32[]{:S(2)}) copy-start(bf16[1024,1024]{1,0:T(8,128)(2,1)} %keys.5) | copy-start | bytes 6291460
  7.3 6.0 %copy-start.3 = (f32[16,8,1024]{2,1,0:T(8,128)S(1)}, f32[16,8,1024]{2,1,0:T(8,128)}, u32[]{:S(2)}) copy-start(f32[16,8,1024]{2,1,0:T(8,128)} %weights.7) | copy-start | bytes 1572868
  11.5 6.0 %collective-permute-start.2 = (f32[256,128]{1,0:T(8,128)S(1)}, f32[256,128]{1,0:T(8,128)S(1)}, u32[]{:S(2)}, u32[]{:S(2)}) collective-permute-start(f32[256,128]{1,0:T(8,128)S(1)} %get-tuple-element.41), channel_id=1, source_target_pairs={{0,4},{1,5},{2,6},{3,7},{4,0},{5,1},{6,2},{7,3},{8,12},{9,13},{10,... | collective-permute-start | bytes 393224 | tf_op jit(solution)/shard_map/ppermute | solution.py:26
  13.3 1.6 %copy-start.2 = (bf16[1024,1024]{1,0:T(8,128)(2,1)S(1)}, bf16[1024,1024]{1,0:T(8,128)(2,1)}, u32[]{:S(2)}) copy-start(bf16[1024,1024]{1,0:T(8,128)(2,1)} %values.5) | copy-start | bytes 6291460
  17.4 11.8 %copy-start.4 = (f32[512,1024]{1,0:T(8,128)}, f32[512,1024]{1,0:T(8,128)S(1)}, u32[]{:S(2)}) copy-start(f32[512,1024]{1,0:T(8,128)S(1)} %shard_map.58.local) | copy-start | bytes 6291460
  17.5 5.0 %collective-permute-start.3 = (f32[256,128]{1,0:T(8,128)S(1)}, f32[256,128]{1,0:T(8,128)S(1)}, u32[]{:S(2)}, u32[]{:S(2)}) collective-permute-start(f32[256,128]{1,0:T(8,128)S(1)} %add.34), channel_id=1, source_target_pairs={{0,8},{8,0},{16,24},{24,16},{1,9},{9,1},{17,25},{25,17},{2,10},{10... | collective-permute-start | bytes 393224 | tf_op jit(solution)/shard_map/ppermute | solution.py:26
  19.1 11.4 %collective-permute-start.7 = (f32[256,128]{1,0:T(8,128)S(1)}, f32[256,128]{1,0:T(8,128)S(1)}, u32[]{:S(2)}, u32[]{:S(2)}) collective-permute-start(f32[256,128]{1,0:T(8,128)S(1)} %get-tuple-element.66), channel_id=1, source_target_pairs={{0,2},{1,3},{2,0},{3,1},{4,6},{5,7},{6,4},{7,5},{8,10},{9,11},{10,... | collective-permute-start | bytes 393224 | tf_op jit(solution)/shard_map/ppermute | solution.py:26
  20.6 10.0 %collective-permute-start.6 = (f32[1,256,128]{2,1,0:T(8,128)S(1)}, f32[1,256,128]{2,1,0:T(8,128)S(1)}, u32[]{:S(2)}, u32[]{:S(2)}) collective-permute-start(f32[1,256,128]{2,1,0:T(8,128)S(1)} %bitcast.27), channel_id=1, source_target_pairs={{0,2},{1,3},{2,0},{3,1},{4,6},{5,7},{6,4},{7,5},{8,10},{9,11},{10,... | collective-permute-start | bytes 393224 | tf_op jit(solution)/shard_map/ppermute | solution.py:26
  22.5 8.0 %collective-permute-start.4 = (f32[256,128]{1,0:T(8,128)S(1)}, f32[256,128]{1,0:T(8,128)}, u32[]{:S(2)}, u32[]{:S(2)}) collective-permute-start(f32[256,128]{1,0:T(8,128)S(1)} %add.35), channel_id=1, source_target_pairs={{0,16},{8,24},{16,0},{24,8},{1,17},{9,25},{17,1},{25,9},{2,18},{10... | collective-permute-start | bytes 393224 | tf_op jit(solution)/shard_map/ppermute | solution.py:26
  25.2 5.4 %collective-permute-start.5 = (f32[256,128]{1,0:T(8,128)S(1)}, f32[256,128]{1,0:T(8,128)S(1)}, u32[]{:S(2)}, u32[]{:S(2)}) collective-permute-start(f32[256,128]{1,0:T(8,128)S(1)} %collective-permute-done.3), channel_id=1, source_target_pairs={{0,2},{1,3},{2,0},{3,1},{4,6},{5,7},{6,4},{7,5},{8,10},{9,11},{10,... | collective-permute-start | bytes 393224 | tf_op jit(solution)/shard_map/ppermute | solution.py:26
  29.3 1.3 %copy-start.6 = (f32[512,1024]{1,0:T(8,128)}, f32[512,1024]{1,0:T(8,128)S(1)}, u32[]{:S(2)}) copy-start(f32[512,1024]{1,0:T(8,128)S(1)} %shard_map.59.local) | copy-start | bytes 6291460
  30.6 0.6 %copy-start.11 = (f32[256,128]{1,0:T(8,128)}, f32[256,128]{1,0:T(8,128)S(1)}, u32[]{:S(2)}) copy-start(f32[256,128]{1,0:T(8,128)S(1)} %collective-permute-done.5) | copy-start | bytes 393220
  31.3 2.5 %collective-permute-start.9 = (f32[3,2,256,128]{3,2,1,0:T(8,128)S(1)}, f32[3,2,256,128]{3,2,1,0:T(8,128)}, u32[]{:S(2)}, u32[]{:S(2)}) collective-permute-start(f32[3,2,256,128]{3,2,1,0:T(8,128)S(1)} %pad_maximum_fusion.mine), channel_id=1, source_target_pairs={{0,1},{1,0},{2,3},{3,2},{4,5},{5,4},{6,7},{7,6},{8,9},{9,8},{10,11... | collective-permute-start | bytes 2359304 | tf_op jit(solution)/shard_map/ppermute | solution.py:26
  31.4 10.0 %collective-permute-start.8 = (f32[256,128]{1,0:T(8,128)}, f32[256,128]{1,0:T(8,128)}, u32[]{:S(2)}, u32[]{:S(2)}) collective-permute-start(f32[256,128]{1,0:T(8,128)} %collective-permute-done.4), channel_id=1, source_target_pairs={{0,2},{1,3},{2,0},{3,1},{4,6},{5,7},{6,4},{7,5},{8,10},{9,11},{10,... | collective-permute-start | bytes 393224 | tf_op jit(solution)/shard_map/ppermute | solution.py:26
  32.6 6.3 %copy-start.5 = (f32[512,1024]{1,0:T(8,128)S(1)}, f32[512,1024]{1,0:T(8,128)}, u32[]{:S(2)}) copy-start(f32[512,1024]{1,0:T(8,128)} %copy-done.4) | copy-start | bytes 6291460
  33.8 1.6 %copy-start.7 = (f32[512,1024]{1,0:T(8,128)S(1)}, f32[512,1024]{1,0:T(8,128)}, u32[]{:S(2)}) copy-start(f32[512,1024]{1,0:T(8,128)} %copy-done.6) | copy-start | bytes 6291460
  35.4 0.9 %copy-start.9 = (f32[512,128]{1,0:T(8,128)S(1)}, f32[512,128]{1,0:T(8,128)}, u32[]{:S(2)}) copy-start(f32[512,128]{1,0:T(8,128)} %copy-done.8) | copy-start | bytes 786436
  38.9 2.6 %copy-start.12 = (f32[256,128]{1,0:T(8,128)S(1)}, f32[256,128]{1,0:T(8,128)}, u32[]{:S(2)}) copy-start(f32[256,128]{1,0:T(8,128)} %copy-done.11) | copy-start | bytes 393220
  41.4 3.2 %copy-start.10 = (bf16[1024,1024]{1,0:T(8,128)(2,1)S(1)}, bf16[1024,1024]{1,0:T(8,128)(2,1)}, u32[]{:S(2)}) copy-start(bf16[1024,1024]{1,0:T(8,128)(2,1)} %rest_2_.1) | copy-start | bytes 6291460
  42.6 2.0 %collective-permute-start.10 = (f32[2,2,256,128]{3,2,1,0:T(8,128)S(1)}, f32[2,2,256,128]{3,2,1,0:T(8,128)S(1)}, u32[]{:S(2)}, u32[]{:S(2)}) collective-permute-start(f32[2,2,256,128]{3,2,1,0:T(8,128)S(1)} %pad_maximum_fusion.1.rest_0_), channel_id=1, source_target_pairs={{0,1},{1,0},{2,3},{3,2},{4,5},{5,4},{6,7},{7,6},{8,9},{9,8},{10,11... | collective-permute-start | bytes 1572872 | tf_op jit(solution)/shard_map/ppermute | solution.py:26

commit v3 on v2

--- a/solution.py
+++ b/solution.py
@@ -38,6 +38,10 @@
 
 def params(limit):
     return pltpu.CompilerParams(vmem_limit_bytes=limit * MIB)
+
+
+def outside(*parts):
+    return tuple(pltpu.with_memory_space_constraint(part, pltpu.HBM) for part in parts)
 
 
 def product(left, right):
@@ -102,14 +106,14 @@
     return jnp.concatenate(parts, axis=0)
 
 
-def local_kernel(first_head, queries, keys, values, weights, local, rows):
+def local_kernel(half, queries, keys, values, weights, local, rows):
     tokens, width = queries.shape
     chunks = tokens // CHUNK
     levels = rows.shape[1]
     top = bits_of(CHUNK)
     spans = [slice(low, low + CHUNK) for low in range(0, tokens, CHUNK)]
     parts = [slice(low, low + HEAD) for low in range(0, width, HEAD)]
-    first = first_head + pl.program_id(0) * len(parts)
+    first = (half[0] * pl.num_programs(0) + pl.program_id(0)) * len(parts)
     for at in range(len(parts)):
         rows[at] = weights[:, pl.ds(first + at, 1), :].reshape(levels, tokens)
     flipped = turned(values[...])
@@ -160,54 +164,50 @@
     tokens, width = queries.shape
     step = 2 * HEAD
     steps = width // step // 2
-    column = pl.BlockSpec((tokens, step), lambda pair: (0, half * steps + pair))
+    column = pl.BlockSpec((tokens, step), lambda pair, half: (0, half[0] * steps + pair))
     return pl.pallas_call(
-        functools.partial(local_kernel, half * steps * 2),
-        grid=(steps,),
-        in_specs=[column, column, column, pl.BlockSpec(level_weights.shape, lambda pair: (0, 0, 0))],
-        out_specs=pl.BlockSpec((step, tokens), lambda pair: (pair, 0)),
-        out_shape=jax.ShapeDtypeStruct((width // 2, tokens), F32),
-        scratch_shapes=[pltpu.VMEM((2, level_weights.shape[0], tokens), F32)],
+        local_kernel,
+        grid_spec=pltpu.PrefetchScalarGridSpec(
+            num_scalar_prefetch=1,
+            grid=(steps,),
+            in_specs=[column, column, column, pl.BlockSpec(level_weights.shape, lambda pair, half: (0, 0, 0))],
+            out_specs=pl.BlockSpec((step, tokens), lambda pair, half: (pair, 0)),
+            scratch_shapes=[pltpu.VMEM((2, level_weights.shape[0], tokens), F32)],
+        ),
+        out_shape=pltpu.HBM((width // 2, tokens), F32),
         cost_estimate=cost(tokens * width, MIB // 4),
         compiler_params=params(16),
-    )(queries, keys, values, level_weights)
+    )(half.reshape(1), queries, keys, values, level_weights)
 
 
 def has_bit(place, bit):
     return jnp.bitwise_and(jnp.right_shift(place, bit), 1) == 1
 
 
-def fill(states, base, half, place, digit_place, first_digit, mine, other, first=None):
-    core = jnp.bitwise_and(place, 1)
-    side = jnp.bitwise_and(jnp.right_shift(place, 1), 1)
-    count, quarters, size = mine.shape[:3]
-    for quarter in range(quarters):
-        slot = jnp.bitwise_xor(side, quarter)
-        for bit in range(count):
-            if first is not None and bit == 0:
-                here, there = first[quarter * size : (quarter + 1) * size, :], other[0, slot]
-            else:
-                here, there = mine[bit, slot], other[bit, slot]
-            state = jnp.where(core == half, here, there)
-            state = jnp.where(has_bit(digit_place, first_digit + bit), state, 0.0).astype(BF16)
-            for at in range(0, size, HEAD):
-                head = (base + quarter * size + at) // HEAD
-                low = (first_digit + bit) * HEAD
-                states[head, low : low + HEAD, :] = state[at : at + HEAD]
-
-
-def near_kernel(half, heads, place, queries, weights, local, first, mine, other, near, states, rows):
+def near_kernel(half, place, queries, weights, local, held, *rest):
+    *first, near, states, rows = rest
     step = pl.program_id(0)
     bits = states.shape[1] // HEAD
+    size = held.shape[1]
 
     @pl.when(step == 0)
     def _():
-        fill(states, 0, half, place[0], place[0], 0, mine, other, first)
+        side = jnp.bitwise_and(jnp.right_shift(place[0], 1), 1)
+        for quarter in range(2):
+            slot = jnp.bitwise_xor(side, quarter)
+            for bit in range(bits):
+                if first and bit == 0:
+                    state = first[0][quarter * size : (quarter + 1) * size, :]
+                else:
+                    state = held[2 * bit + slot]
+                state = jnp.where(has_bit(place[0], bit), state, 0.0).astype(BF16)
+                for at in range(0, size, HEAD):
+                    states[(quarter * size + at) // HEAD, bit * HEAD : (bit + 1) * HEAD, :] = state[at : at + HEAD]
 
     for at in range(rows.shape[0]):
         part = slice(at * HEAD, (at + 1) * HEAD)
         head = step * rows.shape[0] + at
-        rows[at] = weights[:, pl.ds(half * heads + head, 1), :].reshape(rows.shape[1:])
+        rows[at] = weights[:, pl.ds(half[0] * states.shape[0] + head, 1), :].reshape(rows.shape[1:])
         products = product_nt(states[head], queries[:, part])
         total = local[part, :]
         for bit in range(bits):
@@ -216,57 +216,68 @@
         near[part, :] = total
 
 
-def near_part(half, bits, place, queries, level_weights, local, first, mine, other):
+def near_part(half, place, bits, queries, level_weights, local, held, *first):
     tokens, width = queries.shape
     heads = width // HEAD // 2
     step = 2 * HEAD
     steps = width // step // 2
-    column = pl.BlockSpec((tokens, step), lambda pair: (0, half * steps + pair))
-    band = pl.BlockSpec((step, tokens), lambda pair: (pair, 0))
-    fixed = [pl.BlockSpec(part.shape, lambda pair, rank=part.ndim: (0,) * rank)
-             for part in (first, mine, other)]
     return pl.pallas_call(
-        functools.partial(near_kernel, half, heads),
-        grid=(steps,),
-        in_specs=[
-            pl.BlockSpec(memory_space=pltpu.SMEM),
-            column,
-            pl.BlockSpec(level_weights.shape, lambda pair: (0, 0, 0)),
-            band,
-            *fixed,
-        ],
-        out_specs=band,
-        out_shape=jax.ShapeDtypeStruct((width // 2, tokens), F32),
-        scratch_shapes=[
-            pltpu.VMEM((heads, bits * HEAD, HEAD), BF16),
-            pltpu.VMEM((2, level_weights.shape[0], tokens), F32),
-        ],
+        near_kernel,
+        grid_spec=pltpu.PrefetchScalarGridSpec(
+            num_scalar_prefetch=2,
+            grid=(steps,),
+            in_specs=[
+                pl.BlockSpec((tokens, step), lambda pair, half, place: (0, half[0] * steps + pair)),
+                pl.BlockSpec(level_weights.shape, lambda pair, half, place: (0, 0, 0)),
+                pl.BlockSpec((step, tokens), lambda pair, half, place: (pair, 0)),
+                pl.BlockSpec((2 * bits,) + held.shape[1:], lambda pair, half, place: (0, 0, 0)),
+                *[pl.BlockSpec(part.shape, lambda pair, half, place: (0, 0)) for part in first],
+            ],
+            out_specs=pl.BlockSpec((step, tokens), lambda pair, half, place: (pair, 0)),
+            scratch_shapes=[
+                pltpu.VMEM((heads, bits * HEAD, HEAD), BF16),
+                pltpu.VMEM((2, level_weights.shape[0], tokens), F32),
+            ],
+        ),
+        out_shape=pltpu.VMEM((width // 2, tokens), F32),
         cost_estimate=cost(tokens * width, MIB // 4),
         compiler_params=params(16),
-    )(place, queries, level_weights, local, first, mine, other)
-
-
-def far_kernel(first_level, place, queries, weights, lower, upper, *rest):
-    arrived, (out_weight, mixed, states, flipped, attended) = rest[:-5], rest[-5:]
+    )(half.reshape(1), place, *outside(queries, level_weights, local), held, *first)
+
+
+def far_kernel(first_level, place, queries, weights, near_mine, near_other, early, early_other, late, late_other,
+               out_weight, mixed, states, flipped, attended):
     rows, width = attended.shape
     bits = states.shape[1] // HEAD
+    size = late.shape[0]
+    skip = early.shape[0] + 1 - 2 * bits
+    core = jnp.bitwise_and(place[0], 1)
 
     @pl.when(pl.program_id(0) == 0)
     def _():
-        for half in range(2):
-            digit = 0
-            for mine, other in zip(arrived[::2], arrived[1::2]):
-                fill(states, half * (width // 2), half, place[0], place[1], digit, mine, other)
-                digit += mine.shape[0]
-
-    for half, near in enumerate((lower, upper)):
+        side = jnp.bitwise_and(jnp.right_shift(place[0], 1), 1)
+        for bit in range(bits):
+            mine, other = ([part[skip + 2 * bit], part[skip + 2 * bit + 1] if bit + 1 < bits else final[...]]
+                           for part, final in ((early, late), (early_other, late_other)))
+            for quarter in range(4):
+                here, there = (jnp.where(side == quarter % 2, *part) for part in (mine, other))
+                state = jnp.where(core == quarter // 2, here, there)
+                state = jnp.where(has_bit(place[1], bit), state, 0.0).astype(BF16)
+                for at in range(0, size, HEAD):
+                    head = (quarter * size + at) // HEAD
+                    states[head, bit * HEAD : (bit + 1) * HEAD, :] = state[at : at + HEAD]
+
+    start = pl.multiple_of(pl.program_id(0) * rows, rows)
+    band = pl.ds(start, rows)
+    for half in range(2):
         for low in range(0, width // 2, HEAD):
             part = slice(half * (width // 2) + low, half * (width // 2) + low + HEAD)
             head = part.start // HEAD
-            products = product_nt(states[head], queries[:, part])
-            total = near[low : low + HEAD, :]
+            products = product_nt(states[head], queries[band, part])
+            span = slice(low, low + HEAD)
+            total = jnp.where(core == half, near_mine[span, band], near_other[span, band])
             for bit in range(bits):
-                row = weights[first_level + bit, head : head + 1, :]
+                row = weights[first_level + bit, head : head + 1, band]
                 total = total + row * products[bit * HEAD : (bit + 1) * HEAD]
             flipped[part, :] = total.astype(BF16)
     unit = identity(CHUNK)
@@ -277,26 +288,16 @@
     mixed[...] = product(attended[...], out_weight[...]).astype(BF16)
 
 
-def far_part(first_level, place, queries, level_weights, lower, upper, arrived, out_weight):
+def far_part(first_level, bits, place, *operands):
+    queries = operands[0]
     tokens, width = queries.shape
-    bits = sum(part.shape[0] for part in arrived[::2])
     rows = min(2 * CHUNK, tokens)
-    band = pl.BlockSpec((rows, width), lambda step: (step, 0))
-    near = pl.BlockSpec((width // 2, rows), lambda step: (0, step))
-    fixed = [pl.BlockSpec(part.shape, lambda step: (0, 0, 0, 0)) for part in arrived]
     return pl.pallas_call(
         functools.partial(far_kernel, first_level),
         grid=(tokens // rows,),
-        in_specs=[
-            pl.BlockSpec(memory_space=pltpu.SMEM),
-            band,
-            pl.BlockSpec(level_weights.shape[:2] + (rows,), lambda step: (0, 0, step)),
-            near,
-            near,
-            *fixed,
-            pl.BlockSpec(out_weight.shape, lambda step: (0, 0)),
-        ],
-        out_specs=band,
+        in_specs=[pl.BlockSpec(memory_space=pltpu.SMEM)]
+        + [pl.BlockSpec(memory_space=pltpu.VMEM)] * len(operands),
+        out_specs=pl.BlockSpec((rows, width), lambda step: (step, 0)),
         out_shape=jax.ShapeDtypeStruct((tokens, width), BF16),
         scratch_shapes=[
             pltpu.VMEM((width // HEAD, bits * HEAD, HEAD), BF16),
@@ -305,7 +306,7 @@
         ],
         cost_estimate=cost(2 * tokens * width * (width + bits * HEAD), 12 * MIB),
         compiler_params=params(28),
-    )(place, queries, level_weights, lower, upper, *arrived, out_weight)
+    )(place, *(pltpu.with_memory_space_constraint(part, pltpu.VMEM) for part in operands))
 
 
 def body(queries, keys, values, level_weights, out_weight):
@@ -313,13 +314,13 @@
     inner_bits, outer_bits = bits_of(inner), bits_of(outer)
     inner_place, outer_place = lax.axis_index("inner"), lax.axis_index("outer")
     place = jnp.stack([inner_place, outer_place]).astype(jnp.int32)
-    core = jnp.bitwise_and(inner_place, 1)
+    core = jnp.bitwise_and(inner_place, 1).astype(jnp.int32)
     side = jnp.bitwise_and(jnp.right_shift(inner_place, 1), 1)
     half = keys.shape[1] // 2
     quarter = half // 2
     tie = lax.optimization_barrier
 
-    inputs = tuple(pltpu.with_memory_space_constraint(part, pltpu.HBM) for part in (keys, values))
+    inputs = outside(keys, values)
     give = block_state(1 - core, 2, *inputs)
     give, inputs = tie((give, inputs))
     first = swap(give, "inner", 1)
@@ -332,16 +333,16 @@
     passed, inputs = tie((passed, inputs))
     buckets = [swap(passed, "inner", 2)]
     keep_ours = block_state(2 * core + side, 4, *inputs)
-    inputs = (queries, keys, values, level_weights)
+    inputs = outside(queries, keys, values, level_weights)
     own = quarter_of(side, keep_ours)
     others = [swap(own, "inner", 2)]
     running = own + buckets[0]
     running, inputs = tie((running, inputs))
-    local = [local_part(0, *inputs)]
+    local = [local_part(core, *inputs)]
     for bit in range(2, inner_bits):
         arrived = swap(running, "inner", 1 << bit)
         if bit == 2:
-            arrived, local[0] = tie((arrived, local[0]))
+            arrived, others, local[0] = tie((arrived, others, local[0]))
         buckets.append(arrived)
         running = running + arrived
     sent = swap(jnp.stack(buckets[1:]), "inner", 2)
@@ -354,23 +355,26 @@
         far.append(swap(running, "outer", 1 << bit))
         beside.append(swap(far[-2], "inner", 2))
         if bit == 1:
-            local.append(local_part(1, *inputs))
+            local.append(local_part(1 - core, *inputs))
             far[-1], beside, sent, others, local[1] = tie((far[-1], beside, sent, others, local[1]))
     if len(local) < 2:
-        local.append(local_part(1, *inputs))
+        local.append(local_part(1 - core, *inputs))
+        far[-1], sent, others, local[1] = tie((far[-1], sent, others, local[1]))
+    late = swap(far[-1], "inner", 2)
     others += [sent[at] for at in range(inner_bits - 2)]
-    mine = jnp.stack([jnp.stack([keep_ours, keep_theirs])] + [jnp.stack(pair) for pair in zip(buckets, others)])
+    pairs = [(keep_ours, keep_theirs), *zip(buckets, others), *zip(far, beside)]
+    mine = jnp.stack([part for pair in pairs for part in pair] + far[-1:])
     other = swap(mine, "inner", 1)
-    far[-1], local = tie((far[-1], local))
-    last = swap(far[-1], "inner", 2)
     nears = [
-        near_part(part, inner_bits, place, queries, level_weights, local[part], first, mine, other) for part in range(2)
+        near_part(core, place, inner_bits, queries, level_weights, local[0], mine, first),
+        near_part(1 - core, place, inner_bits, queries, level_weights, local[1], other),
     ]
-    last, beside, nears = tie((last, beside, nears))
-    far_mine = jnp.stack([jnp.stack(pair) for pair in zip(far, beside + [last])])
-    arrivals = [far_mine, swap(far_mine, "inner", 1)]
+    late, nears = tie((late, nears))
+    late_other = swap(late, "inner", 1)
     first_level = LOCAL_BITS + 1 + inner_bits
-    return far_part(first_level, place, queries, level_weights, *nears, arrivals, out_weight)
+    return far_part(
+        first_level, outer_bits, place, queries, level_weights, *nears, mine, other, late, late_other, out_weight
+    )
 
 
 def solution(mesh):

time: 51.2 us -> 50.2 us (0.980)
  Pallas kernels: 22.3 us -> 29.5 us
  local copies, waits for them, and re-layouts: 6.08 us -> 0.12 us
  other arithmetic: 1.48 us -> 0.16 us
    pallas_call x4, Pallas kernels: 10 us -> 16.7 us  [the longest x2 9.68 us: local_part(): pl.pallas_call(local_kernel, grid_spec=pltpu.PrefetchScalarGridSpec(num_s...]
    unnamed x26 -> x14, local copies, waits for them, and re-layouts: 6.08 us -> 0.11 us
    another operation x6 -> x0, other arithmetic: 1.32 us -> none  [the longest x3 1.19 us: body(): jnp.stack([jnp.stack(pair) for pair in zip(far, beside + [last])])]
    pallas_call x1, Pallas kernels: 6.23 us -> 6.84 us  [far_part(): pl.pallas_call(functools.partial(far_kernel, first_level), grid=(tokens /...]
  transfers between devices with their start and end apart: 11 -> 11, of which waited for: 4 -> 3; matrix products, arithmetic and copies ran while one was open for 0% -> 0% of each run, Pallas kernels for 27% -> 41%
where the time goes in v3:
time: 50.2 us; the launch traced here: 50 us
  Pallas kernels  29.5 us (59%)
  starting transfers between devices  13.7 us (27%)
  waiting for transfers between devices  6.36 us (13%)
    ppermute x11, starting transfers between devices, swap(): lax.ppermute(block, axis, [(place, place ^ stride) for place in range(cou...  13.7 us
    pallas_call x2, Pallas kernels, local_part(): pl.pallas_call(local_kernel, grid_spec=pltpu.PrefetchScalarGridSpec(num_s...  9.68 us
    pallas_call x2, Pallas kernels, near_part(): pl.pallas_call(near_kernel, grid_spec=pltpu.PrefetchScalarGridSpec(num_sc...  7.04 us
    pallas_call x1, Pallas kernels, far_part(): pl.pallas_call(functools.partial(far_kernel, first_level), grid=(tokens /...  6.84 us
    ppermute x11, waiting for transfers between devices, swap(): lax.ppermute(block, axis, [(place, place ^ stride) for place in range(cou...  6.36 us
    pallas_call x3, Pallas kernels, block_state(): pl.pallas_call(state_kernel, grid_spec=pltpu.PrefetchScalarGridSpec(num_s...  5.93 us
  transfers between devices with their start and end apart: 11, of which 3 were waited for; matrix products, arithmetic and copies ran while one was open for 0% of the time, Pallas kernels for 41%

profile of v3, /device:TPU:0, one launch (start us, length us, event | category | flops | bytes accessed | tf_op | source)
XLA Modules:
  0.0 50.0 jit_solution(2129927297055304641)
XLA Ops:
  0.0 2.4 %shard_map.55 = f32[512,128]{1,0:T(8,128)S(1)} custom-call(s32[1]{0:T(128)} %bitcast.4.place.half, bf16[1024,1024]{1,0:T(8,128)(2,1)} %keys.5, bf16[1024,1024]{1,0:T(8,128)(2,1)} %values.5), custom_call_target="tpu_custom_call" | custom-call | flops 134217728 | bytes 2621440 | tf_op jit(solution)/shard_map/pallas_call | solution.py:77
  2.4 0.5 %collective-permute-start = (f32[512,128]{1,0:T(8,128)S(1)}, f32[512,128]{1,0:T(8,128)S(1)}, u32[]{:S(2)}, u32[]{:S(2)}) collective-permute-start(f32[512,128]{1,0:T(8,128)S(1)} %shard_map.55), channel_id=1, source_target_pairs={{0,1},{1,0},{2,3},{3,2},{4,5},{5,4},{6,7},{7,6},{8,9},{9,8},{10,11... | collective-permute-start | bytes 786440 | tf_op jit(solution)/shard_map/ppermute | solution.py:26
  2.9 1.8 %shard_map.56 = f32[256,128]{1,0:T(8,128)S(1)} custom-call(s32[1]{0:T(128)} %bitcast.3.place, bf16[1024,1024]{1,0:T(8,128)(2,1)} %keys.5, bf16[1024,1024]{1,0:T(8,128)(2,1)} %values.5), custom_call_target="tpu_custom_call" | custom-call | flops 67108864 | bytes 1310720 | tf_op jit(solution)/shard_map/pallas_call | solution.py:77
  4.7 0.0 collective-permute-done.rest_0_
  4.7 2.6 %collective-permute-start.1 = (f32[256,128]{1,0:T(8,128)S(1)}, f32[256,128]{1,0:T(8,128)S(1)}, u32[]{:S(2)}, u32[]{:S(2)}) collective-permute-start(f32[256,128]{1,0:T(8,128)S(1)} %dynamic-slice_add_fusion.1), channel_id=1, source_target_pairs={{0,2},{1,3},{2,0},{3,1},{4,6},{5,7},{6,4},{7,5},{8,10},{9,11},{10,... | collective-permute-start | bytes 393224 | tf_op jit(solution)/shard_map/ppermute | solution.py:26
  7.3 1.8 %shard_map.57 = f32[256,128]{1,0:T(8,128)S(1)} custom-call(s32[1]{0:T(128)} %bitcast.2.place, bf16[1024,1024]{1,0:T(8,128)(2,1)} %keys.5, bf16[1024,1024]{1,0:T(8,128)(2,1)} %values.5), custom_call_target="tpu_custom_call" | custom-call | flops 67108864 | bytes 1310720 | tf_op jit(solution)/shard_map/pallas_call | solution.py:77
  9.1 2.4 %collective-permute-done.1 = f32[256,128]{1,0:T(8,128)S(1)} collective-permute-done((f32[256,128]{1,0:T(8,128)S(1)}, f32[256,128]{1,0:T(8,128)S(1)}, u32[]{:S(2)}, u32[]{:S(2)}) %collective-permute-start.1) | collective-permute-done | bytes 131104 | tf_op jit(solution)/shard_map/ppermute | solution.py:26
  11.5 1.8 %collective-permute-start.2 = (f32[256,128]{1,0:T(8,128)S(1)}, f32[256,128]{1,0:T(8,128)S(1)}, u32[]{:S(2)}, u32[]{:S(2)}) collective-permute-start(f32[256,128]{1,0:T(8,128)S(1)} %get-tuple-element.38), channel_id=1, source_target_pairs={{0,4},{1,5},{2,6},{3,7},{4,0},{5,1},{6,2},{7,3},{8,12},{9,13},{10,... | collective-permute-start | bytes 393224 | tf_op jit(solution)/shard_map/ppermute | solution.py:26
  13.3 1.5 %collective-permute-start.3 = (f32[256,128]{1,0:T(8,128)S(1)}, f32[256,128]{1,0:T(8,128)S(1)}, u32[]{:S(2)}, u32[]{:S(2)}) collective-permute-start(f32[256,128]{1,0:T(8,128)S(1)} %get-tuple-element.60), channel_id=1, source_target_pairs={{0,2},{1,3},{2,0},{3,1},{4,6},{5,7},{6,4},{7,5},{8,10},{9,11},{10,... | collective-permute-start | bytes 393224 | tf_op jit(solution)/shard_map/ppermute | solution.py:26
  14.8 4.8 %shard_map.58.local = f32[512,1024]{1,0:T(8,128)} custom-call(s32[1]{0:T(128)} %bitcast.5.half, bf16[1024,1024]{1,0:T(8,128)(2,1)} %queries.7, bf16[1024,1024]{1,0:T(8,128)(2,1)} %keys.5, bf16[1024,1024]{1,0:T(8,128)(2,1)} %values.5, f32[16,8,1024]{2,1,0:T(8,128)} %weights.7), custom_call_target="tpu_custom_call" | custom-call | flops 1048576 | bytes 262144 | tf_op jit(solution)/shard_map/pallas_call | solution.py:168
  19.7 0.0 collective-permute-done.2
  19.7 0.0 collective-permute-done.3
  19.7 1.6 %collective-permute-start.4 = (f32[256,128]{1,0:T(8,128)S(1)}, f32[256,128]{1,0:T(8,128)S(1)}, u32[]{:S(2)}, u32[]{:S(2)}) collective-permute-start(f32[256,128]{1,0:T(8,128)S(1)} %add.34), channel_id=1, source_target_pairs={{0,8},{8,0},{16,24},{24,16},{1,9},{9,1},{17,25},{25,17},{2,10},{10... | collective-permute-start | bytes 393224 | tf_op jit(solution)/shard_map/ppermute | solution.py:26
  21.3 0.6 %collective-permute-start.7 = (f32[1,256,128]{2,1,0:T(8,128)S(1)}, f32[1,256,128]{2,1,0:T(8,128)S(1)}, u32[]{:S(2)}, u32[]{:S(2)}) collective-permute-start(f32[1,256,128]{2,1,0:T(8,128)S(1)} %bitcast.22), channel_id=1, source_target_pairs={{0,2},{1,3},{2,0},{3,1},{4,6},{5,7},{6,4},{7,5},{8,10},{9,11},{10,... | collective-permute-start | bytes 393224 | tf_op jit(solution)/shard_map/ppermute | solution.py:26
  21.9 2.8 %collective-permute-done.4 = f32[256,128]{1,0:T(8,128)S(1)} collective-permute-done((f32[256,128]{1,0:T(8,128)S(1)}, f32[256,128]{1,0:T(8,128)S(1)}, u32[]{:S(2)}, u32[]{:S(2)}) %collective-permute-start.4) | collective-permute-done | bytes 131104 | tf_op jit(solution)/shard_map/ppermute | solution.py:26
  24.7 2.6 %collective-permute-start.5 = (f32[256,128]{1,0:T(8,128)S(1)}, f32[256,128]{1,0:T(8,128)S(1)}, u32[]{:S(2)}, u32[]{:S(2)}) collective-permute-start(f32[256,128]{1,0:T(8,128)S(1)} %add.35), channel_id=1, source_target_pairs={{0,16},{8,24},{16,0},{24,8},{1,17},{9,25},{17,1},{25,9},{2,18},{10... | collective-permute-start | bytes 393224 | tf_op jit(solution)/shard_map/ppermute | solution.py:26
  27.4 0.5 %collective-permute-start.6 = (f32[256,128]{1,0:T(8,128)S(1)}, f32[256,128]{1,0:T(8,128)S(1)}, u32[]{:S(2)}, u32[]{:S(2)}) collective-permute-start(f32[256,128]{1,0:T(8,128)S(1)} %collective-permute-done.4), channel_id=1, source_target_pairs={{0,2},{1,3},{2,0},{3,1},{4,6},{5,7},{6,4},{7,5},{8,10},{9,11},{10,... | collective-permute-start | bytes 393224 | tf_op jit(solution)/shard_map/ppermute | solution.py:26
  27.9 4.9 %shard_map.59.local = f32[512,1024]{1,0:T(8,128)} custom-call(s32[1]{0:T(128)} %bitcast.4.place.half, bf16[1024,1024]{1,0:T(8,128)(2,1)} %queries.7, bf16[1024,1024]{1,0:T(8,128)(2,1)} %keys.5, bf16[1024,1024]{1,0:T(8,128)(2,1)} %values.5, f32[16,8,1024]{2,1,0:T(8,128)} %weights.7), custom_call_target="tpu_custom_call" | custom-call | flops 1048576 | bytes 262144 | tf_op jit(solution)/shard_map/pallas_call | solution.py:168
  32.8 0.0 collective-permute-done.7
  32.8 0.0 collective-permute-done.5
  32.8 0.0 collective-permute-done.6
  32.9 0.1 collective-permute-start.9
  33.0 1.6 %collective-permute-start.8 = (f32[256,128]{1,0:T(8,128)S(1)}, f32[256,128]{1,0:T(8,128)S(1)}, u32[]{:S(2)}, u32[]{:S(2)}) collective-permute-start(f32[256,128]{1,0:T(8,128)S(1)} %collective-permute-done.5), channel_id=1, source_target_pairs={{0,2},{1,3},{2,0},{3,1},{4,6},{5,7},{6,4},{7,5},{8,10},{9,11},{10,... | collective-permute-start | bytes 393224 | tf_op jit(solution)/shard_map/ppermute | solution.py:26
  34.6 0.1 pad_add_fusion.place
  34.6 3.3 %shard_map.60.near_mine = f32[512,1024]{1,0:T(8,128)S(1)} custom-call(s32[1]{0:T(128)} %bitcast.5.half, s32[2]{0:T(128)S(1)} %pad_add_fusion.place, bf16[1024,1024]{1,0:T(8,128)(2,1)} %queries.7, f32[16,8,1024]{2,1,0:T(8,128)} %weights.7, f32[512,1024]{1,0:T(8,128)} %shard_map.58.local, f32[9,256,128]{2,1,0:T(8,128)S(1)} %bitcast_dynamic-update-slice_fusion.held.early, ...), custom_call_target="tpu_custom_call" | custom-call | flops 1048576 | bytes 262144 | tf_op jit(solution)/shard_map/pallas_call | solution.py:224
  38.0 0.0 copy-start.1
  38.0 0.0 collective-permute-done.9.held.early_other
  38.0 0.0 copy-start
  38.0 0.0 copy-start.2
  38.0 3.7 %shard_map.61.near_other = f32[512,1024]{1,0:T(8,128)S(1)} custom-call(s32[1]{0:T(128)} %bitcast.4.place.half, s32[2]{0:T(128)S(1)} %pad_add_fusion.place, bf16[1024,1024]{1,0:T(8,128)(2,1)} %queries.7, f32[16,8,1024]{2,1,0:T(8,128)} %weights.7, f32[512,1024]{1,0:T(8,128)} %shard_map.59.local, f32[9,256,128]{2,1,0:T(8,128)S(1)} %collective-permute-done.9.held.early_other), custom_call_target="tpu_custom_call" | custom-call | flops 1048576 | bytes 262144 | tf_op jit(solution)/shard_map/pallas_call | solution.py:224
  41.7 0.0 collective-permute-done.8.late
  41.8 0.2 collective-permute-start.10
  42.0 1.2 %collective-permute-done.10.late_other = f32[256,128]{1,0:T(8,128)S(1)} collective-permute-done((f32[256,128]{1,0:T(8,128)S(1)}, f32[256,128]{1,0:T(8,128)S(1)}, u32[]{:S(2)}, u32[]{:S(2)}) %collective-permute-start.10) | collective-permute-done | bytes 131104 | tf_op jit(solution)/shard_map/ppermute | solution.py:26
  43.2 0.0 copy-done.1
  43.2 0.0 copy-done
  43.2 0.0 copy-done.2
  43.2 6.8 %shard_map.62 = bf16[1024,1024]{1,0:T(8,128)(2,1)} custom-call(s32[2]{0:T(128)S(1)} %pad_add_fusion.place, bf16[1024,1024]{1,0:T(8,128)(2,1)S(1)} %copy-done, f32[16,8,1024]{2,1,0:T(8,128)S(1)} %copy-done.1, f32[512,1024]{1,0:T(8,128)S(1)} %shard_map.60.near_mine, f32[512,1024]{1,0:T(8,128)S(1)} %shard_map.61.near_other, ...), custom_call_target="tpu_custom_call" | custom-call | flops 2684354560 | bytes 12582912 | tf_op jit(solution)/shard_map/pallas_call | solution.py:295
  (13 shorter events, 0.2 us)
Async XLA Ops:
  2.4 2.3 %collective-permute-start = (f32[512,128]{1,0:T(8,128)S(1)}, f32[512,128]{1,0:T(8,128)S(1)}, u32[]{:S(2)}, u32[]{:S(2)}) collective-permute-start(f32[512,128]{1,0:T(8,128)S(1)} %shard_map.55), channel_id=1, source_target_pairs={{0,1},{1,0},{2,3},{3,2},{4,5},{5,4},{6,7},{7,6},{8,9},{9,8},{10,11... | collective-permute-start | bytes 786440 | tf_op jit(solution)/shard_map/ppermute | solution.py:26
  4.7 6.7 %collective-permute-start.1 = (f32[256,128]{1,0:T(8,128)S(1)}, f32[256,128]{1,0:T(8,128)S(1)}, u32[]{:S(2)}, u32[]{:S(2)}) collective-permute-start(f32[256,128]{1,0:T(8,128)S(1)} %dynamic-slice_add_fusion.1), channel_id=1, source_target_pairs={{0,2},{1,3},{2,0},{3,1},{4,6},{5,7},{6,4},{7,5},{8,10},{9,11},{10,... | collective-permute-start | bytes 393224 | tf_op jit(solution)/shard_map/ppermute | solution.py:26
  11.5 8.2 %collective-permute-start.2 = (f32[256,128]{1,0:T(8,128)S(1)}, f32[256,128]{1,0:T(8,128)S(1)}, u32[]{:S(2)}, u32[]{:S(2)}) collective-permute-start(f32[256,128]{1,0:T(8,128)S(1)} %get-tuple-element.38), channel_id=1, source_target_pairs={{0,4},{1,5},{2,6},{3,7},{4,0},{5,1},{6,2},{7,3},{8,12},{9,13},{10,... | collective-permute-start | bytes 393224 | tf_op jit(solution)/shard_map/ppermute | solution.py:26
  13.3 6.3 %collective-permute-start.3 = (f32[256,128]{1,0:T(8,128)S(1)}, f32[256,128]{1,0:T(8,128)S(1)}, u32[]{:S(2)}, u32[]{:S(2)}) collective-permute-start(f32[256,128]{1,0:T(8,128)S(1)} %get-tuple-element.60), channel_id=1, source_target_pairs={{0,2},{1,3},{2,0},{3,1},{4,6},{5,7},{6,4},{7,5},{8,10},{9,11},{10,... | collective-permute-start | bytes 393224 | tf_op jit(solution)/shard_map/ppermute | solution.py:26
  19.7 5.0 %collective-permute-start.4 = (f32[256,128]{1,0:T(8,128)S(1)}, f32[256,128]{1,0:T(8,128)S(1)}, u32[]{:S(2)}, u32[]{:S(2)}) collective-permute-start(f32[256,128]{1,0:T(8,128)S(1)} %add.34), channel_id=1, source_target_pairs={{0,8},{8,0},{16,24},{24,16},{1,9},{9,1},{17,25},{25,17},{2,10},{10... | collective-permute-start | bytes 393224 | tf_op jit(solution)/shard_map/ppermute | solution.py:26
  21.3 11.5 %collective-permute-start.7 = (f32[1,256,128]{2,1,0:T(8,128)S(1)}, f32[1,256,128]{2,1,0:T(8,128)S(1)}, u32[]{:S(2)}, u32[]{:S(2)}) collective-permute-start(f32[1,256,128]{2,1,0:T(8,128)S(1)} %bitcast.22), channel_id=1, source_target_pairs={{0,2},{1,3},{2,0},{3,1},{4,6},{5,7},{6,4},{7,5},{8,10},{9,11},{10,... | collective-permute-start | bytes 393224 | tf_op jit(solution)/shard_map/ppermute | solution.py:26
  24.7 8.1 %collective-permute-start.5 = (f32[256,128]{1,0:T(8,128)S(1)}, f32[256,128]{1,0:T(8,128)S(1)}, u32[]{:S(2)}, u32[]{:S(2)}) collective-permute-start(f32[256,128]{1,0:T(8,128)S(1)} %add.35), channel_id=1, source_target_pairs={{0,16},{8,24},{16,0},{24,8},{1,17},{9,25},{17,1},{25,9},{2,18},{10... | collective-permute-start | bytes 393224 | tf_op jit(solution)/shard_map/ppermute | solution.py:26
  27.4 5.4 %collective-permute-start.6 = (f32[256,128]{1,0:T(8,128)S(1)}, f32[256,128]{1,0:T(8,128)S(1)}, u32[]{:S(2)}, u32[]{:S(2)}) collective-permute-start(f32[256,128]{1,0:T(8,128)S(1)} %collective-permute-done.4), channel_id=1, source_target_pairs={{0,2},{1,3},{2,0},{3,1},{4,6},{5,7},{6,4},{7,5},{8,10},{9,11},{10,... | collective-permute-start | bytes 393224 | tf_op jit(solution)/shard_map/ppermute | solution.py:26
  32.9 5.1 %collective-permute-start.9 = (f32[9,256,128]{2,1,0:T(8,128)S(1)}, f32[9,256,128]{2,1,0:T(8,128)S(1)}, u32[]{:S(2)}, u32[]{:S(2)}) collective-permute-start(f32[9,256,128]{2,1,0:T(8,128)S(1)} %bitcast_dynamic-update-slice_fusion.held.early), channel_id=1, source_target_pairs={{0,1},{1,0},{2,3},{3,2},{4,5},{5,4},{6,7},{7,6},{8,9},{9,8},{10,11... | collective-permute-start | bytes 3538952 | tf_op jit(solution)/shard_map/ppermute | solution.py:26
  33.0 8.7 %collective-permute-start.8 = (f32[256,128]{1,0:T(8,128)S(1)}, f32[256,128]{1,0:T(8,128)S(1)}, u32[]{:S(2)}, u32[]{:S(2)}) collective-permute-start(f32[256,128]{1,0:T(8,128)S(1)} %collective-permute-done.5), channel_id=1, source_target_pairs={{0,2},{1,3},{2,0},{3,1},{4,6},{5,7},{6,4},{7,5},{8,10},{9,11},{10,... | collective-permute-start | bytes 393224 | tf_op jit(solution)/shard_map/ppermute | solution.py:26
  38.0 5.2 %copy-start.1 = (f32[16,8,1024]{2,1,0:T(8,128)S(1)}, f32[16,8,1024]{2,1,0:T(8,128)}, u32[]{:S(2)}) copy-start(f32[16,8,1024]{2,1,0:T(8,128)} %weights.7) | copy-start | bytes 1572868
  38.0 5.2 %copy-start = (bf16[1024,1024]{1,0:T(8,128)(2,1)S(1)}, bf16[1024,1024]{1,0:T(8,128)(2,1)}, u32[]{:S(2)}) copy-start(bf16[1024,1024]{1,0:T(8,128)(2,1)} %queries.7) | copy-start | bytes 6291460
  38.0 5.2 %copy-start.2 = (bf16[1024,1024]{1,0:T(8,128)(2,1)S(1)}, bf16[1024,1024]{1,0:T(8,128)(2,1)}, u32[]{:S(2)}) copy-start(bf16[1024,1024]{1,0:T(8,128)(2,1)} %out_weight.1) | copy-start | bytes 6291460
  41.8 1.4 %collective-permute-start.10 = (f32[256,128]{1,0:T(8,128)S(1)}, f32[256,128]{1,0:T(8,128)S(1)}, u32[]{:S(2)}, u32[]{:S(2)}) collective-permute-start(f32[256,128]{1,0:T(8,128)S(1)} %collective-permute-done.8.late), channel_id=1, source_target_pairs={{0,1},{1,0},{2,3},{3,2},{4,5},{5,4},{6,7},{7,6},{8,9},{9,8},{10,11... | collective-permute-start | bytes 393224 | tf_op jit(solution)/shard_map/ppermute | solution.py:26

commit v4 on v3

--- a/solution.py
+++ b/solution.py
@@ -42,6 +42,10 @@
 
 def outside(*parts):
     return tuple(pltpu.with_memory_space_constraint(part, pltpu.HBM) for part in parts)
+
+
+def inside(*parts):
+    return tuple(pltpu.with_memory_space_constraint(part, pltpu.VMEM) for part in parts)
 
 
 def product(left, right):
@@ -174,7 +178,7 @@
             out_specs=pl.BlockSpec((step, tokens), lambda pair, half: (pair, 0)),
             scratch_shapes=[pltpu.VMEM((2, level_weights.shape[0], tokens), F32)],
         ),
-        out_shape=pltpu.HBM((width // 2, tokens), F32),
+        out_shape=pltpu.VMEM((width // 2, tokens), F32),
         cost_estimate=cost(tokens * width, MIB // 4),
         compiler_params=params(16),
     )(half.reshape(1), queries, keys, values, level_weights)
@@ -184,11 +188,18 @@
     return jnp.bitwise_and(jnp.right_shift(place, bit), 1) == 1
 
 
-def near_kernel(half, place, queries, weights, local, held, *rest):
-    *first, near, states, rows = rest
+def near_kernel(half, place, queries, weights, local, *rest):
+    *held, near, states, rows = rest
     step = pl.program_id(0)
     bits = states.shape[1] // HEAD
-    size = held.shape[1]
+    size = states.shape[0] * HEAD // 2
+
+    def quarter_state(bit, quarter, slot):
+        if len(held) == 1:
+            return held[0][2 * bit + slot]
+        if bit == 0:
+            return held[0][quarter * size : (quarter + 1) * size, :]
+        return jnp.where(slot == 0, held[2 * bit - 1][...], held[2 * bit][...])
 
     @pl.when(step == 0)
     def _():
@@ -196,11 +207,7 @@
         for quarter in range(2):
             slot = jnp.bitwise_xor(side, quarter)
             for bit in range(bits):
-                if first and bit == 0:
-                    state = first[0][quarter * size : (quarter + 1) * size, :]
-                else:
-                    state = held[2 * bit + slot]
-                state = jnp.where(has_bit(place[0], bit), state, 0.0).astype(BF16)
+                state = jnp.where(has_bit(place[0], bit), quarter_state(bit, quarter, slot), 0.0).astype(BF16)
                 for at in range(0, size, HEAD):
                     states[(quarter * size + at) // HEAD, bit * HEAD : (bit + 1) * HEAD, :] = state[at : at + HEAD]
 
@@ -216,7 +223,7 @@
         near[part, :] = total
 
 
-def near_part(half, place, bits, queries, level_weights, local, held, *first):
+def near_part(half, place, bits, queries, level_weights, local, *held):
     tokens, width = queries.shape
     heads = width // HEAD // 2
     step = 2 * HEAD
@@ -230,8 +237,13 @@
                 pl.BlockSpec((tokens, step), lambda pair, half, place: (0, half[0] * steps + pair)),
                 pl.BlockSpec(level_weights.shape, lambda pair, half, place: (0, 0, 0)),
                 pl.BlockSpec((step, tokens), lambda pair, half, place: (pair, 0)),
-                pl.BlockSpec((2 * bits,) + held.shape[1:], lambda pair, half, place: (0, 0, 0)),
-                *[pl.BlockSpec(part.shape, lambda pair, half, place: (0, 0)) for part in first],
+                *[
+                    pl.BlockSpec(
+                        (2 * bits,) + part.shape[1:] if part.ndim == 3 else part.shape,
+                        lambda pair, half, place, rank=part.ndim: (0,) * rank,
+                    )
+                    for part in held
+                ],
             ],
             out_specs=pl.BlockSpec((step, tokens), lambda pair, half, place: (pair, 0)),
             scratch_shapes=[
@@ -242,7 +254,7 @@
         out_shape=pltpu.VMEM((width // 2, tokens), F32),
         cost_estimate=cost(tokens * width, MIB // 4),
         compiler_params=params(16),
-    )(half.reshape(1), place, *outside(queries, level_weights, local), held, *first)
+    )(half.reshape(1), place, queries, level_weights, local, *held)
 
 
 def far_kernel(first_level, place, queries, weights, near_mine, near_other, early, early_other, late, late_other,
@@ -267,17 +279,15 @@
                     head = (quarter * size + at) // HEAD
                     states[head, bit * HEAD : (bit + 1) * HEAD, :] = state[at : at + HEAD]
 
-    start = pl.multiple_of(pl.program_id(0) * rows, rows)
-    band = pl.ds(start, rows)
     for half in range(2):
         for low in range(0, width // 2, HEAD):
             part = slice(half * (width // 2) + low, half * (width // 2) + low + HEAD)
             head = part.start // HEAD
-            products = product_nt(states[head], queries[band, part])
+            products = product_nt(states[head], queries[:, part])
             span = slice(low, low + HEAD)
-            total = jnp.where(core == half, near_mine[span, band], near_other[span, band])
+            total = jnp.where(core == half, near_mine[span, :], near_other[span, :])
             for bit in range(bits):
-                row = weights[first_level + bit, head : head + 1, band]
+                row = weights[first_level + bit, head : head + 1, :]
                 total = total + row * products[bit * HEAD : (bit + 1) * HEAD]
             flipped[part, :] = total.astype(BF16)
     unit = identity(CHUNK)
@@ -288,16 +298,23 @@
     mixed[...] = product(attended[...], out_weight[...]).astype(BF16)
 
 
-def far_part(first_level, bits, place, *operands):
-    queries = operands[0]
+def far_part(first_level, bits, place, queries, level_weights, near_mine, near_other, *fixed):
     tokens, width = queries.shape
     rows = min(2 * CHUNK, tokens)
+    band = pl.BlockSpec((rows, width), lambda step: (step, 0))
+    near = pl.BlockSpec((width // 2, rows), lambda step: (0, step))
     return pl.pallas_call(
         functools.partial(far_kernel, first_level),
         grid=(tokens // rows,),
-        in_specs=[pl.BlockSpec(memory_space=pltpu.SMEM)]
-        + [pl.BlockSpec(memory_space=pltpu.VMEM)] * len(operands),
-        out_specs=pl.BlockSpec((rows, width), lambda step: (step, 0)),
+        in_specs=[
+            pl.BlockSpec(memory_space=pltpu.SMEM),
+            band,
+            pl.BlockSpec(level_weights.shape[:2] + (rows,), lambda step: (0, 0, step)),
+            near,
+            near,
+            *[pl.BlockSpec(part.shape, lambda step, rank=part.ndim: (0,) * rank) for part in fixed],
+        ],
+        out_specs=band,
         out_shape=jax.ShapeDtypeStruct((tokens, width), BF16),
         scratch_shapes=[
             pltpu.VMEM((width // HEAD, bits * HEAD, HEAD), BF16),
@@ -306,7 +323,7 @@
         ],
         cost_estimate=cost(2 * tokens * width * (width + bits * HEAD), 12 * MIB),
         compiler_params=params(28),
-    )(place, *(pltpu.with_memory_space_constraint(part, pltpu.VMEM) for part in operands))
+    )(place, queries, level_weights, near_mine, near_other, *fixed)
 
 
 def body(queries, keys, values, level_weights, out_weight):
@@ -333,7 +350,7 @@
     passed, inputs = tie((passed, inputs))
     buckets = [swap(passed, "inner", 2)]
     keep_ours = block_state(2 * core + side, 4, *inputs)
-    inputs = outside(queries, keys, values, level_weights)
+    inputs = inside(queries, keys, values, level_weights)
     own = quarter_of(side, keep_ours)
     others = [swap(own, "inner", 2)]
     running = own + buckets[0]
@@ -347,6 +364,15 @@
         running = running + arrived
     sent = swap(jnp.stack(buckets[1:]), "inner", 2)
 
+    pairs = [(keep_ours, keep_theirs)]
+
+    def own_near(local):
+        nonlocal sent, others
+        sent, others, local[:] = tie((sent, others, local))
+        pairs.extend(zip(buckets, others + [sent[at] for at in range(inner_bits - 2)]))
+        held = [part for pair in pairs[1:] for part in pair]
+        return near_part(core, place, inner_bits, inputs[0], inputs[3], local[0], first, *held)
+
     far = [swap(running, "outer", 1)]
     beside = []
     for bit in range(1, outer_bits):
@@ -356,19 +382,17 @@
         beside.append(swap(far[-2], "inner", 2))
         if bit == 1:
             local.append(local_part(1 - core, *inputs))
-            far[-1], beside, sent, others, local[1] = tie((far[-1], beside, sent, others, local[1]))
+            near_mine = own_near(local)
+            far[-1], beside, near_mine, local[1], pairs = tie((far[-1], beside, near_mine, local[1], pairs))
     if len(local) < 2:
         local.append(local_part(1 - core, *inputs))
-        far[-1], sent, others, local[1] = tie((far[-1], sent, others, local[1]))
+        near_mine = own_near(local)
+        far[-1], near_mine, local[1], pairs = tie((far[-1], near_mine, local[1], pairs))
     late = swap(far[-1], "inner", 2)
-    others += [sent[at] for at in range(inner_bits - 2)]
-    pairs = [(keep_ours, keep_theirs), *zip(buckets, others), *zip(far, beside)]
+    pairs += zip(far, beside)
     mine = jnp.stack([part for pair in pairs for part in pair] + far[-1:])
     other = swap(mine, "inner", 1)
-    nears = [
-        near_part(core, place, inner_bits, queries, level_weights, local[0], mine, first),
-        near_part(1 - core, place, inner_bits, queries, level_weights, local[1], other),
-    ]
+    nears = [near_mine, near_part(1 - core, place, inner_bits, inputs[0], inputs[3], local[1], other)]
     late, nears = tie((late, nears))
     late_other = swap(late, "inner", 1)
     first_level = LOCAL_BITS + 1 + inner_bits

time: 50.2 us -> 57.5 us (1.15)
  local copies, waits for them, and re-layouts: 0.12 us -> 9.82 us
  Pallas kernels: 29.5 us -> 22.9 us
  waiting for transfers between devices: 6.36 us -> 9.12 us
  other arithmetic: 0.16 us -> 1.71 us
    unnamed x14 -> x28, local copies, waits for them, and re-layouts: 0.11 us -> 8.91 us
    pallas_call x2, Pallas kernels: 9.68 us -> 5.08 us  [local_part(): pl.pallas_call(local_kernel, grid_spec=pltpu.PrefetchScalarGridSpec(num_s...]
    ppermute x11, waiting for transfers between devices: 6.36 us -> 9.12 us  [swap(): lax.ppermute(block, axis, [(place, place ^ stride) for place in range(cou...]
    pallas_call x2, Pallas kernels: 7.04 us -> 4.8 us  [near_part(): pl.pallas_call(near_kernel, grid_spec=pltpu.PrefetchScalarGridSpec(num_sc...]
    add x1, other arithmetic: 0.02 us -> 1.57 us  [body(): running = running + far[-1]]
    another operation x1, local copies, waits for them, and re-layouts: 0.01 us -> 0.92 us  [body(): mine = jnp.stack([part for pair in pairs for part in pair] + far[-1:])]
  transfers between devices with their start and end apart: 11 -> 11, of which waited for: 3 -> 5; matrix products, arithmetic and copies ran while one was open for 0% -> 3% of each run, Pallas kernels for 41% -> 24%
where the time goes in v4:
time: 57.5 us; the launch traced here: 57.1 us
  Pallas kernels  22.9 us (40%)
  starting transfers between devices  13.3 us (23%)
  local copies, waits for them, and re-layouts  9.82 us (17%)
  waiting for transfers between devices  9.12 us (16%)
  other arithmetic  1.71 us (3%)
    ppermute x11, starting transfers between devices, swap(): lax.ppermute(block, axis, [(place, place ^ stride) for place in range(cou...  13.3 us
    ppermute x11, waiting for transfers between devices, swap(): lax.ppermute(block, axis, [(place, place ^ stride) for place in range(cou...  9.12 us
    unnamed x28, local copies, waits for them, and re-layouts  8.91 us
    pallas_call x1, Pallas kernels, far_part(): pl.pallas_call(functools.partial(far_kernel, first_level), grid=(tokens /...  6.95 us
    pallas_call x3, Pallas kernels, block_state(): pl.pallas_call(state_kernel, grid_spec=pltpu.PrefetchScalarGridSpec(num_s...  6.08 us
    pallas_call x2, Pallas kernels, local_part(): pl.pallas_call(local_kernel, grid_spec=pltpu.PrefetchScalarGridSpec(num_s...  5.08 us
    pallas_call x2, Pallas kernels, near_part(): pl.pallas_call(near_kernel, grid_spec=pltpu.PrefetchScalarGridSpec(num_sc...  4.8 us
    add x1, other arithmetic, body(): running = running + far[-1]  1.57 us
  transfers between devices with their start and end apart: 11, of which 5 were waited for; matrix products, arithmetic and copies ran while one was open for 3% of the time, Pallas kernels for 24%

profile of v4, /device:TPU:0, one launch (start us, length us, event | category | flops | bytes accessed | tf_op | source)
XLA Modules:
  0.0 57.1 jit_solution(10349594106072720633)
XLA Ops:
  0.0 2.4 %shard_map.55 = f32[512,128]{1,0:T(8,128)S(1)} custom-call(s32[1]{0:T(128)} %bitcast.4.place.half, bf16[1024,1024]{1,0:T(8,128)(2,1)} %keys.5, bf16[1024,1024]{1,0:T(8,128)(2,1)} %values.5), custom_call_target="tpu_custom_call" | custom-call | flops 134217728 | bytes 2621440 | tf_op jit(solution)/shard_map/pallas_call | solution.py:81
  2.4 0.5 collective-permute-start
  2.9 1.8 %shard_map.56 = f32[256,128]{1,0:T(8,128)S(1)} custom-call(s32[1]{0:T(128)} %bitcast.3.place, bf16[1024,1024]{1,0:T(8,128)(2,1)} %keys.5, bf16[1024,1024]{1,0:T(8,128)(2,1)} %values.5), custom_call_target="tpu_custom_call" | custom-call | flops 67108864 | bytes 1310720 | tf_op jit(solution)/shard_map/pallas_call | solution.py:81
  4.7 0.0 collective-permute-done.rest_0_
  4.7 2.6 %collective-permute-start.1 = (f32[256,128]{1,0:T(8,128)S(1)}, f32[256,128]{1,0:T(8,128)S(1)}, u32[]{:S(2)}, u32[]{:S(2)}) collective-permute-start(f32[256,128]{1,0:T(8,128)S(1)} %dynamic-slice_add_fusion.1), channel_id=1, source_target_pairs={{0,2},{1,3},{2,0},{3,1},{4,6},{5,7},{6,4},{7,5},{8,10},{9,11},{10,... | collective-permute-start | bytes 393224 | tf_op jit(solution)/shard_map/ppermute | solution.py:26
  7.3 0.0 copy-start
  7.3 0.0 copy-start.1
  7.3 0.0 copy-start.6
  7.3 1.9 %shard_map.57 = f32[256,128]{1,0:T(8,128)S(1)} custom-call(s32[1]{0:T(128)} %bitcast.2.place, bf16[1024,1024]{1,0:T(8,128)(2,1)} %keys.5, bf16[1024,1024]{1,0:T(8,128)(2,1)} %values.5), custom_call_target="tpu_custom_call" | custom-call | flops 67108864 | bytes 1310720 | tf_op jit(solution)/shard_map/pallas_call | solution.py:81
  9.3 2.2 %collective-permute-done.1.rest_1_ = f32[256,128]{1,0:T(8,128)S(1)} collective-permute-done((f32[256,128]{1,0:T(8,128)S(1)}, f32[256,128]{1,0:T(8,128)S(1)}, u32[]{:S(2)}, u32[]{:S(2)}) %collective-permute-start.1) | collective-permute-done | bytes 131104 | tf_op jit(solution)/shard_map/ppermute | solution.py:26
  11.5 1.8 %collective-permute-start.2 = (f32[256,128]{1,0:T(8,128)S(1)}, f32[256,128]{1,0:T(8,128)S(1)}, u32[]{:S(2)}, u32[]{:S(2)}) collective-permute-start(f32[256,128]{1,0:T(8,128)S(1)} %get-tuple-element.47), channel_id=1, source_target_pairs={{0,4},{1,5},{2,6},{3,7},{4,0},{5,1},{6,2},{7,3},{8,12},{9,13},{10,... | collective-permute-start | bytes 393224 | tf_op jit(solution)/shard_map/ppermute | solution.py:26
  13.3 1.5 %collective-permute-start.3 = (f32[256,128]{1,0:T(8,128)S(1)}, f32[256,128]{1,0:T(8,128)S(1)}, u32[]{:S(2)}, u32[]{:S(2)}) collective-permute-start(f32[256,128]{1,0:T(8,128)S(1)} %get-tuple-element.78), channel_id=1, source_target_pairs={{0,2},{1,3},{2,0},{3,1},{4,6},{5,7},{6,4},{7,5},{8,10},{9,11},{10,... | collective-permute-start | bytes 393224 | tf_op jit(solution)/shard_map/ppermute | solution.py:26
  14.8 0.0 copy-done
  14.8 0.0 copy-done.1
  14.8 0.0 copy-done.6
  14.8 0.0 copy-start.3
  14.8 1.6 %copy-done.3 = bf16[1024,1024]{1,0:T(8,128)(2,1)S(1)} copy-done((bf16[1024,1024]{1,0:T(8,128)(2,1)S(1)}, bf16[1024,1024]{1,0:T(8,128)(2,1)}, u32[]{:S(2)}) %copy-start.3) | copy-done | bytes 2097176
  16.4 2.5 %shard_map.58.local = f32[512,1024]{1,0:T(8,128)S(1)} custom-call(s32[1]{0:T(128)} %bitcast.5.half, bf16[1024,1024]{1,0:T(8,128)(2,1)S(1)} %copy-done.3, bf16[1024,1024]{1,0:T(8,128)(2,1)S(1)} %copy-done, bf16[1024,1024]{1,0:T(8,128)(2,1)S(1)} %copy-done.1, f32[16,8,1024]{2,1,0:T(8,128)S(1)} %copy-done.6), custom_call_target="tpu_custom_call" | custom-call | flops 1048576 | bytes 262144 | tf_op jit(solution)/shard_map/pallas_call | solution.py:172
  19.0 0.0 copy-start.7
  19.0 1.3 %copy-done.7 = f32[512,1024]{1,0:T(8,128)} copy-done((f32[512,1024]{1,0:T(8,128)}, f32[512,1024]{1,0:T(8,128)S(1)}, u32[]{:S(2)}) %copy-start.7) | copy-done | bytes 2097176
  20.3 0.0 collective-permute-done.2.rest_3_
  20.3 0.0 collective-permute-done.3.rest_2_
  20.3 1.6 %collective-permute-start.4 = (f32[256,128]{1,0:T(8,128)S(1)}, f32[256,128]{1,0:T(8,128)}, u32[]{:S(2)}, u32[]{:S(2)}) collective-permute-start(f32[256,128]{1,0:T(8,128)S(1)} %add.34), channel_id=1, source_target_pairs={{0,8},{8,0},{16,24},{24,16},{1,9},{9,1},{17,25},{25,17},{2,10},{10... | collective-permute-start | bytes 393224 | tf_op jit(solution)/shard_map/ppermute | solution.py:26
  21.9 0.5 collective-permute-start.7
  22.5 3.0 %collective-permute-done.4 = f32[256,128]{1,0:T(8,128)} collective-permute-done((f32[256,128]{1,0:T(8,128)S(1)}, f32[256,128]{1,0:T(8,128)}, u32[]{:S(2)}, u32[]{:S(2)}) %collective-permute-start.4) | collective-permute-done | bytes 131104 | tf_op jit(solution)/shard_map/ppermute | solution.py:26
  25.4 1.6 %add.35 = f32[256,128]{1,0:T(8,128)} add(f32[256,128]{1,0:T(8,128)S(1)} %add.34, f32[256,128]{1,0:T(8,128)} %collective-permute-done.4) | non-fusion elementwise | flops 32768 | bytes 393216 | tf_op jit(solution)/shard_map/add | solution.py:379
  27.0 2.6 %collective-permute-start.5 = (f32[256,128]{1,0:T(8,128)}, f32[256,128]{1,0:T(8,128)}, u32[]{:S(2)}, u32[]{:S(2)}) collective-permute-start(f32[256,128]{1,0:T(8,128)} %add.35), channel_id=1, source_target_pairs={{0,16},{8,24},{16,0},{24,8},{1,17},{9,25},{17,1},{25,9},{2,18},{10... | collective-permute-start | bytes 393224 | tf_op jit(solution)/shard_map/ppermute | solution.py:26
  29.6 0.5 collective-permute-start.6
  30.1 0.1 pad_add_fusion.place
  30.2 0.0 copy-start.2
  30.2 1.6 %copy-done.2 = bf16[1024,1024]{1,0:T(8,128)(2,1)S(1)} copy-done((bf16[1024,1024]{1,0:T(8,128)(2,1)S(1)}, bf16[1024,1024]{1,0:T(8,128)(2,1)}, u32[]{:S(2)}) %copy-start.2) | copy-done | bytes 2097176
  31.8 0.0 copy-start.4
  31.8 1.6 %copy-done.4 = bf16[1024,1024]{1,0:T(8,128)(2,1)S(1)} copy-done((bf16[1024,1024]{1,0:T(8,128)(2,1)S(1)}, bf16[1024,1024]{1,0:T(8,128)(2,1)}, u32[]{:S(2)}) %copy-start.4) | copy-done | bytes 2097176
  33.4 0.0 copy-start.5
  33.4 0.0 copy-start.8
  33.4 2.5 %shard_map.59.local = f32[512,1024]{1,0:T(8,128)S(1)} custom-call(s32[1]{0:T(128)} %bitcast.4.place.half, bf16[1024,1024]{1,0:T(8,128)(2,1)S(1)} %copy-done.4, bf16[1024,1024]{1,0:T(8,128)(2,1)S(1)} %copy-done, bf16[1024,1024]{1,0:T(8,128)(2,1)S(1)} %copy-done.2, f32[16,8,1024]{2,1,0:T(8,128)S(1)} %copy-done.6), custom_call_target="tpu_custom_call" | custom-call | flops 1048576 | bytes 262144 | tf_op jit(solution)/shard_map/pallas_call | solution.py:172
  36.0 0.0 collective-permute-done.7
  36.0 0.0 copy-done.5
  36.0 0.0 copy-done.8
  36.0 2.8 %shard_map.60.near_mine = f32[512,1024]{1,0:T(8,128)S(1)} custom-call(s32[1]{0:T(128)} %bitcast.5.half, s32[2]{0:T(128)S(1)} %pad_add_fusion.place, bf16[1024,1024]{1,0:T(8,128)(2,1)S(1)} %copy-done.5, f32[16,8,1024]{2,1,0:T(8,128)S(1)} %copy-done.6, f32[512,1024]{1,0:T(8,128)S(1)} %copy-done.8, f32[512,128]{1,0:T(8,128)S(1)} %collective-permute-done.rest_0_, ...), custom_call_target="tpu_custom_call" | custom-call | flops 1048576 | bytes 262144 | tf_op jit(solution)/shard_map/pallas_call | solution.py:231
  38.8 0.0 collective-permute-done.5
  38.8 0.0 collective-permute-done.6
  38.9 0.9 %bitcast_dynamic-update-slice_fusion.3 = f32[9,256,128]{2,1,0:T(8,128)S(1)} fusion(f32[9,256,128]{2,1,0:T(8,128)S(1)} %bitcast_dynamic-update-slice_fusion.4, f32[256,128]{1,0:T(8,128)} %bitcast.7.rest_4_), kind=kLoop, calls=%fused_computation.3 | loop fusion | bytes 262144
  39.9 0.9 %bitcast_dynamic-update-slice_fusion.2 = f32[9,256,128]{2,1,0:T(8,128)S(1)} fusion(f32[9,256,128]{2,1,0:T(8,128)S(1)} %bitcast_dynamic-update-slice_fusion.3, f32[256,128]{1,0:T(8,128)} %collective-permute-done.4), kind=kLoop, calls=%fused_computation.2 | loop fusion | bytes 262144
  40.8 0.9 %bitcast_dynamic-update-slice_fusion.1 = f32[9,256,128]{2,1,0:T(8,128)S(1)} fusion(f32[9,256,128]{2,1,0:T(8,128)S(1)} %bitcast_dynamic-update-slice_fusion.2, f32[256,128]{1,0:T(8,128)} %collective-permute-done.6), kind=kLoop, calls=%fused_computation.1 | loop fusion | bytes 262144
  41.7 0.9 %bitcast_dynamic-update-slice_fusion.early = f32[9,256,128]{2,1,0:T(8,128)S(1)} fusion(f32[9,256,128]{2,1,0:T(8,128)S(1)} %bitcast_dynamic-update-slice_fusion.1, f32[256,128]{1,0:T(8,128)} %collective-permute-done.5), kind=kLoop, calls=%fused_computation | loop fusion | bytes 262144 | tf_op jit(solution)/shard_map/stack | solution.py:393
  42.6 0.1 collective-permute-start.9
  42.7 1.6 %collective-permute-start.8 = (f32[256,128]{1,0:T(8,128)}, f32[256,128]{1,0:T(8,128)S(1)}, u32[]{:S(2)}, u32[]{:S(2)}) collective-permute-start(f32[256,128]{1,0:T(8,128)} %collective-permute-done.5), channel_id=1, source_target_pairs={{0,2},{1,3},{2,0},{3,1},{4,6},{5,7},{6,4},{7,5},{8,10},{9,11},{10,... | collective-permute-start | bytes 393224 | tf_op jit(solution)/shard_map/ppermute | solution.py:26
  44.2 1.3 %collective-permute-done.9.rest_0_.early_other = f32[9,256,128]{2,1,0:T(8,128)S(1)} collective-permute-done((f32[9,256,128]{2,1,0:T(8,128)S(1)}, f32[9,256,128]{2,1,0:T(8,128)S(1)}, u32[]{:S(2)}, u32[]{:S(2)}) %collective-permute-start.9) | collective-permute-done | bytes 1179680 | tf_op jit(solution)/shard_map/ppermute | solution.py:26
  45.5 0.0 copy-start.9
  45.5 2.0 %shard_map.61.near_other = f32[512,1024]{1,0:T(8,128)S(1)} custom-call(s32[1]{0:T(128)} %bitcast.4.place.half, s32[2]{0:T(128)S(1)} %pad_add_fusion.place, bf16[1024,1024]{1,0:T(8,128)(2,1)S(1)} %copy-done.5, f32[16,8,1024]{2,1,0:T(8,128)S(1)} %copy-done.6, f32[512,1024]{1,0:T(8,128)S(1)} %shard_map.59.local, ...), custom_call_target="tpu_custom_call" | custom-call | flops 1048576 | bytes 262144 | tf_op jit(solution)/shard_map/pallas_call | solution.py:231
  47.5 1.3 %collective-permute-done.8.late = f32[256,128]{1,0:T(8,128)S(1)} collective-permute-done((f32[256,128]{1,0:T(8,128)}, f32[256,128]{1,0:T(8,128)S(1)}, u32[]{:S(2)}, u32[]{:S(2)}) %collective-permute-start.8) | collective-permute-done | bytes 131104 | tf_op jit(solution)/shard_map/ppermute | solution.py:26
  48.8 0.0 collective-permute-start.10
  48.8 1.3 %collective-permute-done.10.late_other = f32[256,128]{1,0:T(8,128)S(1)} collective-permute-done((f32[256,128]{1,0:T(8,128)S(1)}, f32[256,128]{1,0:T(8,128)S(1)}, u32[]{:S(2)}, u32[]{:S(2)}) %collective-permute-start.10) | collective-permute-done | bytes 131104 | tf_op jit(solution)/shard_map/ppermute | solution.py:26
  50.2 0.0 copy-done.9
  50.2 7.0 %shard_map.62 = bf16[1024,1024]{1,0:T(8,128)(2,1)} custom-call(s32[2]{0:T(128)S(1)} %pad_add_fusion.place, bf16[1024,1024]{1,0:T(8,128)(2,1)S(1)} %copy-done.5, f32[16,8,1024]{2,1,0:T(8,128)S(1)} %copy-done.6, f32[512,1024]{1,0:T(8,128)S(1)} %shard_map.60.near_mine, f32[512,1024]{1,0:T(8,128)S(1)} %shard_map.61.near_other, ...), custom_call_target="tpu_custom_call" | custom-call | flops 2684354560 | bytes 12582912 | tf_op jit(solution)/shard_map/pallas_call | solution.py:306
  (8 shorter events, 0.1 us)
Async XLA Ops:
  2.4 2.3 %collective-permute-start = (f32[512,128]{1,0:T(8,128)S(1)}, f32[512,128]{1,0:T(8,128)S(1)}, u32[]{:S(2)}, u32[]{:S(2)}) collective-permute-start(f32[512,128]{1,0:T(8,128)S(1)} %shard_map.55), channel_id=1, source_target_pairs={{0,1},{1,0},{2,3},{3,2},{4,5},{5,4},{6,7},{7,6},{8,9},{9,8},{10,11... | collective-permute-start | bytes 786440 | tf_op jit(solution)/shard_map/ppermute | solution.py:26
  4.7 6.7 %collective-permute-start.1 = (f32[256,128]{1,0:T(8,128)S(1)}, f32[256,128]{1,0:T(8,128)S(1)}, u32[]{:S(2)}, u32[]{:S(2)}) collective-permute-start(f32[256,128]{1,0:T(8,128)S(1)} %dynamic-slice_add_fusion.1), channel_id=1, source_target_pairs={{0,2},{1,3},{2,0},{3,1},{4,6},{5,7},{6,4},{7,5},{8,10},{9,11},{10,... | collective-permute-start | bytes 393224 | tf_op jit(solution)/shard_map/ppermute | solution.py:26
  7.3 7.5 %copy-start = (bf16[1024,1024]{1,0:T(8,128)(2,1)S(1)}, bf16[1024,1024]{1,0:T(8,128)(2,1)}, u32[]{:S(2)}) copy-start(bf16[1024,1024]{1,0:T(8,128)(2,1)} %keys.5) | copy-start | bytes 6291460
  7.3 7.5 %copy-start.1 = (bf16[1024,1024]{1,0:T(8,128)(2,1)S(1)}, bf16[1024,1024]{1,0:T(8,128)(2,1)}, u32[]{:S(2)}) copy-start(bf16[1024,1024]{1,0:T(8,128)(2,1)} %values.5) | copy-start | bytes 6291460
  7.3 7.5 %copy-start.6 = (f32[16,8,1024]{2,1,0:T(8,128)S(1)}, f32[16,8,1024]{2,1,0:T(8,128)}, u32[]{:S(2)}) copy-start(f32[16,8,1024]{2,1,0:T(8,128)} %weights.5) | copy-start | bytes 1572868
  11.5 8.8 %collective-permute-start.2 = (f32[256,128]{1,0:T(8,128)S(1)}, f32[256,128]{1,0:T(8,128)S(1)}, u32[]{:S(2)}, u32[]{:S(2)}) collective-permute-start(f32[256,128]{1,0:T(8,128)S(1)} %get-tuple-element.47), channel_id=1, source_target_pairs={{0,4},{1,5},{2,6},{3,7},{4,0},{5,1},{6,2},{7,3},{8,12},{9,13},{10,... | collective-permute-start | bytes 393224 | tf_op jit(solution)/shard_map/ppermute | solution.py:26
  13.3 7.0 %collective-permute-start.3 = (f32[256,128]{1,0:T(8,128)S(1)}, f32[256,128]{1,0:T(8,128)S(1)}, u32[]{:S(2)}, u32[]{:S(2)}) collective-permute-start(f32[256,128]{1,0:T(8,128)S(1)} %get-tuple-element.78), channel_id=1, source_target_pairs={{0,2},{1,3},{2,0},{3,1},{4,6},{5,7},{6,4},{7,5},{8,10},{9,11},{10,... | collective-permute-start | bytes 393224 | tf_op jit(solution)/shard_map/ppermute | solution.py:26
  14.8 1.6 %copy-start.3 = (bf16[1024,1024]{1,0:T(8,128)(2,1)S(1)}, bf16[1024,1024]{1,0:T(8,128)(2,1)}, u32[]{:S(2)}) copy-start(bf16[1024,1024]{1,0:T(8,128)(2,1)} %queries.5) | copy-start | bytes 6291460
  19.0 1.3 %copy-start.7 = (f32[512,1024]{1,0:T(8,128)}, f32[512,1024]{1,0:T(8,128)S(1)}, u32[]{:S(2)}) copy-start(f32[512,1024]{1,0:T(8,128)S(1)} %shard_map.58.local) | copy-start | bytes 6291460
  20.3 5.1 %collective-permute-start.4 = (f32[256,128]{1,0:T(8,128)S(1)}, f32[256,128]{1,0:T(8,128)}, u32[]{:S(2)}, u32[]{:S(2)}) collective-permute-start(f32[256,128]{1,0:T(8,128)S(1)} %add.34), channel_id=1, source_target_pairs={{0,8},{8,0},{16,24},{24,16},{1,9},{9,1},{17,25},{25,17},{2,10},{10... | collective-permute-start | bytes 393224 | tf_op jit(solution)/shard_map/ppermute | solution.py:26
  21.9 14.0 %collective-permute-start.7 = (f32[1,256,128]{2,1,0:T(8,128)S(1)}, f32[1,256,128]{2,1,0:T(8,128)}, u32[]{:S(2)}, u32[]{:S(2)}) collective-permute-start(f32[1,256,128]{2,1,0:T(8,128)S(1)} %bitcast.26), channel_id=1, source_target_pairs={{0,2},{1,3},{2,0},{3,1},{4,6},{5,7},{6,4},{7,5},{8,10},{9,11},{10,... | collective-permute-start | bytes 393224 | tf_op jit(solution)/shard_map/ppermute | solution.py:26
  27.0 11.8 %collective-permute-start.5 = (f32[256,128]{1,0:T(8,128)}, f32[256,128]{1,0:T(8,128)}, u32[]{:S(2)}, u32[]{:S(2)}) collective-permute-start(f32[256,128]{1,0:T(8,128)} %add.35), channel_id=1, source_target_pairs={{0,16},{8,24},{16,0},{24,8},{1,17},{9,25},{17,1},{25,9},{2,18},{10... | collective-permute-start | bytes 393224 | tf_op jit(solution)/shard_map/ppermute | solution.py:26
  29.6 9.2 %collective-permute-start.6 = (f32[256,128]{1,0:T(8,128)}, f32[256,128]{1,0:T(8,128)}, u32[]{:S(2)}, u32[]{:S(2)}) collective-permute-start(f32[256,128]{1,0:T(8,128)} %collective-permute-done.4), channel_id=1, source_target_pairs={{0,2},{1,3},{2,0},{3,1},{4,6},{5,7},{6,4},{7,5},{8,10},{9,11},{10,... | collective-permute-start | bytes 393224 | tf_op jit(solution)/shard_map/ppermute | solution.py:26
  30.2 1.6 %copy-start.2 = (bf16[1024,1024]{1,0:T(8,128)(2,1)S(1)}, bf16[1024,1024]{1,0:T(8,128)(2,1)}, u32[]{:S(2)}) copy-start(bf16[1024,1024]{1,0:T(8,128)(2,1)} %values.5) | copy-start | bytes 6291460
  31.8 1.6 %copy-start.4 = (bf16[1024,1024]{1,0:T(8,128)(2,1)S(1)}, bf16[1024,1024]{1,0:T(8,128)(2,1)}, u32[]{:S(2)}) copy-start(bf16[1024,1024]{1,0:T(8,128)(2,1)} %queries.5) | copy-start | bytes 6291460
  33.4 2.6 %copy-start.5 = (bf16[1024,1024]{1,0:T(8,128)(2,1)S(1)}, bf16[1024,1024]{1,0:T(8,128)(2,1)}, u32[]{:S(2)}) copy-start(bf16[1024,1024]{1,0:T(8,128)(2,1)} %queries.5) | copy-start | bytes 6291460
  33.4 2.6 %copy-start.8 = (f32[512,1024]{1,0:T(8,128)S(1)}, f32[512,1024]{1,0:T(8,128)}, u32[]{:S(2)}) copy-start(f32[512,1024]{1,0:T(8,128)} %copy-done.7) | copy-start | bytes 6291460
  42.6 2.9 %collective-permute-start.9 = (f32[9,256,128]{2,1,0:T(8,128)S(1)}, f32[9,256,128]{2,1,0:T(8,128)S(1)}, u32[]{:S(2)}, u32[]{:S(2)}) collective-permute-start(f32[9,256,128]{2,1,0:T(8,128)S(1)} %bitcast_dynamic-update-slice_fusion.early), channel_id=1, source_target_pairs={{0,1},{1,0},{2,3},{3,2},{4,5},{5,4},{6,7},{7,6},{8,9},{9,8},{10,11... | collective-permute-start | bytes 3538952 | tf_op jit(solution)/shard_map/ppermute | solution.py:26
  42.7 6.1 %collective-permute-start.8 = (f32[256,128]{1,0:T(8,128)}, f32[256,128]{1,0:T(8,128)S(1)}, u32[]{:S(2)}, u32[]{:S(2)}) collective-permute-start(f32[256,128]{1,0:T(8,128)} %collective-permute-done.5), channel_id=1, source_target_pairs={{0,2},{1,3},{2,0},{3,1},{4,6},{5,7},{6,4},{7,5},{8,10},{9,11},{10,... | collective-permute-start | bytes 393224 | tf_op jit(solution)/shard_map/ppermute | solution.py:26
  45.5 4.6 %copy-start.9 = (bf16[1024,1024]{1,0:T(8,128)(2,1)S(1)}, bf16[1024,1024]{1,0:T(8,128)(2,1)}, u32[]{:S(2)}) copy-start(bf16[1024,1024]{1,0:T(8,128)(2,1)} %out_weight.1) | copy-start | bytes 6291460
  48.8 1.3 %collective-permute-start.10 = (f32[256,128]{1,0:T(8,128)S(1)}, f32[256,128]{1,0:T(8,128)S(1)}, u32[]{:S(2)}, u32[]{:S(2)}) collective-permute-start(f32[256,128]{1,0:T(8,128)S(1)} %collective-permute-done.8.late), channel_id=1, source_target_pairs={{0,1},{1,0},{2,3},{3,2},{4,5},{5,4},{6,7},{7,6},{8,9},{9,8},{10,11... | collective-permute-start | bytes 393224 | tf_op jit(solution)/shard_map/ppermute | solution.py:26

commit v5 on v3

--- a/solution.py
+++ b/solution.py
@@ -157,7 +157,7 @@
                 if chunk >> bit & 1:
                     total = total + row(at, top + 1 + bit, low, CHUNK) * score[below : below + HEAD, :]
                     below += HEAD
-            local[part, span] = total
+            local[part, span] = total.astype(BF16)
 
 
 def local_part(half, queries, keys, values, level_weights):
@@ -174,7 +174,7 @@
             out_specs=pl.BlockSpec((step, tokens), lambda pair, half: (pair, 0)),
             scratch_shapes=[pltpu.VMEM((2, level_weights.shape[0], tokens), F32)],
         ),
-        out_shape=pltpu.HBM((width // 2, tokens), F32),
+        out_shape=pltpu.HBM((width // 2, tokens), BF16),
         cost_estimate=cost(tokens * width, MIB // 4),
         compiler_params=params(16),
     )(half.reshape(1), queries, keys, values, level_weights)
@@ -209,11 +209,11 @@
         head = step * rows.shape[0] + at
         rows[at] = weights[:, pl.ds(half[0] * states.shape[0] + head, 1), :].reshape(rows.shape[1:])
         products = product_nt(states[head], queries[:, part])
-        total = local[part, :]
+        total = local[part, :].astype(F32)
         for bit in range(bits):
             level = LOCAL_BITS + 1 + bit
             total = total + rows[at, level : level + 1, :] * products[bit * HEAD : (bit + 1) * HEAD]
-        near[part, :] = total
+        near[part, :] = total.astype(BF16)
 
 
 def near_part(half, place, bits, queries, level_weights, local, held, *first):
@@ -239,22 +239,24 @@
                 pltpu.VMEM((2, level_weights.shape[0], tokens), F32),
             ],
         ),
-        out_shape=pltpu.VMEM((width // 2, tokens), F32),
+        out_shape=jax.ShapeDtypeStruct((width // 2, tokens), BF16),
         cost_estimate=cost(tokens * width, MIB // 4),
         compiler_params=params(16),
-    )(half.reshape(1), place, *outside(queries, level_weights, local), held, *first)
+    )(half.reshape(1), place, queries, level_weights, *outside(local), held, *first)
 
 
 def far_kernel(first_level, place, queries, weights, near_mine, near_other, early, early_other, late, late_other,
-               out_weight, mixed, states, flipped, attended):
+               out_weight, mixed, states, flipped, attended, projection, ready):
     rows, width = attended.shape
     bits = states.shape[1] // HEAD
     size = late.shape[0]
     skip = early.shape[0] + 1 - 2 * bits
     core = jnp.bitwise_and(place[0], 1)
+    fetch = pltpu.make_async_copy(out_weight, projection, ready)
 
     @pl.when(pl.program_id(0) == 0)
     def _():
+        fetch.start()
         side = jnp.bitwise_and(jnp.right_shift(place[0], 1), 1)
         for bit in range(bits):
             mine, other = ([part[skip + 2 * bit], part[skip + 2 * bit + 1] if bit + 1 < bits else final[...]]
@@ -267,17 +269,15 @@
                     head = (quarter * size + at) // HEAD
                     states[head, bit * HEAD : (bit + 1) * HEAD, :] = state[at : at + HEAD]
 
-    start = pl.multiple_of(pl.program_id(0) * rows, rows)
-    band = pl.ds(start, rows)
     for half in range(2):
         for low in range(0, width // 2, HEAD):
             part = slice(half * (width // 2) + low, half * (width // 2) + low + HEAD)
             head = part.start // HEAD
-            products = product_nt(states[head], queries[band, part])
+            products = product_nt(states[head], queries[:, part])
             span = slice(low, low + HEAD)
-            total = jnp.where(core == half, near_mine[span, band], near_other[span, band])
+            total = jnp.where(core == half, near_mine[span, :], near_other[span, :]).astype(F32)
             for bit in range(bits):
-                row = weights[first_level + bit, head : head + 1, band]
+                row = weights[first_level + bit, head : head + 1, :]
                 total = total + row * products[bit * HEAD : (bit + 1) * HEAD]
             flipped[part, :] = total.astype(BF16)
     unit = identity(CHUNK)
@@ -285,28 +285,52 @@
         for low in range(0, width, CHUNK):
             block = flipped[low : low + CHUNK, top : top + CHUNK]
             attended[top : top + CHUNK, low : low + CHUNK] = product_nt(unit, block).astype(BF16)
-    mixed[...] = product(attended[...], out_weight[...]).astype(BF16)
-
-
-def far_part(first_level, bits, place, *operands):
-    queries = operands[0]
+
+    @pl.when(pl.program_id(0) == 0)
+    def _():
+        fetch.wait()
+
+    mixed[...] = product(attended[...], projection[...]).astype(BF16)
+
+
+def far_part(first_level, bits, place, queries, level_weights, near_mine, near_other, *rest):
+    *fixed, out_weight = rest
     tokens, width = queries.shape
     rows = min(2 * CHUNK, tokens)
+    band = pl.BlockSpec((rows, width), lambda step: (step, 0))
+    near = pl.BlockSpec((width // 2, rows), lambda step: (0, step))
+
+    def tail(part):
+        count = 2 * bits - 1
+        if part.ndim == 3 and part.shape[0] % count == 0:
+            last = part.shape[0] // count - 1
+            return pl.BlockSpec((count,) + part.shape[1:], lambda step: (last, 0, 0))
+        return pl.BlockSpec(part.shape, lambda step: (0,) * part.ndim)
+
     return pl.pallas_call(
         functools.partial(far_kernel, first_level),
         grid=(tokens // rows,),
-        in_specs=[pl.BlockSpec(memory_space=pltpu.SMEM)]
-        + [pl.BlockSpec(memory_space=pltpu.VMEM)] * len(operands),
-        out_specs=pl.BlockSpec((rows, width), lambda step: (step, 0)),
+        in_specs=[
+            pl.BlockSpec(memory_space=pltpu.SMEM),
+            band,
+            pl.BlockSpec(level_weights.shape[:2] + (rows,), lambda step: (0, 0, step)),
+            near,
+            near,
+            *[tail(part) for part in fixed],
+            pl.BlockSpec(memory_space=pl.ANY),
+        ],
+        out_specs=band,
         out_shape=jax.ShapeDtypeStruct((tokens, width), BF16),
         scratch_shapes=[
             pltpu.VMEM((width // HEAD, bits * HEAD, HEAD), BF16),
             pltpu.VMEM((width, rows), BF16),
             pltpu.VMEM((rows, width), BF16),
+            pltpu.VMEM(out_weight.shape, BF16),
+            pltpu.SemaphoreType.DMA,
         ],
         cost_estimate=cost(2 * tokens * width * (width + bits * HEAD), 12 * MIB),
         compiler_params=params(28),
-    )(place, *(pltpu.with_memory_space_constraint(part, pltpu.VMEM) for part in operands))
+    )(place, queries, level_weights, near_mine, near_other, *fixed, *outside(out_weight))
 
 
 def body(queries, keys, values, level_weights, out_weight):
@@ -333,7 +357,7 @@
     passed, inputs = tie((passed, inputs))
     buckets = [swap(passed, "inner", 2)]
     keep_ours = block_state(2 * core + side, 4, *inputs)
-    inputs = outside(queries, keys, values, level_weights)
+    inputs = (queries, keys, values, level_weights)
     own = quarter_of(side, keep_ours)
     others = [swap(own, "inner", 2)]
     running = own + buckets[0]
@@ -366,8 +390,8 @@
     mine = jnp.stack([part for pair in pairs for part in pair] + far[-1:])
     other = swap(mine, "inner", 1)
     nears = [
-        near_part(core, place, inner_bits, queries, level_weights, local[0], mine, first),
-        near_part(1 - core, place, inner_bits, queries, level_weights, local[1], other),
+        near_part(core, place, inner_bits, inputs[0], inputs[3], local[0], mine, first),
+        near_part(1 - core, place, inner_bits, inputs[0], inputs[3], local[1], other),
     ]
     late, nears = tie((late, nears))
     late_other = swap(late, "inner", 1)

time: 50.2 us -> 53.8 us (1.072)
  local copies, waits for them, and re-layouts: 0.12 us -> 7.51 us
  Pallas kernels: 29.5 us -> 26.6 us
    unnamed x14 -> x16, local copies, waits for them, and re-layouts: 0.11 us -> 6.85 us
    pallas_call x2, Pallas kernels: 9.68 us -> 6.64 us  [local_part(): pl.pallas_call(local_kernel, grid_spec=pltpu.PrefetchScalarGridSpec(num_s...]
    pallas_call x1, Pallas kernels: 6.84 us -> 7.54 us  [far_part(): pl.pallas_call(functools.partial(far_kernel, first_level), grid=(tokens /...]
    pallas_call x2, Pallas kernels: 7.04 us -> 6.37 us  [near_part(): pl.pallas_call(near_kernel, grid_spec=pltpu.PrefetchScalarGridSpec(num_sc...]
    another operation x1, local copies, waits for them, and re-layouts: 0.01 us -> 0.66 us  [body(): mine = jnp.stack([part for pair in pairs for part in pair] + far[-1:])]
  transfers between devices with their start and end apart: 11 -> 11, of which waited for: 3 -> 5; matrix products, arithmetic and copies ran while one was open for 0% -> 4% of each run, Pallas kernels for 41% -> 31%
where the time goes in v5:
time: 53.8 us; the launch traced here: 53.5 us
  Pallas kernels  26.6 us (49%)
  starting transfers between devices  13.2 us (25%)
  local copies, waits for them, and re-layouts  7.51 us (14%)
  waiting for transfers between devices  5.97 us (11%)
    ppermute x11, starting transfers between devices, swap(): lax.ppermute(block, axis, [(place, place ^ stride) for place in range(cou...  13.2 us
    pallas_call x1, Pallas kernels, far_part(): pl.pallas_call(functools.partial(far_kernel, first_level), grid=(tokens /...  7.54 us
    unnamed x16, local copies, waits for them, and re-layouts  6.85 us
    pallas_call x2, Pallas kernels, local_part(): pl.pallas_call(local_kernel, grid_spec=pltpu.PrefetchScalarGridSpec(num_s...  6.64 us
    pallas_call x2, Pallas kernels, near_part(): pl.pallas_call(near_kernel, grid_spec=pltpu.PrefetchScalarGridSpec(num_sc...  6.37 us
    pallas_call x3, Pallas kernels, block_state(): pl.pallas_call(state_kernel, grid_spec=pltpu.PrefetchScalarGridSpec(num_s...  6.08 us
    ppermute x11, waiting for transfers between devices, swap(): lax.ppermute(block, axis, [(place, place ^ stride) for place in range(cou...  5.97 us
  transfers between devices with their start and end apart: 11, of which 5 were waited for; matrix products, arithmetic and copies ran while one was open for 4% of the time, Pallas kernels for 31%

profile of v5, /device:TPU:0, one launch (start us, length us, event | category | flops | bytes accessed | tf_op | source)
XLA Modules:
  0.0 53.5 jit_solution(14874199882322282899)
XLA Ops:
  0.0 2.4 %shard_map.55 = f32[512,128]{1,0:T(8,128)S(1)} custom-call(s32[1]{0:T(128)} %bitcast.4.place.half, bf16[1024,1024]{1,0:T(8,128)(2,1)} %keys.5, bf16[1024,1024]{1,0:T(8,128)(2,1)} %values.5), custom_call_target="tpu_custom_call" | custom-call | flops 134217728 | bytes 2621440 | tf_op jit(solution)/shard_map/pallas_call | solution.py:77
  2.4 0.5 collective-permute-start
  2.9 1.8 %shard_map.56 = f32[256,128]{1,0:T(8,128)S(1)} custom-call(s32[1]{0:T(128)} %bitcast.3.place, bf16[1024,1024]{1,0:T(8,128)(2,1)} %keys.5, bf16[1024,1024]{1,0:T(8,128)(2,1)} %values.5), custom_call_target="tpu_custom_call" | custom-call | flops 67108864 | bytes 1310720 | tf_op jit(solution)/shard_map/pallas_call | solution.py:77
  4.7 0.0 collective-permute-done.rest_0_
  4.7 2.6 %collective-permute-start.1 = (f32[256,128]{1,0:T(8,128)S(1)}, f32[256,128]{1,0:T(8,128)S(1)}, u32[]{:S(2)}, u32[]{:S(2)}) collective-permute-start(f32[256,128]{1,0:T(8,128)S(1)} %dynamic-slice_add_fusion.1), channel_id=1, source_target_pairs={{0,2},{1,3},{2,0},{3,1},{4,6},{5,7},{6,4},{7,5},{8,10},{9,11},{10,... | collective-permute-start | bytes 393224 | tf_op jit(solution)/shard_map/ppermute | solution.py:26
  7.3 0.0 copy-start
  7.3 0.0 copy-start.1
  7.3 1.9 %shard_map.57 = f32[256,128]{1,0:T(8,128)S(1)} custom-call(s32[1]{0:T(128)} %bitcast.2.place, bf16[1024,1024]{1,0:T(8,128)(2,1)} %keys.5, bf16[1024,1024]{1,0:T(8,128)(2,1)} %values.5), custom_call_target="tpu_custom_call" | custom-call | flops 67108864 | bytes 1310720 | tf_op jit(solution)/shard_map/pallas_call | solution.py:77
  9.3 0.0 copy-start.3
  9.3 2.2 %collective-permute-done.1 = f32[256,128]{1,0:T(8,128)S(1)} collective-permute-done((f32[256,128]{1,0:T(8,128)S(1)}, f32[256,128]{1,0:T(8,128)S(1)}, u32[]{:S(2)}, u32[]{:S(2)}) %collective-permute-start.1) | collective-permute-done | bytes 131104 | tf_op jit(solution)/shard_map/ppermute | solution.py:26
  11.5 1.8 %collective-permute-start.2 = (f32[256,128]{1,0:T(8,128)S(1)}, f32[256,128]{1,0:T(8,128)S(1)}, u32[]{:S(2)}, u32[]{:S(2)}) collective-permute-start(f32[256,128]{1,0:T(8,128)S(1)} %get-tuple-element.38), channel_id=1, source_target_pairs={{0,4},{1,5},{2,6},{3,7},{4,0},{5,1},{6,2},{7,3},{8,12},{9,13},{10,... | collective-permute-start | bytes 393224 | tf_op jit(solution)/shard_map/ppermute | solution.py:26
  13.3 1.5 %collective-permute-start.3 = (f32[256,128]{1,0:T(8,128)S(1)}, f32[256,128]{1,0:T(8,128)S(1)}, u32[]{:S(2)}, u32[]{:S(2)}) collective-permute-start(f32[256,128]{1,0:T(8,128)S(1)} %get-tuple-element.60), channel_id=1, source_target_pairs={{0,2},{1,3},{2,0},{3,1},{4,6},{5,7},{6,4},{7,5},{8,10},{9,11},{10,... | collective-permute-start | bytes 393224 | tf_op jit(solution)/shard_map/ppermute | solution.py:26
  14.8 0.7 %bitcast_dynamic-update-slice_fusion.6 = f32[9,256,128]{2,1,0:T(8,128)} fusion(f32[256,128]{1,0:T(8,128)S(1)} %shard_map.57), kind=kLoop, calls=%fused_computation.6 | loop fusion | bytes 262144
  15.5 0.0 copy-done
  15.5 0.0 copy-done.1
  15.5 0.0 copy-done.3
  15.5 0.0 copy-start.2
  15.5 1.6 %copy-done.2 = bf16[1024,1024]{1,0:T(8,128)(2,1)S(1)} copy-done((bf16[1024,1024]{1,0:T(8,128)(2,1)S(1)}, bf16[1024,1024]{1,0:T(8,128)(2,1)}, u32[]{:S(2)}) %copy-start.2) | copy-done | bytes 2097176
  17.1 3.3 %shard_map.58.local = bf16[512,1024]{1,0:T(8,128)(2,1)} custom-call(s32[1]{0:T(128)} %bitcast.5.half, bf16[1024,1024]{1,0:T(8,128)(2,1)S(1)} %copy-done, bf16[1024,1024]{1,0:T(8,128)(2,1)S(1)} %copy-done.1, bf16[1024,1024]{1,0:T(8,128)(2,1)S(1)} %copy-done.2, f32[16,8,1024]{2,1,0:T(8,128)S(1)} %copy-done.3), custom_call_target="tpu_custom_call" | custom-call | flops 1048576 | bytes 262144 | tf_op jit(solution)/shard_map/pallas_call | solution.py:168
  20.4 0.0 collective-permute-done.2
  20.4 0.0 collective-permute-done.3
  20.4 1.6 %collective-permute-start.4 = (f32[256,128]{1,0:T(8,128)S(1)}, f32[256,128]{1,0:T(8,128)S(1)}, u32[]{:S(2)}, u32[]{:S(2)}) collective-permute-start(f32[256,128]{1,0:T(8,128)S(1)} %add.34), channel_id=1, source_target_pairs={{0,8},{8,0},{16,24},{24,16},{1,9},{9,1},{17,25},{25,17},{2,10},{10... | collective-permute-start | bytes 393224 | tf_op jit(solution)/shard_map/ppermute | solution.py:26
  22.1 0.7 %bitcast_dynamic-update-slice_fusion.5 = f32[9,256,128]{2,1,0:T(8,128)} fusion(f32[9,256,128]{2,1,0:T(8,128)} %bitcast_dynamic-update-slice_fusion.6, f32[256,128]{1,0:T(8,128)S(1)} %shard_map.56), kind=kLoop, calls=%fused_computation.5 | loop fusion | bytes 262144
  22.7 0.5 %collective-permute-start.7 = (f32[1,256,128]{2,1,0:T(8,128)S(1)}, f32[1,256,128]{2,1,0:T(8,128)S(1)}, u32[]{:S(2)}, u32[]{:S(2)}) collective-permute-start(f32[1,256,128]{2,1,0:T(8,128)S(1)} %bitcast.22), channel_id=1, source_target_pairs={{0,2},{1,3},{2,0},{3,1},{4,6},{5,7},{6,4},{7,5},{8,10},{9,11},{10,... | collective-permute-start | bytes 393224 | tf_op jit(solution)/shard_map/ppermute | solution.py:26
  23.3 2.2 %collective-permute-done.4 = f32[256,128]{1,0:T(8,128)S(1)} collective-permute-done((f32[256,128]{1,0:T(8,128)S(1)}, f32[256,128]{1,0:T(8,128)S(1)}, u32[]{:S(2)}, u32[]{:S(2)}) %collective-permute-start.4) | collective-permute-done | bytes 131104 | tf_op jit(solution)/shard_map/ppermute | solution.py:26
  25.5 2.7 %collective-permute-start.5 = (f32[256,128]{1,0:T(8,128)S(1)}, f32[256,128]{1,0:T(8,128)S(1)}, u32[]{:S(2)}, u32[]{:S(2)}) collective-permute-start(f32[256,128]{1,0:T(8,128)S(1)} %add.35), channel_id=1, source_target_pairs={{0,16},{8,24},{16,0},{24,8},{1,17},{9,25},{17,1},{25,9},{2,18},{10... | collective-permute-start | bytes 393224 | tf_op jit(solution)/shard_map/ppermute | solution.py:26
  28.1 0.5 %collective-permute-start.6 = (f32[256,128]{1,0:T(8,128)S(1)}, f32[256,128]{1,0:T(8,128)S(1)}, u32[]{:S(2)}, u32[]{:S(2)}) collective-permute-start(f32[256,128]{1,0:T(8,128)S(1)} %collective-permute-done.4), channel_id=1, source_target_pairs={{0,2},{1,3},{2,0},{3,1},{4,6},{5,7},{6,4},{7,5},{8,10},{9,11},{10,... | collective-permute-start | bytes 393224 | tf_op jit(solution)/shard_map/ppermute | solution.py:26
  28.7 0.7 %bitcast_dynamic-update-slice_fusion.4 = f32[9,256,128]{2,1,0:T(8,128)} fusion(f32[9,256,128]{2,1,0:T(8,128)} %bitcast_dynamic-update-slice_fusion.5, f32[256,128]{1,0:T(8,128)S(1)} %collective-permute-done.1), kind=kLoop, calls=%fused_computation.4 | loop fusion | bytes 262144
  29.3 3.3 %shard_map.59.local = bf16[512,1024]{1,0:T(8,128)(2,1)} custom-call(s32[1]{0:T(128)} %bitcast.4.place.half, bf16[1024,1024]{1,0:T(8,128)(2,1)S(1)} %copy-done, bf16[1024,1024]{1,0:T(8,128)(2,1)S(1)} %copy-done.1, bf16[1024,1024]{1,0:T(8,128)(2,1)S(1)} %copy-done.2, f32[16,8,1024]{2,1,0:T(8,128)S(1)} %copy-done.3), custom_call_target="tpu_custom_call" | custom-call | flops 1048576 | bytes 262144 | tf_op jit(solution)/shard_map/pallas_call | solution.py:168
  32.7 0.0 collective-permute-done.7
  32.7 0.2 collective-permute-done.5
  32.8 0.3 collective-permute-done.6
  33.1 0.6 %bitcast_dynamic-update-slice_fusion.3 = f32[9,256,128]{2,1,0:T(8,128)} fusion(f32[9,256,128]{2,1,0:T(8,128)} %bitcast_dynamic-update-slice_fusion.4, f32[256,128]{1,0:T(8,128)S(1)} %collective-permute-done.3), kind=kLoop, calls=%fused_computation.3 | loop fusion | bytes 262144
  33.8 0.7 %constant_dynamic-update-slice_fusion.1 = f32[9,256,128]{2,1,0:T(8,128)} fusion(f32[9,256,128]{2,1,0:T(8,128)} %bitcast_dynamic-update-slice_fusion.3, f32[256,128]{1,0:T(8,128)S(1)} %collective-permute-done.2), kind=kLoop, calls=%fused_computation.10 | loop fusion | bytes 262144
  34.4 0.7 %constant_dynamic-update-slice_fusion = f32[9,256,128]{2,1,0:T(8,128)} fusion(f32[9,256,128]{2,1,0:T(8,128)} %constant_dynamic-update-slice_fusion.1, f32[1,256,128]{2,1,0:T(8,128)S(1)} %collective-permute-done.7), kind=kLoop, calls=%fused_computation.9 | loop fusion | bytes 262144
  35.1 0.7 %bitcast_dynamic-update-slice_fusion.2 = f32[9,256,128]{2,1,0:T(8,128)} fusion(f32[9,256,128]{2,1,0:T(8,128)} %constant_dynamic-update-slice_fusion, f32[256,128]{1,0:T(8,128)S(1)} %collective-permute-done.4), kind=kLoop, calls=%fused_computation.2 | loop fusion | bytes 262144
  35.7 0.7 %bitcast_dynamic-update-slice_fusion.1 = f32[9,256,128]{2,1,0:T(8,128)} fusion(f32[9,256,128]{2,1,0:T(8,128)} %bitcast_dynamic-update-slice_fusion.2, f32[256,128]{1,0:T(8,128)S(1)} %collective-permute-done.6), kind=kLoop, calls=%fused_computation.1 | loop fusion | bytes 262144
  36.4 0.7 %bitcast_dynamic-update-slice_fusion.held.early = f32[9,256,128]{2,1,0:T(8,128)} fusion(f32[9,256,128]{2,1,0:T(8,128)} %bitcast_dynamic-update-slice_fusion.1, f32[256,128]{1,0:T(8,128)S(1)} %collective-permute-done.5), kind=kLoop, calls=%fused_computation | loop fusion | bytes 262144 | tf_op jit(solution)/shard_map/stack | solution.py:390
  37.0 0.0 collective-permute-start.9
  37.1 1.1 %collective-permute-start.8 = (f32[256,128]{1,0:T(8,128)S(1)}, f32[256,128]{1,0:T(8,128)S(1)}, u32[]{:S(2)}, u32[]{:S(2)}) collective-permute-start(f32[256,128]{1,0:T(8,128)S(1)} %collective-permute-done.5), channel_id=1, source_target_pairs={{0,2},{1,3},{2,0},{3,1},{4,6},{5,7},{6,4},{7,5},{8,10},{9,11},{10,... | collective-permute-start | bytes 393224 | tf_op jit(solution)/shard_map/ppermute | solution.py:26
  38.1 0.1 pad_add_fusion.place
  38.2 3.2 %shard_map.60.near_mine = bf16[512,1024]{1,0:T(8,128)(2,1)S(1)} custom-call(s32[1]{0:T(128)} %bitcast.5.half, s32[2]{0:T(128)S(1)} %pad_add_fusion.place, bf16[1024,1024]{1,0:T(8,128)(2,1)S(1)} %copy-done, f32[16,8,1024]{2,1,0:T(8,128)S(1)} %copy-done.3, bf16[512,1024]{1,0:T(8,128)(2,1)} %shard_map.58.local, ...), custom_call_target="tpu_custom_call" | custom-call | flops 1048576 | bytes 262144 | tf_op jit(solution)/shard_map/pallas_call | solution.py:224
  41.4 0.0 collective-permute-done.9.held.early_other
  41.4 3.2 %shard_map.61.near_other = bf16[512,1024]{1,0:T(8,128)(2,1)S(1)} custom-call(s32[1]{0:T(128)} %bitcast.4.place.half, s32[2]{0:T(128)S(1)} %pad_add_fusion.place, bf16[1024,1024]{1,0:T(8,128)(2,1)S(1)} %copy-done, f32[16,8,1024]{2,1,0:T(8,128)S(1)} %copy-done.3, bf16[512,1024]{1,0:T(8,128)(2,1)} %shard_map.59.local, ...), custom_call_target="tpu_custom_call" | custom-call | flops 1048576 | bytes 262144 | tf_op jit(solution)/shard_map/pallas_call | solution.py:224
  44.6 0.0 collective-permute-done.8.late
  44.6 0.3 collective-permute-start.10
  44.9 1.1 %collective-permute-done.10.late_other = f32[256,128]{1,0:T(8,128)S(1)} collective-permute-done((f32[256,128]{1,0:T(8,128)S(1)}, f32[256,128]{1,0:T(8,128)S(1)}, u32[]{:S(2)}, u32[]{:S(2)}) %collective-permute-start.10) | collective-permute-done | bytes 131104 | tf_op jit(solution)/shard_map/ppermute | solution.py:26
  46.0 7.5 %shard_map.62 = bf16[1024,1024]{1,0:T(8,128)(2,1)} custom-call(s32[2]{0:T(128)S(1)} %pad_add_fusion.place, bf16[1024,1024]{1,0:T(8,128)(2,1)S(1)} %copy-done, f32[16,8,1024]{2,1,0:T(8,128)S(1)} %copy-done.3, bf16[512,1024]{1,0:T(8,128)(2,1)S(1)} %shard_map.60.near_mine, bf16[512,1024]{1,0:T(8,128)(2,1)S(1)} %shard_map.61.near_other, ...), custom_call_target="tpu_custom_call" | custom-call | flops 2684354560 | bytes 12582912 | tf_op jit(solution)/shard_map/pallas_call | solution.py:310
  (4 shorter events, 0.1 us)
Async XLA Ops:
  2.4 2.3 %collective-permute-start = (f32[512,128]{1,0:T(8,128)S(1)}, f32[512,128]{1,0:T(8,128)S(1)}, u32[]{:S(2)}, u32[]{:S(2)}) collective-permute-start(f32[512,128]{1,0:T(8,128)S(1)} %shard_map.55), channel_id=1, source_target_pairs={{0,1},{1,0},{2,3},{3,2},{4,5},{5,4},{6,7},{7,6},{8,9},{9,8},{10,11... | collective-permute-start | bytes 786440 | tf_op jit(solution)/shard_map/ppermute | solution.py:26
  4.7 6.7 %collective-permute-start.1 = (f32[256,128]{1,0:T(8,128)S(1)}, f32[256,128]{1,0:T(8,128)S(1)}, u32[]{:S(2)}, u32[]{:S(2)}) collective-permute-start(f32[256,128]{1,0:T(8,128)S(1)} %dynamic-slice_add_fusion.1), channel_id=1, source_target_pairs={{0,2},{1,3},{2,0},{3,1},{4,6},{5,7},{6,4},{7,5},{8,10},{9,11},{10,... | collective-permute-start | bytes 393224 | tf_op jit(solution)/shard_map/ppermute | solution.py:26
  7.3 8.2 %copy-start = (bf16[1024,1024]{1,0:T(8,128)(2,1)S(1)}, bf16[1024,1024]{1,0:T(8,128)(2,1)}, u32[]{:S(2)}) copy-start(bf16[1024,1024]{1,0:T(8,128)(2,1)} %queries.5) | copy-start | bytes 6291460
  7.3 8.2 %copy-start.1 = (bf16[1024,1024]{1,0:T(8,128)(2,1)S(1)}, bf16[1024,1024]{1,0:T(8,128)(2,1)}, u32[]{:S(2)}) copy-start(bf16[1024,1024]{1,0:T(8,128)(2,1)} %keys.5) | copy-start | bytes 6291460
  9.3 6.2 %copy-start.3 = (f32[16,8,1024]{2,1,0:T(8,128)S(1)}, f32[16,8,1024]{2,1,0:T(8,128)}, u32[]{:S(2)}) copy-start(f32[16,8,1024]{2,1,0:T(8,128)} %weights.5) | copy-start | bytes 1572868
  11.5 8.9 %collective-permute-start.2 = (f32[256,128]{1,0:T(8,128)S(1)}, f32[256,128]{1,0:T(8,128)S(1)}, u32[]{:S(2)}, u32[]{:S(2)}) collective-permute-start(f32[256,128]{1,0:T(8,128)S(1)} %get-tuple-element.38), channel_id=1, source_target_pairs={{0,4},{1,5},{2,6},{3,7},{4,0},{5,1},{6,2},{7,3},{8,12},{9,13},{10,... | collective-permute-start | bytes 393224 | tf_op jit(solution)/shard_map/ppermute | solution.py:26
  13.3 7.1 %collective-permute-start.3 = (f32[256,128]{1,0:T(8,128)S(1)}, f32[256,128]{1,0:T(8,128)S(1)}, u32[]{:S(2)}, u32[]{:S(2)}) collective-permute-start(f32[256,128]{1,0:T(8,128)S(1)} %get-tuple-element.60), channel_id=1, source_target_pairs={{0,2},{1,3},{2,0},{3,1},{4,6},{5,7},{6,4},{7,5},{8,10},{9,11},{10,... | collective-permute-start | bytes 393224 | tf_op jit(solution)/shard_map/ppermute | solution.py:26
  15.5 1.6 %copy-start.2 = (bf16[1024,1024]{1,0:T(8,128)(2,1)S(1)}, bf16[1024,1024]{1,0:T(8,128)(2,1)}, u32[]{:S(2)}) copy-start(bf16[1024,1024]{1,0:T(8,128)(2,1)} %values.5) | copy-start | bytes 6291460
  20.4 5.0 %collective-permute-start.4 = (f32[256,128]{1,0:T(8,128)S(1)}, f32[256,128]{1,0:T(8,128)S(1)}, u32[]{:S(2)}, u32[]{:S(2)}) collective-permute-start(f32[256,128]{1,0:T(8,128)S(1)} %add.34), channel_id=1, source_target_pairs={{0,8},{8,0},{16,24},{24,16},{1,9},{9,1},{17,25},{25,17},{2,10},{10... | collective-permute-start | bytes 393224 | tf_op jit(solution)/shard_map/ppermute | solution.py:26
  22.7 9.9 %collective-permute-start.7 = (f32[1,256,128]{2,1,0:T(8,128)S(1)}, f32[1,256,128]{2,1,0:T(8,128)S(1)}, u32[]{:S(2)}, u32[]{:S(2)}) collective-permute-start(f32[1,256,128]{2,1,0:T(8,128)S(1)} %bitcast.22), channel_id=1, source_target_pairs={{0,2},{1,3},{2,0},{3,1},{4,6},{5,7},{6,4},{7,5},{8,10},{9,11},{10,... | collective-permute-start | bytes 393224 | tf_op jit(solution)/shard_map/ppermute | solution.py:26
  25.5 7.3 %collective-permute-start.5 = (f32[256,128]{1,0:T(8,128)S(1)}, f32[256,128]{1,0:T(8,128)S(1)}, u32[]{:S(2)}, u32[]{:S(2)}) collective-permute-start(f32[256,128]{1,0:T(8,128)S(1)} %add.35), channel_id=1, source_target_pairs={{0,16},{8,24},{16,0},{24,8},{1,17},{9,25},{17,1},{25,9},{2,18},{10... | collective-permute-start | bytes 393224 | tf_op jit(solution)/shard_map/ppermute | solution.py:26
  28.1 5.0 %collective-permute-start.6 = (f32[256,128]{1,0:T(8,128)S(1)}, f32[256,128]{1,0:T(8,128)S(1)}, u32[]{:S(2)}, u32[]{:S(2)}) collective-permute-start(f32[256,128]{1,0:T(8,128)S(1)} %collective-permute-done.4), channel_id=1, source_target_pairs={{0,2},{1,3},{2,0},{3,1},{4,6},{5,7},{6,4},{7,5},{8,10},{9,11},{10,... | collective-permute-start | bytes 393224 | tf_op jit(solution)/shard_map/ppermute | solution.py:26
  37.0 4.3 %collective-permute-start.9 = (f32[9,256,128]{2,1,0:T(8,128)}, f32[9,256,128]{2,1,0:T(8,128)}, u32[]{:S(2)}, u32[]{:S(2)}) collective-permute-start(f32[9,256,128]{2,1,0:T(8,128)} %bitcast_dynamic-update-slice_fusion.held.early), channel_id=1, source_target_pairs={{0,1},{1,0},{2,3},{3,2},{4,5},{5,4},{6,7},{7,6},{8,9},{9,8},{10,11... | collective-permute-start | bytes 3538952 | tf_op jit(solution)/shard_map/ppermute | solution.py:26
  37.1 7.5 %collective-permute-start.8 = (f32[256,128]{1,0:T(8,128)S(1)}, f32[256,128]{1,0:T(8,128)S(1)}, u32[]{:S(2)}, u32[]{:S(2)}) collective-permute-start(f32[256,128]{1,0:T(8,128)S(1)} %collective-permute-done.5), channel_id=1, source_target_pairs={{0,2},{1,3},{2,0},{3,1},{4,6},{5,7},{6,4},{7,5},{8,10},{9,11},{10,... | collective-permute-start | bytes 393224 | tf_op jit(solution)/shard_map/ppermute | solution.py:26
  44.6 1.4 %collective-permute-start.10 = (f32[256,128]{1,0:T(8,128)S(1)}, f32[256,128]{1,0:T(8,128)S(1)}, u32[]{:S(2)}, u32[]{:S(2)}) collective-permute-start(f32[256,128]{1,0:T(8,128)S(1)} %collective-permute-done.8.late), channel_id=1, source_target_pairs={{0,1},{1,0},{2,3},{3,2},{4,5},{5,4},{6,7},{7,6},{8,9},{9,8},{10,11... | collective-permute-start | bytes 393224 | tf_op jit(solution)/shard_map/ppermute | solution.py:26

commit v6 on v4

--- a/solution.py
+++ b/solution.py
@@ -42,10 +42,6 @@
 
 def outside(*parts):
     return tuple(pltpu.with_memory_space_constraint(part, pltpu.HBM) for part in parts)
-
-
-def inside(*parts):
-    return tuple(pltpu.with_memory_space_constraint(part, pltpu.VMEM) for part in parts)
 
 
 def product(left, right):
@@ -110,7 +106,8 @@
     return jnp.concatenate(parts, axis=0)
 
 
-def local_kernel(half, queries, keys, values, weights, local, rows):
+def local_kernel(half, queries, keys, values, weights, local, *rest):
+    *state, rows = rest
     tokens, width = queries.shape
     chunks = tokens // CHUNK
     levels = rows.shape[1]
@@ -127,7 +124,9 @@
 
     nodes = []
     for part in parts:
-        line = [product(flipped[part, span], keys[span, part]) for span in spans[:-1]]
+        line = [product(flipped[part, span], keys[span, part]) for span in (spans if state else spans[:-1])]
+        if state:
+            state[0][part, :] = functools.reduce(jnp.add, line)
         known = [line]
         while len(known[-1]) > 1:
             below = known[-1]
@@ -161,10 +160,10 @@
                 if chunk >> bit & 1:
                     total = total + row(at, top + 1 + bit, low, CHUNK) * score[below : below + HEAD, :]
                     below += HEAD
-            local[part, span] = total
-
-
-def local_part(half, queries, keys, values, level_weights):
+            local[part, span] = total.astype(BF16)
+
+
+def local_part(half, with_state, queries, keys, values, level_weights):
     tokens, width = queries.shape
     step = 2 * HEAD
     steps = width // step // 2
@@ -175,10 +174,13 @@
             num_scalar_prefetch=1,
             grid=(steps,),
             in_specs=[column, column, column, pl.BlockSpec(level_weights.shape, lambda pair, half: (0, 0, 0))],
-            out_specs=pl.BlockSpec((step, tokens), lambda pair, half: (pair, 0)),
+            out_specs=[
+                pl.BlockSpec((step, tokens), lambda pair, half: (pair, 0)),
+                pl.BlockSpec((step, HEAD), lambda pair, half: (pair, 0)),
+            ][: 1 + with_state],
             scratch_shapes=[pltpu.VMEM((2, level_weights.shape[0], tokens), F32)],
         ),
-        out_shape=pltpu.VMEM((width // 2, tokens), F32),
+        out_shape=[pltpu.HBM((width // 2, tokens), BF16), pltpu.VMEM((width // 2, HEAD), F32)][: 1 + with_state],
         cost_estimate=cost(tokens * width, MIB // 4),
         compiler_params=params(16),
     )(half.reshape(1), queries, keys, values, level_weights)
@@ -216,7 +218,7 @@
         head = step * rows.shape[0] + at
         rows[at] = weights[:, pl.ds(half[0] * states.shape[0] + head, 1), :].reshape(rows.shape[1:])
         products = product_nt(states[head], queries[:, part])
-        total = local[part, :]
+        total = local[part, :].astype(F32)
         for bit in range(bits):
             level = LOCAL_BITS + 1 + bit
             total = total + rows[at, level : level + 1, :] * products[bit * HEAD : (bit + 1) * HEAD]
@@ -254,7 +256,7 @@
         out_shape=pltpu.VMEM((width // 2, tokens), F32),
         cost_estimate=cost(tokens * width, MIB // 4),
         compiler_params=params(16),
-    )(half.reshape(1), place, queries, level_weights, local, *held)
+    )(half.reshape(1), place, *outside(queries, level_weights, local), *held)
 
 
 def far_kernel(first_level, place, queries, weights, near_mine, near_other, early, early_other, late, late_other,
@@ -303,6 +305,14 @@
     rows = min(2 * CHUNK, tokens)
     band = pl.BlockSpec((rows, width), lambda step: (step, 0))
     near = pl.BlockSpec((width // 2, rows), lambda step: (0, step))
+
+    def tail(part):
+        count = 2 * bits - 1
+        if part.ndim == 3 and part.shape[0] % count == 0:
+            last = part.shape[0] // count - 1
+            return pl.BlockSpec((count,) + part.shape[1:], lambda step: (last, 0, 0))
+        return pl.BlockSpec(part.shape, lambda step: (0,) * part.ndim)
+
     return pl.pallas_call(
         functools.partial(far_kernel, first_level),
         grid=(tokens // rows,),
@@ -312,7 +322,7 @@
             pl.BlockSpec(level_weights.shape[:2] + (rows,), lambda step: (0, 0, step)),
             near,
             near,
-            *[pl.BlockSpec(part.shape, lambda step, rank=part.ndim: (0,) * rank) for part in fixed],
+            *[tail(part) for part in fixed],
         ],
         out_specs=band,
         out_shape=jax.ShapeDtypeStruct((tokens, width), BF16),
@@ -349,50 +359,48 @@
     passed = quarter_of(1 - side, keep_theirs)
     passed, inputs = tie((passed, inputs))
     buckets = [swap(passed, "inner", 2)]
-    keep_ours = block_state(2 * core + side, 4, *inputs)
-    inputs = inside(queries, keys, values, level_weights)
+    inputs = outside(queries, keys, values, level_weights)
+    local = [None, None]
+    local[0], keep = local_part(core, True, *inputs)
+    keep_ours = lax.dynamic_slice_in_dim(keep, side * quarter, quarter, 0)
     own = quarter_of(side, keep_ours)
-    others = [swap(own, "inner", 2)]
     running = own + buckets[0]
     running, inputs = tie((running, inputs))
-    local = [local_part(core, *inputs)]
+    (local[1],) = local_part(1 - core, False, *inputs)
     for bit in range(2, inner_bits):
         arrived = swap(running, "inner", 1 << bit)
         if bit == 2:
-            arrived, others, local[0] = tie((arrived, others, local[0]))
+            arrived, local = tie((arrived, local))
         buckets.append(arrived)
         running = running + arrived
-    sent = swap(jnp.stack(buckets[1:]), "inner", 2)
-
-    pairs = [(keep_ours, keep_theirs)]
-
-    def own_near(local):
-        nonlocal sent, others
-        sent, others, local[:] = tie((sent, others, local))
-        pairs.extend(zip(buckets, others + [sent[at] for at in range(inner_bits - 2)]))
-        held = [part for pair in pairs[1:] for part in pair]
-        return near_part(core, place, inner_bits, inputs[0], inputs[3], local[0], first, *held)
-
+
+    running, sent = tie((running, jnp.stack([own] + buckets[1:])))
     far = [swap(running, "outer", 1)]
+    others = swap(sent, "inner", 2)
     beside = []
+
+    def own_near():
+        held = [part for at, bucket in enumerate(buckets) for part in (bucket, others[at])]
+        return near_part(core, place, inner_bits, queries, level_weights, local[0], first, *held)
+
     for bit in range(1, outer_bits):
         running = running + far[-1]
-        running, inputs = tie((running, inputs))
         far.append(swap(running, "outer", 1 << bit))
         beside.append(swap(far[-2], "inner", 2))
         if bit == 1:
-            local.append(local_part(1 - core, *inputs))
-            near_mine = own_near(local)
-            far[-1], beside, near_mine, local[1], pairs = tie((far[-1], beside, near_mine, local[1], pairs))
-    if len(local) < 2:
-        local.append(local_part(1 - core, *inputs))
-        near_mine = own_near(local)
-        far[-1], near_mine, local[1], pairs = tie((far[-1], near_mine, local[1], pairs))
+            near_mine = own_near()
+            far[-1], beside, others, near_mine = tie((far[-1], beside, others, near_mine))
+    if outer_bits == 1:
+        near_mine = own_near()
+        far[-1], others, near_mine = tie((far[-1], others, near_mine))
     late = swap(far[-1], "inner", 2)
-    pairs += zip(far, beside)
+    pairs = [(keep_ours, keep_theirs), *((bucket, others[at]) for at, bucket in enumerate(buckets)), *zip(far, beside)]
     mine = jnp.stack([part for pair in pairs for part in pair] + far[-1:])
     other = swap(mine, "inner", 1)
-    nears = [near_mine, near_part(1 - core, place, inner_bits, inputs[0], inputs[3], local[1], other)]
+    nears = [
+        near_mine,
+        near_part(1 - core, place, inner_bits, queries, level_weights, local[1], other),
+    ]
     late, nears = tie((late, nears))
     late_other = swap(late, "inner", 1)
     first_level = LOCAL_BITS + 1 + inner_bits

time: 57.5 us -> 47.3 us (0.82)
  local copies, waits for them, and re-layouts: 9.82 us -> 0.13 us
  Pallas kernels: 22.9 us -> 27.1 us
  waiting for transfers between devices: 9.12 us -> 6.83 us
  other arithmetic: 1.71 us -> 0.2 us
  starting transfers between devices: 13.3 us -> 12.7 us
    unnamed x28 -> x14, local copies, waits for them, and re-layouts: 8.91 us -> 0.1 us
    pallas_call x2, Pallas kernels: 5.08 us -> 9.39 us  [local_part(): pl.pallas_call(local_kernel, grid_spec=pltpu.PrefetchScalarGridSpec(num_s...]
    ppermute x11 -> x10, waiting for transfers between devices: 9.12 us -> 6.83 us  [swap(): lax.ppermute(block, axis, [(place, place ^ stride) for place in range(cou...]
    pallas_call x3 -> x2, Pallas kernels: 6.08 us -> 4.16 us  [block_state(): pl.pallas_call(state_kernel, grid_spec=pltpu.PrefetchScalarGridSpec(num_s...]
    pallas_call x2, Pallas kernels: 4.8 us -> 6.68 us  [near_part(): pl.pallas_call(near_kernel, grid_spec=pltpu.PrefetchScalarGridSpec(num_sc...]
    add x1, other arithmetic: 1.57 us -> 0.02 us  [body(): running = running + far[-1]]
    another operation x1, local copies, waits for them, and re-layouts: 0.92 us -> 0.01 us  [body(): mine = jnp.stack([part for pair in pairs for part in pair] + far[-1:])]
    ppermute x11 -> x10, starting transfers between devices: 13.3 us -> 12.7 us  [swap(): lax.ppermute(block, axis, [(place, place ^ stride) for place in range(cou...]
  transfers between devices with their start and end apart: 11 -> 10, of which waited for: 5 -> 5; matrix products, arithmetic and copies ran while one was open for 3% -> 0% of each run, Pallas kernels for 24% -> 38%
where the time goes in v6:
time: 47.3 us; the launch traced here: 47.1 us
  Pallas kernels  27.1 us (57%)
  starting transfers between devices  12.7 us (27%)
  waiting for transfers between devices  6.83 us (14%)
    ppermute x10, starting transfers between devices, swap(): lax.ppermute(block, axis, [(place, place ^ stride) for place in range(cou...  12.7 us
    pallas_call x2, Pallas kernels, local_part(): pl.pallas_call(local_kernel, grid_spec=pltpu.PrefetchScalarGridSpec(num_s...  9.39 us
    pallas_call x1, Pallas kernels, far_part(): pl.pallas_call(functools.partial(far_kernel, first_level), grid=(tokens /...  6.86 us
    ppermute x10, waiting for transfers between devices, swap(): lax.ppermute(block, axis, [(place, place ^ stride) for place in range(cou...  6.83 us
    pallas_call x2, Pallas kernels, near_part(): pl.pallas_call(near_kernel, grid_spec=pltpu.PrefetchScalarGridSpec(num_sc...  6.68 us
    pallas_call x2, Pallas kernels, block_state(): pl.pallas_call(state_kernel, grid_spec=pltpu.PrefetchScalarGridSpec(num_s...  4.16 us
  transfers between devices with their start and end apart: 10, of which 5 were waited for; matrix products, arithmetic and copies ran while one was open for 0% of the time, Pallas kernels for 38%

profile of v6, /device:TPU:0, one launch (start us, length us, event | category | flops | bytes accessed | tf_op | source)
XLA Modules:
  0.0 47.1 jit_solution(15899637576911027312)
XLA Ops:
  0.0 2.4 %shard_map.56 = f32[512,128]{1,0:T(8,128)S(1)} custom-call(s32[1]{0:T(128)} %bitcast.3.place.half, bf16[1024,1024]{1,0:T(8,128)(2,1)} %keys.5, bf16[1024,1024]{1,0:T(8,128)(2,1)} %values.5), custom_call_target="tpu_custom_call" | custom-call | flops 134217728 | bytes 2621440 | tf_op jit(solution)/shard_map/pallas_call | solution.py:77
  2.4 0.5 %collective-permute-start = (f32[512,128]{1,0:T(8,128)S(1)}, f32[512,128]{1,0:T(8,128)S(1)}, u32[]{:S(2)}, u32[]{:S(2)}) collective-permute-start(f32[512,128]{1,0:T(8,128)S(1)} %shard_map.56), channel_id=1, source_target_pairs={{0,1},{1,0},{2,3},{3,2},{4,5},{5,4},{6,7},{7,6},{8,9},{9,8},{10,11... | collective-permute-start | bytes 786440 | tf_op jit(solution)/shard_map/ppermute | solution.py:26
  2.9 1.8 %shard_map.57 = f32[256,128]{1,0:T(8,128)S(1)} custom-call(s32[1]{0:T(128)} %bitcast.4.place, bf16[1024,1024]{1,0:T(8,128)(2,1)} %keys.5, bf16[1024,1024]{1,0:T(8,128)(2,1)} %values.5), custom_call_target="tpu_custom_call" | custom-call | flops 67108864 | bytes 1310720 | tf_op jit(solution)/shard_map/pallas_call | solution.py:77
  4.7 0.0 collective-permute-done.rest_0_
  4.7 2.6 %collective-permute-start.1 = (f32[256,128]{1,0:T(8,128)S(1)}, f32[256,128]{1,0:T(8,128)S(1)}, u32[]{:S(2)}, u32[]{:S(2)}) collective-permute-start(f32[256,128]{1,0:T(8,128)S(1)} %dynamic-slice_add_fusion), channel_id=1, source_target_pairs={{0,2},{1,3},{2,0},{3,1},{4,6},{5,7},{6,4},{7,5},{8,10},{9,11},{10,... | collective-permute-start | bytes 393224 | tf_op jit(solution)/shard_map/ppermute | solution.py:26
  7.3 4.7 %shard_map.55 = (bf16[512,1024]{1,0:T(8,128)(2,1)}, f32[512,128]{1,0:T(8,128)S(1)}) custom-call(s32[1]{0:T(128)} %bitcast.2.half, bf16[1024,1024]{1,0:T(8,128)(2,1)} %queries.8, bf16[1024,1024]{1,0:T(8,128)(2,1)} %keys.5, bf16[1024,1024]{1,0:T(8,128)(2,1)} %values.5, f32[16,8,1024]{2,1,0:T(8,128)} %weights.8), custom_call_target="tpu_custom_call" | custom-call | flops 1048576 | bytes 262144 | tf_op jit(solution)/shard_map/pallas_call | solution.py:171
  12.1 0.0 collective-permute-done.1.rest_1_
  12.1 1.6 %collective-permute-start.2 = (f32[256,128]{1,0:T(8,128)S(1)}, f32[256,128]{1,0:T(8,128)S(1)}, u32[]{:S(2)}, u32[]{:S(2)}) collective-permute-start(f32[256,128]{1,0:T(8,128)S(1)} %get-tuple-element.33), channel_id=1, source_target_pairs={{0,4},{1,5},{2,6},{3,7},{4,0},{5,1},{6,2},{7,3},{8,12},{9,13},{10,... | collective-permute-start | bytes 393224 | tf_op jit(solution)/shard_map/ppermute | solution.py:26
  13.7 4.7 %shard_map.58.local = bf16[512,1024]{1,0:T(8,128)(2,1)} custom-call(s32[1]{0:T(128)} %bitcast.3.place.half, bf16[1024,1024]{1,0:T(8,128)(2,1)} %queries.8, bf16[1024,1024]{1,0:T(8,128)(2,1)} %keys.5, bf16[1024,1024]{1,0:T(8,128)(2,1)} %values.5, f32[16,8,1024]{2,1,0:T(8,128)} %weights.8), custom_call_target="tpu_custom_call" | custom-call | flops 1048576 | bytes 262144 | tf_op jit(solution)/shard_map/pallas_call | solution.py:171
  18.4 0.0 collective-permute-done.2.rest_3_
  18.4 1.2 %collective-permute-start.6 = (f32[2,256,128]{2,1,0:T(8,128)S(1)}, f32[2,256,128]{2,1,0:T(8,128)S(1)}, u32[]{:S(2)}, u32[]{:S(2)}) collective-permute-start(f32[2,256,128]{2,1,0:T(8,128)S(1)} %pad_maximum_fusion), channel_id=1, source_target_pairs={{0,2},{1,3},{2,0},{3,1},{4,6},{5,7},{6,4},{7,5},{8,10},{9,11},{10,... | collective-permute-start | bytes 786440 | tf_op jit(solution)/shard_map/ppermute | solution.py:26
  19.6 0.1 pad_add_fusion.place
  19.7 1.6 %collective-permute-start.3 = (f32[256,128]{1,0:T(8,128)S(1)}, f32[256,128]{1,0:T(8,128)S(1)}, u32[]{:S(2)}, u32[]{:S(2)}) collective-permute-start(f32[256,128]{1,0:T(8,128)S(1)} %add.31), channel_id=1, source_target_pairs={{0,8},{8,0},{16,24},{24,16},{1,9},{9,1},{17,25},{25,17},{2,10},{10... | collective-permute-start | bytes 393224 | tf_op jit(solution)/shard_map/ppermute | solution.py:26
  21.3 3.4 %collective-permute-done.3 = f32[256,128]{1,0:T(8,128)S(1)} collective-permute-done((f32[256,128]{1,0:T(8,128)S(1)}, f32[256,128]{1,0:T(8,128)S(1)}, u32[]{:S(2)}, u32[]{:S(2)}) %collective-permute-start.3) | collective-permute-done | bytes 131104 | tf_op jit(solution)/shard_map/ppermute | solution.py:26
  24.7 2.7 %collective-permute-start.4 = (f32[256,128]{1,0:T(8,128)S(1)}, f32[256,128]{1,0:T(8,128)S(1)}, u32[]{:S(2)}, u32[]{:S(2)}) collective-permute-start(f32[256,128]{1,0:T(8,128)S(1)} %add.32), channel_id=1, source_target_pairs={{0,16},{8,24},{16,0},{24,8},{1,17},{9,25},{17,1},{25,9},{2,18},{10... | collective-permute-start | bytes 393224 | tf_op jit(solution)/shard_map/ppermute | solution.py:26
  27.3 1.0 %collective-permute-start.5 = (f32[256,128]{1,0:T(8,128)S(1)}, f32[256,128]{1,0:T(8,128)S(1)}, u32[]{:S(2)}, u32[]{:S(2)}) collective-permute-start(f32[256,128]{1,0:T(8,128)S(1)} %collective-permute-done.3), channel_id=1, source_target_pairs={{0,2},{1,3},{2,0},{3,1},{4,6},{5,7},{6,4},{7,5},{8,10},{9,11},{10,... | collective-permute-start | bytes 393224 | tf_op jit(solution)/shard_map/ppermute | solution.py:26
  28.3 0.0 collective-permute-done.6
  28.3 3.2 %shard_map.59.near_mine = f32[512,1024]{1,0:T(8,128)S(1)} custom-call(s32[1]{0:T(128)} %bitcast.2.half, s32[2]{0:T(128)S(1)} %pad_add_fusion.place, bf16[1024,1024]{1,0:T(8,128)(2,1)} %queries.8, f32[16,8,1024]{2,1,0:T(8,128)} %weights.8, bf16[512,1024]{1,0:T(8,128)(2,1)} %get-tuple-element.42.local, f32[512,128]{1,0:T(8,128)S(1)} %collective-permute-done.rest_0_, ...), custom_call_target="tpu_custom_call" | custom-call | flops 1048576 | bytes 262144 | tf_op jit(solution)/shard_map/pallas_call | solution.py:233
  31.6 0.5 %collective-permute-done.4 = f32[256,128]{1,0:T(8,128)S(1)} collective-permute-done((f32[256,128]{1,0:T(8,128)S(1)}, f32[256,128]{1,0:T(8,128)S(1)}, u32[]{:S(2)}, u32[]{:S(2)}) %collective-permute-start.4) | collective-permute-done | bytes 131104 | tf_op jit(solution)/shard_map/ppermute | solution.py:26
  32.1 0.2 collective-permute-done.5
  32.4 0.0 copy-start.1
  32.4 0.1 collective-permute-start.8
  32.5 1.3 %collective-permute-start.7 = (f32[256,128]{1,0:T(8,128)S(1)}, f32[256,128]{1,0:T(8,128)S(1)}, u32[]{:S(2)}, u32[]{:S(2)}) collective-permute-start(f32[256,128]{1,0:T(8,128)S(1)} %collective-permute-done.4), channel_id=1, source_target_pairs={{0,2},{1,3},{2,0},{3,1},{4,6},{5,7},{6,4},{7,5},{8,10},{9,11},{10,... | collective-permute-start | bytes 393224 | tf_op jit(solution)/shard_map/ppermute | solution.py:26
  33.8 1.5 %collective-permute-done.8.rest_0_.early_other = f32[9,256,128]{2,1,0:T(8,128)S(1)} collective-permute-done((f32[9,256,128]{2,1,0:T(8,128)S(1)}, f32[9,256,128]{2,1,0:T(8,128)S(1)}, u32[]{:S(2)}, u32[]{:S(2)}) %collective-permute-start.8) | collective-permute-done | bytes 1179680 | tf_op jit(solution)/shard_map/ppermute | solution.py:26
  35.3 0.0 copy-start
  35.3 0.0 copy-start.2
  35.3 3.5 %shard_map.60.near_other = f32[512,1024]{1,0:T(8,128)S(1)} custom-call(s32[1]{0:T(128)} %bitcast.3.place.half, s32[2]{0:T(128)S(1)} %pad_add_fusion.place, bf16[1024,1024]{1,0:T(8,128)(2,1)} %queries.8, f32[16,8,1024]{2,1,0:T(8,128)} %weights.8, bf16[512,1024]{1,0:T(8,128)(2,1)} %shard_map.58.local, f32[9,256,128]{2,1,0:T(8,128)S(1)} %collective-permute-done.8.rest_0_.early_other), custom_call_target="tpu_custom_call" | custom-call | flops 1048576 | bytes 262144 | tf_op jit(solution)/shard_map/pallas_call | solution.py:233
  38.8 0.0 collective-permute-done.7.late
  38.8 0.2 collective-permute-start.9
  39.0 1.2 %collective-permute-done.9.late_other = f32[256,128]{1,0:T(8,128)S(1)} collective-permute-done((f32[256,128]{1,0:T(8,128)S(1)}, f32[256,128]{1,0:T(8,128)S(1)}, u32[]{:S(2)}, u32[]{:S(2)}) %collective-permute-start.9) | collective-permute-done | bytes 131104 | tf_op jit(solution)/shard_map/ppermute | solution.py:26
  40.2 0.0 copy-done.1
  40.2 0.0 copy-done
  40.2 0.0 copy-done.2
  40.2 6.9 %shard_map.61 = bf16[1024,1024]{1,0:T(8,128)(2,1)} custom-call(s32[2]{0:T(128)S(1)} %pad_add_fusion.place, bf16[1024,1024]{1,0:T(8,128)(2,1)S(1)} %copy-done, f32[16,8,1024]{2,1,0:T(8,128)S(1)} %copy-done.1, f32[512,1024]{1,0:T(8,128)S(1)} %shard_map.59.near_mine, f32[512,1024]{1,0:T(8,128)S(1)} %shard_map.60.near_other, ...), custom_call_target="tpu_custom_call" | custom-call | flops 2684354560 | bytes 12582912 | tf_op jit(solution)/shard_map/pallas_call | solution.py:316
  (15 shorter events, 0.2 us)
Async XLA Ops:
  2.4 2.3 %collective-permute-start = (f32[512,128]{1,0:T(8,128)S(1)}, f32[512,128]{1,0:T(8,128)S(1)}, u32[]{:S(2)}, u32[]{:S(2)}) collective-permute-start(f32[512,128]{1,0:T(8,128)S(1)} %shard_map.56), channel_id=1, source_target_pairs={{0,1},{1,0},{2,3},{3,2},{4,5},{5,4},{6,7},{7,6},{8,9},{9,8},{10,11... | collective-permute-start | bytes 786440 | tf_op jit(solution)/shard_map/ppermute | solution.py:26
  4.7 7.3 %collective-permute-start.1 = (f32[256,128]{1,0:T(8,128)S(1)}, f32[256,128]{1,0:T(8,128)S(1)}, u32[]{:S(2)}, u32[]{:S(2)}) collective-permute-start(f32[256,128]{1,0:T(8,128)S(1)} %dynamic-slice_add_fusion), channel_id=1, source_target_pairs={{0,2},{1,3},{2,0},{3,1},{4,6},{5,7},{6,4},{7,5},{8,10},{9,11},{10,... | collective-permute-start | bytes 393224 | tf_op jit(solution)/shard_map/ppermute | solution.py:26
  12.1 6.3 %collective-permute-start.2 = (f32[256,128]{1,0:T(8,128)S(1)}, f32[256,128]{1,0:T(8,128)S(1)}, u32[]{:S(2)}, u32[]{:S(2)}) collective-permute-start(f32[256,128]{1,0:T(8,128)S(1)} %get-tuple-element.33), channel_id=1, source_target_pairs={{0,4},{1,5},{2,6},{3,7},{4,0},{5,1},{6,2},{7,3},{8,12},{9,13},{10,... | collective-permute-start | bytes 393224 | tf_op jit(solution)/shard_map/ppermute | solution.py:26
  18.4 9.9 %collective-permute-start.6 = (f32[2,256,128]{2,1,0:T(8,128)S(1)}, f32[2,256,128]{2,1,0:T(8,128)S(1)}, u32[]{:S(2)}, u32[]{:S(2)}) collective-permute-start(f32[2,256,128]{2,1,0:T(8,128)S(1)} %pad_maximum_fusion), channel_id=1, source_target_pairs={{0,2},{1,3},{2,0},{3,1},{4,6},{5,7},{6,4},{7,5},{8,10},{9,11},{10,... | collective-permute-start | bytes 786440 | tf_op jit(solution)/shard_map/ppermute | solution.py:26
  19.7 5.0 %collective-permute-start.3 = (f32[256,128]{1,0:T(8,128)S(1)}, f32[256,128]{1,0:T(8,128)S(1)}, u32[]{:S(2)}, u32[]{:S(2)}) collective-permute-start(f32[256,128]{1,0:T(8,128)S(1)} %add.31), channel_id=1, source_target_pairs={{0,8},{8,0},{16,24},{24,16},{1,9},{9,1},{17,25},{25,17},{2,10},{10... | collective-permute-start | bytes 393224 | tf_op jit(solution)/shard_map/ppermute | solution.py:26
  24.7 7.4 %collective-permute-start.4 = (f32[256,128]{1,0:T(8,128)S(1)}, f32[256,128]{1,0:T(8,128)S(1)}, u32[]{:S(2)}, u32[]{:S(2)}) collective-permute-start(f32[256,128]{1,0:T(8,128)S(1)} %add.32), channel_id=1, source_target_pairs={{0,16},{8,24},{16,0},{24,8},{1,17},{9,25},{17,1},{25,9},{2,18},{10... | collective-permute-start | bytes 393224 | tf_op jit(solution)/shard_map/ppermute | solution.py:26
  27.3 5.0 %collective-permute-start.5 = (f32[256,128]{1,0:T(8,128)S(1)}, f32[256,128]{1,0:T(8,128)S(1)}, u32[]{:S(2)}, u32[]{:S(2)}) collective-permute-start(f32[256,128]{1,0:T(8,128)S(1)} %collective-permute-done.3), channel_id=1, source_target_pairs={{0,2},{1,3},{2,0},{3,1},{4,6},{5,7},{6,4},{7,5},{8,10},{9,11},{10,... | collective-permute-start | bytes 393224 | tf_op jit(solution)/shard_map/ppermute | solution.py:26
  32.4 7.8 %copy-start.1 = (f32[16,8,1024]{2,1,0:T(8,128)S(1)}, f32[16,8,1024]{2,1,0:T(8,128)}, u32[]{:S(2)}) copy-start(f32[16,8,1024]{2,1,0:T(8,128)} %weights.8) | copy-start | bytes 1572868
  32.4 2.9 %collective-permute-start.8 = (f32[9,256,128]{2,1,0:T(8,128)S(1)}, f32[9,256,128]{2,1,0:T(8,128)S(1)}, u32[]{:S(2)}, u32[]{:S(2)}) collective-permute-start(f32[9,256,128]{2,1,0:T(8,128)S(1)} %bitcast_dynamic-update-slice_fusion.early), channel_id=1, source_target_pairs={{0,1},{1,0},{2,3},{3,2},{4,5},{5,4},{6,7},{7,6},{8,9},{9,8},{10,11... | collective-permute-start | bytes 3538952 | tf_op jit(solution)/shard_map/ppermute | solution.py:26
  32.5 6.3 %collective-permute-start.7 = (f32[256,128]{1,0:T(8,128)S(1)}, f32[256,128]{1,0:T(8,128)S(1)}, u32[]{:S(2)}, u32[]{:S(2)}) collective-permute-start(f32[256,128]{1,0:T(8,128)S(1)} %collective-permute-done.4), channel_id=1, source_target_pairs={{0,2},{1,3},{2,0},{3,1},{4,6},{5,7},{6,4},{7,5},{8,10},{9,11},{10,... | collective-permute-start | bytes 393224 | tf_op jit(solution)/shard_map/ppermute | solution.py:26
  35.3 4.9 %copy-start = (bf16[1024,1024]{1,0:T(8,128)(2,1)S(1)}, bf16[1024,1024]{1,0:T(8,128)(2,1)}, u32[]{:S(2)}) copy-start(bf16[1024,1024]{1,0:T(8,128)(2,1)} %queries.8) | copy-start | bytes 6291460
  35.3 4.9 %copy-start.2 = (bf16[1024,1024]{1,0:T(8,128)(2,1)S(1)}, bf16[1024,1024]{1,0:T(8,128)(2,1)}, u32[]{:S(2)}) copy-start(bf16[1024,1024]{1,0:T(8,128)(2,1)} %out_weight.1) | copy-start | bytes 6291460
  38.8 1.4 %collective-permute-start.9 = (f32[256,128]{1,0:T(8,128)S(1)}, f32[256,128]{1,0:T(8,128)S(1)}, u32[]{:S(2)}, u32[]{:S(2)}) collective-permute-start(f32[256,128]{1,0:T(8,128)S(1)} %collective-permute-done.7.late), channel_id=1, source_target_pairs={{0,1},{1,0},{2,3},{3,2},{4,5},{5,4},{6,7},{7,6},{8,9},{9,8},{10,11... | collective-permute-start | bytes 393224 | tf_op jit(solution)/shard_map/ppermute | solution.py:26

commit v7 on v6

--- a/solution.py
+++ b/solution.py
@@ -190,8 +190,8 @@
     return jnp.bitwise_and(jnp.right_shift(place, bit), 1) == 1
 
 
-def near_kernel(half, place, queries, weights, local, *rest):
-    *held, near, states, rows = rest
+def near_kernel(aliased, half, place, queries, weights, local, *rest):
+    *held, near, states, rows = rest[aliased:]
     step = pl.program_id(0)
     bits = states.shape[1] // HEAD
     size = states.shape[0] * HEAD // 2
@@ -225,13 +225,14 @@
         near[part, :] = total
 
 
-def near_part(half, place, bits, queries, level_weights, local, *held):
+def near_part(half, place, bits, queries, level_weights, local, into, *held):
     tokens, width = queries.shape
     heads = width // HEAD // 2
     step = 2 * HEAD
     steps = width // step // 2
+    into = () if into is None else (pltpu.with_memory_space_constraint(into, pltpu.VMEM),)
     return pl.pallas_call(
-        near_kernel,
+        functools.partial(near_kernel, len(into)),
         grid_spec=pltpu.PrefetchScalarGridSpec(
             num_scalar_prefetch=2,
             grid=(steps,),
@@ -239,6 +240,7 @@
                 pl.BlockSpec((tokens, step), lambda pair, half, place: (0, half[0] * steps + pair)),
                 pl.BlockSpec(level_weights.shape, lambda pair, half, place: (0, 0, 0)),
                 pl.BlockSpec((step, tokens), lambda pair, half, place: (pair, 0)),
+                *[pl.BlockSpec(memory_space=pltpu.VMEM)] * len(into),
                 *[
                     pl.BlockSpec(
                         (2 * bits,) + part.shape[1:] if part.ndim == 3 else part.shape,
@@ -247,20 +249,21 @@
                     for part in held
                 ],
             ],
-            out_specs=pl.BlockSpec((step, tokens), lambda pair, half, place: (pair, 0)),
+            out_specs=pl.BlockSpec((step, tokens), lambda pair, half, place: (half[0] * steps + pair, 0)),
             scratch_shapes=[
                 pltpu.VMEM((heads, bits * HEAD, HEAD), BF16),
                 pltpu.VMEM((2, level_weights.shape[0], tokens), F32),
             ],
         ),
-        out_shape=pltpu.VMEM((width // 2, tokens), F32),
+        out_shape=pltpu.VMEM((width, tokens), F32),
+        input_output_aliases={5: 0} if into else {},
         cost_estimate=cost(tokens * width, MIB // 4),
         compiler_params=params(16),
-    )(half.reshape(1), place, *outside(queries, level_weights, local), *held)
-
-
-def far_kernel(first_level, place, queries, weights, near_mine, near_other, early, early_other, late, late_other,
-               out_weight, mixed, states, flipped, attended):
+    )(half.reshape(1), place, *outside(queries, level_weights, local), *into, *held)
+
+
+def far_kernel(first_level, place, queries, weights, near, early, early_other, late, late_other, out_weight,
+               mixed, states, flipped, attended):
     rows, width = attended.shape
     bits = states.shape[1] // HEAD
     size = late.shape[0]
@@ -286,8 +289,7 @@
             part = slice(half * (width // 2) + low, half * (width // 2) + low + HEAD)
             head = part.start // HEAD
             products = product_nt(states[head], queries[:, part])
-            span = slice(low, low + HEAD)
-            total = jnp.where(core == half, near_mine[span, :], near_other[span, :])
+            total = near[part, :]
             for bit in range(bits):
                 row = weights[first_level + bit, head : head + 1, :]
                 total = total + row * products[bit * HEAD : (bit + 1) * HEAD]
@@ -300,11 +302,10 @@
     mixed[...] = product(attended[...], out_weight[...]).astype(BF16)
 
 
-def far_part(first_level, bits, place, queries, level_weights, near_mine, near_other, *fixed):
+def far_part(first_level, bits, place, queries, level_weights, near, *fixed):
     tokens, width = queries.shape
     rows = min(2 * CHUNK, tokens)
     band = pl.BlockSpec((rows, width), lambda step: (step, 0))
-    near = pl.BlockSpec((width // 2, rows), lambda step: (0, step))
 
     def tail(part):
         count = 2 * bits - 1
@@ -320,8 +321,7 @@
             pl.BlockSpec(memory_space=pltpu.SMEM),
             band,
             pl.BlockSpec(level_weights.shape[:2] + (rows,), lambda step: (0, 0, step)),
-            near,
-            near,
+            pl.BlockSpec((width, rows), lambda step: (0, step)),
             *[tail(part) for part in fixed],
         ],
         out_specs=band,
@@ -333,7 +333,7 @@
         ],
         cost_estimate=cost(2 * tokens * width * (width + bits * HEAD), 12 * MIB),
         compiler_params=params(28),
-    )(place, queries, level_weights, near_mine, near_other, *fixed)
+    )(place, queries, level_weights, near, *fixed)
 
 
 def body(queries, keys, values, level_weights, out_weight):
@@ -374,14 +374,14 @@
         buckets.append(arrived)
         running = running + arrived
 
-    running, sent = tie((running, jnp.stack([own] + buckets[1:])))
+    running, own, later = tie((running, own, buckets[1:]))
     far = [swap(running, "outer", 1)]
-    others = swap(sent, "inner", 2)
+    others = [swap(part, "inner", 2) for part in (own, *later)]
     beside = []
 
     def own_near():
         held = [part for at, bucket in enumerate(buckets) for part in (bucket, others[at])]
-        return near_part(core, place, inner_bits, queries, level_weights, local[0], first, *held)
+        return near_part(core, place, inner_bits, queries, level_weights, local[0], None, first, *held)
 
     for bit in range(1, outer_bits):
         running = running + far[-1]
@@ -397,15 +397,12 @@
     pairs = [(keep_ours, keep_theirs), *((bucket, others[at]) for at, bucket in enumerate(buckets)), *zip(far, beside)]
     mine = jnp.stack([part for pair in pairs for part in pair] + far[-1:])
     other = swap(mine, "inner", 1)
-    nears = [
-        near_mine,
-        near_part(1 - core, place, inner_bits, queries, level_weights, local[1], other),
-    ]
-    late, nears = tie((late, nears))
+    near = near_part(1 - core, place, inner_bits, queries, level_weights, local[1], near_mine, other)
+    late, near = tie((late, near))
     late_other = swap(late, "inner", 1)
     first_level = LOCAL_BITS + 1 + inner_bits
     return far_part(
-        first_level, outer_bits, place, queries, level_weights, *nears, mine, other, late, late_other, out_weight
+        first_level, outer_bits, place, queries, level_weights, near, mine, other, late, late_other, out_weight
     )
 
 

time: 47.3 us -> 46.4 us (0.981)
  Pallas kernels: 27.1 us -> 26.5 us
    pallas_call x1, Pallas kernels: 6.86 us -> 6.28 us  [far_part(): pl.pallas_call(functools.partial(far_kernel, first_level), grid=(tokens /...]
    ppermute x10 -> x11, starting transfers between devices: 12.7 us -> 12.3 us  [swap(): lax.ppermute(block, axis, [(place, place ^ stride) for place in range(cou...]
    ppermute x10 -> x11, waiting for transfers between devices: 6.83 us -> 6.97 us  [swap(): lax.ppermute(block, axis, [(place, place ^ stride) for place in range(cou...]
  transfers between devices with their start and end apart: 10 -> 11, of which waited for: 5 -> 5; matrix products, arithmetic and copies ran while one was open for 0% -> 0% of each run, Pallas kernels for 38% -> 39%
where the time goes in v7:
time: 46.4 us; the launch traced here: 46.2 us
  Pallas kernels  26.5 us (57%)
  starting transfers between devices  12.3 us (27%)
  waiting for transfers between devices  6.97 us (15%)
    ppermute x11, starting transfers between devices, swap(): lax.ppermute(block, axis, [(place, place ^ stride) for place in range(cou...  12.3 us
    pallas_call x2, Pallas kernels, local_part(): pl.pallas_call(local_kernel, grid_spec=pltpu.PrefetchScalarGridSpec(num_s...  9.39 us
    ppermute x11, waiting for transfers between devices, swap(): lax.ppermute(block, axis, [(place, place ^ stride) for place in range(cou...  6.97 us
    pallas_call x2, Pallas kernels, near_part(): pl.pallas_call(functools.partial(near_kernel, len(into)), grid_spec=pltpu...  6.68 us
    pallas_call x1, Pallas kernels, far_part(): pl.pallas_call(functools.partial(far_kernel, first_level), grid=(tokens /...  6.28 us
    pallas_call x2, Pallas kernels, block_state(): pl.pallas_call(state_kernel, grid_spec=pltpu.PrefetchScalarGridSpec(num_s...  4.16 us
  transfers between devices with their start and end apart: 11, of which 5 were waited for; matrix products, arithmetic and copies ran while one was open for 0% of the time, Pallas kernels for 39%

profile of v7, /device:TPU:0, one launch (start us, length us, event | category | flops | bytes accessed | tf_op | source)
XLA Modules:
  0.0 46.2 jit_solution(114215455484276129)
XLA Ops:
  0.0 2.4 %shard_map.56 = f32[512,128]{1,0:T(8,128)S(1)} custom-call(s32[1]{0:T(128)} %bitcast.3.place.half, bf16[1024,1024]{1,0:T(8,128)(2,1)} %keys.5, bf16[1024,1024]{1,0:T(8,128)(2,1)} %values.5), custom_call_target="tpu_custom_call" | custom-call | flops 134217728 | bytes 2621440 | tf_op jit(solution)/shard_map/pallas_call | solution.py:77
  2.4 0.5 %collective-permute-start = (f32[512,128]{1,0:T(8,128)S(1)}, f32[512,128]{1,0:T(8,128)S(1)}, u32[]{:S(2)}, u32[]{:S(2)}) collective-permute-start(f32[512,128]{1,0:T(8,128)S(1)} %shard_map.56), channel_id=1, source_target_pairs={{0,1},{1,0},{2,3},{3,2},{4,5},{5,4},{6,7},{7,6},{8,9},{9,8},{10,11... | collective-permute-start | bytes 786440 | tf_op jit(solution)/shard_map/ppermute | solution.py:26
  2.9 1.8 %shard_map.57 = f32[256,128]{1,0:T(8,128)S(1)} custom-call(s32[1]{0:T(128)} %bitcast.4.place, bf16[1024,1024]{1,0:T(8,128)(2,1)} %keys.5, bf16[1024,1024]{1,0:T(8,128)(2,1)} %values.5), custom_call_target="tpu_custom_call" | custom-call | flops 67108864 | bytes 1310720 | tf_op jit(solution)/shard_map/pallas_call | solution.py:77
  4.7 0.0 collective-permute-done.rest_0_
  4.7 2.6 %collective-permute-start.1 = (f32[256,128]{1,0:T(8,128)S(1)}, f32[256,128]{1,0:T(8,128)S(1)}, u32[]{:S(2)}, u32[]{:S(2)}) collective-permute-start(f32[256,128]{1,0:T(8,128)S(1)} %dynamic-slice_add_fusion), channel_id=1, source_target_pairs={{0,2},{1,3},{2,0},{3,1},{4,6},{5,7},{6,4},{7,5},{8,10},{9,11},{10,... | collective-permute-start | bytes 393224 | tf_op jit(solution)/shard_map/ppermute | solution.py:26
  7.3 4.7 %shard_map.55 = (bf16[512,1024]{1,0:T(8,128)(2,1)}, f32[512,128]{1,0:T(8,128)S(1)}) custom-call(s32[1]{0:T(128)} %bitcast.2.half, bf16[1024,1024]{1,0:T(8,128)(2,1)} %queries.8, bf16[1024,1024]{1,0:T(8,128)(2,1)} %keys.5, bf16[1024,1024]{1,0:T(8,128)(2,1)} %values.5, f32[16,8,1024]{2,1,0:T(8,128)} %weights.8), custom_call_target="tpu_custom_call" | custom-call | flops 1048576 | bytes 262144 | tf_op jit(solution)/shard_map/pallas_call | solution.py:171
  12.0 0.0 collective-permute-done.1.rest_1_
  12.1 1.6 %collective-permute-start.2 = (f32[256,128]{1,0:T(8,128)S(1)}, f32[256,128]{1,0:T(8,128)S(1)}, u32[]{:S(2)}, u32[]{:S(2)}) collective-permute-start(f32[256,128]{1,0:T(8,128)S(1)} %get-tuple-element.34), channel_id=1, source_target_pairs={{0,4},{1,5},{2,6},{3,7},{4,0},{5,1},{6,2},{7,3},{8,12},{9,13},{10,... | collective-permute-start | bytes 393224 | tf_op jit(solution)/shard_map/ppermute | solution.py:26
  13.7 4.7 %shard_map.58.local = bf16[512,1024]{1,0:T(8,128)(2,1)} custom-call(s32[1]{0:T(128)} %bitcast.3.place.half, bf16[1024,1024]{1,0:T(8,128)(2,1)} %queries.8, bf16[1024,1024]{1,0:T(8,128)(2,1)} %keys.5, bf16[1024,1024]{1,0:T(8,128)(2,1)} %values.5, f32[16,8,1024]{2,1,0:T(8,128)} %weights.8), custom_call_target="tpu_custom_call" | custom-call | flops 1048576 | bytes 262144 | tf_op jit(solution)/shard_map/pallas_call | solution.py:171
  18.3 0.0 collective-permute-done.2.rest_3_
  18.4 1.6 %collective-permute-start.3 = (f32[256,128]{1,0:T(8,128)S(1)}, f32[256,128]{1,0:T(8,128)S(1)}, u32[]{:S(2)}, u32[]{:S(2)}) collective-permute-start(f32[256,128]{1,0:T(8,128)S(1)} %add.31), channel_id=1, source_target_pairs={{0,8},{8,0},{16,24},{24,16},{1,9},{9,1},{17,25},{25,17},{2,10},{10... | collective-permute-start | bytes 393224 | tf_op jit(solution)/shard_map/ppermute | solution.py:26
  20.0 0.1 pad_add_fusion.place
  20.1 1.2 %collective-permute-start.6 = (f32[256,128]{1,0:T(8,128)S(1)}, f32[256,128]{1,0:T(8,128)S(1)}, u32[]{:S(2)}, u32[]{:S(2)}) collective-permute-start(f32[256,128]{1,0:T(8,128)S(1)} %get-tuple-element.42), channel_id=1, source_target_pairs={{0,2},{1,3},{2,0},{3,1},{4,6},{5,7},{6,4},{7,5},{8,10},{9,11},{10,... | collective-permute-start | bytes 393224 | tf_op jit(solution)/shard_map/ppermute | solution.py:26
  21.3 0.9 %collective-permute-start.7 = (f32[256,128]{1,0:T(8,128)S(1)}, f32[256,128]{1,0:T(8,128)S(1)}, u32[]{:S(2)}, u32[]{:S(2)}) collective-permute-start(f32[256,128]{1,0:T(8,128)S(1)} %collective-permute-done.2.rest_3_), channel_id=1, source_target_pairs={{0,2},{1,3},{2,0},{3,1},{4,6},{5,7},{6,4},{7,5},{8,10},{9,11},{10,... | collective-permute-start | bytes 393224 | tf_op jit(solution)/shard_map/ppermute | solution.py:26
  22.1 1.6 %collective-permute-done.3 = f32[256,128]{1,0:T(8,128)S(1)} collective-permute-done((f32[256,128]{1,0:T(8,128)S(1)}, f32[256,128]{1,0:T(8,128)S(1)}, u32[]{:S(2)}, u32[]{:S(2)}) %collective-permute-start.3) | collective-permute-done | bytes 131104 | tf_op jit(solution)/shard_map/ppermute | solution.py:26
  23.8 2.7 %collective-permute-start.4 = (f32[256,128]{1,0:T(8,128)S(1)}, f32[256,128]{1,0:T(8,128)S(1)}, u32[]{:S(2)}, u32[]{:S(2)}) collective-permute-start(f32[256,128]{1,0:T(8,128)S(1)} %add.32), channel_id=1, source_target_pairs={{0,16},{8,24},{16,0},{24,8},{1,17},{9,25},{17,1},{25,9},{2,18},{10... | collective-permute-start | bytes 393224 | tf_op jit(solution)/shard_map/ppermute | solution.py:26
  26.4 0.8 %collective-permute-start.5 = (f32[256,128]{1,0:T(8,128)S(1)}, f32[256,128]{1,0:T(8,128)S(1)}, u32[]{:S(2)}, u32[]{:S(2)}) collective-permute-start(f32[256,128]{1,0:T(8,128)S(1)} %collective-permute-done.3), channel_id=1, source_target_pairs={{0,2},{1,3},{2,0},{3,1},{4,6},{5,7},{6,4},{7,5},{8,10},{9,11},{10,... | collective-permute-start | bytes 393224 | tf_op jit(solution)/shard_map/ppermute | solution.py:26
  27.2 0.0 collective-permute-done.6.rest_2_
  27.2 0.8 %collective-permute-done.7.rest_4_ = f32[256,128]{1,0:T(8,128)S(1)} collective-permute-done((f32[256,128]{1,0:T(8,128)S(1)}, f32[256,128]{1,0:T(8,128)S(1)}, u32[]{:S(2)}, u32[]{:S(2)}) %collective-permute-start.7) | collective-permute-done | bytes 131104 | tf_op jit(solution)/shard_map/ppermute | solution.py:26
  28.0 3.2 %shard_map.59.rest_0_ = f32[1024,1024]{1,0:T(8,128)S(1)} custom-call(s32[1]{0:T(128)} %bitcast.2.half, s32[2]{0:T(128)S(1)} %pad_add_fusion.place, bf16[1024,1024]{1,0:T(8,128)(2,1)} %queries.8, f32[16,8,1024]{2,1,0:T(8,128)} %weights.8, bf16[512,1024]{1,0:T(8,128)(2,1)} %get-tuple-element.44.local, f32[512,128]{1,0:T(8,128)S(1)} %collective-permute-done.rest_0_, ...), custom_call_target="tpu_custom_call" | custom-call | flops 1048576 | bytes 262144 | tf_op jit(solution)/shard_map/pallas_call | solution.py:234
  31.3 0.7 %collective-permute-done.4 = f32[256,128]{1,0:T(8,128)S(1)} collective-permute-done((f32[256,128]{1,0:T(8,128)S(1)}, f32[256,128]{1,0:T(8,128)S(1)}, u32[]{:S(2)}, u32[]{:S(2)}) %collective-permute-start.4) | collective-permute-done | bytes 131104 | tf_op jit(solution)/shard_map/ppermute | solution.py:26
  32.0 0.0 collective-permute-done.5
  32.1 0.0 copy-start.1
  32.1 0.1 collective-permute-start.9
  32.2 0.3 collective-permute-start.8
  32.5 2.6 %collective-permute-done.9.rest_1_.early_other = f32[9,256,128]{2,1,0:T(8,128)S(1)} collective-permute-done((f32[9,256,128]{2,1,0:T(8,128)S(1)}, f32[9,256,128]{2,1,0:T(8,128)S(1)}, u32[]{:S(2)}, u32[]{:S(2)}) %collective-permute-start.9) | collective-permute-done | bytes 1179680 | tf_op jit(solution)/shard_map/ppermute | solution.py:26
  35.1 0.0 copy-start
  35.1 0.0 copy-start.2
  35.1 3.5 %shard_map.60.near = f32[1024,1024]{1,0:T(8,128)S(1)} custom-call(s32[1]{0:T(128)} %bitcast.3.place.half, s32[2]{0:T(128)S(1)} %pad_add_fusion.place, bf16[1024,1024]{1,0:T(8,128)(2,1)} %queries.8, f32[16,8,1024]{2,1,0:T(8,128)} %weights.8, bf16[512,1024]{1,0:T(8,128)(2,1)} %shard_map.58.local, ...), custom_call_target="tpu_custom_call", output_to_operand_aliasing={{}: (5, {})} | custom-call | flops 1048576 | bytes 262144 | tf_op jit(solution)/shard_map/pallas_call | solution.py:234
  38.5 0.0 collective-permute-done.8.late
  38.5 0.2 collective-permute-start.10
  38.7 1.2 %collective-permute-done.10.late_other = f32[256,128]{1,0:T(8,128)S(1)} collective-permute-done((f32[256,128]{1,0:T(8,128)S(1)}, f32[256,128]{1,0:T(8,128)S(1)}, u32[]{:S(2)}, u32[]{:S(2)}) %collective-permute-start.10) | collective-permute-done | bytes 131104 | tf_op jit(solution)/shard_map/ppermute | solution.py:26
  40.0 0.0 copy-done.1
  40.0 0.0 copy-done
  40.0 0.0 copy-done.2
  40.0 6.3 %shard_map.61 = bf16[1024,1024]{1,0:T(8,128)(2,1)} custom-call(s32[2]{0:T(128)S(1)} %pad_add_fusion.place, bf16[1024,1024]{1,0:T(8,128)(2,1)S(1)} %copy-done, f32[16,8,1024]{2,1,0:T(8,128)S(1)} %copy-done.1, f32[1024,1024]{1,0:T(8,128)S(1)} %shard_map.60.near, f32[9,256,128]{2,1,0:T(8,128)S(1)} %bitcast_dynamic-update-slice_fusion.early, ...), custom_call_target="tpu_custom_call" | custom-call | flops 2684354560 | bytes 12582912 | tf_op jit(solution)/shard_map/pallas_call | solution.py:317
  (13 shorter events, 0.2 us)
Async XLA Ops:
  2.4 2.3 %collective-permute-start = (f32[512,128]{1,0:T(8,128)S(1)}, f32[512,128]{1,0:T(8,128)S(1)}, u32[]{:S(2)}, u32[]{:S(2)}) collective-permute-start(f32[512,128]{1,0:T(8,128)S(1)} %shard_map.56), channel_id=1, source_target_pairs={{0,1},{1,0},{2,3},{3,2},{4,5},{5,4},{6,7},{7,6},{8,9},{9,8},{10,11... | collective-permute-start | bytes 786440 | tf_op jit(solution)/shard_map/ppermute | solution.py:26
  4.7 7.3 %collective-permute-start.1 = (f32[256,128]{1,0:T(8,128)S(1)}, f32[256,128]{1,0:T(8,128)S(1)}, u32[]{:S(2)}, u32[]{:S(2)}) collective-permute-start(f32[256,128]{1,0:T(8,128)S(1)} %dynamic-slice_add_fusion), channel_id=1, source_target_pairs={{0,2},{1,3},{2,0},{3,1},{4,6},{5,7},{6,4},{7,5},{8,10},{9,11},{10,... | collective-permute-start | bytes 393224 | tf_op jit(solution)/shard_map/ppermute | solution.py:26
  12.1 6.3 %collective-permute-start.2 = (f32[256,128]{1,0:T(8,128)S(1)}, f32[256,128]{1,0:T(8,128)S(1)}, u32[]{:S(2)}, u32[]{:S(2)}) collective-permute-start(f32[256,128]{1,0:T(8,128)S(1)} %get-tuple-element.34), channel_id=1, source_target_pairs={{0,4},{1,5},{2,6},{3,7},{4,0},{5,1},{6,2},{7,3},{8,12},{9,13},{10,... | collective-permute-start | bytes 393224 | tf_op jit(solution)/shard_map/ppermute | solution.py:26
  18.4 5.4 %collective-permute-start.3 = (f32[256,128]{1,0:T(8,128)S(1)}, f32[256,128]{1,0:T(8,128)S(1)}, u32[]{:S(2)}, u32[]{:S(2)}) collective-permute-start(f32[256,128]{1,0:T(8,128)S(1)} %add.31), channel_id=1, source_target_pairs={{0,8},{8,0},{16,24},{24,16},{1,9},{9,1},{17,25},{25,17},{2,10},{10... | collective-permute-start | bytes 393224 | tf_op jit(solution)/shard_map/ppermute | solution.py:26
  20.1 7.1 %collective-permute-start.6 = (f32[256,128]{1,0:T(8,128)S(1)}, f32[256,128]{1,0:T(8,128)S(1)}, u32[]{:S(2)}, u32[]{:S(2)}) collective-permute-start(f32[256,128]{1,0:T(8,128)S(1)} %get-tuple-element.42), channel_id=1, source_target_pairs={{0,2},{1,3},{2,0},{3,1},{4,6},{5,7},{6,4},{7,5},{8,10},{9,11},{10,... | collective-permute-start | bytes 393224 | tf_op jit(solution)/shard_map/ppermute | solution.py:26
  21.3 6.8 %collective-permute-start.7 = (f32[256,128]{1,0:T(8,128)S(1)}, f32[256,128]{1,0:T(8,128)S(1)}, u32[]{:S(2)}, u32[]{:S(2)}) collective-permute-start(f32[256,128]{1,0:T(8,128)S(1)} %collective-permute-done.2.rest_3_), channel_id=1, source_target_pairs={{0,2},{1,3},{2,0},{3,1},{4,6},{5,7},{6,4},{7,5},{8,10},{9,11},{10,... | collective-permute-start | bytes 393224 | tf_op jit(solution)/shard_map/ppermute | solution.py:26
  23.8 8.2 %collective-permute-start.4 = (f32[256,128]{1,0:T(8,128)S(1)}, f32[256,128]{1,0:T(8,128)S(1)}, u32[]{:S(2)}, u32[]{:S(2)}) collective-permute-start(f32[256,128]{1,0:T(8,128)S(1)} %add.32), channel_id=1, source_target_pairs={{0,16},{8,24},{16,0},{24,8},{1,17},{9,25},{17,1},{25,9},{2,18},{10... | collective-permute-start | bytes 393224 | tf_op jit(solution)/shard_map/ppermute | solution.py:26
  26.4 5.6 %collective-permute-start.5 = (f32[256,128]{1,0:T(8,128)S(1)}, f32[256,128]{1,0:T(8,128)S(1)}, u32[]{:S(2)}, u32[]{:S(2)}) collective-permute-start(f32[256,128]{1,0:T(8,128)S(1)} %collective-permute-done.3), channel_id=1, source_target_pairs={{0,2},{1,3},{2,0},{3,1},{4,6},{5,7},{6,4},{7,5},{8,10},{9,11},{10,... | collective-permute-start | bytes 393224 | tf_op jit(solution)/shard_map/ppermute | solution.py:26
  32.1 7.8 %copy-start.1 = (f32[16,8,1024]{2,1,0:T(8,128)S(1)}, f32[16,8,1024]{2,1,0:T(8,128)}, u32[]{:S(2)}) copy-start(f32[16,8,1024]{2,1,0:T(8,128)} %weights.8) | copy-start | bytes 1572868
  32.1 2.9 %collective-permute-start.9 = (f32[9,256,128]{2,1,0:T(8,128)S(1)}, f32[9,256,128]{2,1,0:T(8,128)S(1)}, u32[]{:S(2)}, u32[]{:S(2)}) collective-permute-start(f32[9,256,128]{2,1,0:T(8,128)S(1)} %bitcast_dynamic-update-slice_fusion.early), channel_id=1, source_target_pairs={{0,1},{1,0},{2,3},{3,2},{4,5},{5,4},{6,7},{7,6},{8,9},{9,8},{10,11... | collective-permute-start | bytes 3538952 | tf_op jit(solution)/shard_map/ppermute | solution.py:26
  32.2 6.3 %collective-permute-start.8 = (f32[256,128]{1,0:T(8,128)S(1)}, f32[256,128]{1,0:T(8,128)S(1)}, u32[]{:S(2)}, u32[]{:S(2)}) collective-permute-start(f32[256,128]{1,0:T(8,128)S(1)} %collective-permute-done.4), channel_id=1, source_target_pairs={{0,2},{1,3},{2,0},{3,1},{4,6},{5,7},{6,4},{7,5},{8,10},{9,11},{10,... | collective-permute-start | bytes 393224 | tf_op jit(solution)/shard_map/ppermute | solution.py:26
  35.1 4.9 %copy-start = (bf16[1024,1024]{1,0:T(8,128)(2,1)S(1)}, bf16[1024,1024]{1,0:T(8,128)(2,1)}, u32[]{:S(2)}) copy-start(bf16[1024,1024]{1,0:T(8,128)(2,1)} %queries.8) | copy-start | bytes 6291460
  35.1 4.9 %copy-start.2 = (bf16[1024,1024]{1,0:T(8,128)(2,1)S(1)}, bf16[1024,1024]{1,0:T(8,128)(2,1)}, u32[]{:S(2)}) copy-start(bf16[1024,1024]{1,0:T(8,128)(2,1)} %out_weight.1) | copy-start | bytes 6291460
  38.5 1.4 %collective-permute-start.10 = (f32[256,128]{1,0:T(8,128)S(1)}, f32[256,128]{1,0:T(8,128)S(1)}, u32[]{:S(2)}, u32[]{:S(2)}) collective-permute-start(f32[256,128]{1,0:T(8,128)S(1)} %collective-permute-done.8.late), channel_id=1, source_target_pairs={{0,1},{1,0},{2,3},{3,2},{4,5},{5,4},{6,7},{7,6},{8,9},{9,8},{10,11... | collective-permute-start | bytes 393224 | tf_op jit(solution)/shard_map/ppermute | solution.py:26

commit v8 on v7

--- a/solution.py
+++ b/solution.py
@@ -42,6 +42,10 @@
 
 def outside(*parts):
     return tuple(pltpu.with_memory_space_constraint(part, pltpu.HBM) for part in parts)
+
+
+def inside(*parts):
+    return tuple(pltpu.with_memory_space_constraint(part, pltpu.VMEM) for part in parts)
 
 
 def product(left, right):
@@ -167,18 +171,19 @@
     tokens, width = queries.shape
     step = 2 * HEAD
     steps = width // step // 2
+    levels = LOCAL_BITS + 1
     column = pl.BlockSpec((tokens, step), lambda pair, half: (0, half[0] * steps + pair))
     return pl.pallas_call(
         local_kernel,
         grid_spec=pltpu.PrefetchScalarGridSpec(
             num_scalar_prefetch=1,
             grid=(steps,),
-            in_specs=[column, column, column, pl.BlockSpec(level_weights.shape, lambda pair, half: (0, 0, 0))],
+            in_specs=[column, column, column, pl.BlockSpec((levels,) + level_weights.shape[1:], lambda pair, half: (0, 0, 0))],
             out_specs=[
                 pl.BlockSpec((step, tokens), lambda pair, half: (pair, 0)),
                 pl.BlockSpec((step, HEAD), lambda pair, half: (pair, 0)),
             ][: 1 + with_state],
-            scratch_shapes=[pltpu.VMEM((2, level_weights.shape[0], tokens), F32)],
+            scratch_shapes=[pltpu.VMEM((2, levels, tokens), F32)],
         ),
         out_shape=[pltpu.HBM((width // 2, tokens), BF16), pltpu.VMEM((width // 2, HEAD), F32)][: 1 + with_state],
         cost_estimate=cost(tokens * width, MIB // 4),
@@ -259,7 +264,7 @@
         input_output_aliases={5: 0} if into else {},
         cost_estimate=cost(tokens * width, MIB // 4),
         compiler_params=params(16),
-    )(half.reshape(1), place, *outside(queries, level_weights, local), *into, *held)
+    )(half.reshape(1), place, *inside(queries, level_weights), *outside(local), *into, *held)
 
 
 def far_kernel(first_level, place, queries, weights, near, early, early_other, late, late_other, out_weight,

time: 46.4 us -> 52.3 us (1.13)
  local copies, waits for them, and re-layouts: 0.11 us -> 5.94 us
  waiting for transfers between devices: 6.97 us -> 5.96 us
  starting transfers between devices: 12.3 us -> 13.1 us
  other arithmetic: 0.15 us -> 0.8 us
    unnamed x14, local copies, waits for them, and re-layouts: 0.1 us -> 5.29 us
    ppermute x11, waiting for transfers between devices: 6.97 us -> 5.96 us  [swap(): lax.ppermute(block, axis, [(place, place ^ stride) for place in range(cou...]
    pallas_call x2, Pallas kernels: 6.68 us -> 5.89 us  [near_part(): pl.pallas_call(functools.partial(near_kernel, len(into)), grid_spec=pltpu...]
    ppermute x11, starting transfers between devices: 12.3 us -> 13.1 us  [swap(): lax.ppermute(block, axis, [(place, place ^ stride) for place in range(cou...]
    add x1, other arithmetic: 0.02 us -> 0.68 us  [body(): running = own + buckets[0]]
    another operation x1, local copies, waits for them, and re-layouts: 0.01 us -> 0.65 us  [body(): mine = jnp.stack([part for pair in pairs for part in pair] + far[-1:])]
  transfers between devices with their start and end apart: 11 -> 11, of which waited for: 5 -> 4; matrix products, arithmetic and copies ran while one was open for 0% -> 4% of each run, Pallas kernels for 39% -> 33%
where the time goes in v8:
time: 52.3 us; the launch traced here: 52 us
  Pallas kernels  26.1 us (50%)
  starting transfers between devices  13.1 us (25%)
  waiting for transfers between devices  5.96 us (11%)
  local copies, waits for them, and re-layouts  5.94 us (11%)
  other arithmetic  0.8 us (2%)
    ppermute x11, starting transfers between devices, swap(): lax.ppermute(block, axis, [(place, place ^ stride) for place in range(cou...  13.1 us
    pallas_call x2, Pallas kernels, local_part(): pl.pallas_call(local_kernel, grid_spec=pltpu.PrefetchScalarGridSpec(num_s...  9.36 us
    pallas_call x1, Pallas kernels, far_part(): pl.pallas_call(functools.partial(far_kernel, first_level), grid=(tokens /...  6.71 us
    ppermute x11, waiting for transfers between devices, swap(): lax.ppermute(block, axis, [(place, place ^ stride) for place in range(cou...  5.96 us
    pallas_call x2, Pallas kernels, near_part(): pl.pallas_call(functools.partial(near_kernel, len(into)), grid_spec=pltpu...  5.89 us
    unnamed x14, local copies, waits for them, and re-layouts  5.29 us
    pallas_call x2, Pallas kernels, block_state(): pl.pallas_call(state_kernel, grid_spec=pltpu.PrefetchScalarGridSpec(num_s...  4.16 us
  transfers between devices with their start and end apart: 11, of which 4 were waited for; matrix products, arithmetic and copies ran while one was open for 4% of the time, Pallas kernels for 33%

profile of v8, /device:TPU:0, one launch (start us, length us, event | category | flops | bytes accessed | tf_op | source)
XLA Modules:
  0.0 52.0 jit_solution(6835085686615757262)
XLA Ops:
  0.0 2.4 %shard_map.56 = f32[512,128]{1,0:T(8,128)S(1)} custom-call(s32[1]{0:T(128)} %bitcast.3.place.half, bf16[1024,1024]{1,0:T(8,128)(2,1)} %keys.5, bf16[1024,1024]{1,0:T(8,128)(2,1)} %values.5), custom_call_target="tpu_custom_call" | custom-call | flops 134217728 | bytes 2621440 | tf_op jit(solution)/shard_map/pallas_call | solution.py:81
  2.4 0.5 collective-permute-start
  2.9 1.8 %shard_map.57 = f32[256,128]{1,0:T(8,128)S(1)} custom-call(s32[1]{0:T(128)} %bitcast.4.place, bf16[1024,1024]{1,0:T(8,128)(2,1)} %keys.5, bf16[1024,1024]{1,0:T(8,128)(2,1)} %values.5), custom_call_target="tpu_custom_call" | custom-call | flops 67108864 | bytes 1310720 | tf_op jit(solution)/shard_map/pallas_call | solution.py:81
  4.7 0.0 collective-permute-done.rest_0_
  4.7 2.6 %collective-permute-start.1 = (f32[256,128]{1,0:T(8,128)S(1)}, f32[256,128]{1,0:T(8,128)S(1)}, u32[]{:S(2)}, u32[]{:S(2)}) collective-permute-start(f32[256,128]{1,0:T(8,128)S(1)} %dynamic-slice_add_fusion), channel_id=1, source_target_pairs={{0,2},{1,3},{2,0},{3,1},{4,6},{5,7},{6,4},{7,5},{8,10},{9,11},{10,... | collective-permute-start | bytes 393224 | tf_op jit(solution)/shard_map/ppermute | solution.py:26
  7.3 4.7 %shard_map.55 = (bf16[512,1024]{1,0:T(8,128)(2,1)}, f32[512,128]{1,0:T(8,128)S(1)}) custom-call(s32[1]{0:T(128)} %bitcast.2.half, bf16[1024,1024]{1,0:T(8,128)(2,1)} %queries.8, bf16[1024,1024]{1,0:T(8,128)(2,1)} %keys.5, bf16[1024,1024]{1,0:T(8,128)(2,1)} %values.5, f32[16,8,1024]{2,1,0:T(8,128)} %weights.8), custom_call_target="tpu_custom_call" | custom-call | flops 1048576 | bytes 262144 | tf_op jit(solution)/shard_map/pallas_call | solution.py:176
  12.0 0.0 collective-permute-done.1.rest_1_
  12.0 0.7 %fusion = (f32[256,128]{1,0:T(8,128)S(1)}, f32[256,128]{1,0:T(8,128)}) fusion(f32[256,128]{1,0:T(8,128)S(1)} %collective-permute-done.1.rest_1_, f32[512,128]{1,0:T(8,128)S(1)} %collective-permute-done.rest_0_, s32[]{:T(128)S(6)} %select_n.7, f32[512,128]{1,0:T(8,128)S(1)} %get-tuple-element.29), kind=kLoop, calls=%fused_computation.12 | loop fusion | flops 65536 | bytes 655364 | tf_op jit(solution)/shard_map/add | solution.py:372
  12.7 1.5 %collective-permute-start.2 = (f32[256,128]{1,0:T(8,128)S(1)}, f32[256,128]{1,0:T(8,128)S(1)}, u32[]{:S(2)}, u32[]{:S(2)}) collective-permute-start(f32[256,128]{1,0:T(8,128)S(1)} %get-tuple-element.34), channel_id=1, source_target_pairs={{0,4},{1,5},{2,6},{3,7},{4,0},{5,1},{6,2},{7,3},{8,12},{9,13},{10,... | collective-permute-start | bytes 393224 | tf_op jit(solution)/shard_map/ppermute | solution.py:26
  14.2 0.7 %bitcast_dynamic-update-slice_fusion.8 = f32[9,256,128]{2,1,0:T(8,128)} fusion(f32[512,128]{1,0:T(8,128)S(1)} %get-tuple-element.29, s32[]{:T(128)S(6)} %select_n.7), kind=kLoop, calls=%fused_computation.8 | loop fusion | bytes 262148
  14.9 0.0 copy-start
  14.9 4.7 %shard_map.58.local = bf16[512,1024]{1,0:T(8,128)(2,1)} custom-call(s32[1]{0:T(128)} %bitcast.3.place.half, bf16[1024,1024]{1,0:T(8,128)(2,1)} %queries.8, bf16[1024,1024]{1,0:T(8,128)(2,1)} %keys.5, bf16[1024,1024]{1,0:T(8,128)(2,1)} %values.5, f32[16,8,1024]{2,1,0:T(8,128)} %weights.8), custom_call_target="tpu_custom_call" | custom-call | flops 1048576 | bytes 262144 | tf_op jit(solution)/shard_map/pallas_call | solution.py:176
  19.5 0.0 copy-start.1
  19.5 0.0 collective-permute-done.2.rest_3_
  19.6 1.6 %collective-permute-start.3 = (f32[256,128]{1,0:T(8,128)S(1)}, f32[256,128]{1,0:T(8,128)S(1)}, u32[]{:S(2)}, u32[]{:S(2)}) collective-permute-start(f32[256,128]{1,0:T(8,128)S(1)} %add.31), channel_id=1, source_target_pairs={{0,8},{8,0},{16,24},{24,16},{1,9},{9,1},{17,25},{25,17},{2,10},{10... | collective-permute-start | bytes 393224 | tf_op jit(solution)/shard_map/ppermute | solution.py:26
  21.2 0.7 %bitcast_dynamic-update-slice_fusion.7 = f32[9,256,128]{2,1,0:T(8,128)} fusion(f32[9,256,128]{2,1,0:T(8,128)} %bitcast_dynamic-update-slice_fusion.8, f32[256,128]{1,0:T(8,128)S(1)} %shard_map.57), kind=kLoop, calls=%fused_computation.7 | loop fusion | bytes 262144
  21.9 0.1 pad_add_fusion.place
  22.0 1.2 %collective-permute-start.6 = (f32[256,128]{1,0:T(8,128)}, f32[256,128]{1,0:T(8,128)S(1)}, u32[]{:S(2)}, u32[]{:S(2)}) collective-permute-start(f32[256,128]{1,0:T(8,128)} %get-tuple-element.42), channel_id=1, source_target_pairs={{0,2},{1,3},{2,0},{3,1},{4,6},{5,7},{6,4},{7,5},{8,10},{9,11},{10,... | collective-permute-start | bytes 393224 | tf_op jit(solution)/shard_map/ppermute | solution.py:26
  23.2 0.8 %collective-permute-start.7 = (f32[256,128]{1,0:T(8,128)S(1)}, f32[256,128]{1,0:T(8,128)S(1)}, u32[]{:S(2)}, u32[]{:S(2)}) collective-permute-start(f32[256,128]{1,0:T(8,128)S(1)} %collective-permute-done.2.rest_3_), channel_id=1, source_target_pairs={{0,2},{1,3},{2,0},{3,1},{4,6},{5,7},{6,4},{7,5},{8,10},{9,11},{10,... | collective-permute-start | bytes 393224 | tf_op jit(solution)/shard_map/ppermute | solution.py:26
  24.0 1.0 %collective-permute-done.3 = f32[256,128]{1,0:T(8,128)S(1)} collective-permute-done((f32[256,128]{1,0:T(8,128)S(1)}, f32[256,128]{1,0:T(8,128)S(1)}, u32[]{:S(2)}, u32[]{:S(2)}) %collective-permute-start.3) | collective-permute-done | bytes 131104 | tf_op jit(solution)/shard_map/ppermute | solution.py:26
  25.0 2.7 %collective-permute-start.4 = (f32[256,128]{1,0:T(8,128)S(1)}, f32[256,128]{1,0:T(8,128)S(1)}, u32[]{:S(2)}, u32[]{:S(2)}) collective-permute-start(f32[256,128]{1,0:T(8,128)S(1)} %add.32), channel_id=1, source_target_pairs={{0,16},{8,24},{16,0},{24,8},{1,17},{9,25},{17,1},{25,9},{2,18},{10... | collective-permute-start | bytes 393224 | tf_op jit(solution)/shard_map/ppermute | solution.py:26
  27.6 0.8 %collective-permute-start.5 = (f32[256,128]{1,0:T(8,128)S(1)}, f32[256,128]{1,0:T(8,128)S(1)}, u32[]{:S(2)}, u32[]{:S(2)}) collective-permute-start(f32[256,128]{1,0:T(8,128)S(1)} %collective-permute-done.3), channel_id=1, source_target_pairs={{0,2},{1,3},{2,0},{3,1},{4,6},{5,7},{6,4},{7,5},{8,10},{9,11},{10,... | collective-permute-start | bytes 393224 | tf_op jit(solution)/shard_map/ppermute | solution.py:26
  28.5 0.7 %bitcast_dynamic-update-slice_fusion.6 = f32[9,256,128]{2,1,0:T(8,128)} fusion(f32[9,256,128]{2,1,0:T(8,128)} %bitcast_dynamic-update-slice_fusion.7, f32[256,128]{1,0:T(8,128)S(1)} %collective-permute-done.1.rest_1_), kind=kLoop, calls=%fused_computation.6 | loop fusion | bytes 262144
  29.2 0.0 collective-permute-done.6.rest_2_
  29.2 1.8 %collective-permute-done.7.rest_4_ = f32[256,128]{1,0:T(8,128)S(1)} collective-permute-done((f32[256,128]{1,0:T(8,128)S(1)}, f32[256,128]{1,0:T(8,128)S(1)}, u32[]{:S(2)}, u32[]{:S(2)}) %collective-permute-start.7) | collective-permute-done | bytes 131104 | tf_op jit(solution)/shard_map/ppermute | solution.py:26
  31.0 0.0 copy-done
  31.0 0.0 copy-done.1
  31.0 2.9 %shard_map.59.rest_0_ = f32[1024,1024]{1,0:T(8,128)S(1)} custom-call(s32[1]{0:T(128)} %bitcast.2.half, s32[2]{0:T(128)S(1)} %pad_add_fusion.place, bf16[1024,1024]{1,0:T(8,128)(2,1)S(1)} %copy-done, f32[16,8,1024]{2,1,0:T(8,128)S(1)} %copy-done.1, bf16[512,1024]{1,0:T(8,128)(2,1)} %get-tuple-element.44.local, f32[512,128]{1,0:T(8,128)S(1)} %collective-permute-done.rest_0_, ...), custom_call_target="tpu_custom_call" | custom-call | flops 1048576 | bytes 262144 | tf_op jit(solution)/shard_map/pallas_call | solution.py:239
  33.9 0.0 collective-permute-done.4
  33.9 0.0 collective-permute-done.5
  33.9 0.6 %bitcast_dynamic-update-slice_fusion.5 = f32[9,256,128]{2,1,0:T(8,128)} fusion(f32[9,256,128]{2,1,0:T(8,128)} %bitcast_dynamic-update-slice_fusion.6, f32[256,128]{1,0:T(8,128)S(1)} %collective-permute-done.6.rest_2_), kind=kLoop, calls=%fused_computation.5 | loop fusion | bytes 262144
  34.6 0.7 %bitcast_dynamic-update-slice_fusion.4 = f32[9,256,128]{2,1,0:T(8,128)} fusion(f32[9,256,128]{2,1,0:T(8,128)} %bitcast_dynamic-update-slice_fusion.5, f32[256,128]{1,0:T(8,128)S(1)} %collective-permute-done.2.rest_3_), kind=kLoop, calls=%fused_computation.4 | loop fusion | bytes 262144
  35.2 0.7 %bitcast_dynamic-update-slice_fusion.3 = f32[9,256,128]{2,1,0:T(8,128)} fusion(f32[9,256,128]{2,1,0:T(8,128)} %bitcast_dynamic-update-slice_fusion.4, f32[256,128]{1,0:T(8,128)S(1)} %collective-permute-done.7.rest_4_), kind=kLoop, calls=%fused_computation.3 | loop fusion | bytes 262144
  35.9 0.7 %bitcast_dynamic-update-slice_fusion.2 = f32[9,256,128]{2,1,0:T(8,128)} fusion(f32[9,256,128]{2,1,0:T(8,128)} %bitcast_dynamic-update-slice_fusion.3, f32[256,128]{1,0:T(8,128)S(1)} %collective-permute-done.3), kind=kLoop, calls=%fused_computation.2 | loop fusion | bytes 262144
  36.6 0.7 %bitcast_dynamic-update-slice_fusion.1 = f32[9,256,128]{2,1,0:T(8,128)} fusion(f32[9,256,128]{2,1,0:T(8,128)} %bitcast_dynamic-update-slice_fusion.2, f32[256,128]{1,0:T(8,128)S(1)} %collective-permute-done.5), kind=kLoop, calls=%fused_computation.1 | loop fusion | bytes 262144
  37.2 0.7 %bitcast_dynamic-update-slice_fusion.early = f32[9,256,128]{2,1,0:T(8,128)} fusion(f32[9,256,128]{2,1,0:T(8,128)} %bitcast_dynamic-update-slice_fusion.1, f32[256,128]{1,0:T(8,128)S(1)} %collective-permute-done.4), kind=kLoop, calls=%fused_computation | loop fusion | bytes 262144 | tf_op jit(solution)/shard_map/stack | solution.py:403
  37.9 0.0 collective-permute-start.9
  37.9 1.1 %collective-permute-start.8 = (f32[256,128]{1,0:T(8,128)S(1)}, f32[256,128]{1,0:T(8,128)S(1)}, u32[]{:S(2)}, u32[]{:S(2)}) collective-permute-start(f32[256,128]{1,0:T(8,128)S(1)} %collective-permute-done.4), channel_id=1, source_target_pairs={{0,2},{1,3},{2,0},{3,1},{4,6},{5,7},{6,4},{7,5},{8,10},{9,11},{10,... | collective-permute-start | bytes 393224 | tf_op jit(solution)/shard_map/ppermute | solution.py:26
  39.0 2.0 %collective-permute-done.9.rest_1_.early_other = f32[9,256,128]{2,1,0:T(8,128)S(1)} collective-permute-done((f32[9,256,128]{2,1,0:T(8,128)}, f32[9,256,128]{2,1,0:T(8,128)S(1)}, u32[]{:S(2)}, u32[]{:S(2)}) %collective-permute-start.9) | collective-permute-done | bytes 1179680 | tf_op jit(solution)/shard_map/ppermute | solution.py:26
  40.9 0.0 copy-start.2
  40.9 2.9 %shard_map.60.near = f32[1024,1024]{1,0:T(8,128)S(1)} custom-call(s32[1]{0:T(128)} %bitcast.3.place.half, s32[2]{0:T(128)S(1)} %pad_add_fusion.place, bf16[1024,1024]{1,0:T(8,128)(2,1)S(1)} %copy-done, f32[16,8,1024]{2,1,0:T(8,128)S(1)} %copy-done.1, bf16[512,1024]{1,0:T(8,128)(2,1)} %shard_map.58.local, ...), custom_call_target="tpu_custom_call", output_to_operand_aliasing={{}: (5, {})} | custom-call | flops 1048576 | bytes 262144 | tf_op jit(solution)/shard_map/pallas_call | solution.py:239
  43.9 0.0 collective-permute-done.8.late
  43.9 0.2 collective-permute-start.10
  44.1 1.2 %collective-permute-done.10.late_other = f32[256,128]{1,0:T(8,128)S(1)} collective-permute-done((f32[256,128]{1,0:T(8,128)S(1)}, f32[256,128]{1,0:T(8,128)S(1)}, u32[]{:S(2)}, u32[]{:S(2)}) %collective-permute-start.10) | collective-permute-done | bytes 131104 | tf_op jit(solution)/shard_map/ppermute | solution.py:26
  45.3 0.0 copy-done.2
  45.3 6.7 %shard_map.61 = bf16[1024,1024]{1,0:T(8,128)(2,1)} custom-call(s32[2]{0:T(128)S(1)} %pad_add_fusion.place, bf16[1024,1024]{1,0:T(8,128)(2,1)S(1)} %copy-done, f32[16,8,1024]{2,1,0:T(8,128)S(1)} %copy-done.1, f32[1024,1024]{1,0:T(8,128)S(1)} %shard_map.60.near, f32[9,256,128]{2,1,0:T(8,128)} %bitcast_dynamic-update-slice_fusion.early, ...), custom_call_target="tpu_custom_call" | custom-call | flops 2684354560 | bytes 12582912 | tf_op jit(solution)/shard_map/pallas_call | solution.py:322
  (3 shorter events, 0.1 us)
Async XLA Ops:
  2.4 2.3 %collective-permute-start = (f32[512,128]{1,0:T(8,128)S(1)}, f32[512,128]{1,0:T(8,128)S(1)}, u32[]{:S(2)}, u32[]{:S(2)}) collective-permute-start(f32[512,128]{1,0:T(8,128)S(1)} %shard_map.56), channel_id=1, source_target_pairs={{0,1},{1,0},{2,3},{3,2},{4,5},{5,4},{6,7},{7,6},{8,9},{9,8},{10,11... | collective-permute-start | bytes 786440 | tf_op jit(solution)/shard_map/ppermute | solution.py:26
  4.7 7.3 %collective-permute-start.1 = (f32[256,128]{1,0:T(8,128)S(1)}, f32[256,128]{1,0:T(8,128)S(1)}, u32[]{:S(2)}, u32[]{:S(2)}) collective-permute-start(f32[256,128]{1,0:T(8,128)S(1)} %dynamic-slice_add_fusion), channel_id=1, source_target_pairs={{0,2},{1,3},{2,0},{3,1},{4,6},{5,7},{6,4},{7,5},{8,10},{9,11},{10,... | collective-permute-start | bytes 393224 | tf_op jit(solution)/shard_map/ppermute | solution.py:26
  12.7 6.9 %collective-permute-start.2 = (f32[256,128]{1,0:T(8,128)S(1)}, f32[256,128]{1,0:T(8,128)S(1)}, u32[]{:S(2)}, u32[]{:S(2)}) collective-permute-start(f32[256,128]{1,0:T(8,128)S(1)} %get-tuple-element.34), channel_id=1, source_target_pairs={{0,4},{1,5},{2,6},{3,7},{4,0},{5,1},{6,2},{7,3},{8,12},{9,13},{10,... | collective-permute-start | bytes 393224 | tf_op jit(solution)/shard_map/ppermute | solution.py:26
  14.9 16.1 %copy-start = (bf16[1024,1024]{1,0:T(8,128)(2,1)S(1)}, bf16[1024,1024]{1,0:T(8,128)(2,1)}, u32[]{:S(2)}) copy-start(bf16[1024,1024]{1,0:T(8,128)(2,1)} %queries.8) | copy-start | bytes 6291460
  19.5 11.4 %copy-start.1 = (f32[16,8,1024]{2,1,0:T(8,128)S(1)}, f32[16,8,1024]{2,1,0:T(8,128)}, u32[]{:S(2)}) copy-start(f32[16,8,1024]{2,1,0:T(8,128)} %weights.8) | copy-start | bytes 1572868
  19.6 5.4 %collective-permute-start.3 = (f32[256,128]{1,0:T(8,128)S(1)}, f32[256,128]{1,0:T(8,128)S(1)}, u32[]{:S(2)}, u32[]{:S(2)}) collective-permute-start(f32[256,128]{1,0:T(8,128)S(1)} %add.31), channel_id=1, source_target_pairs={{0,8},{8,0},{16,24},{24,16},{1,9},{9,1},{17,25},{25,17},{2,10},{10... | collective-permute-start | bytes 393224 | tf_op jit(solution)/shard_map/ppermute | solution.py:26
  22.0 7.2 %collective-permute-start.6 = (f32[256,128]{1,0:T(8,128)}, f32[256,128]{1,0:T(8,128)S(1)}, u32[]{:S(2)}, u32[]{:S(2)}) collective-permute-start(f32[256,128]{1,0:T(8,128)} %get-tuple-element.42), channel_id=1, source_target_pairs={{0,2},{1,3},{2,0},{3,1},{4,6},{5,7},{6,4},{7,5},{8,10},{9,11},{10,... | collective-permute-start | bytes 393224 | tf_op jit(solution)/shard_map/ppermute | solution.py:26
  23.2 7.8 %collective-permute-start.7 = (f32[256,128]{1,0:T(8,128)S(1)}, f32[256,128]{1,0:T(8,128)S(1)}, u32[]{:S(2)}, u32[]{:S(2)}) collective-permute-start(f32[256,128]{1,0:T(8,128)S(1)} %collective-permute-done.2.rest_3_), channel_id=1, source_target_pairs={{0,2},{1,3},{2,0},{3,1},{4,6},{5,7},{6,4},{7,5},{8,10},{9,11},{10,... | collective-permute-start | bytes 393224 | tf_op jit(solution)/shard_map/ppermute | solution.py:26
  25.0 8.9 %collective-permute-start.4 = (f32[256,128]{1,0:T(8,128)S(1)}, f32[256,128]{1,0:T(8,128)S(1)}, u32[]{:S(2)}, u32[]{:S(2)}) collective-permute-start(f32[256,128]{1,0:T(8,128)S(1)} %add.32), channel_id=1, source_target_pairs={{0,16},{8,24},{16,0},{24,8},{1,17},{9,25},{17,1},{25,9},{2,18},{10... | collective-permute-start | bytes 393224 | tf_op jit(solution)/shard_map/ppermute | solution.py:26
  27.6 6.3 %collective-permute-start.5 = (f32[256,128]{1,0:T(8,128)S(1)}, f32[256,128]{1,0:T(8,128)S(1)}, u32[]{:S(2)}, u32[]{:S(2)}) collective-permute-start(f32[256,128]{1,0:T(8,128)S(1)} %collective-permute-done.3), channel_id=1, source_target_pairs={{0,2},{1,3},{2,0},{3,1},{4,6},{5,7},{6,4},{7,5},{8,10},{9,11},{10,... | collective-permute-start | bytes 393224 | tf_op jit(solution)/shard_map/ppermute | solution.py:26
  37.9 3.1 %collective-permute-start.9 = (f32[9,256,128]{2,1,0:T(8,128)}, f32[9,256,128]{2,1,0:T(8,128)S(1)}, u32[]{:S(2)}, u32[]{:S(2)}) collective-permute-start(f32[9,256,128]{2,1,0:T(8,128)} %bitcast_dynamic-update-slice_fusion.early), channel_id=1, source_target_pairs={{0,1},{1,0},{2,3},{3,2},{4,5},{5,4},{6,7},{7,6},{8,9},{9,8},{10,11... | collective-permute-start | bytes 3538952 | tf_op jit(solution)/shard_map/ppermute | solution.py:26
  37.9 6.0 %collective-permute-start.8 = (f32[256,128]{1,0:T(8,128)S(1)}, f32[256,128]{1,0:T(8,128)S(1)}, u32[]{:S(2)}, u32[]{:S(2)}) collective-permute-start(f32[256,128]{1,0:T(8,128)S(1)} %collective-permute-done.4), channel_id=1, source_target_pairs={{0,2},{1,3},{2,0},{3,1},{4,6},{5,7},{6,4},{7,5},{8,10},{9,11},{10,... | collective-permute-start | bytes 393224 | tf_op jit(solution)/shard_map/ppermute | solution.py:26
  40.9 4.4 %copy-start.2 = (bf16[1024,1024]{1,0:T(8,128)(2,1)S(1)}, bf16[1024,1024]{1,0:T(8,128)(2,1)}, u32[]{:S(2)}) copy-start(bf16[1024,1024]{1,0:T(8,128)(2,1)} %out_weight.1) | copy-start | bytes 6291460
  43.9 1.4 %collective-permute-start.10 = (f32[256,128]{1,0:T(8,128)S(1)}, f32[256,128]{1,0:T(8,128)S(1)}, u32[]{:S(2)}, u32[]{:S(2)}) collective-permute-start(f32[256,128]{1,0:T(8,128)S(1)} %collective-permute-done.8.late), channel_id=1, source_target_pairs={{0,1},{1,0},{2,3},{3,2},{4,5},{5,4},{6,7},{7,6},{8,9},{9,8},{10,11... | collective-permute-start | bytes 393224 | tf_op jit(solution)/shard_map/ppermute | solution.py:26

commit v9 on v8

--- a/solution.py
+++ b/solution.py
@@ -44,10 +44,6 @@
     return tuple(pltpu.with_memory_space_constraint(part, pltpu.HBM) for part in parts)
 
 
-def inside(*parts):
-    return tuple(pltpu.with_memory_space_constraint(part, pltpu.VMEM) for part in parts)
-
-
 def product(left, right):
     return jnp.dot(left, right, preferred_element_type=F32)
 
@@ -67,24 +63,35 @@
 
 
 def state_kernel(place, keys, values, state):
-    both = product(turned(values[...]), keys[...])
-    for low in range(0, keys.shape[1], HEAD):
-        part = slice(low, low + HEAD)
-        state[part, :] = both[part, part]
+    step = pl.program_id(0)
+    found = []
+    for low in range(0, keys.shape[1], 2 * HEAD):
+        pair = slice(low, low + 2 * HEAD)
+        both = product(turned(values[:, pair]), keys[:, pair])
+        found += [both[:HEAD, :HEAD], both[HEAD:, HEAD:]]
+
+    @pl.when(step == 0)
+    def _():
+        for at, part in enumerate(found):
+            state[at * HEAD : (at + 1) * HEAD, :] = part
+
+    @pl.when(step > 0)
+    def _():
+        for at, part in enumerate(found):
+            state[at * HEAD : (at + 1) * HEAD, :] += part
 
 
 def block_state(place, share, keys, values):
     tokens, width = keys.shape
-    step = 2 * HEAD
-    steps = width // share // step
-    column = pl.BlockSpec((tokens, step), lambda pair, place: (0, place[0] * steps + pair))
+    rows = min(tokens, share // 2 * CHUNK)
+    band = pl.BlockSpec((rows, width // share), lambda step, place: (step, place[0]))
     return pl.pallas_call(
         state_kernel,
         grid_spec=pltpu.PrefetchScalarGridSpec(
             num_scalar_prefetch=1,
-            grid=(steps,),
-            in_specs=[column, column],
-            out_specs=pl.BlockSpec((step, HEAD), lambda pair, place: (pair, 0)),
+            grid=(tokens // rows,),
+            in_specs=[band, band],
+            out_specs=pl.BlockSpec((width // share, HEAD), lambda step, place: (0, 0)),
         ),
         out_shape=pltpu.VMEM((width // share, HEAD), F32),
         cost_estimate=cost(2 * tokens * width * HEAD // share, 5 * MIB // share),
@@ -264,7 +271,7 @@
         input_output_aliases={5: 0} if into else {},
         cost_estimate=cost(tokens * width, MIB // 4),
         compiler_params=params(16),
-    )(half.reshape(1), place, *inside(queries, level_weights), *outside(local), *into, *held)
+    )(half.reshape(1), place, *outside(queries, level_weights, local), *into, *held)
 
 
 def far_kernel(first_level, place, queries, weights, near, early, early_other, late, late_other, out_weight,

time: 52.3 us -> 47.9 us (0.916)
  local copies, waits for them, and re-layouts: 5.94 us -> 0.11 us
  Pallas kernels: 26.1 us -> 28 us
  waiting for transfers between devices: 5.96 us -> 6.63 us
  other arithmetic: 0.8 us -> 0.15 us
    unnamed x14, local copies, waits for them, and re-layouts: 5.29 us -> 0.1 us
    pallas_call x2, Pallas kernels: 4.16 us -> 5.81 us  [block_state(): pl.pallas_call(state_kernel, grid_spec=pltpu.PrefetchScalarGridSpec(num_s...]
    pallas_call x2, Pallas kernels: 5.89 us -> 6.68 us  [near_part(): pl.pallas_call(functools.partial(near_kernel, len(into)), grid_spec=pltpu...]
    ppermute x11, waiting for transfers between devices: 5.96 us -> 6.63 us  [swap(): lax.ppermute(block, axis, [(place, place ^ stride) for place in range(cou...]
    add x1, other arithmetic: 0.68 us -> 0.02 us  [body(): running = own + buckets[0]]
    another operation x1, local copies, waits for them, and re-layouts: 0.65 us -> 0.01 us  [body(): mine = jnp.stack([part for pair in pairs for part in pair] + far[-1:])]
  transfers between devices with their start and end apart: 11 -> 11, of which waited for: 4 -> 5; matrix products, arithmetic and copies ran while one was open for 4% -> 0% of each run, Pallas kernels for 33% -> 37%
where the time goes in v9:
time: 47.9 us; the launch traced here: 47.7 us
  Pallas kernels  28 us (58%)
  starting transfers between devices  12.6 us (26%)
  waiting for transfers between devices  6.63 us (14%)
    ppermute x11, starting transfers between devices, swap(): lax.ppermute(block, axis, [(place, place ^ stride) for place in range(cou...  12.6 us
    pallas_call x2, Pallas kernels, local_part(): pl.pallas_call(local_kernel, grid_spec=pltpu.PrefetchScalarGridSpec(num_s...  9.23 us
    pallas_call x2, Pallas kernels, near_part(): pl.pallas_call(functools.partial(near_kernel, len(into)), grid_spec=pltpu...  6.68 us
    ppermute x11, waiting for transfers between devices, swap(): lax.ppermute(block, axis, [(place, place ^ stride) for place in range(cou...  6.63 us
    pallas_call x1, Pallas kernels, far_part(): pl.pallas_call(functools.partial(far_kernel, first_level), grid=(tokens /...  6.28 us
    pallas_call x2, Pallas kernels, block_state(): pl.pallas_call(state_kernel, grid_spec=pltpu.PrefetchScalarGridSpec(num_s...  5.81 us
  transfers between devices with their start and end apart: 11, of which 5 were waited for; matrix products, arithmetic and copies ran while one was open for 0% of the time, Pallas kernels for 37%

profile of v9, /device:TPU:0, one launch (start us, length us, event | category | flops | bytes accessed | tf_op | source)
XLA Modules:
  0.0 47.7 jit_solution(14035776477455315808)
XLA Ops:
  0.0 3.9 %shard_map.56 = f32[512,128]{1,0:T(8,128)S(1)} custom-call(s32[1]{0:T(128)} %bitcast.3.place.half, bf16[1024,1024]{1,0:T(8,128)(2,1)} %keys.5, bf16[1024,1024]{1,0:T(8,128)(2,1)} %values.5), custom_call_target="tpu_custom_call" | custom-call | flops 134217728 | bytes 2621440 | tf_op jit(solution)/shard_map/pallas_call | solution.py:88
  3.9 0.5 %collective-permute-start = (f32[512,128]{1,0:T(8,128)S(1)}, f32[512,128]{1,0:T(8,128)S(1)}, u32[]{:S(2)}, u32[]{:S(2)}) collective-permute-start(f32[512,128]{1,0:T(8,128)S(1)} %shard_map.56), channel_id=1, source_target_pairs={{0,1},{1,0},{2,3},{3,2},{4,5},{5,4},{6,7},{7,6},{8,9},{9,8},{10,11... | collective-permute-start | bytes 786440 | tf_op jit(solution)/shard_map/ppermute | solution.py:26
  4.4 2.0 %shard_map.57 = f32[256,128]{1,0:T(8,128)S(1)} custom-call(s32[1]{0:T(128)} %bitcast.4.place, bf16[1024,1024]{1,0:T(8,128)(2,1)} %keys.5, bf16[1024,1024]{1,0:T(8,128)(2,1)} %values.5), custom_call_target="tpu_custom_call" | custom-call | flops 67108864 | bytes 1310720 | tf_op jit(solution)/shard_map/pallas_call | solution.py:88
  6.4 0.0 collective-permute-done.rest_0_
  6.4 2.6 %collective-permute-start.1 = (f32[256,128]{1,0:T(8,128)S(1)}, f32[256,128]{1,0:T(8,128)S(1)}, u32[]{:S(2)}, u32[]{:S(2)}) collective-permute-start(f32[256,128]{1,0:T(8,128)S(1)} %dynamic-slice_add_fusion), channel_id=1, source_target_pairs={{0,2},{1,3},{2,0},{3,1},{4,6},{5,7},{6,4},{7,5},{8,10},{9,11},{10,... | collective-permute-start | bytes 393224 | tf_op jit(solution)/shard_map/ppermute | solution.py:26
  9.0 4.7 %shard_map.55 = (bf16[512,1024]{1,0:T(8,128)(2,1)}, f32[512,128]{1,0:T(8,128)S(1)}) custom-call(s32[1]{0:T(128)} %bitcast.2.half, bf16[1024,1024]{1,0:T(8,128)(2,1)} %queries.8, bf16[1024,1024]{1,0:T(8,128)(2,1)} %keys.5, bf16[1024,1024]{1,0:T(8,128)(2,1)} %values.5, f32[16,8,1024]{2,1,0:T(8,128)} %weights.8), custom_call_target="tpu_custom_call" | custom-call | flops 1048576 | bytes 262144 | tf_op jit(solution)/shard_map/pallas_call | solution.py:183
  13.6 0.0 collective-permute-done.1.rest_1_
  13.7 1.6 %collective-permute-start.2 = (f32[256,128]{1,0:T(8,128)S(1)}, f32[256,128]{1,0:T(8,128)S(1)}, u32[]{:S(2)}, u32[]{:S(2)}) collective-permute-start(f32[256,128]{1,0:T(8,128)S(1)} %get-tuple-element.34), channel_id=1, source_target_pairs={{0,4},{1,5},{2,6},{3,7},{4,0},{5,1},{6,2},{7,3},{8,12},{9,13},{10,... | collective-permute-start | bytes 393224 | tf_op jit(solution)/shard_map/ppermute | solution.py:26
  15.3 4.6 %shard_map.58.local = bf16[512,1024]{1,0:T(8,128)(2,1)} custom-call(s32[1]{0:T(128)} %bitcast.3.place.half, bf16[1024,1024]{1,0:T(8,128)(2,1)} %queries.8, bf16[1024,1024]{1,0:T(8,128)(2,1)} %keys.5, bf16[1024,1024]{1,0:T(8,128)(2,1)} %values.5, f32[16,8,1024]{2,1,0:T(8,128)} %weights.8), custom_call_target="tpu_custom_call" | custom-call | flops 1048576 | bytes 262144 | tf_op jit(solution)/shard_map/pallas_call | solution.py:183
  19.8 0.0 collective-permute-done.2.rest_3_
  19.9 1.6 %collective-permute-start.3 = (f32[256,128]{1,0:T(8,128)S(1)}, f32[256,128]{1,0:T(8,128)S(1)}, u32[]{:S(2)}, u32[]{:S(2)}) collective-permute-start(f32[256,128]{1,0:T(8,128)S(1)} %add.31), channel_id=1, source_target_pairs={{0,8},{8,0},{16,24},{24,16},{1,9},{9,1},{17,25},{25,17},{2,10},{10... | collective-permute-start | bytes 393224 | tf_op jit(solution)/shard_map/ppermute | solution.py:26
  21.5 0.1 pad_add_fusion.place
  21.6 1.2 %collective-permute-start.6 = (f32[256,128]{1,0:T(8,128)S(1)}, f32[256,128]{1,0:T(8,128)S(1)}, u32[]{:S(2)}, u32[]{:S(2)}) collective-permute-start(f32[256,128]{1,0:T(8,128)S(1)} %get-tuple-element.42), channel_id=1, source_target_pairs={{0,2},{1,3},{2,0},{3,1},{4,6},{5,7},{6,4},{7,5},{8,10},{9,11},{10,... | collective-permute-start | bytes 393224 | tf_op jit(solution)/shard_map/ppermute | solution.py:26
  22.8 0.8 %collective-permute-start.7 = (f32[256,128]{1,0:T(8,128)S(1)}, f32[256,128]{1,0:T(8,128)S(1)}, u32[]{:S(2)}, u32[]{:S(2)}) collective-permute-start(f32[256,128]{1,0:T(8,128)S(1)} %collective-permute-done.2.rest_3_), channel_id=1, source_target_pairs={{0,2},{1,3},{2,0},{3,1},{4,6},{5,7},{6,4},{7,5},{8,10},{9,11},{10,... | collective-permute-start | bytes 393224 | tf_op jit(solution)/shard_map/ppermute | solution.py:26
  23.6 1.6 %collective-permute-done.3 = f32[256,128]{1,0:T(8,128)S(1)} collective-permute-done((f32[256,128]{1,0:T(8,128)S(1)}, f32[256,128]{1,0:T(8,128)S(1)}, u32[]{:S(2)}, u32[]{:S(2)}) %collective-permute-start.3) | collective-permute-done | bytes 131104 | tf_op jit(solution)/shard_map/ppermute | solution.py:26
  25.3 2.7 %collective-permute-start.4 = (f32[256,128]{1,0:T(8,128)S(1)}, f32[256,128]{1,0:T(8,128)S(1)}, u32[]{:S(2)}, u32[]{:S(2)}) collective-permute-start(f32[256,128]{1,0:T(8,128)S(1)} %add.32), channel_id=1, source_target_pairs={{0,16},{8,24},{16,0},{24,8},{1,17},{9,25},{17,1},{25,9},{2,18},{10... | collective-permute-start | bytes 393224 | tf_op jit(solution)/shard_map/ppermute | solution.py:26
  27.9 0.9 %collective-permute-start.5 = (f32[256,128]{1,0:T(8,128)S(1)}, f32[256,128]{1,0:T(8,128)S(1)}, u32[]{:S(2)}, u32[]{:S(2)}) collective-permute-start(f32[256,128]{1,0:T(8,128)S(1)} %collective-permute-done.3), channel_id=1, source_target_pairs={{0,2},{1,3},{2,0},{3,1},{4,6},{5,7},{6,4},{7,5},{8,10},{9,11},{10,... | collective-permute-start | bytes 393224 | tf_op jit(solution)/shard_map/ppermute | solution.py:26
  28.8 0.0 collective-permute-done.6.rest_2_
  28.8 0.7 %collective-permute-done.7.rest_4_ = f32[256,128]{1,0:T(8,128)S(1)} collective-permute-done((f32[256,128]{1,0:T(8,128)S(1)}, f32[256,128]{1,0:T(8,128)S(1)}, u32[]{:S(2)}, u32[]{:S(2)}) %collective-permute-start.7) | collective-permute-done | bytes 131104 | tf_op jit(solution)/shard_map/ppermute | solution.py:26
  29.5 3.2 %shard_map.59.rest_0_ = f32[1024,1024]{1,0:T(8,128)S(1)} custom-call(s32[1]{0:T(128)} %bitcast.2.half, s32[2]{0:T(128)S(1)} %pad_add_fusion.place, bf16[1024,1024]{1,0:T(8,128)(2,1)} %queries.8, f32[16,8,1024]{2,1,0:T(8,128)} %weights.8, bf16[512,1024]{1,0:T(8,128)(2,1)} %get-tuple-element.44.local, f32[512,128]{1,0:T(8,128)S(1)} %collective-permute-done.rest_0_, ...), custom_call_target="tpu_custom_call" | custom-call | flops 1048576 | bytes 262144 | tf_op jit(solution)/shard_map/pallas_call | solution.py:246
  32.8 0.7 %collective-permute-done.4 = f32[256,128]{1,0:T(8,128)S(1)} collective-permute-done((f32[256,128]{1,0:T(8,128)S(1)}, f32[256,128]{1,0:T(8,128)S(1)}, u32[]{:S(2)}, u32[]{:S(2)}) %collective-permute-start.4) | collective-permute-done | bytes 131104 | tf_op jit(solution)/shard_map/ppermute | solution.py:26
  33.5 0.0 collective-permute-done.5
  33.6 0.0 copy-start.1
  33.6 0.1 collective-permute-start.9
  33.7 0.5 %collective-permute-start.8 = (f32[256,128]{1,0:T(8,128)S(1)}, f32[256,128]{1,0:T(8,128)S(1)}, u32[]{:S(2)}, u32[]{:S(2)}) collective-permute-start(f32[256,128]{1,0:T(8,128)S(1)} %collective-permute-done.4), channel_id=1, source_target_pairs={{0,2},{1,3},{2,0},{3,1},{4,6},{5,7},{6,4},{7,5},{8,10},{9,11},{10,... | collective-permute-start | bytes 393224 | tf_op jit(solution)/shard_map/ppermute | solution.py:26
  34.2 2.3 %collective-permute-done.9.rest_1_.early_other = f32[9,256,128]{2,1,0:T(8,128)S(1)} collective-permute-done((f32[9,256,128]{2,1,0:T(8,128)S(1)}, f32[9,256,128]{2,1,0:T(8,128)S(1)}, u32[]{:S(2)}, u32[]{:S(2)}) %collective-permute-start.9) | collective-permute-done | bytes 1179680 | tf_op jit(solution)/shard_map/ppermute | solution.py:26
  36.5 0.0 copy-start
  36.5 0.0 copy-start.2
  36.5 3.5 %shard_map.60.near = f32[1024,1024]{1,0:T(8,128)S(1)} custom-call(s32[1]{0:T(128)} %bitcast.3.place.half, s32[2]{0:T(128)S(1)} %pad_add_fusion.place, bf16[1024,1024]{1,0:T(8,128)(2,1)} %queries.8, f32[16,8,1024]{2,1,0:T(8,128)} %weights.8, bf16[512,1024]{1,0:T(8,128)(2,1)} %shard_map.58.local, ...), custom_call_target="tpu_custom_call", output_to_operand_aliasing={{}: (5, {})} | custom-call | flops 1048576 | bytes 262144 | tf_op jit(solution)/shard_map/pallas_call | solution.py:246
  40.0 0.0 collective-permute-done.8.late
  40.0 0.2 collective-permute-start.10
  40.2 1.2 %collective-permute-done.10.late_other = f32[256,128]{1,0:T(8,128)S(1)} collective-permute-done((f32[256,128]{1,0:T(8,128)S(1)}, f32[256,128]{1,0:T(8,128)S(1)}, u32[]{:S(2)}, u32[]{:S(2)}) %collective-permute-start.10) | collective-permute-done | bytes 131104 | tf_op jit(solution)/shard_map/ppermute | solution.py:26
  41.4 0.0 copy-done.1
  41.4 0.0 copy-done
  41.4 0.0 copy-done.2
  41.4 6.3 %shard_map.61 = bf16[1024,1024]{1,0:T(8,128)(2,1)} custom-call(s32[2]{0:T(128)S(1)} %pad_add_fusion.place, bf16[1024,1024]{1,0:T(8,128)(2,1)S(1)} %copy-done, f32[16,8,1024]{2,1,0:T(8,128)S(1)} %copy-done.1, f32[1024,1024]{1,0:T(8,128)S(1)} %shard_map.60.near, f32[9,256,128]{2,1,0:T(8,128)S(1)} %bitcast_dynamic-update-slice_fusion.early, ...), custom_call_target="tpu_custom_call" | custom-call | flops 2684354560 | bytes 12582912 | tf_op jit(solution)/shard_map/pallas_call | solution.py:329
  (13 shorter events, 0.2 us)
Async XLA Ops:
  3.9 2.5 %collective-permute-start = (f32[512,128]{1,0:T(8,128)S(1)}, f32[512,128]{1,0:T(8,128)S(1)}, u32[]{:S(2)}, u32[]{:S(2)}) collective-permute-start(f32[512,128]{1,0:T(8,128)S(1)} %shard_map.56), channel_id=1, source_target_pairs={{0,1},{1,0},{2,3},{3,2},{4,5},{5,4},{6,7},{7,6},{8,9},{9,8},{10,11... | collective-permute-start | bytes 786440 | tf_op jit(solution)/shard_map/ppermute | solution.py:26
  6.4 7.3 %collective-permute-start.1 = (f32[256,128]{1,0:T(8,128)S(1)}, f32[256,128]{1,0:T(8,128)S(1)}, u32[]{:S(2)}, u32[]{:S(2)}) collective-permute-start(f32[256,128]{1,0:T(8,128)S(1)} %dynamic-slice_add_fusion), channel_id=1, source_target_pairs={{0,2},{1,3},{2,0},{3,1},{4,6},{5,7},{6,4},{7,5},{8,10},{9,11},{10,... | collective-permute-start | bytes 393224 | tf_op jit(solution)/shard_map/ppermute | solution.py:26
  13.7 6.2 %collective-permute-start.2 = (f32[256,128]{1,0:T(8,128)S(1)}, f32[256,128]{1,0:T(8,128)S(1)}, u32[]{:S(2)}, u32[]{:S(2)}) collective-permute-start(f32[256,128]{1,0:T(8,128)S(1)} %get-tuple-element.34), channel_id=1, source_target_pairs={{0,4},{1,5},{2,6},{3,7},{4,0},{5,1},{6,2},{7,3},{8,12},{9,13},{10,... | collective-permute-start | bytes 393224 | tf_op jit(solution)/shard_map/ppermute | solution.py:26
  19.9 5.4 %collective-permute-start.3 = (f32[256,128]{1,0:T(8,128)S(1)}, f32[256,128]{1,0:T(8,128)S(1)}, u32[]{:S(2)}, u32[]{:S(2)}) collective-permute-start(f32[256,128]{1,0:T(8,128)S(1)} %add.31), channel_id=1, source_target_pairs={{0,8},{8,0},{16,24},{24,16},{1,9},{9,1},{17,25},{25,17},{2,10},{10... | collective-permute-start | bytes 393224 | tf_op jit(solution)/shard_map/ppermute | solution.py:26
  21.6 7.2 %collective-permute-start.6 = (f32[256,128]{1,0:T(8,128)S(1)}, f32[256,128]{1,0:T(8,128)S(1)}, u32[]{:S(2)}, u32[]{:S(2)}) collective-permute-start(f32[256,128]{1,0:T(8,128)S(1)} %get-tuple-element.42), channel_id=1, source_target_pairs={{0,2},{1,3},{2,0},{3,1},{4,6},{5,7},{6,4},{7,5},{8,10},{9,11},{10,... | collective-permute-start | bytes 393224 | tf_op jit(solution)/shard_map/ppermute | solution.py:26
  22.8 6.7 %collective-permute-start.7 = (f32[256,128]{1,0:T(8,128)S(1)}, f32[256,128]{1,0:T(8,128)S(1)}, u32[]{:S(2)}, u32[]{:S(2)}) collective-permute-start(f32[256,128]{1,0:T(8,128)S(1)} %collective-permute-done.2.rest_3_), channel_id=1, source_target_pairs={{0,2},{1,3},{2,0},{3,1},{4,6},{5,7},{6,4},{7,5},{8,10},{9,11},{10,... | collective-permute-start | bytes 393224 | tf_op jit(solution)/shard_map/ppermute | solution.py:26
  25.3 8.2 %collective-permute-start.4 = (f32[256,128]{1,0:T(8,128)S(1)}, f32[256,128]{1,0:T(8,128)S(1)}, u32[]{:S(2)}, u32[]{:S(2)}) collective-permute-start(f32[256,128]{1,0:T(8,128)S(1)} %add.32), channel_id=1, source_target_pairs={{0,16},{8,24},{16,0},{24,8},{1,17},{9,25},{17,1},{25,9},{2,18},{10... | collective-permute-start | bytes 393224 | tf_op jit(solution)/shard_map/ppermute | solution.py:26
  27.9 5.6 %collective-permute-start.5 = (f32[256,128]{1,0:T(8,128)S(1)}, f32[256,128]{1,0:T(8,128)S(1)}, u32[]{:S(2)}, u32[]{:S(2)}) collective-permute-start(f32[256,128]{1,0:T(8,128)S(1)} %collective-permute-done.3), channel_id=1, source_target_pairs={{0,2},{1,3},{2,0},{3,1},{4,6},{5,7},{6,4},{7,5},{8,10},{9,11},{10,... | collective-permute-start | bytes 393224 | tf_op jit(solution)/shard_map/ppermute | solution.py:26
  33.6 7.8 %copy-start.1 = (f32[16,8,1024]{2,1,0:T(8,128)S(1)}, f32[16,8,1024]{2,1,0:T(8,128)}, u32[]{:S(2)}) copy-start(f32[16,8,1024]{2,1,0:T(8,128)} %weights.8) | copy-start | bytes 1572868
  33.6 2.9 %collective-permute-start.9 = (f32[9,256,128]{2,1,0:T(8,128)S(1)}, f32[9,256,128]{2,1,0:T(8,128)S(1)}, u32[]{:S(2)}, u32[]{:S(2)}) collective-permute-start(f32[9,256,128]{2,1,0:T(8,128)S(1)} %bitcast_dynamic-update-slice_fusion.early), channel_id=1, source_target_pairs={{0,1},{1,0},{2,3},{3,2},{4,5},{5,4},{6,7},{7,6},{8,9},{9,8},{10,11... | collective-permute-start | bytes 3538952 | tf_op jit(solution)/shard_map/ppermute | solution.py:26
  33.7 6.3 %collective-permute-start.8 = (f32[256,128]{1,0:T(8,128)S(1)}, f32[256,128]{1,0:T(8,128)S(1)}, u32[]{:S(2)}, u32[]{:S(2)}) collective-permute-start(f32[256,128]{1,0:T(8,128)S(1)} %collective-permute-done.4), channel_id=1, source_target_pairs={{0,2},{1,3},{2,0},{3,1},{4,6},{5,7},{6,4},{7,5},{8,10},{9,11},{10,... | collective-permute-start | bytes 393224 | tf_op jit(solution)/shard_map/ppermute | solution.py:26
  36.5 4.9 %copy-start = (bf16[1024,1024]{1,0:T(8,128)(2,1)S(1)}, bf16[1024,1024]{1,0:T(8,128)(2,1)}, u32[]{:S(2)}) copy-start(bf16[1024,1024]{1,0:T(8,128)(2,1)} %queries.8) | copy-start | bytes 6291460
  36.5 4.9 %copy-start.2 = (bf16[1024,1024]{1,0:T(8,128)(2,1)S(1)}, bf16[1024,1024]{1,0:T(8,128)(2,1)}, u32[]{:S(2)}) copy-start(bf16[1024,1024]{1,0:T(8,128)(2,1)} %out_weight.1) | copy-start | bytes 6291460
  40.0 1.4 %collective-permute-start.10 = (f32[256,128]{1,0:T(8,128)S(1)}, f32[256,128]{1,0:T(8,128)S(1)}, u32[]{:S(2)}, u32[]{:S(2)}) collective-permute-start(f32[256,128]{1,0:T(8,128)S(1)} %collective-permute-done.8.late), channel_id=1, source_target_pairs={{0,1},{1,0},{2,3},{3,2},{4,5},{5,4},{6,7},{7,6},{8,9},{9,8},{10,11... | collective-permute-start | bytes 393224 | tf_op jit(solution)/shard_map/ppermute | solution.py:26

commit v10 on v8

--- a/solution.py
+++ b/solution.py
@@ -42,10 +42,6 @@
 
 def outside(*parts):
     return tuple(pltpu.with_memory_space_constraint(part, pltpu.HBM) for part in parts)
-
-
-def inside(*parts):
-    return tuple(pltpu.with_memory_space_constraint(part, pltpu.VMEM) for part in parts)
 
 
 def product(left, right):
@@ -264,7 +260,7 @@
         input_output_aliases={5: 0} if into else {},
         cost_estimate=cost(tokens * width, MIB // 4),
         compiler_params=params(16),
-    )(half.reshape(1), place, *inside(queries, level_weights), *outside(local), *into, *held)
+    )(half.reshape(1), place, *outside(queries, level_weights, local), *into, *held)
 
 
 def far_kernel(first_level, place, queries, weights, near, early, early_other, late, late_other, out_weight,
@@ -399,15 +395,16 @@
         near_mine = own_near()
         far[-1], others, near_mine = tie((far[-1], others, near_mine))
     late = swap(far[-1], "inner", 2)
-    pairs = [(keep_ours, keep_theirs), *((bucket, others[at]) for at, bucket in enumerate(buckets)), *zip(far, beside)]
-    mine = jnp.stack([part for pair in pairs for part in pair] + far[-1:])
-    other = swap(mine, "inner", 1)
+    pairs = [(keep_ours, keep_theirs), *((bucket, others[at]) for at, bucket in enumerate(buckets))]
+    other = swap(jnp.stack([part for pair in pairs for part in pair]), "inner", 1)
+    early = jnp.stack([part for pair in zip(far, beside) for part in pair] + far[-1:])
+    early_other = swap(early, "inner", 1)
     near = near_part(1 - core, place, inner_bits, queries, level_weights, local[1], near_mine, other)
-    late, near = tie((late, near))
+    late, near, early_other = tie((late, near, early_other))
     late_other = swap(late, "inner", 1)
     first_level = LOCAL_BITS + 1 + inner_bits
     return far_part(
-        first_level, outer_bits, place, queries, level_weights, near, mine, other, late, late_other, out_weight
+        first_level, outer_bits, place, queries, level_weights, near, early, early_other, late, late_other, out_weight
     )
 
 

time: 52.3 us -> 46 us (0.88)
  local copies, waits for them, and re-layouts: 5.94 us -> 0.08 us
  other arithmetic: 0.8 us -> 0.19 us
    unnamed x14 -> x11, local copies, waits for them, and re-layouts: 5.29 us -> 0.07 us
    add x1, other arithmetic: 0.68 us -> 0.02 us  [body(): running = own + buckets[0]]
    another operation x1, local copies, waits for them, and re-layouts: 0.65 us -> 0.01 us  [body(): jnp.stack([part for pair in pairs for part in pair])]
    ppermute x11 -> x12, waiting for transfers between devices: 5.96 us -> 6.33 us  [swap(): lax.ppermute(block, axis, [(place, place ^ stride) for place in range(cou...]
    ppermute x11 -> x12, starting transfers between devices: 13.1 us -> 12.9 us  [swap(): lax.ppermute(block, axis, [(place, place ^ stride) for place in range(cou...]
  transfers between devices with their start and end apart: 11 -> 12, of which waited for: 4 -> 6; matrix products, arithmetic and copies ran while one was open for 4% -> 0% of each run, Pallas kernels for 33% -> 38%
where the time goes in v10:
time: 46 us; the launch traced here: 45.7 us
  Pallas kernels  26.1 us (57%)
  starting transfers between devices  12.9 us (28%)
  waiting for transfers between devices  6.33 us (14%)
    ppermute x12, starting transfers between devices, swap(): lax.ppermute(block, axis, [(place, place ^ stride) for place in range(cou...  12.9 us
    pallas_call x2, Pallas kernels, local_part(): pl.pallas_call(local_kernel, grid_spec=pltpu.PrefetchScalarGridSpec(num_s...  9.23 us
    pallas_call x2, Pallas kernels, near_part(): pl.pallas_call(functools.partial(near_kernel, len(into)), grid_spec=pltpu...  6.41 us
    ppermute x12, waiting for transfers between devices, swap(): lax.ppermute(block, axis, [(place, place ^ stride) for place in range(cou...  6.33 us
    pallas_call x1, Pallas kernels, far_part(): pl.pallas_call(functools.partial(far_kernel, first_level), grid=(tokens /...  6.27 us
    pallas_call x2, Pallas kernels, block_state(): pl.pallas_call(state_kernel, grid_spec=pltpu.PrefetchScalarGridSpec(num_s...  4.16 us
  transfers between devices with their start and end apart: 12, of which 6 were waited for; matrix products, arithmetic and copies ran while one was open for 0% of the time, Pallas kernels for 38%

profile of v10, /device:TPU:0, one launch (start us, length us, event | category | flops | bytes accessed | tf_op | source)
XLA Modules:
  0.0 45.7 jit_solution(16548177987926990822)
XLA Ops:
  0.0 2.4 %shard_map.56 = f32[512,128]{1,0:T(8,128)S(1)} custom-call(s32[1]{0:T(128)} %bitcast.3.place.half, bf16[1024,1024]{1,0:T(8,128)(2,1)} %keys.5, bf16[1024,1024]{1,0:T(8,128)(2,1)} %values.5), custom_call_target="tpu_custom_call" | custom-call | flops 134217728 | bytes 2621440 | tf_op jit(solution)/shard_map/pallas_call | solution.py:77
  2.4 0.5 %collective-permute-start = (f32[512,128]{1,0:T(8,128)S(1)}, f32[512,128]{1,0:T(8,128)S(1)}, u32[]{:S(2)}, u32[]{:S(2)}) collective-permute-start(f32[512,128]{1,0:T(8,128)S(1)} %shard_map.56), channel_id=1, source_target_pairs={{0,1},{1,0},{2,3},{3,2},{4,5},{5,4},{6,7},{7,6},{8,9},{9,8},{10,11... | collective-permute-start | bytes 786440 | tf_op jit(solution)/shard_map/ppermute | solution.py:26
  2.9 1.8 %shard_map.57 = f32[256,128]{1,0:T(8,128)S(1)} custom-call(s32[1]{0:T(128)} %bitcast.4.place, bf16[1024,1024]{1,0:T(8,128)(2,1)} %keys.5, bf16[1024,1024]{1,0:T(8,128)(2,1)} %values.5), custom_call_target="tpu_custom_call" | custom-call | flops 67108864 | bytes 1310720 | tf_op jit(solution)/shard_map/pallas_call | solution.py:77
  4.7 0.0 collective-permute-done.rest_0_
  4.7 2.6 %collective-permute-start.1 = (f32[256,128]{1,0:T(8,128)S(1)}, f32[256,128]{1,0:T(8,128)S(1)}, u32[]{:S(2)}, u32[]{:S(2)}) collective-permute-start(f32[256,128]{1,0:T(8,128)S(1)} %dynamic-slice_add_fusion), channel_id=1, source_target_pairs={{0,2},{1,3},{2,0},{3,1},{4,6},{5,7},{6,4},{7,5},{8,10},{9,11},{10,... | collective-permute-start | bytes 393224 | tf_op jit(solution)/shard_map/ppermute | solution.py:26
  7.3 4.7 %shard_map.55 = (bf16[512,1024]{1,0:T(8,128)(2,1)}, f32[512,128]{1,0:T(8,128)S(1)}) custom-call(s32[1]{0:T(128)} %bitcast.2.half, bf16[1024,1024]{1,0:T(8,128)(2,1)} %queries.8, bf16[1024,1024]{1,0:T(8,128)(2,1)} %keys.5, bf16[1024,1024]{1,0:T(8,128)(2,1)} %values.5, f32[16,8,1024]{2,1,0:T(8,128)} %weights.8), custom_call_target="tpu_custom_call" | custom-call | flops 1048576 | bytes 262144 | tf_op jit(solution)/shard_map/pallas_call | solution.py:172
  12.0 0.0 collective-permute-done.1.rest_1_
  12.0 1.6 %collective-permute-start.2 = (f32[256,128]{1,0:T(8,128)S(1)}, f32[256,128]{1,0:T(8,128)S(1)}, u32[]{:S(2)}, u32[]{:S(2)}) collective-permute-start(f32[256,128]{1,0:T(8,128)S(1)} %get-tuple-element.35), channel_id=1, source_target_pairs={{0,4},{1,5},{2,6},{3,7},{4,0},{5,1},{6,2},{7,3},{8,12},{9,13},{10,... | collective-permute-start | bytes 393224 | tf_op jit(solution)/shard_map/ppermute | solution.py:26
  13.6 4.6 %shard_map.58.local = bf16[512,1024]{1,0:T(8,128)(2,1)} custom-call(s32[1]{0:T(128)} %bitcast.3.place.half, bf16[1024,1024]{1,0:T(8,128)(2,1)} %queries.8, bf16[1024,1024]{1,0:T(8,128)(2,1)} %keys.5, bf16[1024,1024]{1,0:T(8,128)(2,1)} %values.5, f32[16,8,1024]{2,1,0:T(8,128)} %weights.8), custom_call_target="tpu_custom_call" | custom-call | flops 1048576 | bytes 262144 | tf_op jit(solution)/shard_map/pallas_call | solution.py:172
  18.2 0.0 collective-permute-done.2.rest_3_
  18.2 1.6 %collective-permute-start.3 = (f32[256,128]{1,0:T(8,128)S(1)}, f32[256,128]{1,0:T(8,128)S(1)}, u32[]{:S(2)}, u32[]{:S(2)}) collective-permute-start(f32[256,128]{1,0:T(8,128)S(1)} %add.31), channel_id=1, source_target_pairs={{0,8},{8,0},{16,24},{24,16},{1,9},{9,1},{17,25},{25,17},{2,10},{10... | collective-permute-start | bytes 393224 | tf_op jit(solution)/shard_map/ppermute | solution.py:26
  19.9 0.1 pad_add_fusion.place
  19.9 1.2 %collective-permute-start.6 = (f32[256,128]{1,0:T(8,128)S(1)}, f32[256,128]{1,0:T(8,128)S(1)}, u32[]{:S(2)}, u32[]{:S(2)}) collective-permute-start(f32[256,128]{1,0:T(8,128)S(1)} %get-tuple-element.43), channel_id=1, source_target_pairs={{0,2},{1,3},{2,0},{3,1},{4,6},{5,7},{6,4},{7,5},{8,10},{9,11},{10,... | collective-permute-start | bytes 393224 | tf_op jit(solution)/shard_map/ppermute | solution.py:26
  21.2 0.8 %collective-permute-start.7 = (f32[256,128]{1,0:T(8,128)S(1)}, f32[256,128]{1,0:T(8,128)S(1)}, u32[]{:S(2)}, u32[]{:S(2)}) collective-permute-start(f32[256,128]{1,0:T(8,128)S(1)} %collective-permute-done.2.rest_3_), channel_id=1, source_target_pairs={{0,2},{1,3},{2,0},{3,1},{4,6},{5,7},{6,4},{7,5},{8,10},{9,11},{10,... | collective-permute-start | bytes 393224 | tf_op jit(solution)/shard_map/ppermute | solution.py:26
  22.0 1.6 %collective-permute-done.3 = f32[256,128]{1,0:T(8,128)S(1)} collective-permute-done((f32[256,128]{1,0:T(8,128)S(1)}, f32[256,128]{1,0:T(8,128)S(1)}, u32[]{:S(2)}, u32[]{:S(2)}) %collective-permute-start.3) | collective-permute-done | bytes 131104 | tf_op jit(solution)/shard_map/ppermute | solution.py:26
  23.6 2.7 %collective-permute-start.4 = (f32[256,128]{1,0:T(8,128)S(1)}, f32[256,128]{1,0:T(8,128)S(1)}, u32[]{:S(2)}, u32[]{:S(2)}) collective-permute-start(f32[256,128]{1,0:T(8,128)S(1)} %add.32), channel_id=1, source_target_pairs={{0,16},{8,24},{16,0},{24,8},{1,17},{9,25},{17,1},{25,9},{2,18},{10... | collective-permute-start | bytes 393224 | tf_op jit(solution)/shard_map/ppermute | solution.py:26
  26.3 0.9 %collective-permute-start.5 = (f32[256,128]{1,0:T(8,128)S(1)}, f32[256,128]{1,0:T(8,128)S(1)}, u32[]{:S(2)}, u32[]{:S(2)}) collective-permute-start(f32[256,128]{1,0:T(8,128)S(1)} %collective-permute-done.3), channel_id=1, source_target_pairs={{0,2},{1,3},{2,0},{3,1},{4,6},{5,7},{6,4},{7,5},{8,10},{9,11},{10,... | collective-permute-start | bytes 393224 | tf_op jit(solution)/shard_map/ppermute | solution.py:26
  27.1 0.0 collective-permute-done.6.rest_2_
  27.1 0.7 %collective-permute-done.7.rest_4_ = f32[256,128]{1,0:T(8,128)S(1)} collective-permute-done((f32[256,128]{1,0:T(8,128)S(1)}, f32[256,128]{1,0:T(8,128)S(1)}, u32[]{:S(2)}, u32[]{:S(2)}) %collective-permute-start.7) | collective-permute-done | bytes 131104 | tf_op jit(solution)/shard_map/ppermute | solution.py:26
  27.9 3.2 %shard_map.59.rest_0_ = f32[1024,1024]{1,0:T(8,128)S(1)} custom-call(s32[1]{0:T(128)} %bitcast.2.half, s32[2]{0:T(128)S(1)} %pad_add_fusion.place, bf16[1024,1024]{1,0:T(8,128)(2,1)} %queries.8, f32[16,8,1024]{2,1,0:T(8,128)} %weights.8, bf16[512,1024]{1,0:T(8,128)(2,1)} %get-tuple-element.45.local, f32[512,128]{1,0:T(8,128)S(1)} %collective-permute-done.rest_0_, ...), custom_call_target="tpu_custom_call" | custom-call | flops 1048576 | bytes 262144 | tf_op jit(solution)/shard_map/pallas_call | solution.py:235
  31.1 0.7 %collective-permute-done.4 = f32[256,128]{1,0:T(8,128)S(1)} collective-permute-done((f32[256,128]{1,0:T(8,128)S(1)}, f32[256,128]{1,0:T(8,128)S(1)}, u32[]{:S(2)}, u32[]{:S(2)}) %collective-permute-start.4) | collective-permute-done | bytes 131104 | tf_op jit(solution)/shard_map/ppermute | solution.py:26
  31.9 0.0 collective-permute-done.5
  31.9 0.1 collective-permute-start.9
  32.0 0.0 copy-start
  32.0 0.0 copy-start.1
  32.1 0.0 copy-start.2
  32.1 0.6 %collective-permute-start.10 = (f32[3,256,128]{2,1,0:T(8,128)S(1)}, f32[3,256,128]{2,1,0:T(8,128)S(1)}, u32[]{:S(2)}, u32[]{:S(2)}) collective-permute-start(f32[3,256,128]{2,1,0:T(8,128)S(1)} %pad_maximum_fusion.early), channel_id=1, source_target_pairs={{0,1},{1,0},{2,3},{3,2},{4,5},{5,4},{6,7},{7,6},{8,9},{9,8},{10,11... | collective-permute-start | bytes 1179656 | tf_op jit(solution)/shard_map/ppermute | solution.py:26
  32.6 0.4 collective-permute-start.8
  33.0 1.2 %collective-permute-done.9.rest_1_ = f32[6,256,128]{2,1,0:T(8,128)S(1)} collective-permute-done((f32[6,256,128]{2,1,0:T(8,128)S(1)}, f32[6,256,128]{2,1,0:T(8,128)S(1)}, u32[]{:S(2)}, u32[]{:S(2)}) %collective-permute-start.9) | collective-permute-done | bytes 786464 | tf_op jit(solution)/shard_map/ppermute | solution.py:26
  34.3 3.2 %shard_map.60.near = f32[1024,1024]{1,0:T(8,128)S(1)} custom-call(s32[1]{0:T(128)} %bitcast.3.place.half, s32[2]{0:T(128)S(1)} %pad_add_fusion.place, bf16[1024,1024]{1,0:T(8,128)(2,1)} %queries.8, f32[16,8,1024]{2,1,0:T(8,128)} %weights.8, bf16[512,1024]{1,0:T(8,128)(2,1)} %shard_map.58.local, ...), custom_call_target="tpu_custom_call", output_to_operand_aliasing={{}: (5, {})} | custom-call | flops 1048576 | bytes 262144 | tf_op jit(solution)/shard_map/pallas_call | solution.py:235
  37.5 0.7 %collective-permute-done.8.late = f32[256,128]{1,0:T(8,128)S(1)} collective-permute-done((f32[256,128]{1,0:T(8,128)S(1)}, f32[256,128]{1,0:T(8,128)S(1)}, u32[]{:S(2)}, u32[]{:S(2)}) %collective-permute-start.8) | collective-permute-done | bytes 131104 | tf_op jit(solution)/shard_map/ppermute | solution.py:26
  38.1 0.0 collective-permute-done.10.early_other
  38.1 0.0 collective-permute-start.11
  38.1 1.3 %collective-permute-done.11.late_other = f32[256,128]{1,0:T(8,128)S(1)} collective-permute-done((f32[256,128]{1,0:T(8,128)S(1)}, f32[256,128]{1,0:T(8,128)S(1)}, u32[]{:S(2)}, u32[]{:S(2)}) %collective-permute-start.11) | collective-permute-done | bytes 131104 | tf_op jit(solution)/shard_map/ppermute | solution.py:26
  39.5 0.0 copy-done
  39.5 0.0 copy-done.1
  39.5 0.0 copy-done.2
  39.5 6.3 %shard_map.61 = bf16[1024,1024]{1,0:T(8,128)(2,1)} custom-call(s32[2]{0:T(128)S(1)} %pad_add_fusion.place, bf16[1024,1024]{1,0:T(8,128)(2,1)S(1)} %copy-done, f32[16,8,1024]{2,1,0:T(8,128)S(1)} %copy-done.1, f32[1024,1024]{1,0:T(8,128)S(1)} %shard_map.60.near, f32[3,256,128]{2,1,0:T(8,128)S(1)} %pad_maximum_fusion.early, ...), custom_call_target="tpu_custom_call" | custom-call | flops 2684354560 | bytes 12582912 | tf_op jit(solution)/shard_map/pallas_call | solution.py:318
  (11 shorter events, 0.2 us)
Async XLA Ops:
  2.4 2.3 %collective-permute-start = (f32[512,128]{1,0:T(8,128)S(1)}, f32[512,128]{1,0:T(8,128)S(1)}, u32[]{:S(2)}, u32[]{:S(2)}) collective-permute-start(f32[512,128]{1,0:T(8,128)S(1)} %shard_map.56), channel_id=1, source_target_pairs={{0,1},{1,0},{2,3},{3,2},{4,5},{5,4},{6,7},{7,6},{8,9},{9,8},{10,11... | collective-permute-start | bytes 786440 | tf_op jit(solution)/shard_map/ppermute | solution.py:26
  4.7 7.2 %collective-permute-start.1 = (f32[256,128]{1,0:T(8,128)S(1)}, f32[256,128]{1,0:T(8,128)S(1)}, u32[]{:S(2)}, u32[]{:S(2)}) collective-permute-start(f32[256,128]{1,0:T(8,128)S(1)} %dynamic-slice_add_fusion), channel_id=1, source_target_pairs={{0,2},{1,3},{2,0},{3,1},{4,6},{5,7},{6,4},{7,5},{8,10},{9,11},{10,... | collective-permute-start | bytes 393224 | tf_op jit(solution)/shard_map/ppermute | solution.py:26
  12.0 6.2 %collective-permute-start.2 = (f32[256,128]{1,0:T(8,128)S(1)}, f32[256,128]{1,0:T(8,128)S(1)}, u32[]{:S(2)}, u32[]{:S(2)}) collective-permute-start(f32[256,128]{1,0:T(8,128)S(1)} %get-tuple-element.35), channel_id=1, source_target_pairs={{0,4},{1,5},{2,6},{3,7},{4,0},{5,1},{6,2},{7,3},{8,12},{9,13},{10,... | collective-permute-start | bytes 393224 | tf_op jit(solution)/shard_map/ppermute | solution.py:26
  18.2 5.4 %collective-permute-start.3 = (f32[256,128]{1,0:T(8,128)S(1)}, f32[256,128]{1,0:T(8,128)S(1)}, u32[]{:S(2)}, u32[]{:S(2)}) collective-permute-start(f32[256,128]{1,0:T(8,128)S(1)} %add.31), channel_id=1, source_target_pairs={{0,8},{8,0},{16,24},{24,16},{1,9},{9,1},{17,25},{25,17},{2,10},{10... | collective-permute-start | bytes 393224 | tf_op jit(solution)/shard_map/ppermute | solution.py:26
  19.9 7.2 %collective-permute-start.6 = (f32[256,128]{1,0:T(8,128)S(1)}, f32[256,128]{1,0:T(8,128)S(1)}, u32[]{:S(2)}, u32[]{:S(2)}) collective-permute-start(f32[256,128]{1,0:T(8,128)S(1)} %get-tuple-element.43), channel_id=1, source_target_pairs={{0,2},{1,3},{2,0},{3,1},{4,6},{5,7},{6,4},{7,5},{8,10},{9,11},{10,... | collective-permute-start | bytes 393224 | tf_op jit(solution)/shard_map/ppermute | solution.py:26
  21.2 6.7 %collective-permute-start.7 = (f32[256,128]{1,0:T(8,128)S(1)}, f32[256,128]{1,0:T(8,128)S(1)}, u32[]{:S(2)}, u32[]{:S(2)}) collective-permute-start(f32[256,128]{1,0:T(8,128)S(1)} %collective-permute-done.2.rest_3_), channel_id=1, source_target_pairs={{0,2},{1,3},{2,0},{3,1},{4,6},{5,7},{6,4},{7,5},{8,10},{9,11},{10,... | collective-permute-start | bytes 393224 | tf_op jit(solution)/shard_map/ppermute | solution.py:26
  23.6 8.2 %collective-permute-start.4 = (f32[256,128]{1,0:T(8,128)S(1)}, f32[256,128]{1,0:T(8,128)S(1)}, u32[]{:S(2)}, u32[]{:S(2)}) collective-permute-start(f32[256,128]{1,0:T(8,128)S(1)} %add.32), channel_id=1, source_target_pairs={{0,16},{8,24},{16,0},{24,8},{1,17},{9,25},{17,1},{25,9},{2,18},{10... | collective-permute-start | bytes 393224 | tf_op jit(solution)/shard_map/ppermute | solution.py:26
  26.3 5.6 %collective-permute-start.5 = (f32[256,128]{1,0:T(8,128)S(1)}, f32[256,128]{1,0:T(8,128)S(1)}, u32[]{:S(2)}, u32[]{:S(2)}) collective-permute-start(f32[256,128]{1,0:T(8,128)S(1)} %collective-permute-done.3), channel_id=1, source_target_pairs={{0,2},{1,3},{2,0},{3,1},{4,6},{5,7},{6,4},{7,5},{8,10},{9,11},{10,... | collective-permute-start | bytes 393224 | tf_op jit(solution)/shard_map/ppermute | solution.py:26
  31.9 2.4 %collective-permute-start.9 = (f32[6,256,128]{2,1,0:T(8,128)S(1)}, f32[6,256,128]{2,1,0:T(8,128)S(1)}, u32[]{:S(2)}, u32[]{:S(2)}) collective-permute-start(f32[6,256,128]{2,1,0:T(8,128)S(1)} %bitcast_dynamic-update-slice_fusion), channel_id=1, source_target_pairs={{0,1},{1,0},{2,3},{3,2},{4,5},{5,4},{6,7},{7,6},{8,9},{9,8},{10,11... | collective-permute-start | bytes 2359304 | tf_op jit(solution)/shard_map/ppermute | solution.py:26
  32.0 7.4 %copy-start = (bf16[1024,1024]{1,0:T(8,128)(2,1)S(1)}, bf16[1024,1024]{1,0:T(8,128)(2,1)}, u32[]{:S(2)}) copy-start(bf16[1024,1024]{1,0:T(8,128)(2,1)} %queries.8) | copy-start | bytes 6291460
  32.0 7.4 %copy-start.1 = (f32[16,8,1024]{2,1,0:T(8,128)S(1)}, f32[16,8,1024]{2,1,0:T(8,128)}, u32[]{:S(2)}) copy-start(f32[16,8,1024]{2,1,0:T(8,128)} %weights.8) | copy-start | bytes 1572868
  32.1 7.4 %copy-start.2 = (bf16[1024,1024]{1,0:T(8,128)(2,1)S(1)}, bf16[1024,1024]{1,0:T(8,128)(2,1)}, u32[]{:S(2)}) copy-start(bf16[1024,1024]{1,0:T(8,128)(2,1)} %out_weight.1) | copy-start | bytes 6291460
  32.1 6.0 %collective-permute-start.10 = (f32[3,256,128]{2,1,0:T(8,128)S(1)}, f32[3,256,128]{2,1,0:T(8,128)S(1)}, u32[]{:S(2)}, u32[]{:S(2)}) collective-permute-start(f32[3,256,128]{2,1,0:T(8,128)S(1)} %pad_maximum_fusion.early), channel_id=1, source_target_pairs={{0,1},{1,0},{2,3},{3,2},{4,5},{5,4},{6,7},{7,6},{8,9},{9,8},{10,11... | collective-permute-start | bytes 1179656 | tf_op jit(solution)/shard_map/ppermute | solution.py:26
  32.6 5.5 %collective-permute-start.8 = (f32[256,128]{1,0:T(8,128)S(1)}, f32[256,128]{1,0:T(8,128)S(1)}, u32[]{:S(2)}, u32[]{:S(2)}) collective-permute-start(f32[256,128]{1,0:T(8,128)S(1)} %collective-permute-done.4), channel_id=1, source_target_pairs={{0,2},{1,3},{2,0},{3,1},{4,6},{5,7},{6,4},{7,5},{8,10},{9,11},{10,... | collective-permute-start | bytes 393224 | tf_op jit(solution)/shard_map/ppermute | solution.py:26
  38.1 1.3 %collective-permute-start.11 = (f32[256,128]{1,0:T(8,128)S(1)}, f32[256,128]{1,0:T(8,128)S(1)}, u32[]{:S(2)}, u32[]{:S(2)}) collective-permute-start(f32[256,128]{1,0:T(8,128)S(1)} %collective-permute-done.8.late), channel_id=1, source_target_pairs={{0,1},{1,0},{2,3},{3,2},{4,5},{5,4},{6,7},{7,6},{8,9},{9,8},{10,11... | collective-permute-start | bytes 393224 | tf_op jit(solution)/shard_map/ppermute | solution.py:26

commit v11 on v10

--- a/solution.py
+++ b/solution.py
@@ -191,7 +191,7 @@
     return jnp.bitwise_and(jnp.right_shift(place, bit), 1) == 1
 
 
-def near_kernel(aliased, half, place, queries, weights, local, *rest):
+def near_kernel(aliased, lowest, half, place, queries, weights, local, *rest):
     *held, near, states, rows = rest[aliased:]
     step = pl.program_id(0)
     bits = states.shape[1] // HEAD
@@ -221,9 +221,17 @@
         products = product_nt(states[head], queries[:, part])
         total = local[part, :].astype(F32)
         for bit in range(bits):
-            level = LOCAL_BITS + 1 + bit
+            level = LOCAL_BITS + 1 + bit - lowest
             total = total + rows[at, level : level + 1, :] * products[bit * HEAD : (bit + 1) * HEAD]
         near[part, :] = total
+
+
+def level_block(level_weights, first, count):
+    size = 8
+    lowest = first // size * size
+    if first + count <= lowest + size <= level_weights.shape[0]:
+        return lowest, size
+    return 0, level_weights.shape[0]
 
 
 def near_part(half, place, bits, queries, level_weights, local, into, *held):
@@ -231,15 +239,16 @@
     heads = width // HEAD // 2
     step = 2 * HEAD
     steps = width // step // 2
+    lowest, levels = level_block(level_weights, LOCAL_BITS + 1, bits)
     into = () if into is None else (pltpu.with_memory_space_constraint(into, pltpu.VMEM),)
     return pl.pallas_call(
-        functools.partial(near_kernel, len(into)),
+        functools.partial(near_kernel, len(into), lowest),
         grid_spec=pltpu.PrefetchScalarGridSpec(
             num_scalar_prefetch=2,
             grid=(steps,),
             in_specs=[
                 pl.BlockSpec((tokens, step), lambda pair, half, place: (0, half[0] * steps + pair)),
-                pl.BlockSpec(level_weights.shape, lambda pair, half, place: (0, 0, 0)),
+                pl.BlockSpec((levels,) + level_weights.shape[1:], lambda pair, half, place: (lowest // levels, 0, 0)),
                 pl.BlockSpec((step, tokens), lambda pair, half, place: (pair, 0)),
                 *[pl.BlockSpec(memory_space=pltpu.VMEM)] * len(into),
                 *[
@@ -253,7 +262,7 @@
             out_specs=pl.BlockSpec((step, tokens), lambda pair, half, place: (half[0] * steps + pair, 0)),
             scratch_shapes=[
                 pltpu.VMEM((heads, bits * HEAD, HEAD), BF16),
-                pltpu.VMEM((2, level_weights.shape[0], tokens), F32),
+                pltpu.VMEM((2, levels, tokens), F32),
             ],
         ),
         out_shape=pltpu.VMEM((width, tokens), F32),

time: 46 us -> 46 us (level)
  no operation moved by 1% of the time
where the time goes in v11:
time: 46 us; the launch traced here: 45.7 us
  Pallas kernels  25.9 us (56%)
  starting transfers between devices  12.8 us (28%)
  waiting for transfers between devices  6.61 us (14%)
    ppermute x12, starting transfers between devices, swap(): lax.ppermute(block, axis, [(place, place ^ stride) for place in range(cou...  12.8 us
    pallas_call x2, Pallas kernels, local_part(): pl.pallas_call(local_kernel, grid_spec=pltpu.PrefetchScalarGridSpec(num_s...  9.23 us
    ppermute x12, waiting for transfers between devices, swap(): lax.ppermute(block, axis, [(place, place ^ stride) for place in range(cou...  6.61 us
    pallas_call x1, Pallas kernels, far_part(): pl.pallas_call(functools.partial(far_kernel, first_level), grid=(tokens /...  6.27 us
    pallas_call x2, Pallas kernels, near_part(): pl.pallas_call(functools.partial(near_kernel, len(into), lowest), grid_sp...  6.22 us
    pallas_call x2, Pallas kernels, block_state(): pl.pallas_call(state_kernel, grid_spec=pltpu.PrefetchScalarGridSpec(num_s...  4.16 us
  transfers between devices with their start and end apart: 12, of which 6 were waited for; matrix products, arithmetic and copies ran while one was open for 0% of the time, Pallas kernels for 38%

profile of v11, /device:TPU:0, one launch (start us, length us, event | category | flops | bytes accessed | tf_op | source)
XLA Modules:
  0.0 45.7 jit_solution(6774855266366574199)
XLA Ops:
  0.0 2.4 %shard_map.56 = f32[512,128]{1,0:T(8,128)S(1)} custom-call(s32[1]{0:T(128)} %bitcast.3.place.half, bf16[1024,1024]{1,0:T(8,128)(2,1)} %keys.5, bf16[1024,1024]{1,0:T(8,128)(2,1)} %values.5), custom_call_target="tpu_custom_call" | custom-call | flops 134217728 | bytes 2621440 | tf_op jit(solution)/shard_map/pallas_call | solution.py:77
  2.4 0.5 %collective-permute-start = (f32[512,128]{1,0:T(8,128)S(1)}, f32[512,128]{1,0:T(8,128)S(1)}, u32[]{:S(2)}, u32[]{:S(2)}) collective-permute-start(f32[512,128]{1,0:T(8,128)S(1)} %shard_map.56), channel_id=1, source_target_pairs={{0,1},{1,0},{2,3},{3,2},{4,5},{5,4},{6,7},{7,6},{8,9},{9,8},{10,11... | collective-permute-start | bytes 786440 | tf_op jit(solution)/shard_map/ppermute | solution.py:26
  2.9 1.8 %shard_map.57 = f32[256,128]{1,0:T(8,128)S(1)} custom-call(s32[1]{0:T(128)} %bitcast.4.place, bf16[1024,1024]{1,0:T(8,128)(2,1)} %keys.5, bf16[1024,1024]{1,0:T(8,128)(2,1)} %values.5), custom_call_target="tpu_custom_call" | custom-call | flops 67108864 | bytes 1310720 | tf_op jit(solution)/shard_map/pallas_call | solution.py:77
  4.7 0.0 collective-permute-done.rest_0_
  4.7 2.6 %collective-permute-start.1 = (f32[256,128]{1,0:T(8,128)S(1)}, f32[256,128]{1,0:T(8,128)S(1)}, u32[]{:S(2)}, u32[]{:S(2)}) collective-permute-start(f32[256,128]{1,0:T(8,128)S(1)} %dynamic-slice_add_fusion), channel_id=1, source_target_pairs={{0,2},{1,3},{2,0},{3,1},{4,6},{5,7},{6,4},{7,5},{8,10},{9,11},{10,... | collective-permute-start | bytes 393224 | tf_op jit(solution)/shard_map/ppermute | solution.py:26
  7.3 4.7 %shard_map.55 = (bf16[512,1024]{1,0:T(8,128)(2,1)}, f32[512,128]{1,0:T(8,128)S(1)}) custom-call(s32[1]{0:T(128)} %bitcast.2.half, bf16[1024,1024]{1,0:T(8,128)(2,1)} %queries.8, bf16[1024,1024]{1,0:T(8,128)(2,1)} %keys.5, bf16[1024,1024]{1,0:T(8,128)(2,1)} %values.5, f32[16,8,1024]{2,1,0:T(8,128)} %weights.8), custom_call_target="tpu_custom_call" | custom-call | flops 1048576 | bytes 262144 | tf_op jit(solution)/shard_map/pallas_call | solution.py:172
  12.0 0.0 collective-permute-done.1.rest_1_
  12.0 1.6 %collective-permute-start.2 = (f32[256,128]{1,0:T(8,128)S(1)}, f32[256,128]{1,0:T(8,128)S(1)}, u32[]{:S(2)}, u32[]{:S(2)}) collective-permute-start(f32[256,128]{1,0:T(8,128)S(1)} %get-tuple-element.35), channel_id=1, source_target_pairs={{0,4},{1,5},{2,6},{3,7},{4,0},{5,1},{6,2},{7,3},{8,12},{9,13},{10,... | collective-permute-start | bytes 393224 | tf_op jit(solution)/shard_map/ppermute | solution.py:26
  13.6 4.6 %shard_map.58.local = bf16[512,1024]{1,0:T(8,128)(2,1)} custom-call(s32[1]{0:T(128)} %bitcast.3.place.half, bf16[1024,1024]{1,0:T(8,128)(2,1)} %queries.8, bf16[1024,1024]{1,0:T(8,128)(2,1)} %keys.5, bf16[1024,1024]{1,0:T(8,128)(2,1)} %values.5, f32[16,8,1024]{2,1,0:T(8,128)} %weights.8), custom_call_target="tpu_custom_call" | custom-call | flops 1048576 | bytes 262144 | tf_op jit(solution)/shard_map/pallas_call | solution.py:172
  18.2 0.0 collective-permute-done.2.rest_3_
  18.2 1.6 %collective-permute-start.3 = (f32[256,128]{1,0:T(8,128)S(1)}, f32[256,128]{1,0:T(8,128)S(1)}, u32[]{:S(2)}, u32[]{:S(2)}) collective-permute-start(f32[256,128]{1,0:T(8,128)S(1)} %add.31), channel_id=1, source_target_pairs={{0,8},{8,0},{16,24},{24,16},{1,9},{9,1},{17,25},{25,17},{2,10},{10... | collective-permute-start | bytes 393224 | tf_op jit(solution)/shard_map/ppermute | solution.py:26
  19.9 0.1 pad_add_fusion.place
  19.9 1.2 %collective-permute-start.6 = (f32[256,128]{1,0:T(8,128)S(1)}, f32[256,128]{1,0:T(8,128)S(1)}, u32[]{:S(2)}, u32[]{:S(2)}) collective-permute-start(f32[256,128]{1,0:T(8,128)S(1)} %get-tuple-element.43), channel_id=1, source_target_pairs={{0,2},{1,3},{2,0},{3,1},{4,6},{5,7},{6,4},{7,5},{8,10},{9,11},{10,... | collective-permute-start | bytes 393224 | tf_op jit(solution)/shard_map/ppermute | solution.py:26
  21.2 0.8 %collective-permute-start.7 = (f32[256,128]{1,0:T(8,128)S(1)}, f32[256,128]{1,0:T(8,128)S(1)}, u32[]{:S(2)}, u32[]{:S(2)}) collective-permute-start(f32[256,128]{1,0:T(8,128)S(1)} %collective-permute-done.2.rest_3_), channel_id=1, source_target_pairs={{0,2},{1,3},{2,0},{3,1},{4,6},{5,7},{6,4},{7,5},{8,10},{9,11},{10,... | collective-permute-start | bytes 393224 | tf_op jit(solution)/shard_map/ppermute | solution.py:26
  22.0 1.6 %collective-permute-done.3 = f32[256,128]{1,0:T(8,128)S(1)} collective-permute-done((f32[256,128]{1,0:T(8,128)S(1)}, f32[256,128]{1,0:T(8,128)S(1)}, u32[]{:S(2)}, u32[]{:S(2)}) %collective-permute-start.3) | collective-permute-done | bytes 131104 | tf_op jit(solution)/shard_map/ppermute | solution.py:26
  23.6 2.7 %collective-permute-start.4 = (f32[256,128]{1,0:T(8,128)S(1)}, f32[256,128]{1,0:T(8,128)S(1)}, u32[]{:S(2)}, u32[]{:S(2)}) collective-permute-start(f32[256,128]{1,0:T(8,128)S(1)} %add.32), channel_id=1, source_target_pairs={{0,16},{8,24},{16,0},{24,8},{1,17},{9,25},{17,1},{25,9},{2,18},{10... | collective-permute-start | bytes 393224 | tf_op jit(solution)/shard_map/ppermute | solution.py:26
  26.3 0.9 %collective-permute-start.5 = (f32[256,128]{1,0:T(8,128)S(1)}, f32[256,128]{1,0:T(8,128)S(1)}, u32[]{:S(2)}, u32[]{:S(2)}) collective-permute-start(f32[256,128]{1,0:T(8,128)S(1)} %collective-permute-done.3), channel_id=1, source_target_pairs={{0,2},{1,3},{2,0},{3,1},{4,6},{5,7},{6,4},{7,5},{8,10},{9,11},{10,... | collective-permute-start | bytes 393224 | tf_op jit(solution)/shard_map/ppermute | solution.py:26
  27.1 0.0 collective-permute-done.6.rest_2_
  27.1 0.7 %collective-permute-done.7.rest_4_ = f32[256,128]{1,0:T(8,128)S(1)} collective-permute-done((f32[256,128]{1,0:T(8,128)S(1)}, f32[256,128]{1,0:T(8,128)S(1)}, u32[]{:S(2)}, u32[]{:S(2)}) %collective-permute-start.7) | collective-permute-done | bytes 131104 | tf_op jit(solution)/shard_map/ppermute | solution.py:26
  27.9 3.1 %shard_map.59.rest_0_ = f32[1024,1024]{1,0:T(8,128)S(1)} custom-call(s32[1]{0:T(128)} %bitcast.2.half, s32[2]{0:T(128)S(1)} %pad_add_fusion.place, bf16[1024,1024]{1,0:T(8,128)(2,1)} %queries.8, f32[16,8,1024]{2,1,0:T(8,128)} %weights.8, bf16[512,1024]{1,0:T(8,128)(2,1)} %get-tuple-element.45.local, f32[512,128]{1,0:T(8,128)S(1)} %collective-permute-done.rest_0_, ...), custom_call_target="tpu_custom_call" | custom-call | flops 1048576 | bytes 262144 | tf_op jit(solution)/shard_map/pallas_call | solution.py:244
  31.0 0.8 %collective-permute-done.4 = f32[256,128]{1,0:T(8,128)S(1)} collective-permute-done((f32[256,128]{1,0:T(8,128)S(1)}, f32[256,128]{1,0:T(8,128)S(1)}, u32[]{:S(2)}, u32[]{:S(2)}) %collective-permute-start.4) | collective-permute-done | bytes 131104 | tf_op jit(solution)/shard_map/ppermute | solution.py:26
  31.9 0.0 collective-permute-done.5
  31.9 0.1 collective-permute-start.9
  32.0 0.0 copy-start
  32.0 0.0 copy-start.1
  32.1 0.0 copy-start.2
  32.1 0.6 %collective-permute-start.10 = (f32[3,256,128]{2,1,0:T(8,128)S(1)}, f32[3,256,128]{2,1,0:T(8,128)S(1)}, u32[]{:S(2)}, u32[]{:S(2)}) collective-permute-start(f32[3,256,128]{2,1,0:T(8,128)S(1)} %pad_maximum_fusion.early), channel_id=1, source_target_pairs={{0,1},{1,0},{2,3},{3,2},{4,5},{5,4},{6,7},{7,6},{8,9},{9,8},{10,11... | collective-permute-start | bytes 1179656 | tf_op jit(solution)/shard_map/ppermute | solution.py:26
  32.6 0.3 collective-permute-start.8
  32.9 1.3 %collective-permute-done.9.rest_1_ = f32[6,256,128]{2,1,0:T(8,128)S(1)} collective-permute-done((f32[6,256,128]{2,1,0:T(8,128)S(1)}, f32[6,256,128]{2,1,0:T(8,128)S(1)}, u32[]{:S(2)}, u32[]{:S(2)}) %collective-permute-start.9) | collective-permute-done | bytes 786464 | tf_op jit(solution)/shard_map/ppermute | solution.py:26
  34.3 3.1 %shard_map.60.near = f32[1024,1024]{1,0:T(8,128)S(1)} custom-call(s32[1]{0:T(128)} %bitcast.3.place.half, s32[2]{0:T(128)S(1)} %pad_add_fusion.place, bf16[1024,1024]{1,0:T(8,128)(2,1)} %queries.8, f32[16,8,1024]{2,1,0:T(8,128)} %weights.8, bf16[512,1024]{1,0:T(8,128)(2,1)} %shard_map.58.local, ...), custom_call_target="tpu_custom_call", output_to_operand_aliasing={{}: (5, {})} | custom-call | flops 1048576 | bytes 262144 | tf_op jit(solution)/shard_map/pallas_call | solution.py:244
  37.4 0.7 %collective-permute-done.8.late = f32[256,128]{1,0:T(8,128)S(1)} collective-permute-done((f32[256,128]{1,0:T(8,128)S(1)}, f32[256,128]{1,0:T(8,128)S(1)}, u32[]{:S(2)}, u32[]{:S(2)}) %collective-permute-start.8) | collective-permute-done | bytes 131104 | tf_op jit(solution)/shard_map/ppermute | solution.py:26
  38.1 0.0 collective-permute-done.10.early_other
  38.1 0.0 collective-permute-start.11
  38.1 1.3 %collective-permute-done.11.late_other = f32[256,128]{1,0:T(8,128)S(1)} collective-permute-done((f32[256,128]{1,0:T(8,128)S(1)}, f32[256,128]{1,0:T(8,128)S(1)}, u32[]{:S(2)}, u32[]{:S(2)}) %collective-permute-start.11) | collective-permute-done | bytes 131104 | tf_op jit(solution)/shard_map/ppermute | solution.py:26
  39.5 0.0 copy-done
  39.5 0.0 copy-done.1
  39.5 0.0 copy-done.2
  39.5 6.3 %shard_map.61 = bf16[1024,1024]{1,0:T(8,128)(2,1)} custom-call(s32[2]{0:T(128)S(1)} %pad_add_fusion.place, bf16[1024,1024]{1,0:T(8,128)(2,1)S(1)} %copy-done, f32[16,8,1024]{2,1,0:T(8,128)S(1)} %copy-done.1, f32[1024,1024]{1,0:T(8,128)S(1)} %shard_map.60.near, f32[3,256,128]{2,1,0:T(8,128)S(1)} %pad_maximum_fusion.early, ...), custom_call_target="tpu_custom_call" | custom-call | flops 2684354560 | bytes 12582912 | tf_op jit(solution)/shard_map/pallas_call | solution.py:327
  (11 shorter events, 0.2 us)
Async XLA Ops:
  2.4 2.3 %collective-permute-start = (f32[512,128]{1,0:T(8,128)S(1)}, f32[512,128]{1,0:T(8,128)S(1)}, u32[]{:S(2)}, u32[]{:S(2)}) collective-permute-start(f32[512,128]{1,0:T(8,128)S(1)} %shard_map.56), channel_id=1, source_target_pairs={{0,1},{1,0},{2,3},{3,2},{4,5},{5,4},{6,7},{7,6},{8,9},{9,8},{10,11... | collective-permute-start | bytes 786440 | tf_op jit(solution)/shard_map/ppermute | solution.py:26
  4.7 7.2 %collective-permute-start.1 = (f32[256,128]{1,0:T(8,128)S(1)}, f32[256,128]{1,0:T(8,128)S(1)}, u32[]{:S(2)}, u32[]{:S(2)}) collective-permute-start(f32[256,128]{1,0:T(8,128)S(1)} %dynamic-slice_add_fusion), channel_id=1, source_target_pairs={{0,2},{1,3},{2,0},{3,1},{4,6},{5,7},{6,4},{7,5},{8,10},{9,11},{10,... | collective-permute-start | bytes 393224 | tf_op jit(solution)/shard_map/ppermute | solution.py:26
  12.0 6.2 %collective-permute-start.2 = (f32[256,128]{1,0:T(8,128)S(1)}, f32[256,128]{1,0:T(8,128)S(1)}, u32[]{:S(2)}, u32[]{:S(2)}) collective-permute-start(f32[256,128]{1,0:T(8,128)S(1)} %get-tuple-element.35), channel_id=1, source_target_pairs={{0,4},{1,5},{2,6},{3,7},{4,0},{5,1},{6,2},{7,3},{8,12},{9,13},{10,... | collective-permute-start | bytes 393224 | tf_op jit(solution)/shard_map/ppermute | solution.py:26
  18.2 5.4 %collective-permute-start.3 = (f32[256,128]{1,0:T(8,128)S(1)}, f32[256,128]{1,0:T(8,128)S(1)}, u32[]{:S(2)}, u32[]{:S(2)}) collective-permute-start(f32[256,128]{1,0:T(8,128)S(1)} %add.31), channel_id=1, source_target_pairs={{0,8},{8,0},{16,24},{24,16},{1,9},{9,1},{17,25},{25,17},{2,10},{10... | collective-permute-start | bytes 393224 | tf_op jit(solution)/shard_map/ppermute | solution.py:26
  19.9 7.2 %collective-permute-start.6 = (f32[256,128]{1,0:T(8,128)S(1)}, f32[256,128]{1,0:T(8,128)S(1)}, u32[]{:S(2)}, u32[]{:S(2)}) collective-permute-start(f32[256,128]{1,0:T(8,128)S(1)} %get-tuple-element.43), channel_id=1, source_target_pairs={{0,2},{1,3},{2,0},{3,1},{4,6},{5,7},{6,4},{7,5},{8,10},{9,11},{10,... | collective-permute-start | bytes 393224 | tf_op jit(solution)/shard_map/ppermute | solution.py:26
  21.2 6.7 %collective-permute-start.7 = (f32[256,128]{1,0:T(8,128)S(1)}, f32[256,128]{1,0:T(8,128)S(1)}, u32[]{:S(2)}, u32[]{:S(2)}) collective-permute-start(f32[256,128]{1,0:T(8,128)S(1)} %collective-permute-done.2.rest_3_), channel_id=1, source_target_pairs={{0,2},{1,3},{2,0},{3,1},{4,6},{5,7},{6,4},{7,5},{8,10},{9,11},{10,... | collective-permute-start | bytes 393224 | tf_op jit(solution)/shard_map/ppermute | solution.py:26
  23.6 8.2 %collective-permute-start.4 = (f32[256,128]{1,0:T(8,128)S(1)}, f32[256,128]{1,0:T(8,128)S(1)}, u32[]{:S(2)}, u32[]{:S(2)}) collective-permute-start(f32[256,128]{1,0:T(8,128)S(1)} %add.32), channel_id=1, source_target_pairs={{0,16},{8,24},{16,0},{24,8},{1,17},{9,25},{17,1},{25,9},{2,18},{10... | collective-permute-start | bytes 393224 | tf_op jit(solution)/shard_map/ppermute | solution.py:26
  26.3 5.6 %collective-permute-start.5 = (f32[256,128]{1,0:T(8,128)S(1)}, f32[256,128]{1,0:T(8,128)S(1)}, u32[]{:S(2)}, u32[]{:S(2)}) collective-permute-start(f32[256,128]{1,0:T(8,128)S(1)} %collective-permute-done.3), channel_id=1, source_target_pairs={{0,2},{1,3},{2,0},{3,1},{4,6},{5,7},{6,4},{7,5},{8,10},{9,11},{10,... | collective-permute-start | bytes 393224 | tf_op jit(solution)/shard_map/ppermute | solution.py:26
  31.9 2.4 %collective-permute-start.9 = (f32[6,256,128]{2,1,0:T(8,128)S(1)}, f32[6,256,128]{2,1,0:T(8,128)S(1)}, u32[]{:S(2)}, u32[]{:S(2)}) collective-permute-start(f32[6,256,128]{2,1,0:T(8,128)S(1)} %bitcast_dynamic-update-slice_fusion), channel_id=1, source_target_pairs={{0,1},{1,0},{2,3},{3,2},{4,5},{5,4},{6,7},{7,6},{8,9},{9,8},{10,11... | collective-permute-start | bytes 2359304 | tf_op jit(solution)/shard_map/ppermute | solution.py:26
  32.0 7.4 %copy-start = (bf16[1024,1024]{1,0:T(8,128)(2,1)S(1)}, bf16[1024,1024]{1,0:T(8,128)(2,1)}, u32[]{:S(2)}) copy-start(bf16[1024,1024]{1,0:T(8,128)(2,1)} %queries.8) | copy-start | bytes 6291460
  32.0 7.4 %copy-start.1 = (f32[16,8,1024]{2,1,0:T(8,128)S(1)}, f32[16,8,1024]{2,1,0:T(8,128)}, u32[]{:S(2)}) copy-start(f32[16,8,1024]{2,1,0:T(8,128)} %weights.8) | copy-start | bytes 1572868
  32.1 7.4 %copy-start.2 = (bf16[1024,1024]{1,0:T(8,128)(2,1)S(1)}, bf16[1024,1024]{1,0:T(8,128)(2,1)}, u32[]{:S(2)}) copy-start(bf16[1024,1024]{1,0:T(8,128)(2,1)} %out_weight.1) | copy-start | bytes 6291460
  32.1 6.0 %collective-permute-start.10 = (f32[3,256,128]{2,1,0:T(8,128)S(1)}, f32[3,256,128]{2,1,0:T(8,128)S(1)}, u32[]{:S(2)}, u32[]{:S(2)}) collective-permute-start(f32[3,256,128]{2,1,0:T(8,128)S(1)} %pad_maximum_fusion.early), channel_id=1, source_target_pairs={{0,1},{1,0},{2,3},{3,2},{4,5},{5,4},{6,7},{7,6},{8,9},{9,8},{10,11... | collective-permute-start | bytes 1179656 | tf_op jit(solution)/shard_map/ppermute | solution.py:26
  32.6 5.5 %collective-permute-start.8 = (f32[256,128]{1,0:T(8,128)S(1)}, f32[256,128]{1,0:T(8,128)S(1)}, u32[]{:S(2)}, u32[]{:S(2)}) collective-permute-start(f32[256,128]{1,0:T(8,128)S(1)} %collective-permute-done.4), channel_id=1, source_target_pairs={{0,2},{1,3},{2,0},{3,1},{4,6},{5,7},{6,4},{7,5},{8,10},{9,11},{10,... | collective-permute-start | bytes 393224 | tf_op jit(solution)/shard_map/ppermute | solution.py:26
  38.1 1.3 %collective-permute-start.11 = (f32[256,128]{1,0:T(8,128)S(1)}, f32[256,128]{1,0:T(8,128)S(1)}, u32[]{:S(2)}, u32[]{:S(2)}) collective-permute-start(f32[256,128]{1,0:T(8,128)S(1)} %collective-permute-done.8.late), channel_id=1, source_target_pairs={{0,1},{1,0},{2,3},{3,2},{4,5},{5,4},{6,7},{7,6},{8,9},{9,8},{10,11... | collective-permute-start | bytes 393224 | tf_op jit(solution)/shard_map/ppermute | solution.py:26

commit v12 on v11

--- a/solution.py
+++ b/solution.py
@@ -314,6 +314,7 @@
 
 def far_part(first_level, bits, place, queries, level_weights, near, *fixed):
     tokens, width = queries.shape
+    lowest, levels = level_block(level_weights, first_level, bits)
     rows = min(2 * CHUNK, tokens)
     band = pl.BlockSpec((rows, width), lambda step: (step, 0))
 
@@ -325,12 +326,12 @@
         return pl.BlockSpec(part.shape, lambda step: (0,) * part.ndim)
 
     return pl.pallas_call(
-        functools.partial(far_kernel, first_level),
+        functools.partial(far_kernel, first_level - lowest),
         grid=(tokens // rows,),
         in_specs=[
             pl.BlockSpec(memory_space=pltpu.SMEM),
             band,
-            pl.BlockSpec(level_weights.shape[:2] + (rows,), lambda step: (0, 0, step)),
+            pl.BlockSpec((levels, level_weights.shape[1], rows), lambda step: (lowest // levels, 0, step)),
             pl.BlockSpec((width, rows), lambda step: (0, step)),
             *[tail(part) for part in fixed],
         ],

time: 46 us -> 46 us (level)
  no operation moved by 1% of the time
where the time goes in v12:
time: 46 us; the launch traced here: 45.7 us
  Pallas kernels  25.9 us (56%)
  starting transfers between devices  12.8 us (28%)
  waiting for transfers between devices  6.61 us (14%)
    ppermute x12, starting transfers between devices, swap(): lax.ppermute(block, axis, [(place, place ^ stride) for place in range(cou...  12.8 us
    pallas_call x2, Pallas kernels, local_part(): pl.pallas_call(local_kernel, grid_spec=pltpu.PrefetchScalarGridSpec(num_s...  9.23 us
    ppermute x12, waiting for transfers between devices, swap(): lax.ppermute(block, axis, [(place, place ^ stride) for place in range(cou...  6.61 us
    pallas_call x1, Pallas kernels, far_part(): pl.pallas_call(functools.partial(far_kernel, first_level - lowest), grid=...  6.26 us
    pallas_call x2, Pallas kernels, near_part(): pl.pallas_call(functools.partial(near_kernel, len(into), lowest), grid_sp...  6.22 us
    pallas_call x2, Pallas kernels, block_state(): pl.pallas_call(state_kernel, grid_spec=pltpu.PrefetchScalarGridSpec(num_s...  4.16 us
  transfers between devices with their start and end apart: 12, of which 6 were waited for; matrix products, arithmetic and copies ran while one was open for 0% of the time, Pallas kernels for 38%

profile of v12, /device:TPU:0, one launch (start us, length us, event | category | flops | bytes accessed | tf_op | source)
XLA Modules:
  0.0 45.7 jit_solution(18116008989443275587)
XLA Ops:
  0.0 2.4 %shard_map.56 = f32[512,128]{1,0:T(8,128)S(1)} custom-call(s32[1]{0:T(128)} %bitcast.3.place.half, bf16[1024,1024]{1,0:T(8,128)(2,1)} %keys.5, bf16[1024,1024]{1,0:T(8,128)(2,1)} %values.5), custom_call_target="tpu_custom_call" | custom-call | flops 134217728 | bytes 2621440 | tf_op jit(solution)/shard_map/pallas_call | solution.py:77
  2.4 0.5 %collective-permute-start = (f32[512,128]{1,0:T(8,128)S(1)}, f32[512,128]{1,0:T(8,128)S(1)}, u32[]{:S(2)}, u32[]{:S(2)}) collective-permute-start(f32[512,128]{1,0:T(8,128)S(1)} %shard_map.56), channel_id=1, source_target_pairs={{0,1},{1,0},{2,3},{3,2},{4,5},{5,4},{6,7},{7,6},{8,9},{9,8},{10,11... | collective-permute-start | bytes 786440 | tf_op jit(solution)/shard_map/ppermute | solution.py:26
  2.9 1.8 %shard_map.57 = f32[256,128]{1,0:T(8,128)S(1)} custom-call(s32[1]{0:T(128)} %bitcast.4.place, bf16[1024,1024]{1,0:T(8,128)(2,1)} %keys.5, bf16[1024,1024]{1,0:T(8,128)(2,1)} %values.5), custom_call_target="tpu_custom_call" | custom-call | flops 67108864 | bytes 1310720 | tf_op jit(solution)/shard_map/pallas_call | solution.py:77
  4.7 0.0 collective-permute-done.rest_0_
  4.7 2.6 %collective-permute-start.1 = (f32[256,128]{1,0:T(8,128)S(1)}, f32[256,128]{1,0:T(8,128)S(1)}, u32[]{:S(2)}, u32[]{:S(2)}) collective-permute-start(f32[256,128]{1,0:T(8,128)S(1)} %dynamic-slice_add_fusion), channel_id=1, source_target_pairs={{0,2},{1,3},{2,0},{3,1},{4,6},{5,7},{6,4},{7,5},{8,10},{9,11},{10,... | collective-permute-start | bytes 393224 | tf_op jit(solution)/shard_map/ppermute | solution.py:26
  7.3 4.7 %shard_map.55 = (bf16[512,1024]{1,0:T(8,128)(2,1)}, f32[512,128]{1,0:T(8,128)S(1)}) custom-call(s32[1]{0:T(128)} %bitcast.2.half, bf16[1024,1024]{1,0:T(8,128)(2,1)} %queries.8, bf16[1024,1024]{1,0:T(8,128)(2,1)} %keys.5, bf16[1024,1024]{1,0:T(8,128)(2,1)} %values.5, f32[16,8,1024]{2,1,0:T(8,128)} %weights.8), custom_call_target="tpu_custom_call" | custom-call | flops 1048576 | bytes 262144 | tf_op jit(solution)/shard_map/pallas_call | solution.py:172
  12.0 0.0 collective-permute-done.1.rest_1_
  12.0 1.6 %collective-permute-start.2 = (f32[256,128]{1,0:T(8,128)S(1)}, f32[256,128]{1,0:T(8,128)S(1)}, u32[]{:S(2)}, u32[]{:S(2)}) collective-permute-start(f32[256,128]{1,0:T(8,128)S(1)} %get-tuple-element.35), channel_id=1, source_target_pairs={{0,4},{1,5},{2,6},{3,7},{4,0},{5,1},{6,2},{7,3},{8,12},{9,13},{10,... | collective-permute-start | bytes 393224 | tf_op jit(solution)/shard_map/ppermute | solution.py:26
  13.6 4.6 %shard_map.58.local = bf16[512,1024]{1,0:T(8,128)(2,1)} custom-call(s32[1]{0:T(128)} %bitcast.3.place.half, bf16[1024,1024]{1,0:T(8,128)(2,1)} %queries.8, bf16[1024,1024]{1,0:T(8,128)(2,1)} %keys.5, bf16[1024,1024]{1,0:T(8,128)(2,1)} %values.5, f32[16,8,1024]{2,1,0:T(8,128)} %weights.8), custom_call_target="tpu_custom_call" | custom-call | flops 1048576 | bytes 262144 | tf_op jit(solution)/shard_map/pallas_call | solution.py:172
  18.2 0.0 collective-permute-done.2.rest_3_
  18.2 1.6 %collective-permute-start.3 = (f32[256,128]{1,0:T(8,128)S(1)}, f32[256,128]{1,0:T(8,128)S(1)}, u32[]{:S(2)}, u32[]{:S(2)}) collective-permute-start(f32[256,128]{1,0:T(8,128)S(1)} %add.31), channel_id=1, source_target_pairs={{0,8},{8,0},{16,24},{24,16},{1,9},{9,1},{17,25},{25,17},{2,10},{10... | collective-permute-start | bytes 393224 | tf_op jit(solution)/shard_map/ppermute | solution.py:26
  19.9 0.1 pad_add_fusion.place
  19.9 1.2 %collective-permute-start.6 = (f32[256,128]{1,0:T(8,128)S(1)}, f32[256,128]{1,0:T(8,128)S(1)}, u32[]{:S(2)}, u32[]{:S(2)}) collective-permute-start(f32[256,128]{1,0:T(8,128)S(1)} %get-tuple-element.43), channel_id=1, source_target_pairs={{0,2},{1,3},{2,0},{3,1},{4,6},{5,7},{6,4},{7,5},{8,10},{9,11},{10,... | collective-permute-start | bytes 393224 | tf_op jit(solution)/shard_map/ppermute | solution.py:26
  21.2 0.8 %collective-permute-start.7 = (f32[256,128]{1,0:T(8,128)S(1)}, f32[256,128]{1,0:T(8,128)S(1)}, u32[]{:S(2)}, u32[]{:S(2)}) collective-permute-start(f32[256,128]{1,0:T(8,128)S(1)} %collective-permute-done.2.rest_3_), channel_id=1, source_target_pairs={{0,2},{1,3},{2,0},{3,1},{4,6},{5,7},{6,4},{7,5},{8,10},{9,11},{10,... | collective-permute-start | bytes 393224 | tf_op jit(solution)/shard_map/ppermute | solution.py:26
  22.0 1.6 %collective-permute-done.3 = f32[256,128]{1,0:T(8,128)S(1)} collective-permute-done((f32[256,128]{1,0:T(8,128)S(1)}, f32[256,128]{1,0:T(8,128)S(1)}, u32[]{:S(2)}, u32[]{:S(2)}) %collective-permute-start.3) | collective-permute-done | bytes 131104 | tf_op jit(solution)/shard_map/ppermute | solution.py:26
  23.6 2.7 %collective-permute-start.4 = (f32[256,128]{1,0:T(8,128)S(1)}, f32[256,128]{1,0:T(8,128)S(1)}, u32[]{:S(2)}, u32[]{:S(2)}) collective-permute-start(f32[256,128]{1,0:T(8,128)S(1)} %add.32), channel_id=1, source_target_pairs={{0,16},{8,24},{16,0},{24,8},{1,17},{9,25},{17,1},{25,9},{2,18},{10... | collective-permute-start | bytes 393224 | tf_op jit(solution)/shard_map/ppermute | solution.py:26
  26.3 0.9 %collective-permute-start.5 = (f32[256,128]{1,0:T(8,128)S(1)}, f32[256,128]{1,0:T(8,128)S(1)}, u32[]{:S(2)}, u32[]{:S(2)}) collective-permute-start(f32[256,128]{1,0:T(8,128)S(1)} %collective-permute-done.3), channel_id=1, source_target_pairs={{0,2},{1,3},{2,0},{3,1},{4,6},{5,7},{6,4},{7,5},{8,10},{9,11},{10,... | collective-permute-start | bytes 393224 | tf_op jit(solution)/shard_map/ppermute | solution.py:26
  27.1 0.0 collective-permute-done.6.rest_2_
  27.1 0.7 %collective-permute-done.7.rest_4_ = f32[256,128]{1,0:T(8,128)S(1)} collective-permute-done((f32[256,128]{1,0:T(8,128)S(1)}, f32[256,128]{1,0:T(8,128)S(1)}, u32[]{:S(2)}, u32[]{:S(2)}) %collective-permute-start.7) | collective-permute-done | bytes 131104 | tf_op jit(solution)/shard_map/ppermute | solution.py:26
  27.9 3.1 %shard_map.59.rest_0_ = f32[1024,1024]{1,0:T(8,128)S(1)} custom-call(s32[1]{0:T(128)} %bitcast.2.half, s32[2]{0:T(128)S(1)} %pad_add_fusion.place, bf16[1024,1024]{1,0:T(8,128)(2,1)} %queries.8, f32[16,8,1024]{2,1,0:T(8,128)} %weights.8, bf16[512,1024]{1,0:T(8,128)(2,1)} %get-tuple-element.45.local, f32[512,128]{1,0:T(8,128)S(1)} %collective-permute-done.rest_0_, ...), custom_call_target="tpu_custom_call" | custom-call | flops 1048576 | bytes 262144 | tf_op jit(solution)/shard_map/pallas_call | solution.py:244
  31.0 0.8 %collective-permute-done.4 = f32[256,128]{1,0:T(8,128)S(1)} collective-permute-done((f32[256,128]{1,0:T(8,128)S(1)}, f32[256,128]{1,0:T(8,128)S(1)}, u32[]{:S(2)}, u32[]{:S(2)}) %collective-permute-start.4) | collective-permute-done | bytes 131104 | tf_op jit(solution)/shard_map/ppermute | solution.py:26
  31.9 0.0 collective-permute-done.5
  31.9 0.1 collective-permute-start.9
  32.0 0.0 copy-start
  32.0 0.0 copy-start.1
  32.1 0.0 copy-start.2
  32.1 0.6 %collective-permute-start.10 = (f32[3,256,128]{2,1,0:T(8,128)S(1)}, f32[3,256,128]{2,1,0:T(8,128)S(1)}, u32[]{:S(2)}, u32[]{:S(2)}) collective-permute-start(f32[3,256,128]{2,1,0:T(8,128)S(1)} %pad_maximum_fusion.early), channel_id=1, source_target_pairs={{0,1},{1,0},{2,3},{3,2},{4,5},{5,4},{6,7},{7,6},{8,9},{9,8},{10,11... | collective-permute-start | bytes 1179656 | tf_op jit(solution)/shard_map/ppermute | solution.py:26
  32.6 0.3 collective-permute-start.8
  32.9 1.3 %collective-permute-done.9.rest_1_ = f32[6,256,128]{2,1,0:T(8,128)S(1)} collective-permute-done((f32[6,256,128]{2,1,0:T(8,128)S(1)}, f32[6,256,128]{2,1,0:T(8,128)S(1)}, u32[]{:S(2)}, u32[]{:S(2)}) %collective-permute-start.9) | collective-permute-done | bytes 786464 | tf_op jit(solution)/shard_map/ppermute | solution.py:26
  34.3 3.1 %shard_map.60.near = f32[1024,1024]{1,0:T(8,128)S(1)} custom-call(s32[1]{0:T(128)} %bitcast.3.place.half, s32[2]{0:T(128)S(1)} %pad_add_fusion.place, bf16[1024,1024]{1,0:T(8,128)(2,1)} %queries.8, f32[16,8,1024]{2,1,0:T(8,128)} %weights.8, bf16[512,1024]{1,0:T(8,128)(2,1)} %shard_map.58.local, ...), custom_call_target="tpu_custom_call", output_to_operand_aliasing={{}: (5, {})} | custom-call | flops 1048576 | bytes 262144 | tf_op jit(solution)/shard_map/pallas_call | solution.py:244
  37.4 0.7 %collective-permute-done.8.late = f32[256,128]{1,0:T(8,128)S(1)} collective-permute-done((f32[256,128]{1,0:T(8,128)S(1)}, f32[256,128]{1,0:T(8,128)S(1)}, u32[]{:S(2)}, u32[]{:S(2)}) %collective-permute-start.8) | collective-permute-done | bytes 131104 | tf_op jit(solution)/shard_map/ppermute | solution.py:26
  38.1 0.0 collective-permute-done.10.early_other
  38.1 0.0 collective-permute-start.11
  38.1 1.3 %collective-permute-done.11.late_other = f32[256,128]{1,0:T(8,128)S(1)} collective-permute-done((f32[256,128]{1,0:T(8,128)S(1)}, f32[256,128]{1,0:T(8,128)S(1)}, u32[]{:S(2)}, u32[]{:S(2)}) %collective-permute-start.11) | collective-permute-done | bytes 131104 | tf_op jit(solution)/shard_map/ppermute | solution.py:26
  39.5 0.0 copy-done
  39.5 0.0 copy-done.1
  39.5 0.0 copy-done.2
  39.5 6.3 %shard_map.61 = bf16[1024,1024]{1,0:T(8,128)(2,1)} custom-call(s32[2]{0:T(128)S(1)} %pad_add_fusion.place, bf16[1024,1024]{1,0:T(8,128)(2,1)S(1)} %copy-done, f32[16,8,1024]{2,1,0:T(8,128)S(1)} %copy-done.1, f32[1024,1024]{1,0:T(8,128)S(1)} %shard_map.60.near, f32[3,256,128]{2,1,0:T(8,128)S(1)} %pad_maximum_fusion.early, ...), custom_call_target="tpu_custom_call" | custom-call | flops 2684354560 | bytes 12582912 | tf_op jit(solution)/shard_map/pallas_call | solution.py:328
  (11 shorter events, 0.2 us)
Async XLA Ops:
  2.4 2.3 %collective-permute-start = (f32[512,128]{1,0:T(8,128)S(1)}, f32[512,128]{1,0:T(8,128)S(1)}, u32[]{:S(2)}, u32[]{:S(2)}) collective-permute-start(f32[512,128]{1,0:T(8,128)S(1)} %shard_map.56), channel_id=1, source_target_pairs={{0,1},{1,0},{2,3},{3,2},{4,5},{5,4},{6,7},{7,6},{8,9},{9,8},{10,11... | collective-permute-start | bytes 786440 | tf_op jit(solution)/shard_map/ppermute | solution.py:26
  4.7 7.2 %collective-permute-start.1 = (f32[256,128]{1,0:T(8,128)S(1)}, f32[256,128]{1,0:T(8,128)S(1)}, u32[]{:S(2)}, u32[]{:S(2)}) collective-permute-start(f32[256,128]{1,0:T(8,128)S(1)} %dynamic-slice_add_fusion), channel_id=1, source_target_pairs={{0,2},{1,3},{2,0},{3,1},{4,6},{5,7},{6,4},{7,5},{8,10},{9,11},{10,... | collective-permute-start | bytes 393224 | tf_op jit(solution)/shard_map/ppermute | solution.py:26
  12.0 6.2 %collective-permute-start.2 = (f32[256,128]{1,0:T(8,128)S(1)}, f32[256,128]{1,0:T(8,128)S(1)}, u32[]{:S(2)}, u32[]{:S(2)}) collective-permute-start(f32[256,128]{1,0:T(8,128)S(1)} %get-tuple-element.35), channel_id=1, source_target_pairs={{0,4},{1,5},{2,6},{3,7},{4,0},{5,1},{6,2},{7,3},{8,12},{9,13},{10,... | collective-permute-start | bytes 393224 | tf_op jit(solution)/shard_map/ppermute | solution.py:26
  18.2 5.4 %collective-permute-start.3 = (f32[256,128]{1,0:T(8,128)S(1)}, f32[256,128]{1,0:T(8,128)S(1)}, u32[]{:S(2)}, u32[]{:S(2)}) collective-permute-start(f32[256,128]{1,0:T(8,128)S(1)} %add.31), channel_id=1, source_target_pairs={{0,8},{8,0},{16,24},{24,16},{1,9},{9,1},{17,25},{25,17},{2,10},{10... | collective-permute-start | bytes 393224 | tf_op jit(solution)/shard_map/ppermute | solution.py:26
  19.9 7.2 %collective-permute-start.6 = (f32[256,128]{1,0:T(8,128)S(1)}, f32[256,128]{1,0:T(8,128)S(1)}, u32[]{:S(2)}, u32[]{:S(2)}) collective-permute-start(f32[256,128]{1,0:T(8,128)S(1)} %get-tuple-element.43), channel_id=1, source_target_pairs={{0,2},{1,3},{2,0},{3,1},{4,6},{5,7},{6,4},{7,5},{8,10},{9,11},{10,... | collective-permute-start | bytes 393224 | tf_op jit(solution)/shard_map/ppermute | solution.py:26
  21.2 6.7 %collective-permute-start.7 = (f32[256,128]{1,0:T(8,128)S(1)}, f32[256,128]{1,0:T(8,128)S(1)}, u32[]{:S(2)}, u32[]{:S(2)}) collective-permute-start(f32[256,128]{1,0:T(8,128)S(1)} %collective-permute-done.2.rest_3_), channel_id=1, source_target_pairs={{0,2},{1,3},{2,0},{3,1},{4,6},{5,7},{6,4},{7,5},{8,10},{9,11},{10,... | collective-permute-start | bytes 393224 | tf_op jit(solution)/shard_map/ppermute | solution.py:26
  23.6 8.2 %collective-permute-start.4 = (f32[256,128]{1,0:T(8,128)S(1)}, f32[256,128]{1,0:T(8,128)S(1)}, u32[]{:S(2)}, u32[]{:S(2)}) collective-permute-start(f32[256,128]{1,0:T(8,128)S(1)} %add.32), channel_id=1, source_target_pairs={{0,16},{8,24},{16,0},{24,8},{1,17},{9,25},{17,1},{25,9},{2,18},{10... | collective-permute-start | bytes 393224 | tf_op jit(solution)/shard_map/ppermute | solution.py:26
  26.3 5.6 %collective-permute-start.5 = (f32[256,128]{1,0:T(8,128)S(1)}, f32[256,128]{1,0:T(8,128)S(1)}, u32[]{:S(2)}, u32[]{:S(2)}) collective-permute-start(f32[256,128]{1,0:T(8,128)S(1)} %collective-permute-done.3), channel_id=1, source_target_pairs={{0,2},{1,3},{2,0},{3,1},{4,6},{5,7},{6,4},{7,5},{8,10},{9,11},{10,... | collective-permute-start | bytes 393224 | tf_op jit(solution)/shard_map/ppermute | solution.py:26
  31.9 2.4 %collective-permute-start.9 = (f32[6,256,128]{2,1,0:T(8,128)S(1)}, f32[6,256,128]{2,1,0:T(8,128)S(1)}, u32[]{:S(2)}, u32[]{:S(2)}) collective-permute-start(f32[6,256,128]{2,1,0:T(8,128)S(1)} %bitcast_dynamic-update-slice_fusion), channel_id=1, source_target_pairs={{0,1},{1,0},{2,3},{3,2},{4,5},{5,4},{6,7},{7,6},{8,9},{9,8},{10,11... | collective-permute-start | bytes 2359304 | tf_op jit(solution)/shard_map/ppermute | solution.py:26
  32.0 7.4 %copy-start = (bf16[1024,1024]{1,0:T(8,128)(2,1)S(1)}, bf16[1024,1024]{1,0:T(8,128)(2,1)}, u32[]{:S(2)}) copy-start(bf16[1024,1024]{1,0:T(8,128)(2,1)} %queries.8) | copy-start | bytes 6291460
  32.0 7.4 %copy-start.1 = (f32[16,8,1024]{2,1,0:T(8,128)S(1)}, f32[16,8,1024]{2,1,0:T(8,128)}, u32[]{:S(2)}) copy-start(f32[16,8,1024]{2,1,0:T(8,128)} %weights.8) | copy-start | bytes 1572868
  32.1 7.4 %copy-start.2 = (bf16[1024,1024]{1,0:T(8,128)(2,1)S(1)}, bf16[1024,1024]{1,0:T(8,128)(2,1)}, u32[]{:S(2)}) copy-start(bf16[1024,1024]{1,0:T(8,128)(2,1)} %out_weight.1) | copy-start | bytes 6291460
  32.1 6.0 %collective-permute-start.10 = (f32[3,256,128]{2,1,0:T(8,128)S(1)}, f32[3,256,128]{2,1,0:T(8,128)S(1)}, u32[]{:S(2)}, u32[]{:S(2)}) collective-permute-start(f32[3,256,128]{2,1,0:T(8,128)S(1)} %pad_maximum_fusion.early), channel_id=1, source_target_pairs={{0,1},{1,0},{2,3},{3,2},{4,5},{5,4},{6,7},{7,6},{8,9},{9,8},{10,11... | collective-permute-start | bytes 1179656 | tf_op jit(solution)/shard_map/ppermute | solution.py:26
  32.6 5.5 %collective-permute-start.8 = (f32[256,128]{1,0:T(8,128)S(1)}, f32[256,128]{1,0:T(8,128)S(1)}, u32[]{:S(2)}, u32[]{:S(2)}) collective-permute-start(f32[256,128]{1,0:T(8,128)S(1)} %collective-permute-done.4), channel_id=1, source_target_pairs={{0,2},{1,3},{2,0},{3,1},{4,6},{5,7},{6,4},{7,5},{8,10},{9,11},{10,... | collective-permute-start | bytes 393224 | tf_op jit(solution)/shard_map/ppermute | solution.py:26
  38.1 1.3 %collective-permute-start.11 = (f32[256,128]{1,0:T(8,128)S(1)}, f32[256,128]{1,0:T(8,128)S(1)}, u32[]{:S(2)}, u32[]{:S(2)}) collective-permute-start(f32[256,128]{1,0:T(8,128)S(1)} %collective-permute-done.8.late), channel_id=1, source_target_pairs={{0,1},{1,0},{2,3},{3,2},{4,5},{5,4},{6,7},{7,6},{8,9},{9,8},{10,11... | collective-permute-start | bytes 393224 | tf_op jit(solution)/shard_map/ppermute | solution.py:26
